TPU v7x, 32 devices: a whole 2x2x4 slice. The times are simulated.
32 devices in a mesh: gz: 16 (over z, y, x), gy: 2 (over core).
Axes of the slice: x: 2, y: 2, z: 4, core: 2. Of those that a mesh axis runs over, the one named last changes fastest.
Arguments:
- starting_densities: float32 [16, 4, 128, 128], P(None, 'gy', 'gz'), may hold values from -3 to 5
- medium_admittance: float32 [4, 128, 128], P('gy', 'gz'), may hold values from 0.25 to 2
- local_warmth: float32 [4, 128, 128], P('gy', 'gz'), may hold values from 0.5 to 2
- spreading_coefficient: float32 [16], replicated, may hold values from 1 to 8
- frequency_factors: float32 [16], replicated, may hold values from 0.5 to 2
- barrier_energies: float32 [16], replicated, may hold values from 1 to 4
- molar_proportions: float32 [16, 16], replicated, may hold values from -1.5 to 1.5
Outputs:
- updated: float32 [16, 4, 128, 128], P(None, 'gy', 'gz')
All inputs are finite; a program needn't handle non-finite values.
Results may differ from a plain program's by a relative error of at most 0.0003.
Values sent between devices are 32-bit elements; how exact they have to be, the bound alone decides.
No kernel may reach another device: no remote copies, remote signals or barrier semaphores. Data moves between devices by JAX's collectives and lax.ppermute only.
A program may use at most 64 MiB of HBM per device.

v0:
```python
import jax
import jax.numpy as jnp
from jax import lax
from jax.sharding import PartitionSpec as P

STEPS = 2


def passed_along(x, axis, by):
    count = lax.axis_size(axis)
    pairs = [(i, i + by) for i in range(count) if 0 <= i + by < count]
    return lax.ppermute(x, axis, pairs)


def extended(block, sides, width):
    for axis, dim in sides:
        count = lax.axis_size(axis)
        forward = [(i, i + 1) for i in range(count - 1)]
        backward = [(target, source) for source, target in forward]
        low = lax.ppermute(
            lax.slice_in_dim(block, block.shape[dim] - width, None, axis=dim), axis, forward
        )
        high = lax.ppermute(lax.slice_in_dim(block, 0, width, axis=dim), axis, backward)
        block = jnp.concatenate([low, block, high], axis=dim)
    return block


def moved(values, offset, along):
    length = values.shape[along]
    extent = list(values.shape)
    extent[along] = abs(offset)
    filler = jnp.zeros(extent, values.dtype)
    if offset > 0:
        return jnp.concatenate(
            [filler, lax.slice_in_dim(values, 0, length - offset, axis=along)], axis=along
        )
    return jnp.concatenate(
        [lax.slice_in_dim(values, -offset, length, axis=along), filler], axis=along
    )


def cyclic_reduce(lower, upper, right, along):
    length = lower.shape[along]
    stride = 1
    while stride < length:
        lower_below = moved(lower, stride, along)
        upper_below = moved(upper, stride, along)
        right_below = moved(right, stride, along + 1)
        lower_above = moved(lower, -stride, along)
        upper_above = moved(upper, -stride, along)
        right_above = moved(right, -stride, along + 1)
        scaling = 1.0 / (1.0 - lower * upper_below - upper * lower_above)
        right = (right - lower * right_below - upper * right_above) * scaling
        lower, upper = (-lower * lower_below * scaling, -upper * upper_above * scaling)
        stride *= 2
    return right


def directional(field, after, before, k_after, k_before, rate):
    return rate * (k_after * (after - field) - k_before * (field - before))


def line_solve(lower, upper, right):
    length = lower.shape[2]
    rows = lax.broadcasted_iota(jnp.int32, (1, 1, length, 1), 2)
    inner_lower = jnp.where((rows == 0) | (rows == length - 1), 0.0, lower)
    inner_upper = jnp.where(rows >= length - 2, 0.0, upper)
    targets = jnp.stack(
        [
            jnp.where(rows == length - 1, 0.0, right),
            jnp.where(rows == 0, lower, 0.0),
            jnp.where(rows == length - 2, upper, 0.0),
        ]
    )
    solved = cyclic_reduce(inner_lower, inner_upper, targets, 2)
    following = passed_along(solved[:, :, :, 0], "gz", -1)
    interior_final = solved[:, :, :, length - 2]
    last_lower = lower[:, :, length - 1]
    last_upper = upper[:, :, length - 1]
    last_right = right[:, :, length - 1]
    center = 1.0 - last_lower * interior_final[2] - last_upper * following[1]
    red_lower = -last_lower * interior_final[1] / center
    red_upper = -last_upper * following[2] / center
    red_right = (last_right - last_lower * interior_final[0] - last_upper * following[0]) / center
    devices = lax.axis_size("gz")
    stride = 1
    while stride < devices:
        packed = jnp.stack([red_lower, red_upper, red_right])
        below = passed_along(packed, "gz", stride)
        above = passed_along(packed, "gz", -stride)
        scaling = 1.0 / (1.0 - red_lower * below[1] - red_upper * above[0])
        red_right = (red_right - red_lower * below[2] - red_upper * above[2]) * scaling
        red_lower, red_upper = (-red_lower * below[0] * scaling, -red_upper * above[1] * scaling)
        stride *= 2
    previous_last = passed_along(red_right, "gz", 1)
    result = solved[0] - solved[1] * previous_last[:, :, None] - solved[2] * red_right[:, :, None]
    return jnp.concatenate([result[:, :, : length - 1], red_right[:, :, None]], axis=2)


def per_device(
    starting_densities,
    medium_admittance,
    local_warmth,
    spreading_coefficient,
    frequency_factors,
    barrier_energies,
    molar_proportions,
):
    species = starting_densities.shape[0]
    transfer_rate_x = (8.0 * spreading_coefficient)[:, None, None, None]
    rate_y = (0.015 * spreading_coefficient)[:, None, None, None]
    rate_z = (4096.0 * spreading_coefficient)[:, None, None, None]
    arrhenius = frequency_factors[:, None, None, None] * jnp.exp(
        barrier_energies[:, None, None, None] * (1.0 - 1.0 / local_warmth)[None]
    )
    kx_after = 0.5 * (medium_admittance + moved(medium_admittance, -1, 2))
    kx_before = 0.5 * (medium_admittance + moved(medium_admittance, 1, 2))
    main_diagonal_x = 1.0 + 0.5 * transfer_rate_x * (kx_after + kx_before)
    lower_x = -0.5 * transfer_rate_x * kx_before / main_diagonal_x
    upper_x = -0.5 * transfer_rate_x * kx_after / main_diagonal_x
    current = starting_densities
    for number in range(STEPS):
        stacked = jnp.concatenate([current, medium_admittance[None]], axis=0)
        padded = extended(stacked, (("gz", 2), ("gy", 1)), 1)
        kappa_pad = padded[species]
        field_pad = padded[:species]
        ky_after = 0.5 * (medium_admittance + kappa_pad[2:, 1:-1])
        ky_before = 0.5 * (medium_admittance + kappa_pad[:-2, 1:-1])
        kz_after = 0.5 * (medium_admittance + kappa_pad[1:-1, 2:])
        kz_before = 0.5 * (medium_admittance + kappa_pad[1:-1, :-2])
        lap_x = directional(
            current,
            moved(current, -1, 3),
            moved(current, 1, 3),
            kx_after,
            kx_before,
            transfer_rate_x,
        )
        lap_y = directional(
            current, field_pad[:, 2:, 1:-1], field_pad[:, :-2, 1:-1], ky_after, ky_before, rate_y
        )
        lap_z = directional(
            current, field_pad[:, 1:-1, 2:], field_pad[:, 1:-1, :-2], kz_after, kz_before, rate_z
        )
        source = jnp.einsum(
            "sq,qyzx->syzx",
            molar_proportions,
            arrhenius * jnp.tanh(current),
            precision=lax.Precision.HIGHEST,
        )
        first_rhs = current + 0.5 * lap_x + lap_y + lap_z + source
        section = cyclic_reduce(lower_x, upper_x, (first_rhs / main_diagonal_x)[None], 3)[0]
        second_rhs = section - 0.5 * lap_z
        diag_z = 1.0 + 0.5 * rate_z * (kz_after + kz_before)
        current = line_solve(
            -0.5 * rate_z * kz_before / diag_z,
            -0.5 * rate_z * kz_after / diag_z,
            second_rhs / diag_z,
        )
    return current


def solution(mesh):
    return jax.shard_map(
        per_device,
        mesh=mesh,
        in_specs=(
            P(None, "gy", "gz", None),
            P("gy", "gz", None),
            P("gy", "gz", None),
            P(),
            P(),
            P(),
            P(),
        ),
        out_specs=P(None, "gy", "gz", None),
        check_vma=False,
    )
```

profile of v0, /device:TPU:24, one launch (start us, length us, event | category | flops | bytes accessed | tf_op | source)
XLA Modules:
  0.0 168.0 jit_solution(16330728561752668428)
XLA Ops:
  0.0 0.8 fusion.301
  2.9 1.2 tanh_multiply_fusion.1
  4.1 4.2 %collective-permute-start.1 = (f32[17,2,1,128]{3,1,0,2:T(2,128)S(1)}, f32[17,2,1,128]{3,1,0,2:T(2,128)S(1)}, u32[]{:S(2)}, u32[]{:S(2)}) collective-permute-start(f32[17,2,1,128]{3,1,0,2:T(2,128)S(1)} %get-tuple-element.103), channel_id=1, source_target_pairs={{2,0},{4,2},{6,4},{8,6},{10,8},{12,10},{14,12},{16,14},{18,16},{20... | collective-permute-start | bytes 52232 | tf_op jit(solution)/shard_map/ppermute | solution.py:23
  8.4 1.9 %collective-permute-start = (f32[17,2,1,128]{3,1,0,2:T(2,128)S(1)}, f32[17,2,1,128]{3,1,0,2:T(2,128)S(1)}, u32[]{:S(2)}, u32[]{:S(2)}) collective-permute-start(f32[17,2,1,128]{3,1,0,2:T(2,128)S(1)} %get-tuple-element.102), channel_id=1, source_target_pairs={{0,2},{2,4},{4,6},{6,8},{8,10},{10,12},{12,14},{14,16},{16,18},{18... | collective-permute-start | bytes 52232 | tf_op jit(solution)/shard_map/ppermute | solution.py:20
  12.0 3.9 %collective-permute-done = f32[17,2,1,128]{3,1,0,2:T(2,128)S(1)} collective-permute-done((f32[17,2,1,128]{3,1,0,2:T(2,128)S(1)}, f32[17,2,1,128]{3,1,0,2:T(2,128)S(1)}, u32[]{:S(2)}, u32[]{:S(2)}) %collective-permute-start) | collective-permute-done | bytes 17440 | tf_op jit(solution)/shard_map/ppermute | solution.py:20
  16.0 1.3 collective-permute-start.3
  17.3 3.0 %collective-permute-start.2 = (f32[17,1,10,128]{3,1,2,0:T(1,128)S(1)}, f32[17,1,10,128]{3,1,2,0:T(1,128)S(1)}, u32[]{:S(2)}, u32[]{:S(2)}) collective-permute-start(f32[17,1,10,128]{3,1,2,0:T(1,128)S(1)} %get-tuple-element.96), channel_id=1, source_target_pairs={{0,1},{2,3},{4,5},{6,7},{8,9},{10,11},{12,13},{14,15},{16,17},{18,... | collective-permute-start | bytes 261128 | tf_op jit(solution)/shard_map/ppermute | solution.py:20
  20.3 0.9 collective-permute-done.2
  21.3 0.8 fusion.80
  35.3 1.9 %collective-permute-start.4 = (f32[3,16,2,128]{3,2,1,0:T(2,128)S(1)}, f32[3,16,2,128]{3,2,1,0:T(2,128)S(1)}, u32[]{:S(2)}, u32[]{:S(2)}) collective-permute-start(f32[3,16,2,128]{3,2,1,0:T(2,128)S(1)} %slice_bitcast_fusion.7), channel_id=1, source_target_pairs={{2,0},{4,2},{6,4},{8,6},{10,8},{12,10},{14,12},{16,14},{18,16},{20... | collective-permute-start | bytes 147464 | tf_op jit(solution)/shard_map/ppermute | solution.py:12
  37.2 4.1 %collective-permute-done.4 = f32[3,16,2,128]{3,2,1,0:T(2,128)S(1)} collective-permute-done((f32[3,16,2,128]{3,2,1,0:T(2,128)S(1)}, f32[3,16,2,128]{3,2,1,0:T(2,128)S(1)}, u32[]{:S(2)}, u32[]{:S(2)}) %collective-permute-start.4) | collective-permute-done | bytes 49184 | tf_op jit(solution)/shard_map/ppermute | solution.py:12
  41.4 3.9 %collective-permute-start.6 = (f32[3,16,2,128]{3,2,1,0:T(2,128)S(1)}, f32[3,16,2,128]{3,2,1,0:T(2,128)S(1)}, u32[]{:S(2)}, u32[]{:S(2)}) collective-permute-start(f32[3,16,2,128]{3,2,1,0:T(2,128)S(1)} %pad_maximum_fusion.19), channel_id=1, source_target_pairs={{2,0},{4,2},{6,4},{8,6},{10,8},{12,10},{14,12},{16,14},{18,16},{20... | collective-permute-start | bytes 147464 | tf_op jit(solution)/shard_map/ppermute | solution.py:12
  45.3 1.9 %collective-permute-start.5 = (f32[3,16,2,128]{3,2,1,0:T(2,128)S(1)}, f32[3,16,2,128]{3,2,1,0:T(2,128)S(1)}, u32[]{:S(2)}, u32[]{:S(2)}) collective-permute-start(f32[3,16,2,128]{3,2,1,0:T(2,128)S(1)} %pad_maximum_fusion.19), channel_id=1, source_target_pairs={{0,2},{2,4},{4,6},{6,8},{8,10},{10,12},{12,14},{14,16},{16,18},{18... | collective-permute-start | bytes 147464 | tf_op jit(solution)/shard_map/ppermute | solution.py:12
  47.4 5.7 %collective-permute-done.5 = f32[3,16,2,128]{3,2,1,0:T(2,128)S(1)} collective-permute-done((f32[3,16,2,128]{3,2,1,0:T(2,128)S(1)}, f32[3,16,2,128]{3,2,1,0:T(2,128)S(1)}, u32[]{:S(2)}, u32[]{:S(2)}) %collective-permute-start.5) | collective-permute-done | bytes 49184 | tf_op jit(solution)/shard_map/ppermute | solution.py:12
  53.2 1.9 %collective-permute-start.8 = (f32[3,16,2,128]{3,2,1,0:T(2,128)S(1)}, f32[3,16,2,128]{3,2,1,0:T(2,128)S(1)}, u32[]{:S(2)}, u32[]{:S(2)}) collective-permute-start(f32[3,16,2,128]{3,2,1,0:T(2,128)S(1)} %pad_maximum_fusion.20), channel_id=1, source_target_pairs={{4,0},{6,2},{8,4},{10,6},{12,8},{14,10},{16,12},{18,14},{20,16},{2... | collective-permute-start | bytes 147464 | tf_op jit(solution)/shard_map/ppermute | solution.py:12
  55.1 3.9 %collective-permute-start.7 = (f32[3,16,2,128]{3,2,1,0:T(2,128)S(1)}, f32[3,16,2,128]{3,2,1,0:T(2,128)S(1)}, u32[]{:S(2)}, u32[]{:S(2)}) collective-permute-start(f32[3,16,2,128]{3,2,1,0:T(2,128)S(1)} %pad_maximum_fusion.20), channel_id=1, source_target_pairs={{0,4},{2,6},{4,8},{6,10},{8,12},{10,14},{12,16},{14,18},{16,20},{1... | collective-permute-start | bytes 147464 | tf_op jit(solution)/shard_map/ppermute | solution.py:12
  59.7 2.3 %collective-permute-done.7 = f32[3,16,2,128]{3,2,1,0:T(2,128)S(1)} collective-permute-done((f32[3,16,2,128]{3,2,1,0:T(2,128)S(1)}, f32[3,16,2,128]{3,2,1,0:T(2,128)S(1)}, u32[]{:S(2)}, u32[]{:S(2)}) %collective-permute-start.7) | collective-permute-done | bytes 49184 | tf_op jit(solution)/shard_map/ppermute | solution.py:12
  62.1 1.3 collective-permute-start.9
  63.4 4.5 %collective-permute-start.10 = (f32[3,16,2,128]{3,2,1,0:T(2,128)S(1)}, f32[3,16,2,128]{3,2,1,0:T(2,128)S(1)}, u32[]{:S(2)}, u32[]{:S(2)}) collective-permute-start(f32[3,16,2,128]{3,2,1,0:T(2,128)S(1)} %pad_maximum_fusion.21), channel_id=1, source_target_pairs={{8,0},{10,2},{12,4},{14,6},{16,8},{18,10},{20,12},{22,14},{24,16},... | collective-permute-start | bytes 147464 | tf_op jit(solution)/shard_map/ppermute | solution.py:12
  68.1 1.6 collective-permute-done.10
  69.8 4.1 %collective-permute-start.12 = (f32[3,16,2,128]{3,2,1,0:T(2,128)S(1)}, f32[3,16,2,128]{3,2,1,0:T(2,128)S(1)}, u32[]{:S(2)}, u32[]{:S(2)}) collective-permute-start(f32[3,16,2,128]{3,2,1,0:T(2,128)S(1)} %pad_maximum_fusion.22), channel_id=1, source_target_pairs={{16,0},{18,2},{20,4},{22,6},{24,8},{26,10},{28,12},{30,14},{17,1},... | collective-permute-start | bytes 147464 | tf_op jit(solution)/shard_map/ppermute | solution.py:12
  74.0 1.3 collective-permute-start.11
  75.7 5.6 %collective-permute-done.11 = f32[3,16,2,128]{3,2,1,0:T(2,128)S(1)} collective-permute-done((f32[3,16,2,128]{3,2,1,0:T(2,128)S(1)}, f32[3,16,2,128]{3,2,1,0:T(2,128)S(1)}, u32[]{:S(2)}, u32[]{:S(2)}) %collective-permute-start.11) | collective-permute-done | bytes 49184 | tf_op jit(solution)/shard_map/ppermute | solution.py:12
  81.4 2.1 %collective-permute-start.13 = (f32[16,2,128]{2,1,0:T(2,128)S(1)}, f32[16,2,128]{2,1,0:T(2,128)S(1)}, u32[]{:S(2)}, u32[]{:S(2)}) collective-permute-start(f32[16,2,128]{2,1,0:T(2,128)S(1)} %divide_multiply_fusion.2), channel_id=1, source_target_pairs={{0,2},{2,4},{4,6},{6,8},{8,10},{10,12},{12,14},{14,16},{16,18},{18... | collective-permute-start | bytes 49160 | tf_op jit(solution)/shard_map/ppermute | solution.py:12
  83.8 5.1 %collective-permute-done.13 = f32[16,2,128]{2,1,0:T(2,128)S(1)} collective-permute-done((f32[16,2,128]{2,1,0:T(2,128)S(1)}, f32[16,2,128]{2,1,0:T(2,128)S(1)}, u32[]{:S(2)}, u32[]{:S(2)}) %collective-permute-start.13) | collective-permute-done | bytes 16416 | tf_op jit(solution)/shard_map/ppermute | solution.py:12
  89.3 1.9 %collective-permute-start.15 = (f32[17,2,1,128]{3,1,0,2:T(2,128)S(1)}, f32[17,2,1,128]{3,1,0,2:T(2,128)S(1)}, u32[]{:S(2)}, u32[]{:S(2)}) collective-permute-start(f32[17,2,1,128]{3,1,0,2:T(2,128)S(1)} %get-tuple-element.101), channel_id=1, source_target_pairs={{2,0},{4,2},{6,4},{8,6},{10,8},{12,10},{14,12},{16,14},{18,16},{20... | collective-permute-start | bytes 52232 | tf_op jit(solution)/shard_map/ppermute | solution.py:23
  91.2 3.9 %collective-permute-start.14 = (f32[17,2,1,128]{3,1,0,2:T(2,128)S(1)}, f32[17,2,1,128]{3,1,0,2:T(2,128)S(1)}, u32[]{:S(2)}, u32[]{:S(2)}) collective-permute-start(f32[17,2,1,128]{3,1,0,2:T(2,128)S(1)} %get-tuple-element.100), channel_id=1, source_target_pairs={{0,2},{2,4},{4,6},{6,8},{8,10},{10,12},{12,14},{14,16},{16,18},{18... | collective-permute-start | bytes 52232 | tf_op jit(solution)/shard_map/ppermute | solution.py:20
  95.5 3.2 %collective-permute-done.14 = f32[17,2,1,128]{3,1,0,2:T(2,128)S(1)} collective-permute-done((f32[17,2,1,128]{3,1,0,2:T(2,128)S(1)}, f32[17,2,1,128]{3,1,0,2:T(2,128)S(1)}, u32[]{:S(2)}, u32[]{:S(2)}) %collective-permute-start.14) | collective-permute-done | bytes 17440 | tf_op jit(solution)/shard_map/ppermute | solution.py:20
  98.9 1.3 collective-permute-start.17
  100.2 3.0 %collective-permute-start.16 = (f32[17,1,10,128]{3,1,0,2:T(1,128)S(1)}, f32[17,1,10,128]{3,1,0,2:T(1,128)S(1)}, u32[]{:S(2)}, u32[]{:S(2)}) collective-permute-start(f32[17,1,10,128]{3,1,0,2:T(1,128)S(1)} %get-tuple-element.94), channel_id=1, source_target_pairs={{0,1},{2,3},{4,5},{6,7},{8,9},{10,11},{12,13},{14,15},{16,17},{18,... | collective-permute-start | bytes 261128 | tf_op jit(solution)/shard_map/ppermute | solution.py:20
  114.3 1.9 %collective-permute-start.18 = (f32[3,16,2,128]{3,2,1,0:T(2,128)S(1)}, f32[3,16,2,128]{3,2,1,0:T(2,128)S(1)}, u32[]{:S(2)}, u32[]{:S(2)}) collective-permute-start(f32[3,16,2,128]{3,2,1,0:T(2,128)S(1)} %slice_bitcast_fusion.6), channel_id=1, source_target_pairs={{2,0},{4,2},{6,4},{8,6},{10,8},{12,10},{14,12},{16,14},{18,16},{20... | collective-permute-start | bytes 147464 | tf_op jit(solution)/shard_map/ppermute | solution.py:12
  116.2 4.0 %collective-permute-done.18 = f32[3,16,2,128]{3,2,1,0:T(2,128)S(1)} collective-permute-done((f32[3,16,2,128]{3,2,1,0:T(2,128)S(1)}, f32[3,16,2,128]{3,2,1,0:T(2,128)S(1)}, u32[]{:S(2)}, u32[]{:S(2)}) %collective-permute-start.18) | collective-permute-done | bytes 49184 | tf_op jit(solution)/shard_map/ppermute | solution.py:12
  120.4 3.9 %collective-permute-start.20 = (f32[3,16,2,128]{3,2,1,0:T(2,128)S(1)}, f32[3,16,2,128]{3,2,1,0:T(2,128)S(1)}, u32[]{:S(2)}, u32[]{:S(2)}) collective-permute-start(f32[3,16,2,128]{3,2,1,0:T(2,128)S(1)} %pad_maximum_fusion.23), channel_id=1, source_target_pairs={{2,0},{4,2},{6,4},{8,6},{10,8},{12,10},{14,12},{16,14},{18,16},{20... | collective-permute-start | bytes 147464 | tf_op jit(solution)/shard_map/ppermute | solution.py:12
  124.3 1.9 %collective-permute-start.19 = (f32[3,16,2,128]{3,2,1,0:T(2,128)S(1)}, f32[3,16,2,128]{3,2,1,0:T(2,128)S(1)}, u32[]{:S(2)}, u32[]{:S(2)}) collective-permute-start(f32[3,16,2,128]{3,2,1,0:T(2,128)S(1)} %pad_maximum_fusion.23), channel_id=1, source_target_pairs={{0,2},{2,4},{4,6},{6,8},{8,10},{10,12},{12,14},{14,16},{16,18},{18... | collective-permute-start | bytes 147464 | tf_op jit(solution)/shard_map/ppermute | solution.py:12
  126.3 5.7 %collective-permute-done.19 = f32[3,16,2,128]{3,2,1,0:T(2,128)S(1)} collective-permute-done((f32[3,16,2,128]{3,2,1,0:T(2,128)S(1)}, f32[3,16,2,128]{3,2,1,0:T(2,128)S(1)}, u32[]{:S(2)}, u32[]{:S(2)}) %collective-permute-start.19) | collective-permute-done | bytes 49184 | tf_op jit(solution)/shard_map/ppermute | solution.py:12
  132.2 1.9 %collective-permute-start.22 = (f32[3,16,2,128]{3,2,1,0:T(2,128)S(1)}, f32[3,16,2,128]{3,2,1,0:T(2,128)S(1)}, u32[]{:S(2)}, u32[]{:S(2)}) collective-permute-start(f32[3,16,2,128]{3,2,1,0:T(2,128)S(1)} %pad_maximum_fusion.24), channel_id=1, source_target_pairs={{4,0},{6,2},{8,4},{10,6},{12,8},{14,10},{16,12},{18,14},{20,16},{2... | collective-permute-start | bytes 147464 | tf_op jit(solution)/shard_map/ppermute | solution.py:12
  134.1 3.9 %collective-permute-start.21 = (f32[3,16,2,128]{3,2,1,0:T(2,128)S(1)}, f32[3,16,2,128]{3,2,1,0:T(2,128)S(1)}, u32[]{:S(2)}, u32[]{:S(2)}) collective-permute-start(f32[3,16,2,128]{3,2,1,0:T(2,128)S(1)} %pad_maximum_fusion.24), channel_id=1, source_target_pairs={{0,4},{2,6},{4,8},{6,10},{8,12},{10,14},{12,16},{14,18},{16,20},{1... | collective-permute-start | bytes 147464 | tf_op jit(solution)/shard_map/ppermute | solution.py:12
  138.7 2.3 %collective-permute-done.21 = f32[3,16,2,128]{3,2,1,0:T(2,128)S(1)} collective-permute-done((f32[3,16,2,128]{3,2,1,0:T(2,128)S(1)}, f32[3,16,2,128]{3,2,1,0:T(2,128)S(1)}, u32[]{:S(2)}, u32[]{:S(2)}) %collective-permute-start.21) | collective-permute-done | bytes 49184 | tf_op jit(solution)/shard_map/ppermute | solution.py:12
  141.1 1.3 collective-permute-start.23
  142.4 4.5 %collective-permute-start.24 = (f32[3,16,2,128]{3,2,1,0:T(2,128)S(1)}, f32[3,16,2,128]{3,2,1,0:T(2,128)S(1)}, u32[]{:S(2)}, u32[]{:S(2)}) collective-permute-start(f32[3,16,2,128]{3,2,1,0:T(2,128)S(1)} %pad_maximum_fusion.25), channel_id=1, source_target_pairs={{8,0},{10,2},{12,4},{14,6},{16,8},{18,10},{20,12},{22,14},{24,16},... | collective-permute-start | bytes 147464 | tf_op jit(solution)/shard_map/ppermute | solution.py:12
  147.1 1.6 collective-permute-done.24
  148.8 3.8 %collective-permute-start.26 = (f32[3,16,2,128]{3,2,1,0:T(2,128)S(1)}, f32[3,16,2,128]{3,2,1,0:T(2,128)S(1)}, u32[]{:S(2)}, u32[]{:S(2)}) collective-permute-start(f32[3,16,2,128]{3,2,1,0:T(2,128)S(1)} %pad_maximum_fusion.26), channel_id=1, source_target_pairs={{16,0},{18,2},{20,4},{22,6},{24,8},{26,10},{28,12},{30,14},{17,1},... | collective-permute-start | bytes 147464 | tf_op jit(solution)/shard_map/ppermute | solution.py:12
  152.5 1.3 collective-permute-start.25
  154.3 5.2 %collective-permute-done.25 = f32[3,16,2,128]{3,2,1,0:T(2,128)S(1)} collective-permute-done((f32[3,16,2,128]{3,2,1,0:T(2,128)S(1)}, f32[3,16,2,128]{3,2,1,0:T(2,128)S(1)}, u32[]{:S(2)}, u32[]{:S(2)}) %collective-permute-start.25) | collective-permute-done | bytes 49184 | tf_op jit(solution)/shard_map/ppermute | solution.py:12
  159.6 2.1 %collective-permute-start.27 = (f32[16,2,128]{2,1,0:T(2,128)S(1)}, f32[16,2,128]{2,1,0:T(2,128)S(1)}, u32[]{:S(2)}, u32[]{:S(2)}) collective-permute-start(f32[16,2,128]{2,1,0:T(2,128)S(1)} %divide_multiply_fusion), channel_id=1, source_target_pairs={{0,2},{2,4},{4,6},{6,8},{8,10},{10,12},{12,14},{14,16},{16,18},{18... | collective-permute-start | bytes 49160 | tf_op jit(solution)/shard_map/ppermute | solution.py:12
  161.9 0.7 slice-done
  162.8 4.3 %collective-permute-done.27 = f32[16,2,128]{2,1,0:T(2,128)S(1)} collective-permute-done((f32[16,2,128]{2,1,0:T(2,128)S(1)}, f32[16,2,128]{2,1,0:T(2,128)S(1)}, u32[]{:S(2)}, u32[]{:S(2)}) %collective-permute-start.27) | collective-permute-done | bytes 16416 | tf_op jit(solution)/shard_map/ppermute | solution.py:12
  167.2 0.7 copy.496
  (202 shorter events, 32.7 us)
Async XLA Ops:
  0.0 11.7 %copy-start = (f32[16,16]{1,0:T(8,128)S(1)}, f32[16,16]{1,0:T(8,128)}, u32[]{:S(2)}) copy-start(f32[16,16]{1,0:T(8,128)} %param.13) | copy-start | bytes 3076
  0.9 0.7 copy-start.3
  1.6 0.7 copy-start.1
  2.3 0.7 copy-start.4
  2.3 0.7 copy-start.5
  4.1 7.8 %collective-permute-start.1 = (f32[17,2,1,128]{3,1,0,2:T(2,128)S(1)}, f32[17,2,1,128]{3,1,0,2:T(2,128)S(1)}, u32[]{:S(2)}, u32[]{:S(2)}) collective-permute-start(f32[17,2,1,128]{3,1,0,2:T(2,128)S(1)} %get-tuple-element.103), channel_id=1, source_target_pairs={{2,0},{4,2},{6,4},{8,6},{10,8},{12,10},{14,12},{16,14},{18,16},{20... | collective-permute-start | bytes 52232 | tf_op jit(solution)/shard_map/ppermute | solution.py:23
  8.4 7.4 %collective-permute-start = (f32[17,2,1,128]{3,1,0,2:T(2,128)S(1)}, f32[17,2,1,128]{3,1,0,2:T(2,128)S(1)}, u32[]{:S(2)}, u32[]{:S(2)}) collective-permute-start(f32[17,2,1,128]{3,1,0,2:T(2,128)S(1)} %get-tuple-element.102), channel_id=1, source_target_pairs={{0,2},{2,4},{4,6},{6,8},{8,10},{10,12},{12,14},{14,16},{16,18},{18... | collective-permute-start | bytes 52232 | tf_op jit(solution)/shard_map/ppermute | solution.py:20
  10.4 0.7 copy-start.6
  16.0 4.4 %collective-permute-start.3 = (f32[17,1,10,128]{3,1,2,0:T(1,128)S(1)}, f32[17,1,10,128]{3,1,2,0:T(1,128)S(1)}, u32[]{:S(2)}, u32[]{:S(2)}) collective-permute-start(f32[17,1,10,128]{3,1,2,0:T(1,128)S(1)} %get-tuple-element.97), channel_id=1, source_target_pairs={{1,0},{3,2},{5,4},{7,6},{9,8},{11,10},{13,12},{15,14},{17,16},{19,... | collective-permute-start | bytes 261128 | tf_op jit(solution)/shard_map/ppermute | solution.py:23
  17.3 4.0 %collective-permute-start.2 = (f32[17,1,10,128]{3,1,2,0:T(1,128)S(1)}, f32[17,1,10,128]{3,1,2,0:T(1,128)S(1)}, u32[]{:S(2)}, u32[]{:S(2)}) collective-permute-start(f32[17,1,10,128]{3,1,2,0:T(1,128)S(1)} %get-tuple-element.96), channel_id=1, source_target_pairs={{0,1},{2,3},{4,5},{6,7},{8,9},{10,11},{12,13},{14,15},{16,17},{18,... | collective-permute-start | bytes 261128 | tf_op jit(solution)/shard_map/ppermute | solution.py:20
  35.3 6.0 %collective-permute-start.4 = (f32[3,16,2,128]{3,2,1,0:T(2,128)S(1)}, f32[3,16,2,128]{3,2,1,0:T(2,128)S(1)}, u32[]{:S(2)}, u32[]{:S(2)}) collective-permute-start(f32[3,16,2,128]{3,2,1,0:T(2,128)S(1)} %slice_bitcast_fusion.7), channel_id=1, source_target_pairs={{2,0},{4,2},{6,4},{8,6},{10,8},{12,10},{14,12},{16,14},{18,16},{20... | collective-permute-start | bytes 147464 | tf_op jit(solution)/shard_map/ppermute | solution.py:12
  41.4 6.0 %collective-permute-start.6 = (f32[3,16,2,128]{3,2,1,0:T(2,128)S(1)}, f32[3,16,2,128]{3,2,1,0:T(2,128)S(1)}, u32[]{:S(2)}, u32[]{:S(2)}) collective-permute-start(f32[3,16,2,128]{3,2,1,0:T(2,128)S(1)} %pad_maximum_fusion.19), channel_id=1, source_target_pairs={{2,0},{4,2},{6,4},{8,6},{10,8},{12,10},{14,12},{16,14},{18,16},{20... | collective-permute-start | bytes 147464 | tf_op jit(solution)/shard_map/ppermute | solution.py:12
  45.3 7.8 %collective-permute-start.5 = (f32[3,16,2,128]{3,2,1,0:T(2,128)S(1)}, f32[3,16,2,128]{3,2,1,0:T(2,128)S(1)}, u32[]{:S(2)}, u32[]{:S(2)}) collective-permute-start(f32[3,16,2,128]{3,2,1,0:T(2,128)S(1)} %pad_maximum_fusion.19), channel_id=1, source_target_pairs={{0,2},{2,4},{4,6},{6,8},{8,10},{10,12},{12,14},{14,16},{16,18},{18... | collective-permute-start | bytes 147464 | tf_op jit(solution)/shard_map/ppermute | solution.py:12
  53.2 6.5 %collective-permute-start.8 = (f32[3,16,2,128]{3,2,1,0:T(2,128)S(1)}, f32[3,16,2,128]{3,2,1,0:T(2,128)S(1)}, u32[]{:S(2)}, u32[]{:S(2)}) collective-permute-start(f32[3,16,2,128]{3,2,1,0:T(2,128)S(1)} %pad_maximum_fusion.20), channel_id=1, source_target_pairs={{4,0},{6,2},{8,4},{10,6},{12,8},{14,10},{16,12},{18,14},{20,16},{2... | collective-permute-start | bytes 147464 | tf_op jit(solution)/shard_map/ppermute | solution.py:12
  55.1 6.9 %collective-permute-start.7 = (f32[3,16,2,128]{3,2,1,0:T(2,128)S(1)}, f32[3,16,2,128]{3,2,1,0:T(2,128)S(1)}, u32[]{:S(2)}, u32[]{:S(2)}) collective-permute-start(f32[3,16,2,128]{3,2,1,0:T(2,128)S(1)} %pad_maximum_fusion.20), channel_id=1, source_target_pairs={{0,4},{2,6},{4,8},{6,10},{8,12},{10,14},{12,16},{14,18},{16,20},{1... | collective-permute-start | bytes 147464 | tf_op jit(solution)/shard_map/ppermute | solution.py:12
  62.1 6.0 %collective-permute-start.9 = (f32[3,16,2,128]{3,2,1,0:T(2,128)S(1)}, f32[3,16,2,128]{3,2,1,0:T(2,128)S(1)}, u32[]{:S(2)}, u32[]{:S(2)}) collective-permute-start(f32[3,16,2,128]{3,2,1,0:T(2,128)S(1)} %pad_maximum_fusion.21), channel_id=1, source_target_pairs={{0,8},{2,10},{4,12},{6,14},{8,16},{10,18},{12,20},{14,22},{16,24},... | collective-permute-start | bytes 147464 | tf_op jit(solution)/shard_map/ppermute | solution.py:12
  63.4 6.3 %collective-permute-start.10 = (f32[3,16,2,128]{3,2,1,0:T(2,128)S(1)}, f32[3,16,2,128]{3,2,1,0:T(2,128)S(1)}, u32[]{:S(2)}, u32[]{:S(2)}) collective-permute-start(f32[3,16,2,128]{3,2,1,0:T(2,128)S(1)} %pad_maximum_fusion.21), channel_id=1, source_target_pairs={{8,0},{10,2},{12,4},{14,6},{16,8},{18,10},{20,12},{22,14},{24,16},... | collective-permute-start | bytes 147464 | tf_op jit(solution)/shard_map/ppermute | solution.py:12
  69.8 5.9 %collective-permute-start.12 = (f32[3,16,2,128]{3,2,1,0:T(2,128)S(1)}, f32[3,16,2,128]{3,2,1,0:T(2,128)S(1)}, u32[]{:S(2)}, u32[]{:S(2)}) collective-permute-start(f32[3,16,2,128]{3,2,1,0:T(2,128)S(1)} %pad_maximum_fusion.22), channel_id=1, source_target_pairs={{16,0},{18,2},{20,4},{22,6},{24,8},{26,10},{28,12},{30,14},{17,1},... | collective-permute-start | bytes 147464 | tf_op jit(solution)/shard_map/ppermute | solution.py:12
  74.0 7.3 %collective-permute-start.11 = (f32[3,16,2,128]{3,2,1,0:T(2,128)S(1)}, f32[3,16,2,128]{3,2,1,0:T(2,128)S(1)}, u32[]{:S(2)}, u32[]{:S(2)}) collective-permute-start(f32[3,16,2,128]{3,2,1,0:T(2,128)S(1)} %pad_maximum_fusion.22), channel_id=1, source_target_pairs={{0,16},{2,18},{4,20},{6,22},{8,24},{10,26},{12,28},{14,30},{1,17},... | collective-permute-start | bytes 147464 | tf_op jit(solution)/shard_map/ppermute | solution.py:12
  81.4 7.4 %collective-permute-start.13 = (f32[16,2,128]{2,1,0:T(2,128)S(1)}, f32[16,2,128]{2,1,0:T(2,128)S(1)}, u32[]{:S(2)}, u32[]{:S(2)}) collective-permute-start(f32[16,2,128]{2,1,0:T(2,128)S(1)} %divide_multiply_fusion.2), channel_id=1, source_target_pairs={{0,2},{2,4},{4,6},{6,8},{8,10},{10,12},{12,14},{14,16},{16,18},{18... | collective-permute-start | bytes 49160 | tf_op jit(solution)/shard_map/ppermute | solution.py:12
  89.3 6.2 %collective-permute-start.15 = (f32[17,2,1,128]{3,1,0,2:T(2,128)S(1)}, f32[17,2,1,128]{3,1,0,2:T(2,128)S(1)}, u32[]{:S(2)}, u32[]{:S(2)}) collective-permute-start(f32[17,2,1,128]{3,1,0,2:T(2,128)S(1)} %get-tuple-element.101), channel_id=1, source_target_pairs={{2,0},{4,2},{6,4},{8,6},{10,8},{12,10},{14,12},{16,14},{18,16},{20... | collective-permute-start | bytes 52232 | tf_op jit(solution)/shard_map/ppermute | solution.py:23
  91.2 7.4 %collective-permute-start.14 = (f32[17,2,1,128]{3,1,0,2:T(2,128)S(1)}, f32[17,2,1,128]{3,1,0,2:T(2,128)S(1)}, u32[]{:S(2)}, u32[]{:S(2)}) collective-permute-start(f32[17,2,1,128]{3,1,0,2:T(2,128)S(1)} %get-tuple-element.100), channel_id=1, source_target_pairs={{0,2},{2,4},{4,6},{6,8},{8,10},{10,12},{12,14},{14,16},{16,18},{18... | collective-permute-start | bytes 52232 | tf_op jit(solution)/shard_map/ppermute | solution.py:20
  98.9 4.6 %collective-permute-start.17 = (f32[17,1,10,128]{3,1,0,2:T(1,128)S(1)}, f32[17,1,10,128]{3,1,0,2:T(1,128)S(1)}, u32[]{:S(2)}, u32[]{:S(2)}) collective-permute-start(f32[17,1,10,128]{3,1,0,2:T(1,128)S(1)} %get-tuple-element.95), channel_id=1, source_target_pairs={{1,0},{3,2},{5,4},{7,6},{9,8},{11,10},{13,12},{15,14},{17,16},{19,... | collective-permute-start | bytes 261128 | tf_op jit(solution)/shard_map/ppermute | solution.py:23
  100.2 4.0 %collective-permute-start.16 = (f32[17,1,10,128]{3,1,0,2:T(1,128)S(1)}, f32[17,1,10,128]{3,1,0,2:T(1,128)S(1)}, u32[]{:S(2)}, u32[]{:S(2)}) collective-permute-start(f32[17,1,10,128]{3,1,0,2:T(1,128)S(1)} %get-tuple-element.94), channel_id=1, source_target_pairs={{0,1},{2,3},{4,5},{6,7},{8,9},{10,11},{12,13},{14,15},{16,17},{18,... | collective-permute-start | bytes 261128 | tf_op jit(solution)/shard_map/ppermute | solution.py:20
  114.3 6.0 %collective-permute-start.18 = (f32[3,16,2,128]{3,2,1,0:T(2,128)S(1)}, f32[3,16,2,128]{3,2,1,0:T(2,128)S(1)}, u32[]{:S(2)}, u32[]{:S(2)}) collective-permute-start(f32[3,16,2,128]{3,2,1,0:T(2,128)S(1)} %slice_bitcast_fusion.6), channel_id=1, source_target_pairs={{2,0},{4,2},{6,4},{8,6},{10,8},{12,10},{14,12},{16,14},{18,16},{20... | collective-permute-start | bytes 147464 | tf_op jit(solution)/shard_map/ppermute | solution.py:12
  120.4 6.0 %collective-permute-start.20 = (f32[3,16,2,128]{3,2,1,0:T(2,128)S(1)}, f32[3,16,2,128]{3,2,1,0:T(2,128)S(1)}, u32[]{:S(2)}, u32[]{:S(2)}) collective-permute-start(f32[3,16,2,128]{3,2,1,0:T(2,128)S(1)} %pad_maximum_fusion.23), channel_id=1, source_target_pairs={{2,0},{4,2},{6,4},{8,6},{10,8},{12,10},{14,12},{16,14},{18,16},{20... | collective-permute-start | bytes 147464 | tf_op jit(solution)/shard_map/ppermute | solution.py:12
  124.3 7.8 %collective-permute-start.19 = (f32[3,16,2,128]{3,2,1,0:T(2,128)S(1)}, f32[3,16,2,128]{3,2,1,0:T(2,128)S(1)}, u32[]{:S(2)}, u32[]{:S(2)}) collective-permute-start(f32[3,16,2,128]{3,2,1,0:T(2,128)S(1)} %pad_maximum_fusion.23), channel_id=1, source_target_pairs={{0,2},{2,4},{4,6},{6,8},{8,10},{10,12},{12,14},{14,16},{16,18},{18... | collective-permute-start | bytes 147464 | tf_op jit(solution)/shard_map/ppermute | solution.py:12
  132.2 6.5 %collective-permute-start.22 = (f32[3,16,2,128]{3,2,1,0:T(2,128)S(1)}, f32[3,16,2,128]{3,2,1,0:T(2,128)S(1)}, u32[]{:S(2)}, u32[]{:S(2)}) collective-permute-start(f32[3,16,2,128]{3,2,1,0:T(2,128)S(1)} %pad_maximum_fusion.24), channel_id=1, source_target_pairs={{4,0},{6,2},{8,4},{10,6},{12,8},{14,10},{16,12},{18,14},{20,16},{2... | collective-permute-start | bytes 147464 | tf_op jit(solution)/shard_map/ppermute | solution.py:12
  134.1 6.9 %collective-permute-start.21 = (f32[3,16,2,128]{3,2,1,0:T(2,128)S(1)}, f32[3,16,2,128]{3,2,1,0:T(2,128)S(1)}, u32[]{:S(2)}, u32[]{:S(2)}) collective-permute-start(f32[3,16,2,128]{3,2,1,0:T(2,128)S(1)} %pad_maximum_fusion.24), channel_id=1, source_target_pairs={{0,4},{2,6},{4,8},{6,10},{8,12},{10,14},{12,16},{14,18},{16,20},{1... | collective-permute-start | bytes 147464 | tf_op jit(solution)/shard_map/ppermute | solution.py:12
  141.1 6.0 %collective-permute-start.23 = (f32[3,16,2,128]{3,2,1,0:T(2,128)S(1)}, f32[3,16,2,128]{3,2,1,0:T(2,128)S(1)}, u32[]{:S(2)}, u32[]{:S(2)}) collective-permute-start(f32[3,16,2,128]{3,2,1,0:T(2,128)S(1)} %pad_maximum_fusion.25), channel_id=1, source_target_pairs={{0,8},{2,10},{4,12},{6,14},{8,16},{10,18},{12,20},{14,22},{16,24},... | collective-permute-start | bytes 147464 | tf_op jit(solution)/shard_map/ppermute | solution.py:12
  142.4 6.3 %collective-permute-start.24 = (f32[3,16,2,128]{3,2,1,0:T(2,128)S(1)}, f32[3,16,2,128]{3,2,1,0:T(2,128)S(1)}, u32[]{:S(2)}, u32[]{:S(2)}) collective-permute-start(f32[3,16,2,128]{3,2,1,0:T(2,128)S(1)} %pad_maximum_fusion.25), channel_id=1, source_target_pairs={{8,0},{10,2},{12,4},{14,6},{16,8},{18,10},{20,12},{22,14},{24,16},... | collective-permute-start | bytes 147464 | tf_op jit(solution)/shard_map/ppermute | solution.py:12
  148.8 5.5 %collective-permute-start.26 = (f32[3,16,2,128]{3,2,1,0:T(2,128)S(1)}, f32[3,16,2,128]{3,2,1,0:T(2,128)S(1)}, u32[]{:S(2)}, u32[]{:S(2)}) collective-permute-start(f32[3,16,2,128]{3,2,1,0:T(2,128)S(1)} %pad_maximum_fusion.26), channel_id=1, source_target_pairs={{16,0},{18,2},{20,4},{22,6},{24,8},{26,10},{28,12},{30,14},{17,1},... | collective-permute-start | bytes 147464 | tf_op jit(solution)/shard_map/ppermute | solution.py:12
  152.5 6.9 %collective-permute-start.25 = (f32[3,16,2,128]{3,2,1,0:T(2,128)S(1)}, f32[3,16,2,128]{3,2,1,0:T(2,128)S(1)}, u32[]{:S(2)}, u32[]{:S(2)}) collective-permute-start(f32[3,16,2,128]{3,2,1,0:T(2,128)S(1)} %pad_maximum_fusion.26), channel_id=1, source_target_pairs={{0,16},{2,18},{4,20},{6,22},{8,24},{10,26},{12,28},{14,30},{1,17},... | collective-permute-start | bytes 147464 | tf_op jit(solution)/shard_map/ppermute | solution.py:12
  154.3 7.6 %copy-start.2 = (f32[3,16,2,128]{3,2,1,0:T(2,128)}, f32[3,16,2,128]{3,2,1,0:T(2,128)S(1)}, u32[]{:S(2)}) copy-start(f32[3,16,2,128]{3,2,1,0:T(2,128)S(1)} %collective-permute-done.26) | copy-start | bytes 147460
  159.6 7.4 %collective-permute-start.27 = (f32[16,2,128]{2,1,0:T(2,128)S(1)}, f32[16,2,128]{2,1,0:T(2,128)S(1)}, u32[]{:S(2)}, u32[]{:S(2)}) collective-permute-start(f32[16,2,128]{2,1,0:T(2,128)S(1)} %divide_multiply_fusion), channel_id=1, source_target_pairs={{0,2},{2,4},{4,6},{6,8},{8,10},{10,12},{12,14},{14,16},{16,18},{18... | collective-permute-start | bytes 49160 | tf_op jit(solution)/shard_map/ppermute | solution.py:12
  161.9 0.7 slice-start
where the time goes:
time: 169 us; the launch traced here: 168 us
  starting transfers between devices  74.3 us (44%)
  waiting for transfers between devices  58.4 us (35%)
  other arithmetic  21.6 us (13%)
  local copies, waits for them, and re-layouts  11.8 us (7%)
    ppermute x20, starting transfers between devices, passed_along(): return lax.ppermute(x, axis, pairs)  53.7 us
    ppermute x20, waiting for transfers between devices, passed_along(): return lax.ppermute(x, axis, pairs)  49.8 us
    ppermute x4, starting transfers between devices, extended(): lax.ppermute(lax.slice_in_dim(block, block.shape[dim] - width, None, axis...  11.9 us
    ppermute x4, starting transfers between devices, extended(): lax.ppermute(lax.slice_in_dim(block, 0, width, axis=dim), axis, backward)  8.75 us
    ppermute x4, waiting for transfers between devices, extended(): lax.ppermute(lax.slice_in_dim(block, block.shape[dim] - width, None, axis...  8.57 us
    mul x18, other arithmetic, cyclic_reduce(): right = (right - lower * right_below - upper * right_above) * scaling  7.23 us
    slice x22, local copies, waits for them, and re-layouts, moved(): lax.slice_in_dim(values, 0, length - offset, axis=along)  4.49 us
  transfers between devices with their start and end apart: 28, of which 24 were waited for; matrix products, arithmetic and copies ran while one was open for 1% of the time, Pallas kernels for 0%

commit v1 on v0

v1 whole, which is shorter than its diff:
```python
import functools

import jax
import jax.numpy as jnp
from jax import lax
from jax.experimental import pallas as pl
from jax.experimental.pallas import tpu as pltpu
from jax.sharding import PartitionSpec as P

STEPS = 2
LARGE = 1e30
F32 = jnp.float32


class Sizes:
    def __init__(self, mesh, block):
        self.species, self.ny, self.nz, self.nx = block
        self.tiles = self.ny * self.nz
        self.lines = self.ny * self.species
        self.devices = mesh.shape["gz"]
        self.gy = mesh.shape["gy"]
        self.levels = (self.nx - 1).bit_length()

    def loop(self, start, stop, body, init):
        count = stop - start
        return lax.fori_loop(start, stop, body, init, unroll=count if count <= 16 else 1)


def column(ref, z):
    rows = lax.broadcasted_iota(jnp.int32, (z.species, z.nx), 0)
    value = jnp.zeros((z.species, z.nx), F32)
    for s in range(z.species):
        value = jnp.where(rows == s, ref[s], value)
    return value


def spread(ref, row, z):
    return jnp.broadcast_to(ref[pl.ds(row, 1), :], (z.species, z.nx))


def along_x(v, by, nx):
    return pltpu.roll(v, by % nx, v.ndim - 1)


def y_halo(received, z):
    if z.gy == 2:
        (both,) = received
        second = lax.axis_index("gy") == 1
        below = jnp.where(second, 1.0, 0.0).astype(F32)
        return (both, below), (both, 1.0 - below)
    return (received[0], 1.0), (received[1], 1.0)


def pack_kernel(z, c_ref, k_ref, pay_ref, *y_refs):
    me = lax.axis_index("gz")
    k = k_ref[...]
    for y in range(z.ny):
        base = z.tiles + y * z.species
        first = c_ref[pl.ds(y * z.nz, z.species, stride=z.tiles), :]
        last = c_ref[pl.ds(y * z.nz + z.nz - 1, z.species, stride=z.tiles), :]

        def fill(dest, carry):
            if y == 0:
                pay_ref[dest, 0 : z.tiles, :] = k
            pay_ref[dest, base : base + z.species, :] = jnp.where(dest > me, last, first)
            return carry

        z.loop(0, z.devices, fill, 0)
    if z.gy == 2:
        picks = [jnp.where(lax.axis_index("gy") == 1, 0, z.ny - 1)]
    else:
        picks = [z.ny - 1, 0]
    for ref, y in zip(y_refs, picks):
        for i in range(z.nz):
            ref[i * z.species : (i + 1) * z.species, :] = c_ref[
                pl.ds(y * z.nz + i, z.species, stride=z.tiles), :
            ]
        start = y * z.nz if isinstance(y, int) else pl.multiple_of(y * z.nz, z.nz)
        ref[z.nz * z.species :, :] = k_ref[pl.ds(start, z.nz), :]


def x_coefficients(z, faces, rho, left_ref, right_ref, inverse_ref):
    lanes = lax.broadcasted_iota(jnp.int32, (z.species, z.nx), 1)
    group = 4
    for base in range(0, z.tiles, group):
        tiles = range(base, base + group)
        e, d = [], []
        for t in tiles:
            before = rho * spread(faces.at[0], t, z)
            after = rho * spread(faces.at[1], t, z)
            d.append(1.0 + (before + after))
            e.append(jnp.where(lanes == 0, 0.0, before))
        for level in range(z.levels):
            stride = 1 << level
            for i, t in enumerate(tiles):
                r = 1.0 / d[i]
                above = along_x(e[i], -stride, z.nx)
                left = e[i] * along_x(r, stride, z.nx)
                right = above * along_x(r, -stride, z.nx)
                left_ref[level, t] = left
                right_ref[level, t] = right
                d[i] = d[i] - e[i] * left - above * right
                e[i] = left * along_x(e[i], stride, z.nx)
        for i, t in enumerate(tiles):
            inverse_ref[t] = 1.0 / d[i]


def right_sides(z, c, z_halo, y_low, y_high, faces, arrhenius, proportions, sigma, left, right, inverse, f_ref):
    lanes = lax.broadcasted_iota(jnp.int32, (z.species, z.nx), 1)
    rate_x, rate_y, rate_z = 4.0 * sigma, 0.015 * sigma, 4096.0 * sigma
    group = 4
    weights = proportions[...]
    for base in range(0, z.tiles, group):
        tiles = range(base, base + group)
        values = [c(t) for t in tiles]
        reacting = jnp.concatenate(
            [arrhenius[t] * jnp.tanh(v) for t, v in zip(tiles, values)], axis=1
        )
        source = jnp.dot(
            weights, reacting, precision=lax.Precision.HIGHEST, preferred_element_type=F32
        )
        section, lap = [], []
        for i, t in enumerate(tiles):
            y, row = divmod(t, z.nz)
            v = values[i]
            z_before = c(t - 1) if row else z_halo(0, y)
            z_after = c(t + 1) if row < z.nz - 1 else z_halo(1, y)
            y_before = c(t - z.nz) if y else y_low(row)
            y_after = c(t + z.nz) if y < z.ny - 1 else y_high(row)
            x_before = jnp.where(lanes == 0, 0.0, along_x(v, 1, z.nx))
            x_after = jnp.where(lanes == z.nx - 1, 0.0, along_x(v, -1, z.nx))
            flux = [spread(faces.at[n], t, z) for n in range(6)]
            lap_x = rate_x * (flux[1] * (x_after - v) - flux[0] * (v - x_before))
            lap_y = rate_y * (flux[3] * (y_after - v) - flux[2] * (v - y_before))
            lap_z = rate_z * (flux[5] * (z_after - v) - flux[4] * (v - z_before))
            lap.append(lap_z)
            section.append(v + lap_x + lap_y + lap_z + source[:, i * z.nx : (i + 1) * z.nx])
        for level in range(z.levels):
            stride = 1 << level
            for i, t in enumerate(tiles):
                section[i] = (
                    section[i]
                    + left[level, t] * along_x(section[i], stride, z.nx)
                    + right[level, t] * along_x(section[i], -stride, z.nx)
                )
        for i, t in enumerate(tiles):
            f_ref[t] = section[i] * inverse[t] - 0.5 * lap[i]


def local_lines(z, me, f_ref, m_ref, n_ref, g_ref, x_ref, ends_ref, pay_ref):
    for y in range(z.ny):
        base = y * z.nz
        forward = [f_ref[base]]
        for i in range(1, z.nz):
            forward.append(f_ref[base + i] + m_ref[base + i] * forward[-1])
        backward = f_ref[base + z.nz - 1]
        for i in reversed(range(z.nz)):
            t = base + i
            f = f_ref[t]
            if i < z.nz - 1:
                backward = f + n_ref[t] * backward
            x_ref[t] = (forward[i] + backward - f) * g_ref[t]
        first, last = backward, forward[-1]
        ends_ref[y] = first
        ends_ref[z.ny + y] = last

        def fill(dest, carry):
            pay_ref[dest, y * z.species : (y + 1) * z.species, :] = jnp.where(dest > me, last, first)
            return carry

        z.loop(0, z.devices, fill, 0)


def first_kernel(
    z,
    c_ref,
    k_ref,
    warm_ref,
    sigma_ref,
    frequency_ref,
    barrier_ref,
    proportions_ref,
    gathered,
    *refs,
):
    halos = 1 if z.gy == 2 else 2
    received = refs[:halos]
    (
        pay_ref,
        x_ref,
        ends_ref,
        m_ref,
        n_ref,
        g_ref,
        gm_ref,
        gn_ref,
        carry_ref,
        edge_ref,
        left_ref,
        right_ref,
        inverse_ref,
        arrhenius_ref,
        faces,
        all_faces,
        alpha_at,
        gamma_at,
        transfer_back,
        f_ref,
    ) = refs[halos:]
    me = lax.axis_index("gz")
    shape = (z.species, z.nx)
    sigma = column(sigma_ref, z)
    frequency = column(frequency_ref, z)
    barrier = column(barrier_ref, z)

    heat = 1.0 - 1.0 / warm_ref[...]
    faces[4] = heat
    for t in range(z.tiles):
        arrhenius_ref[t] = frequency * jnp.exp(barrier * spread(faces.at[4], t, z))

    k = k_ref[...]
    lanes = lax.broadcasted_iota(jnp.int32, k.shape, 1)
    faces[0] = 0.5 * (k + jnp.where(lanes == 0, 0.0, along_x(k, 1, z.nx)))
    faces[1] = 0.5 * (k + jnp.where(lanes == z.nx - 1, 0.0, along_x(k, -1, z.nx)))
    (low, low_mask), (high, high_mask) = y_halo(received, z)
    k_base = z.nz * z.species
    below = jnp.concatenate([low[k_base:, :] * low_mask, k[: z.tiles - z.nz]], axis=0)
    above = jnp.concatenate([k[z.nz :], high[k_base:, :] * high_mask], axis=0)
    faces[2] = 0.5 * (k + below)
    faces[3] = 0.5 * (k + above)

    x_coefficients(z, faces, 4.0 * sigma, left_ref, right_ref, inverse_ref)

    rows = lax.broadcasted_iota(jnp.int32, (z.nz, z.nx), 0)
    for y in range(z.ny):

        def add_up(j, last):
            here = gathered[j, y * z.nz : (y + 1) * z.nz, :]
            shifted = jnp.where(rows == 0, last, pltpu.roll(here, 1, 0))
            all_faces[y, pl.ds(pl.multiple_of(j * z.nz, z.nz), z.nz), :] = here + shifted
            return jnp.broadcast_to(here[z.nz - 1 :, :], here.shape)

        last = z.loop(0, z.devices, add_up, jnp.zeros((z.nz, z.nx), F32))
        all_faces[y, z.devices * z.nz :, :] = last

    rho = 1024.0 * sigma

    def face(y, row):
        return rho * spread(all_faces.at[y], row, z)

    def sweep(j, state):
        state = list(state)
        back = z.devices - 1 - j
        for y in range(z.ny):
            alpha_at[j, y] = state[2 * y]
            gamma_at[back, y] = state[2 * y + 1]
        product = [jnp.ones(shape, F32)] * (2 * z.ny)
        for i in range(z.nz):
            for y in range(z.ny):
                for side in range(2):
                    n = 2 * y + side
                    row = j * z.nz + i if side == 0 else (back + 1) * z.nz - i
                    a = face(y, row)
                    grounded = 1.0 + state[n]
                    factor = a / (grounded + a)
                    product[n] = product[n] * factor
                    state[n] = factor * grounded
        for y in range(z.ny):
            carry_ref[j, y] = product[2 * y]
            transfer_back[back, y] = product[2 * y + 1]
        return tuple(state)

    lax.fori_loop(0, z.devices, sweep, (jnp.full(shape, LARGE, F32),) * (2 * z.ny))

    def keep_back(j, carry):
        carry_ref[j] = transfer_back[j]
        return carry

    lax.fori_loop(me + 1, z.devices, keep_back, 0)

    start = me * z.nz
    inner_low = jnp.where(me > 0, 1.0, 0.0).astype(F32)
    inner_high = jnp.where(me < z.devices - 1, 1.0, 0.0).astype(F32)
    for y in range(z.ny):
        base = y * z.nz
        a = [face(y, start + i) for i in range(z.nz + 1)]
        for i in range(z.nz):
            faces[4, base + i : base + i + 1, :] = 0.5 * all_faces[y, pl.ds(start + i, 1), :]
            faces[5, base + i : base + i + 1, :] = 0.5 * all_faces[y, pl.ds(start + i + 1, 1), :]
        alpha_in, gamma_in = alpha_at[me, y], gamma_at[me, y]
        alpha, down = [], []
        state = alpha_in
        through = jnp.ones(shape, F32)
        for i in range(z.nz):
            factor = a[i] / (1.0 + state + a[i])
            state = factor * (1.0 + state)
            through = through * factor
            m_ref[base + i] = factor
            alpha.append(state)
            down.append(through)
        state = gamma_in
        through = jnp.ones(shape, F32)
        for i in reversed(range(z.nz)):
            factor = a[i + 1] / (1.0 + state + a[i + 1])
            state = factor * (1.0 + state)
            through = through * factor
            n_ref[base + i] = factor
            g = 1.0 / (1.0 + alpha[i] + state)
            g_ref[base + i] = g
            gm_ref[base + i] = g * down[i]
            gn_ref[base + i] = g * through
        factor = a[0] / (1.0 + state + a[0])
        g = inner_low / (1.0 + alpha_in + factor * (1.0 + state))
        edge_ref[y] = g
        edge_ref[z.ny + y] = g * factor
        edge_ref[2 * z.ny + y] = through
        factor = a[z.nz] / (1.0 + alpha[-1] + a[z.nz])
        g = inner_high / (1.0 + gamma_in + factor * (1.0 + alpha[-1]))
        edge_ref[3 * z.ny + y] = g
        edge_ref[4 * z.ny + y] = g * factor
        edge_ref[5 * z.ny + y] = down[-1]

    def c(t):
        return c_ref[pl.ds(t, z.species, stride=z.tiles), :]

    def z_halo(side, y):
        base = z.tiles + y * z.species
        other = jnp.minimum(me + 1, z.devices - 1) if side else jnp.maximum(me - 1, 0)
        return gathered[other, base : base + z.species, :] * (inner_high if side else inner_low)

    def y_low(row):
        return low[row * z.species : (row + 1) * z.species, :] * low_mask

    def y_high(row):
        return high[row * z.species : (row + 1) * z.species, :] * high_mask

    right_sides(
        z, c, z_halo, y_low, y_high, faces, arrhenius_ref, proportions_ref, sigma,
        left_ref, right_ref, inverse_ref, f_ref,
    )
    local_lines(z, me, f_ref, m_ref, n_ref, g_ref, x_ref, ends_ref, pay_ref)


def incoming(z, me, received, carry_ref, y):
    lanes = slice(y * z.species, (y + 1) * z.species)
    zero = jnp.zeros((z.species, z.nx), F32)
    below = lax.fori_loop(0, me, lambda j, v: received[j, lanes, :] + carry_ref[j, y] * v, zero)

    def down(i, v):
        j = z.devices - 1 - i
        return received[j, lanes, :] + carry_ref[j, y] * v

    above = lax.fori_loop(0, z.devices - 1 - me, down, zero)
    return below, above


def middle_kernel(z, received, carry_ref, x_ref, gm_ref, gn_ref, ends_ref, edge_ref, c_ref, halo_ref, *y_refs):
    me = lax.axis_index("gz")
    for y in range(z.ny):
        below, above = incoming(z, me, received, carry_ref, y)
        for i in range(z.nz):
            t = y * z.nz + i
            c_ref[t] = x_ref[t] + gm_ref[t] * below + gn_ref[t] * above
        first = ends_ref[y] + edge_ref[2 * z.ny + y] * above
        last = ends_ref[z.ny + y] + edge_ref[5 * z.ny + y] * below
        halo_ref[y] = edge_ref[y] * below + edge_ref[z.ny + y] * first
        halo_ref[z.ny + y] = edge_ref[3 * z.ny + y] * above + edge_ref[4 * z.ny + y] * last
    if z.gy == 2:
        picks = [jnp.where(lax.axis_index("gy") == 1, 0, z.ny - 1)]
    else:
        picks = [z.ny - 1, 0]
    for ref, y in zip(y_refs, picks):
        for i in range(z.nz):
            ref[i * z.species : (i + 1) * z.species, :] = c_ref[y * z.nz + i]


def second_kernel(
    z, c_ref, halo_ref, sigma_ref, proportions_ref, faces, arrhenius_ref, left_ref, right_ref,
    inverse_ref, m_ref, n_ref, g_ref, *refs
):
    halos = 1 if z.gy == 2 else 2
    received = refs[:halos]
    pay_ref, x_ref, ends_ref, f_ref = refs[halos:]
    me = lax.axis_index("gz")
    sigma = column(sigma_ref, z)
    (low, low_mask), (high, high_mask) = y_halo(received, z)
    right_sides(
        z,
        lambda t: c_ref[t],
        lambda side, y: halo_ref[side * z.ny + y],
        lambda row: low[row * z.species : (row + 1) * z.species, :] * low_mask,
        lambda row: high[row * z.species : (row + 1) * z.species, :] * high_mask,
        faces, arrhenius_ref, proportions_ref, sigma, left_ref, right_ref, inverse_ref, f_ref,
    )
    local_lines(z, me, f_ref, m_ref, n_ref, g_ref, x_ref, ends_ref, pay_ref)


def last_kernel(z, received, carry_ref, x_ref, gm_ref, gn_ref, out_ref):
    me = lax.axis_index("gz")
    for y in range(z.ny):
        below, above = incoming(z, me, received, carry_ref, y)
        for i in range(z.nz):
            t = y * z.nz + i
            out_ref[pl.ds(t, z.species, stride=z.tiles), :] = (
                x_ref[t] + gm_ref[t] * below + gn_ref[t] * above
            )


def per_device(z, c, k, warm, sigma, frequency, barrier, proportions):
    vmem = pl.BlockSpec(memory_space=pltpu.VMEM)
    smem = pl.BlockSpec(memory_space=pltpu.SMEM)
    params = pltpu.CompilerParams(vmem_limit_bytes=48 * 2**20)

    def shaped(*shape):
        return jax.ShapeDtypeStruct(shape, F32)

    def call(kernel, outs, ins, scratch=()):
        return pl.pallas_call(
            functools.partial(kernel, z),
            out_shape=outs,
            in_specs=[spec for spec, _ in ins],
            out_specs=jax.tree.map(lambda _: vmem, outs),
            scratch_shapes=list(scratch),
            compiler_params=params,
        )(*[value for _, value in ins])

    def swap(sends):
        count = z.gy
        if count == 2:
            return [lax.ppermute(sends[0], "gy", [(0, 1), (1, 0)])]
        up = [(i, i + 1) for i in range(count - 1)]
        down = [(i + 1, i) for i in range(count - 1)]
        return [lax.ppermute(sends[0], "gy", up), lax.ppermute(sends[1], "gy", down)]

    c = c.reshape(z.species * z.tiles, z.nx)
    k = k.reshape(z.tiles, z.nx)
    warm = warm.reshape(z.tiles, z.nx)
    halos = 1 if z.gy == 2 else 2
    tile = (z.species, z.nx)
    block = shaped(z.tiles, *tile)

    pay, *sends = call(
        pack_kernel,
        [shaped(z.devices, z.tiles + z.lines, z.nx)] + [shaped(z.nz * (z.species + 1), z.nx)] * halos,
        [(vmem, c), (vmem, k)],
    )
    received = swap(sends)
    gathered = lax.all_to_all(pay, "gz", 0, 0, tiled=True)
    per_line = shaped(z.devices, z.lines, z.nx)
    (pay, x, ends, m, n, g, gm, gn, carry, edge, left, right, inverse, arrhenius, faces) = call(
        first_kernel,
        [
            per_line,
            block,
            shaped(2 * z.ny, *tile),
            block,
            block,
            block,
            block,
            block,
            shaped(z.devices, z.ny, *tile),
            shaped(6 * z.ny, *tile),
            shaped(z.levels, z.tiles, *tile),
            shaped(z.levels, z.tiles, *tile),
            block,
            block,
            shaped(6, z.tiles, z.nx),
        ],
        [
            (vmem, c),
            (vmem, k),
            (vmem, warm),
            (smem, sigma),
            (smem, frequency),
            (smem, barrier),
            (vmem, proportions),
            (vmem, gathered),
        ]
        + [(vmem, v) for v in received],
        [
            pltpu.VMEM((z.ny, z.devices * z.nz + z.nz, z.nx), F32),
            pltpu.VMEM((z.devices, z.ny, *tile), F32),
            pltpu.VMEM((z.devices, z.ny, *tile), F32),
            pltpu.VMEM((z.devices, z.ny, *tile), F32),
            pltpu.VMEM((z.tiles, *tile), F32),
        ],
    )
    for _ in range(STEPS - 1):
        below_above = lax.all_to_all(pay, "gz", 0, 0, tiled=True)
        c, halo, *sends = call(
            middle_kernel,
            [block, shaped(2 * z.ny, *tile)] + [shaped(z.nz * z.species, z.nx)] * halos,
            [(vmem, v) for v in (below_above, carry, x, gm, gn, ends, edge)],
        )
        received = swap(sends)
        pay, x, ends = call(
            second_kernel,
            [per_line, block, shaped(2 * z.ny, *tile)],
            [(vmem, c), (vmem, halo), (smem, sigma), (vmem, proportions)]
            + [(vmem, v) for v in (faces, arrhenius, left, right, inverse, m, n, g, *received)],
            [pltpu.VMEM((z.tiles, *tile), F32)],
        )
    below_above = lax.all_to_all(pay, "gz", 0, 0, tiled=True)
    out = call(
        last_kernel,
        shaped(z.species * z.tiles, z.nx),
        [(vmem, v) for v in (below_above, carry, x, gm, gn)],
    )
    return out.reshape(z.species, z.ny, z.nz, z.nx)


def solution(mesh):
    def device_program(starting_densities, *others):
        sizes = Sizes(mesh, starting_densities.shape)
        return per_device(sizes, starting_densities, *others)

    return jax.shard_map(
        device_program,
        mesh=mesh,
        in_specs=(
            P(None, "gy", "gz", None),
            P("gy", "gz", None),
            P("gy", "gz", None),
            P(),
            P(),
            P(),
            P(),
        ),
        out_specs=P(None, "gy", "gz", None),
        check_vma=False,
    )
```

time: 169 us -> 58.9 us (0.35)
  the two profiles are of different devices: /device:TPU:24 before, /device:TPU:0 now
where the time goes in v1:
time: 58.9 us; the launch traced here: 58.6 us
  blocking collectives  26.1 us (44%)
  waiting for transfers between devices  13.8 us (23%)
  starting transfers between devices  8.6 us (15%)
  Pallas kernels  8.39 us (14%)
  local copies, waits for them, and re-layouts  1.63 us (3%)
    all_to_all x2, blocking collectives, per_device(): below_above = lax.all_to_all(pay, 'gz', 0, 0, tiled=True)  26.1 us
    all_to_all x1, waiting for transfers between devices, per_device(): gathered = lax.all_to_all(pay, 'gz', 0, 0, tiled=True)  11.3 us
    all_to_all x1, starting transfers between devices, per_device(): gathered = lax.all_to_all(pay, 'gz', 0, 0, tiled=True)  8.46 us
    pallas_call x5, Pallas kernels, call(): pl.pallas_call(functools.partial(kernel, z), out_shape=outs, in_specs=[sp...  8.39 us
    ppermute x2, waiting for transfers between devices, swap(): return [lax.ppermute(sends[0], 'gy', [(0, 1), (1, 0)])]  2.49 us
    unnamed x18, local copies, waits for them, and re-layouts  1.63 us
  transfers between devices with their start and end apart: 3, of which 3 were waited for; matrix products, arithmetic and copies ran while one was open for 0% of the time, Pallas kernels for 0%

profile of v1, /device:TPU:0, one launch (start us, length us, event | category | flops | bytes accessed | tf_op | source)
XLA Modules:
  0.0 58.6 jit_solution(632443614679405753)
XLA Ops:
  0.0 0.0 copy-start
  0.0 0.9 %copy-done = f32[16,2,8,128]{3,2,1,0:T(8,128)S(1)} copy-done((f32[16,2,8,128]{3,2,1,0:T(8,128)S(1)}, f32[16,2,8,128]{3,2,1,0:T(8,128)}, u32[]{:S(2)}) %copy-start) | copy-done | bytes 131096
  0.9 0.0 copy-start.3
  0.9 0.7 %copy-done.3 = f32[2,8,128]{2,1,0:T(8,128)S(1)} copy-done((f32[2,8,128]{2,1,0:T(8,128)S(1)}, f32[2,8,128]{2,1,0:T(8,128)}, u32[]{:S(2)}) %copy-start.3) | copy-done | bytes 8216
  1.6 0.8 %shard_map.73 = (f32[16,48,128]{2,1,0:T(8,128)}, f32[136,128]{1,0:T(8,128)S(1)}) custom-call(f32[256,128]{1,0:T(8,128)S(1)} %bitcast.4, f32[16,128]{1,0:T(8,128)S(1)} %bitcast.6), custom_call_target="tpu_custom_call" | custom-call | tf_op jit(solution)/shard_map/pallas_call | solution.py:418
  2.4 0.0 copy-start.1
  2.4 0.0 copy-start.2
  2.4 0.0 copy-start.4
  2.4 0.0 copy-start.5
  2.4 8.5 %all-to-all-start = ((f32[16,48,128]{2,1,0:T(8,128)}), f32[16,48,128]{2,1,0:T(8,128)S(1)}, u32[]{:S(2)}, u32[]{:S(2)}) async-start(f32[16,48,128]{2,1,0:T(8,128)} %get-tuple-element.27), calls=%async_computation | async-start | bytes 786432 | tf_op jit(solution)/shard_map/all_to_all | solution.py:448
  10.9 0.0 copy-start.6
  10.9 0.0 copy-start.7
  10.9 0.0 copy-start.8
  10.9 0.1 collective-permute-start
  11.0 1.2 %collective-permute-done.refs_0_ = f32[136,128]{1,0:T(8,128)S(1)} collective-permute-done((f32[136,128]{1,0:T(8,128)S(1)}, f32[136,128]{1,0:T(8,128)S(1)}, u32[]{:S(2)}, u32[]{:S(2)}) %collective-permute-start) | collective-permute-done | bytes 69664 | tf_op jit(solution)/shard_map/ppermute | solution.py:430
  12.3 11.3 %all-to-all-done.gathered = f32[16,48,128]{2,1,0:T(8,128)S(1)} async-done(((f32[16,48,128]{2,1,0:T(8,128)}), f32[16,48,128]{2,1,0:T(8,128)S(1)}, u32[]{:S(2)}, u32[]{:S(2)}) %all-to-all-start) | async-done | bytes 393248 | tf_op jit(solution)/shard_map/all_to_all | solution.py:448
  23.5 0.0 copy-done.1
  23.5 0.0 copy-done.2
  23.5 0.0 copy-done.4
  23.5 0.0 copy-done.5
  23.5 0.0 copy-done.6
  23.6 0.0 copy-done.7
  23.6 0.0 copy-done.8
  23.6 4.5 %shard_map.74 = (f32[16,32,128]{2,1,0:T(8,128)S(1)}, f32[16,16,128]{2,1,0:T(8,128)S(1)}, f32[4,16,128]{2,1,0:T(8,128)S(1)}, f32[16,16,128]{2,1,0:T(8,128)S(1)}, ...) custom-call(f32[256,128]{1,0:T(8,128)S(1)} %bitcast.5, ...), custom_call_target="tpu_custom_call" | custom-call | tf_op jit(solution)/shard_map/pallas_call | solution.py:418
  28.1 12.6 %all_to_all.15.received = f32[16,32,128]{2,1,0:T(8,128)S(1)} all-to-all(f32[16,32,128]{2,1,0:T(8,128)S(1)} %get-tuple-element.29), channel_id=1, replica_groups=mesh['gz'=16,'gy'=2] {'gz'}, dimensions={0} | all-to-all | bytes 524288 | tf_op jit(solution)/shard_map/all_to_all | solution.py:489
  40.7 0.2 shard_map.75
  40.9 0.1 collective-permute-start.1
  40.9 1.2 %collective-permute-done.1.refs_0_ = f32[128,128]{1,0:T(8,128)S(1)} collective-permute-done((f32[128,128]{1,0:T(8,128)S(1)}, f32[128,128]{1,0:T(8,128)S(1)}, u32[]{:S(2)}, u32[]{:S(2)}) %collective-permute-start.1) | collective-permute-done | bytes 65568 | tf_op jit(solution)/shard_map/ppermute | solution.py:430
  42.2 2.0 %shard_map.76 = (f32[16,32,128]{2,1,0:T(8,128)S(1)}, f32[16,16,128]{2,1,0:T(8,128)S(1)}, f32[4,16,128]{2,1,0:T(8,128)}) custom-call(f32[16,16,128]{2,1,0:T(8,128)S(1)} %get-tuple-element.36.c_ref, f32[4,16,128]{2,1,0:T(8,128)S(1)} %get-tuple-element.37.halo_ref, f32[16]{0:T(128)S(1)} %copy-done.6, f32[16,16]{1,0:T(8,128)S(1)} %copy-done.2, ...), custom_call_target="tpu_custom_call" | custom-call | tf_op jit(solution)/shard_map/pallas_call | solution.py:418
  44.2 13.5 %all_to_all.16.received = f32[16,32,128]{2,1,0:T(8,128)S(1)} all-to-all(f32[16,32,128]{2,1,0:T(8,128)S(1)} %get-tuple-element.47), channel_id=1, replica_groups=mesh['gz'=16,'gy'=2] {'gz'}, dimensions={0} | all-to-all | bytes 524288 | tf_op jit(solution)/shard_map/all_to_all | solution.py:503
  57.7 0.9 %shard_map.77 = f32[256,128]{1,0:T(8,128)} custom-call(f32[16,32,128]{2,1,0:T(8,128)S(1)} %all_to_all.16.received, f32[16,2,16,128]{3,2,1,0:T(8,128)S(1)} %get-tuple-element.30.carry_ref, f32[16,16,128]{2,1,0:T(8,128)S(1)} %get-tuple-element.48.x_ref, f32[16,16,128]{2,1,0:T(8,128)S(1)} %get-tuple-element.32.gm_ref, f32[16,16,128]{2,1,0:T(8,128)S(1)} %get-tuple-element.33.gn_ref), custom_call_target="tpu_custom_call" | custom-call | tf_op jit(solution)/shard_map/pallas_call | solution.py:418
Async XLA Ops:
  0.0 0.9 %copy-start = (f32[16,2,8,128]{3,2,1,0:T(8,128)S(1)}, f32[16,2,8,128]{3,2,1,0:T(8,128)}, u32[]{:S(2)}) copy-start(f32[16,2,8,128]{3,2,1,0:T(8,128)} %param.7) | copy-start | bytes 393220
  0.9 0.7 %copy-start.3 = (f32[2,8,128]{2,1,0:T(8,128)S(1)}, f32[2,8,128]{2,1,0:T(8,128)}, u32[]{:S(2)}) copy-start(f32[2,8,128]{2,1,0:T(8,128)} %param.8) | copy-start | bytes 24580
  2.4 21.1 %copy-start.1 = (f32[16,2,8,128]{3,2,1,0:T(8,128)S(1)}, f32[16,2,8,128]{3,2,1,0:T(8,128)}, u32[]{:S(2)}) copy-start(f32[16,2,8,128]{3,2,1,0:T(8,128)} %param.7) | copy-start | bytes 393220
  2.4 21.1 %copy-start.2 = (f32[16,16]{1,0:T(8,128)S(1)}, f32[16,16]{1,0:T(8,128)}, u32[]{:S(2)}) copy-start(f32[16,16]{1,0:T(8,128)} %proportions_ref.3) | copy-start | bytes 3076
  2.4 21.1 %copy-start.4 = (f32[2,8,128]{2,1,0:T(8,128)S(1)}, f32[2,8,128]{2,1,0:T(8,128)}, u32[]{:S(2)}) copy-start(f32[2,8,128]{2,1,0:T(8,128)} %param.8) | copy-start | bytes 24580
  2.4 21.1 %copy-start.5 = (f32[2,8,128]{2,1,0:T(8,128)S(1)}, f32[2,8,128]{2,1,0:T(8,128)}, u32[]{:S(2)}) copy-start(f32[2,8,128]{2,1,0:T(8,128)} %param.9) | copy-start | bytes 24580
  2.4 21.1 %all-to-all-start = ((f32[16,48,128]{2,1,0:T(8,128)}), f32[16,48,128]{2,1,0:T(8,128)S(1)}, u32[]{:S(2)}, u32[]{:S(2)}) async-start(f32[16,48,128]{2,1,0:T(8,128)} %get-tuple-element.27), calls=%async_computation | async-start | bytes 786432 | tf_op jit(solution)/shard_map/all_to_all | solution.py:448
  10.9 12.7 %copy-start.6 = (f32[16]{0:T(128)S(1)}, f32[16]{0:T(128)}, u32[]{:S(2)}) copy-start(f32[16]{0:T(128)} %sigma_ref.3) | copy-start | bytes 196
  10.9 12.7 %copy-start.7 = (f32[16]{0:T(128)S(1)}, f32[16]{0:T(128)}, u32[]{:S(2)}) copy-start(f32[16]{0:T(128)} %frequency_ref.1) | copy-start | bytes 196
  10.9 12.7 %copy-start.8 = (f32[16]{0:T(128)S(1)}, f32[16]{0:T(128)}, u32[]{:S(2)}) copy-start(f32[16]{0:T(128)} %barrier_ref.1) | copy-start | bytes 196
  10.9 1.3 %collective-permute-start = (f32[136,128]{1,0:T(8,128)S(1)}, f32[136,128]{1,0:T(8,128)S(1)}, u32[]{:S(2)}, u32[]{:S(2)}) collective-permute-start(f32[136,128]{1,0:T(8,128)S(1)} %get-tuple-element.28), channel_id=1, source_target_pairs={{0,1},{1,0},{2,3},{3,2},{4,5},{5,4},{6,7},{7,6},{8,9},{9,8},{10,11... | collective-permute-start | bytes 208904 | tf_op jit(solution)/shard_map/ppermute | solution.py:430
  40.9 1.3 %collective-permute-start.1 = (f32[128,128]{1,0:T(8,128)S(1)}, f32[128,128]{1,0:T(8,128)S(1)}, u32[]{:S(2)}, u32[]{:S(2)}) collective-permute-start(f32[128,128]{1,0:T(8,128)S(1)} %get-tuple-element.46), channel_id=1, source_target_pairs={{0,1},{1,0},{2,3},{3,2},{4,5},{5,4},{6,7},{7,6},{8,9},{9,8},{10,11... | collective-permute-start | bytes 196616 | tf_op jit(solution)/shard_map/ppermute | solution.py:430

commit v2 on v0

v2 whole, which is shorter than its diff:
```python
import functools

import jax
import jax.numpy as jnp
from jax import lax
from jax.experimental import pallas as pl
from jax.experimental.pallas import tpu as pltpu
from jax.sharding import PartitionSpec as P

STEPS = 2
F32 = jnp.float32


class Sizes:
    def __init__(self, mesh, block):
        self.species, self.ny, self.nz, self.nx = block
        self.tiles = self.ny * self.nz
        self.lines = self.ny * self.species
        self.devices = mesh.shape["gz"]
        self.gy = mesh.shape["gy"]
        self.levels = (self.nx - 1).bit_length()
        self.tile = (self.species, self.nx)

    def per_device(self, body):
        if self.devices <= 16:
            for j in range(self.devices):
                body(j)
        else:

            def step(j, carry):
                body(j)
                return carry

            lax.fori_loop(0, self.devices, step, 0)

    def groups(self, size):
        for base in range(0, self.tiles, size):
            yield range(base, min(base + size, self.tiles))


def column(ref, z):
    rows = lax.broadcasted_iota(jnp.int32, z.tile, 0)
    value = jnp.zeros(z.tile, F32)
    for s in range(z.species):
        value = jnp.where(rows == s, ref[s], value)
    return value


def spread(ref, row, z):
    return jnp.broadcast_to(ref[pl.ds(row, 1), :], z.tile)


def along_x(v, by, nx):
    return pltpu.roll(v, by % nx, v.ndim - 1)


def flag(condition):
    return jnp.where(condition, 1.0, 0.0).astype(F32)


def inner(axis, count):
    me = lax.axis_index(axis)
    return flag(me > 0), flag(me < count - 1)


def spread_kernel(z, k_ref, pay_ref):
    k = k_ref[...]

    def fill(dest):
        pay_ref[dest] = k

    z.per_device(fill)


def edges_kernel(z, c_ref, k_ref, up_ref, down_ref, *y_refs):
    for y in range(z.ny):
        lines = slice(y * z.species, (y + 1) * z.species)
        down_ref[lines, :] = c_ref[pl.ds(y * z.nz, z.species, stride=z.tiles), :]
        up_ref[lines, :] = c_ref[pl.ds(y * z.nz + z.nz - 1, z.species, stride=z.tiles), :]
    for ref, y in zip(y_refs, y_picks(z)):
        for i in range(z.nz):
            ref[i * z.species : (i + 1) * z.species, :] = c_ref[
                pl.ds(y * z.nz + i, z.species, stride=z.tiles), :
            ]
        start = y * z.nz if isinstance(y, int) else pl.multiple_of(y * z.nz, z.nz)
        ref[z.nz * z.species :, :] = k_ref[pl.ds(start, z.nz), :]


def y_picks(z):
    if z.gy == 2:
        return [jnp.where(lax.axis_index("gy") == 1, 0, z.ny - 1)]
    return [z.ny - 1, 0]


def setup_kernel(
    z, c_ref, k_ref, warm_ref, sigma_ref, frequency_ref, barrier_ref, proportions_ref,
    tiles_ref, rates_ref, faces, arrhenius_ref, left_ref, right_ref, inverse_ref, base_ref, heat_ref,
):
    sigma = column(sigma_ref, z)
    frequency = column(frequency_ref, z)
    barrier = column(barrier_ref, z)
    rates_ref[0] = 4.0 * sigma
    rates_ref[1] = 0.015 * sigma
    rates_ref[2] = 4096.0 * sigma
    rates_ref[3] = 1.0 / (1024.0 * sigma)
    heat_ref[...] = 1.0 - 1.0 / warm_ref[...]
    k = k_ref[...]
    lanes = lax.broadcasted_iota(jnp.int32, k.shape, 1)
    faces[0] = 0.5 * (k + jnp.where(lanes == 0, 0.0, along_x(k, 1, z.nx)))
    faces[1] = 0.5 * (k + jnp.where(lanes == z.nx - 1, 0.0, along_x(k, -1, z.nx)))
    for t in range(z.tiles):
        tiles_ref[t] = c_ref[pl.ds(t, z.species, stride=z.tiles), :]
        arrhenius_ref[t] = frequency * jnp.exp(barrier * spread(heat_ref, t, z))
    base_sides(z, tiles_ref, rates_ref, faces, arrhenius_ref, proportions_ref, base_ref)

    lanes = lax.broadcasted_iota(jnp.int32, z.tile, 1)
    rho = rates_ref[0]
    for tiles in z.groups(8):
        e, d = [], []
        for t in tiles:
            before = rho * spread(faces.at[0], t, z)
            after = rho * spread(faces.at[1], t, z)
            d.append(1.0 + (before + after))
            e.append(jnp.where(lanes == 0, 0.0, before))
        for level in range(z.levels):
            stride = 1 << level
            for i, t in enumerate(tiles):
                r = 1.0 / d[i]
                above = along_x(e[i], -stride, z.nx)
                left = e[i] * along_x(r, stride, z.nx)
                right = above * along_x(r, -stride, z.nx)
                left_ref[level, t] = left
                right_ref[level, t] = right
                d[i] = d[i] - e[i] * left - above * right
                e[i] = left * along_x(e[i], stride, z.nx)
        for i, t in enumerate(tiles):
            inverse_ref[t] = 1.0 / d[i]


def base_sides(z, tiles_ref, rates_ref, faces, arrhenius_ref, proportions_ref, base_ref):
    lanes = lax.broadcasted_iota(jnp.int32, z.tile, 1)
    rate = rates_ref[0]
    reacting = jnp.concatenate(
        [arrhenius_ref[t] * jnp.tanh(tiles_ref[t]) for t in range(z.tiles)], axis=1
    )
    source = jnp.dot(
        proportions_ref[...],
        reacting,
        precision=lax.Precision.HIGHEST,
        preferred_element_type=F32,
    )
    for t in range(z.tiles):
        v = tiles_ref[t]
        before = jnp.where(lanes == 0, 0.0, along_x(v, 1, z.nx))
        after = jnp.where(lanes == z.nx - 1, 0.0, along_x(v, -1, z.nx))
        lap = rate * (
            spread(faces.at[1], t, z) * (after - v) - spread(faces.at[0], t, z) * (v - before)
        )
        base_ref[t] = v + lap + source[:, t * z.nx : (t + 1) * z.nx]


def base_kernel(z, *refs):
    base_sides(z, *refs)


def right_sides(z, tiles_ref, base_ref, z_halo, y_halo, rates_ref, faces, left, right, inverse, f_ref):
    rate_y, rate_z = rates_ref[1], rates_ref[2]
    for tiles in z.groups(8):
        section, lap = [], []
        for t in tiles:
            y, row = divmod(t, z.nz)
            v = tiles_ref[t]
            z_before = tiles_ref[t - 1] if row else z_halo(0, y)
            z_after = tiles_ref[t + 1] if row < z.nz - 1 else z_halo(1, y)
            y_before = tiles_ref[t - z.nz] if y else y_halo(0, row)
            y_after = tiles_ref[t + z.nz] if y < z.ny - 1 else y_halo(1, row)
            flux = [spread(faces.at[n], t, z) for n in range(4)]
            lap_y = rate_y * (flux[1] * (y_after - v) - flux[0] * (v - y_before))
            lap_z = rate_z * (flux[3] * (z_after - v) - flux[2] * (v - z_before))
            lap.append(lap_z)
            section.append(base_ref[t] + lap_y + lap_z)
        for level in range(z.levels):
            stride = 1 << level
            for i, t in enumerate(tiles):
                section[i] = (
                    section[i]
                    + left[level, t] * along_x(section[i], stride, z.nx)
                    + right[level, t] * along_x(section[i], -stride, z.nx)
                )
        for i, t in enumerate(tiles):
            f_ref[t] = section[i] * inverse[t] - 0.5 * lap[i]


def send_sums(z, f_ref, v_ref, u_ref, pay_ref):
    me = lax.axis_index("gz")
    for y in range(z.ny):
        tiles = range(y * z.nz, (y + 1) * z.nz)
        up = functools.reduce(jnp.add, [v_ref[t] * f_ref[t] for t in tiles])
        down = functools.reduce(jnp.add, [u_ref[t] * f_ref[t] for t in tiles])
        lines = slice(y * z.species, (y + 1) * z.species)

        def fill(dest):
            pay_ref[dest, lines, :] = jnp.where(dest > me, up, down)

        z.per_device(fill)
    pay_ref[me] = jnp.zeros((z.lines, z.nx), F32)


def first_kernel(
    z, gathered, k_ref, from_below, from_above, tiles_ref, base_ref, rates_ref, left_ref, right_ref,
    inverse_ref, *refs
):
    halos = 1 if z.gy == 2 else 2
    y_received = refs[:halos]
    pay_ref, f_ref, v_ref, u_ref, ends_ref, faces, resistance = refs[halos:]
    me = lax.axis_index("gz")
    k = k_ref[...]
    low, high = y_received[0], y_received[-1]
    low_mask, high_mask = inner("gy", z.gy)
    k_base = z.nz * z.species
    below = jnp.concatenate([low[k_base:, :] * low_mask, k[: z.tiles - z.nz]], axis=0)
    above = jnp.concatenate([k[z.nz :], high[k_base:, :] * high_mask], axis=0)
    faces[0] = 0.5 * (k + below)
    faces[1] = 0.5 * (k + above)

    rows = lax.broadcasted_iota(jnp.int32, (z.nz, z.nx), 0)
    for y in range(z.ny):
        base = y * z.nz

        def invert(j):
            here = gathered[j, base : base + z.nz, :]
            before = gathered[jnp.maximum(j - 1, 0), base + z.nz - 1 : base + z.nz, :]
            before = jnp.broadcast_to(jnp.where(j > 0, before, 0.0), here.shape)
            total = here + jnp.where(rows == 0, before, pltpu.roll(here, 1, 0))
            resistance[y, pl.ds(pl.multiple_of(j * z.nz, z.nz), z.nz), :] = 1.0 / total

        z.per_device(invert)
        last = gathered[z.devices - 1, base + z.nz - 1 : base + z.nz, :]
        resistance[y, z.devices * z.nz :, :] = jnp.broadcast_to(1.0 / last, (z.nz, z.nx))

    per_species = rates_ref[3]

    def ohm(y, row):
        return per_species * spread(resistance.at[y], row, z)

    def advance(state, row):
        out = []
        for y in range(z.ny):
            v, w = state[2 * y : 2 * y + 2]
            v = v + w * ohm(y, row)
            out += [v, w + v]
        return tuple(out)

    def forward(j, state):
        for i in range(z.nz):
            state = advance(state, j * z.nz + i)
        return state

    def backward(j, state):
        for i in range(z.nz):
            state = advance(state, (z.devices - j) * z.nz - i)
        return state

    start = (jnp.zeros(z.tile, F32), jnp.ones(z.tile, F32)) * z.ny
    first = me * z.nz
    state = lax.fori_loop(0, me, forward, start)
    rising = []
    for y in range(z.ny):
        ends_ref[y] = state[2 * y]
    for i in range(z.nz + 1):
        state = advance(state, first + i)
        rising.append(state)
    for y in range(z.ny):
        ends_ref[z.ny + y] = state[2 * y]
        for i in range(z.nz):
            v_ref[y * z.nz + i] = rising[i][2 * y]
            row = first + i
            faces[2, y * z.nz + i : y * z.nz + i + 1, :] = 0.5 / resistance[y, pl.ds(row, 1), :]
            faces[3, y * z.nz + i : y * z.nz + i + 1, :] = 0.5 / resistance[y, pl.ds(row + 1, 1), :]
    state = lax.fori_loop(0, z.devices - 1 - me, backward, start)
    for y in range(z.ny):
        ends_ref[3 * z.ny + y] = state[2 * y]
    for i in reversed(range(z.nz)):
        state = advance(state, first + i + 1)
        for y in range(z.ny):
            u_ref[y * z.nz + i] = state[2 * y]
            if i == 0:
                u, wu = state[2 * y : 2 * y + 2]
                v, wv = rising[0][2 * y : 2 * y + 2]
                ends_ref[4 * z.ny + y] = 1.0 / (wv * u + v * (wu - u))
    state = advance(state, first)
    for y in range(z.ny):
        ends_ref[2 * z.ny + y] = state[2 * y]

    z_low, z_high = inner("gz", z.devices)

    def z_halo(side, y):
        lines = slice(y * z.species, (y + 1) * z.species)
        return from_above[lines, :] * z_high if side else from_below[lines, :] * z_low

    def y_halo(side, row):
        lines = slice(row * z.species, (row + 1) * z.species)
        return high[lines, :] * high_mask if side else low[lines, :] * low_mask

    right_sides(
        z, tiles_ref, base_ref, z_halo, y_halo, rates_ref, faces, left_ref, right_ref, inverse_ref, f_ref
    )
    send_sums(z, f_ref, v_ref, u_ref, pay_ref)


def solve_lines(z, received, f_ref, v_ref, u_ref, ends_ref, store):
    me = lax.axis_index("gz")
    halos = []
    for y in range(z.ny):
        lines = slice(y * z.species, (y + 1) * z.species)
        zero = jnp.zeros(z.tile, F32)
        sums = [zero, zero]

        def add(j, pair):
            value = received[j, lines, :]
            lower = j < me
            return [pair[0] + jnp.where(lower, value, 0.0), pair[1] + jnp.where(lower, 0.0, value)]

        if z.devices <= 16:
            for j in range(z.devices):
                sums = add(j, sums)
        else:
            sums = lax.fori_loop(0, z.devices, add, sums)
        below, above = sums
        scale = ends_ref[4 * z.ny + y]
        tiles = range(y * z.nz, (y + 1) * z.nz)
        after = {}
        total = above
        for t in reversed(tiles):
            after[t] = total
            total = total + u_ref[t] * f_ref[t]
        low = scale * (ends_ref[2 * z.ny + y] * below + ends_ref[y] * total)
        total = below
        for t in tiles:
            total = total + v_ref[t] * f_ref[t]
            store(t, scale * (u_ref[t] * total + v_ref[t] * after[t]))
        high = scale * (ends_ref[3 * z.ny + y] * total + ends_ref[z.ny + y] * above)
        halos.append((low, high))
    return halos


def middle_kernel(z, received, f_ref, v_ref, u_ref, ends_ref, tiles_ref, halo_ref, *y_refs):
    def store(t, value):
        tiles_ref[t] = value

    for y, (low, high) in enumerate(solve_lines(z, received, f_ref, v_ref, u_ref, ends_ref, store)):
        halo_ref[y] = low
        halo_ref[z.ny + y] = high
    for ref, y in zip(y_refs, y_picks(z)):
        for i in range(z.nz):
            ref[i * z.species : (i + 1) * z.species, :] = tiles_ref[y * z.nz + i]


def second_kernel(
    z, tiles_ref, base_ref, halo_ref, rates_ref, faces, left_ref, right_ref, inverse_ref, v_ref, u_ref,
    *refs
):
    halos = 1 if z.gy == 2 else 2
    low, high = refs[0], refs[halos - 1]
    pay_ref, f_ref = refs[halos:]
    low_mask, high_mask = inner("gy", z.gy)

    def y_halo(side, row):
        lines = slice(row * z.species, (row + 1) * z.species)
        return high[lines, :] * high_mask if side else low[lines, :] * low_mask

    right_sides(
        z, tiles_ref, base_ref, lambda side, y: halo_ref[side * z.ny + y], y_halo, rates_ref, faces,
        left_ref, right_ref, inverse_ref, f_ref,
    )
    send_sums(z, f_ref, v_ref, u_ref, pay_ref)


def last_kernel(z, received, f_ref, v_ref, u_ref, ends_ref, out_ref):
    def store(t, value):
        out_ref[pl.ds(t, z.species, stride=z.tiles), :] = value

    solve_lines(z, received, f_ref, v_ref, u_ref, ends_ref, store)


def per_device(z, c, k, warm, sigma, frequency, barrier, proportions):
    vmem = pl.BlockSpec(memory_space=pltpu.VMEM)
    smem = pl.BlockSpec(memory_space=pltpu.SMEM)
    params = pltpu.CompilerParams(vmem_limit_bytes=48 * 2**20)

    def shaped(*shape):
        return jax.ShapeDtypeStruct(shape, F32)

    def call(kernel, outs, ins, scratch=(), flops=1000000):
        specs = [spec for spec, _ in ins]
        return pl.pallas_call(
            functools.partial(kernel, z),
            out_shape=outs,
            in_specs=specs,
            out_specs=jax.tree.map(lambda _: vmem, outs),
            scratch_shapes=list(scratch),
            compiler_params=params,
            cost_estimate=pl.CostEstimate(flops=flops, bytes_accessed=1000000, transcendentals=0),
        )(*[value for _, value in ins])

    def shift(value, axis, by):
        count = lax.axis_size(axis)
        return lax.ppermute(value, axis, [(i, (i + by) % count) for i in range(count)])

    def swap(sends):
        return [shift(value, "gy", by) for value, by in zip(sends, (1, -1))]

    def in_vmem(*values):
        return [(vmem, value) for value in values]

    c = c.reshape(z.species * z.tiles, z.nx)
    k = k.reshape(z.tiles, z.nx)
    warm = warm.reshape(z.tiles, z.nx)
    halos = 1 if z.gy == 2 else 2
    block = shaped(z.tiles, *z.tile)
    per_line = shaped(z.devices, z.lines, z.nx)

    pay = call(spread_kernel, shaped(z.devices, z.tiles, z.nx), in_vmem(k))
    gathered = lax.all_to_all(pay, "gz", 0, 0, tiled=True)
    up, down, *sends = call(
        edges_kernel,
        [shaped(z.lines, z.nx)] * 2 + [shaped(z.nz * (z.species + 1), z.nx)] * halos,
        in_vmem(c, k),
    )
    from_below, from_above = shift(up, "gz", 1), shift(down, "gz", -1)
    received = swap(sends)
    tiles, rates, x_faces, arrhenius, left, right, inverse, base = call(
        setup_kernel,
        [
            block,
            shaped(4, *z.tile),
            shaped(2, z.tiles, z.nx),
            block,
            shaped(z.levels, z.tiles, *z.tile),
            shaped(z.levels, z.tiles, *z.tile),
            block,
            block,
        ],
        in_vmem(c, k, warm)
        + [(smem, sigma), (smem, frequency), (smem, barrier)]
        + in_vmem(proportions),
        [pltpu.VMEM((z.tiles, z.nx), F32)],
    )
    pay, f, v, u, ends, faces = call(
        first_kernel,
        [per_line, block, block, block, shaped(5 * z.ny, *z.tile), shaped(4, z.tiles, z.nx)],
        in_vmem(gathered, k, from_below, from_above, tiles, base, rates, left, right, inverse, *received),
        [pltpu.VMEM((z.ny, z.devices * z.nz + z.nz, z.nx), F32)],
    )
    for _ in range(STEPS - 1):
        sums = lax.all_to_all(pay, "gz", 0, 0, tiled=True)
        tiles, halo, *sends = call(
            middle_kernel,
            [block, shaped(2 * z.ny, *z.tile)] + [shaped(z.nz * z.species, z.nx)] * halos,
            in_vmem(sums, f, v, u, ends),
        )
        received = swap(sends)
        base = call(base_kernel, block, in_vmem(tiles, rates, x_faces, arrhenius, proportions))
        pay, f = call(
            second_kernel,
            [per_line, block],
            in_vmem(tiles, base, halo, rates, faces, left, right, inverse, v, u, *received),
        )
    sums = lax.all_to_all(pay, "gz", 0, 0, tiled=True)
    out = call(last_kernel, shaped(z.species * z.tiles, z.nx), in_vmem(sums, f, v, u, ends))
    return out.reshape(z.species, z.ny, z.nz, z.nx)


def solution(mesh):
    def device_program(starting_densities, *others):
        sizes = Sizes(mesh, starting_densities.shape)
        return per_device(sizes, starting_densities, *others)

    return jax.shard_map(
        device_program,
        mesh=mesh,
        in_specs=(
            P(None, "gy", "gz", None),
            P("gy", "gz", None),
            P("gy", "gz", None),
            P(),
            P(),
            P(),
            P(),
        ),
        out_specs=P(None, "gy", "gz", None),
        check_vma=False,
    )
```

time: 169 us -> 51.6 us (0.31)
  the two profiles are of different devices: /device:TPU:24 before, /device:TPU:0 now
where the time goes in v2:
time: 51.6 us; the launch traced here: 51.3 us
  blocking collectives  28.7 us (56%)
  starting transfers between devices  14.3 us (28%)
  Pallas kernels  5.82 us (11%)
  waiting for transfers between devices  1.61 us (3%)
  local copies, waits for them, and re-layouts  0.73 us (1%)
    all_to_all x2, blocking collectives, per_device(): sums = lax.all_to_all(pay, 'gz', 0, 0, tiled=True)  28.7 us
    all_to_all x1, starting transfers between devices, per_device(): gathered = lax.all_to_all(pay, 'gz', 0, 0, tiled=True)  8.44 us
    ppermute x4, starting transfers between devices, shift(): lax.ppermute(value, axis, [(i, (i + by) % count) for i in range(count)])  5.83 us
    pallas_call x8, Pallas kernels, call(): pl.pallas_call(functools.partial(kernel, z), out_shape=outs, in_specs=spe...  5.82 us
    ppermute x4, waiting for transfers between devices, shift(): lax.ppermute(value, axis, [(i, (i + by) % count) for i in range(count)])  1.61 us
  transfers between devices with their start and end apart: 5, of which 2 were waited for; matrix products, arithmetic and copies ran while one was open for 0% of the time, Pallas kernels for 4%

profile of v2, /device:TPU:0, one launch (start us, length us, event | category | flops | bytes accessed | tf_op | source)
XLA Modules:
  0.0 51.3 jit_solution(1945612787555392204)
XLA Ops:
  0.0 0.0 copy-start.1
  0.0 0.7 %copy-done.1 = f32[2,8,128]{2,1,0:T(8,128)S(1)} copy-done((f32[2,8,128]{2,1,0:T(8,128)S(1)}, f32[2,8,128]{2,1,0:T(8,128)}, u32[]{:S(2)}) %copy-start.1) | copy-done | bytes 8216
  0.7 0.7 %shard_map.73 = f32[16,16,128]{2,1,0:T(8,128)} custom-call(f32[16,128]{1,0:T(8,128)S(1)} %bitcast.6), custom_call_target="tpu_custom_call" | custom-call | flops 1000000 | bytes 1000000 | tf_op jit(solution)/shard_map/pallas_call | solution.py:396
  1.4 0.0 copy-start
  1.4 0.0 copy-start.2
  1.4 8.4 %all-to-all-start = ((f32[16,16,128]{2,1,0:T(8,128)}), f32[16,16,128]{2,1,0:T(8,128)S(1)}, u32[]{:S(2)}, u32[]{:S(2)}) async-start(f32[16,16,128]{2,1,0:T(8,128)} %shard_map.73), calls=%async_computation | async-start | bytes 262144 | tf_op jit(solution)/shard_map/all_to_all | solution.py:424
  9.8 0.0 copy-done
  9.8 0.0 copy-done.2
  9.8 0.0 copy-start.3
  9.9 0.0 copy-start.4
  9.9 0.1 collective-permute-start.2
  10.0 2.0 %collective-permute-start = (f32[32,128]{1,0:T(8,128)S(1)}, f32[32,128]{1,0:T(8,128)S(1)}, u32[]{:S(2)}, u32[]{:S(2)}) collective-permute-start(f32[32,128]{1,0:T(8,128)S(1)} %get-tuple-element.27), channel_id=1, source_target_pairs={{0,2},{2,4},{4,6},{6,8},{8,10},{10,12},{12,14},{14,16},{16,18},{18... | collective-permute-start | bytes 49160 | tf_op jit(solution)/shard_map/ppermute | solution.py:408
  12.0 0.0 copy-start.5
  12.0 0.0 copy-start.6
  12.0 0.0 copy-start.7
  12.0 3.7 %collective-permute-start.1 = (f32[32,128]{1,0:T(8,128)S(1)}, f32[32,128]{1,0:T(8,128)S(1)}, u32[]{:S(2)}, u32[]{:S(2)}) collective-permute-start(f32[32,128]{1,0:T(8,128)S(1)} %get-tuple-element.28), channel_id=1, source_target_pairs={{0,30},{2,0},{4,2},{6,4},{8,6},{10,8},{12,10},{14,12},{16,14},{18,... | collective-permute-start | bytes 49160 | tf_op jit(solution)/shard_map/ppermute | solution.py:408
  15.7 0.0 copy-done.3
  15.7 0.0 copy-done.4
  15.7 0.0 copy-done.5
  15.7 0.0 copy-done.6
  15.7 0.0 copy-done.7
  15.7 2.0 %shard_map.75 = (f32[16,16,128]{2,1,0:T(8,128)S(1)}, f32[4,16,128]{2,1,0:T(8,128)S(1)}, f32[2,16,128]{2,1,0:T(8,128)S(1)}, f32[16,16,128]{2,1,0:T(8,128)S(1)}, f...) custom-call(f32[256,128]{1,0:T(8,128)S(1)} %bitcast.5, ...), custom_call_target="tpu_custom_call" | custom-call | flops 1000000 | bytes 1000000 | tf_op jit(solution)/shard_map/pallas_call | solution.py:396
  17.7 0.7 %collective-permute-done.from_below = f32[32,128]{1,0:T(8,128)S(1)} collective-permute-done((f32[32,128]{1,0:T(8,128)S(1)}, f32[32,128]{1,0:T(8,128)S(1)}, u32[]{:S(2)}, u32[]{:S(2)}) %collective-permute-start) | collective-permute-done | bytes 16416 | tf_op jit(solution)/shard_map/ppermute | solution.py:408
  18.3 0.0 collective-permute-done.1.from_above
  18.3 0.0 collective-permute-done.2.refs_0_
  18.3 0.0 all-to-all-done.gathered
  18.3 1.3 %shard_map.76 = (f32[16,32,128]{2,1,0:T(8,128)S(1)}, f32[16,16,128]{2,1,0:T(8,128)S(1)}, f32[16,16,128]{2,1,0:T(8,128)S(1)}, f32[16,16,128]{2,1,0:T(8,128)S(1)},...) custom-call(f32[16,16,128]{2,1,0:T(8,128)S(1)} %all-to-all-done.gathered, f32[16,128]{1,0:T(8,128)S(1)} %bitcast.9, ...), custom_call_target="tpu_custom_call" | custom-call | flops 1000000 | bytes 1000000 | tf_op jit(solution)/shard_map/pallas_call | solution.py:396
  19.6 15.2 %all_to_all.15.received = f32[16,32,128]{2,1,0:T(8,128)S(1)} all-to-all(f32[16,32,128]{2,1,0:T(8,128)S(1)} %get-tuple-element.36), channel_id=1, replica_groups=mesh['gz'=16,'gy'=2] {'gz'}, dimensions={0} | all-to-all | bytes 524288 | tf_op jit(solution)/shard_map/all_to_all | solution.py:456
  34.8 0.1 shard_map.77
  34.9 0.1 collective-permute-start.3
  35.0 0.3 shard_map.78.base_ref
  35.3 0.9 %collective-permute-done.3.refs_0_ = f32[128,128]{1,0:T(8,128)S(1)} collective-permute-done((f32[128,128]{1,0:T(8,128)S(1)}, f32[128,128]{1,0:T(8,128)S(1)}, u32[]{:S(2)}, u32[]{:S(2)}) %collective-permute-start.3) | collective-permute-done | bytes 65568 | tf_op jit(solution)/shard_map/ppermute | solution.py:408
  36.2 0.8 %shard_map.79 = (f32[16,32,128]{2,1,0:T(8,128)S(1)}, f32[16,16,128]{2,1,0:T(8,128)S(1)}) custom-call(f32[16,16,128]{2,1,0:T(8,128)S(1)} %get-tuple-element.41.refs_0_.tiles_ref, f32[16,16,128]{2,1,0:T(8,128)S(1)} %shard_map.78.base_ref, f32[4,16,128]{2,1,0:T(8,128)S(1)} %get-tuple-element.44.halo_ref, f32[4,16,128]{2,1,0:T(8,128)S(1)} %get-tuple-element.31.rates_ref.refs_1_, ...), custom_call_target="tpu_custom_call" | custom-call | flops 1000000 | bytes 1000000 | tf_op jit(solution)/shard_map/pallas_call | solution.py:396
  37.0 13.5 %all_to_all.16.received = f32[16,32,128]{2,1,0:T(8,128)S(1)} all-to-all(f32[16,32,128]{2,1,0:T(8,128)S(1)} %get-tuple-element.47), channel_id=1, replica_groups=mesh['gz'=16,'gy'=2] {'gz'}, dimensions={0} | all-to-all | bytes 524288 | tf_op jit(solution)/shard_map/all_to_all | solution.py:469
  50.5 0.7 %shard_map.80 = f32[256,128]{1,0:T(8,128)} custom-call(f32[16,32,128]{2,1,0:T(8,128)S(1)} %all_to_all.16.received, f32[16,16,128]{2,1,0:T(8,128)S(1)} %get-tuple-element.48.f_ref, f32[16,16,128]{2,1,0:T(8,128)S(1)} %get-tuple-element.38.v_ref, f32[16,16,128]{2,1,0:T(8,128)S(1)} %get-tuple-element.39.u_ref, f32[10,16,128]{2,1,0:T(8,128)S(1)} %get-tuple-element.40.ends_ref), custom_call_target="tpu_custom_call" | custom-call | flops 1000000 | bytes 1000000 | tf_op jit(solution)/shard_map/pallas_call | solution.py:396
  (1 shorter events, 0.0 us)
Async XLA Ops:
  0.0 0.7 %copy-start.1 = (f32[2,8,128]{2,1,0:T(8,128)S(1)}, f32[2,8,128]{2,1,0:T(8,128)}, u32[]{:S(2)}) copy-start(f32[2,8,128]{2,1,0:T(8,128)} %param.8) | copy-start | bytes 24580
  1.4 8.5 %copy-start = (f32[16,2,8,128]{3,2,1,0:T(8,128)S(1)}, f32[16,2,8,128]{3,2,1,0:T(8,128)}, u32[]{:S(2)}) copy-start(f32[16,2,8,128]{3,2,1,0:T(8,128)} %param.7) | copy-start | bytes 393220
  1.4 8.5 %copy-start.2 = (f32[2,8,128]{2,1,0:T(8,128)S(1)}, f32[2,8,128]{2,1,0:T(8,128)}, u32[]{:S(2)}) copy-start(f32[2,8,128]{2,1,0:T(8,128)} %param.8) | copy-start | bytes 24580
  1.4 17.0 %all-to-all-start = ((f32[16,16,128]{2,1,0:T(8,128)}), f32[16,16,128]{2,1,0:T(8,128)S(1)}, u32[]{:S(2)}, u32[]{:S(2)}) async-start(f32[16,16,128]{2,1,0:T(8,128)} %shard_map.73), calls=%async_computation | async-start | bytes 262144 | tf_op jit(solution)/shard_map/all_to_all | solution.py:424
  9.8 5.8 %copy-start.3 = (f32[16,16]{1,0:T(8,128)S(1)}, f32[16,16]{1,0:T(8,128)}, u32[]{:S(2)}) copy-start(f32[16,16]{1,0:T(8,128)} %refs_4_.1) | copy-start | bytes 3076
  9.9 5.8 %copy-start.4 = (f32[2,8,128]{2,1,0:T(8,128)S(1)}, f32[2,8,128]{2,1,0:T(8,128)}, u32[]{:S(2)}) copy-start(f32[2,8,128]{2,1,0:T(8,128)} %param.9) | copy-start | bytes 24580
  9.9 8.4 %collective-permute-start.2 = (f32[136,128]{1,0:T(8,128)S(1)}, f32[136,128]{1,0:T(8,128)S(1)}, u32[]{:S(2)}, u32[]{:S(2)}) collective-permute-start(f32[136,128]{1,0:T(8,128)S(1)} %get-tuple-element.35), channel_id=1, source_target_pairs={{0,1},{1,0},{2,3},{3,2},{4,5},{5,4},{6,7},{7,6},{8,9},{9,8},{10,11... | collective-permute-start | bytes 208904 | tf_op jit(solution)/shard_map/ppermute | solution.py:408
  10.0 8.3 %collective-permute-start = (f32[32,128]{1,0:T(8,128)S(1)}, f32[32,128]{1,0:T(8,128)S(1)}, u32[]{:S(2)}, u32[]{:S(2)}) collective-permute-start(f32[32,128]{1,0:T(8,128)S(1)} %get-tuple-element.27), channel_id=1, source_target_pairs={{0,2},{2,4},{4,6},{6,8},{8,10},{10,12},{12,14},{14,16},{16,18},{18... | collective-permute-start | bytes 49160 | tf_op jit(solution)/shard_map/ppermute | solution.py:408
  12.0 3.7 %copy-start.5 = (f32[16]{0:T(128)S(1)}, f32[16]{0:T(128)}, u32[]{:S(2)}) copy-start(f32[16]{0:T(128)} %sigma_ref.1) | copy-start | bytes 196
  12.0 3.7 %copy-start.6 = (f32[16]{0:T(128)S(1)}, f32[16]{0:T(128)}, u32[]{:S(2)}) copy-start(f32[16]{0:T(128)} %frequency_ref.1) | copy-start | bytes 196
  12.0 3.7 %copy-start.7 = (f32[16]{0:T(128)S(1)}, f32[16]{0:T(128)}, u32[]{:S(2)}) copy-start(f32[16]{0:T(128)} %barrier_ref.1) | copy-start | bytes 196
  12.0 6.4 %collective-permute-start.1 = (f32[32,128]{1,0:T(8,128)S(1)}, f32[32,128]{1,0:T(8,128)S(1)}, u32[]{:S(2)}, u32[]{:S(2)}) collective-permute-start(f32[32,128]{1,0:T(8,128)S(1)} %get-tuple-element.28), channel_id=1, source_target_pairs={{0,30},{2,0},{4,2},{6,4},{8,6},{10,8},{12,10},{14,12},{16,14},{18,... | collective-permute-start | bytes 49160 | tf_op jit(solution)/shard_map/ppermute | solution.py:408
  34.9 1.3 %collective-permute-start.3 = (f32[128,128]{1,0:T(8,128)S(1)}, f32[128,128]{1,0:T(8,128)S(1)}, u32[]{:S(2)}, u32[]{:S(2)}) collective-permute-start(f32[128,128]{1,0:T(8,128)S(1)} %get-tuple-element.46), channel_id=1, source_target_pairs={{0,1},{1,0},{2,3},{3,2},{4,5},{5,4},{6,7},{7,6},{8,9},{9,8},{10,11... | collective-permute-start | bytes 196616 | tf_op jit(solution)/shard_map/ppermute | solution.py:408

commit v3 on v2

--- a/solution.py
+++ b/solution.py
@@ -20,6 +20,14 @@
         self.gy = mesh.shape["gy"]
         self.levels = (self.nx - 1).bit_length()
         self.tile = (self.species, self.nx)
+        padded = -(-self.ny // 8) * 8
+        self.edge_rows = self.lines + padded
+        self.members = 1 << (self.devices.bit_length() // 2)
+        self.groups_z = self.devices // self.members
+        self.faces_at = 2 * self.lines
+        self.block_rows = self.faces_at + self.tiles + padded
+        self.group_top = self.faces_at + self.members * self.tiles
+        self.group_rows = self.group_top + padded
 
     def per_device(self, body):
         if self.devices <= 16:
@@ -63,20 +71,15 @@
     return flag(me > 0), flag(me < count - 1)
 
 
-def spread_kernel(z, k_ref, pay_ref):
-    k = k_ref[...]
-
-    def fill(dest):
-        pay_ref[dest] = k
-
-    z.per_device(fill)
-
-
 def edges_kernel(z, c_ref, k_ref, up_ref, down_ref, *y_refs):
-    for y in range(z.ny):
-        lines = slice(y * z.species, (y + 1) * z.species)
-        down_ref[lines, :] = c_ref[pl.ds(y * z.nz, z.species, stride=z.tiles), :]
-        up_ref[lines, :] = c_ref[pl.ds(y * z.nz + z.nz - 1, z.species, stride=z.tiles), :]
+    for ref, row in ((down_ref, 0), (up_ref, z.nz - 1)):
+        for y in range(z.ny):
+            at = y * z.nz + row
+            ref[y * z.species : (y + 1) * z.species, :] = c_ref[
+                pl.ds(at, z.species, stride=z.tiles), :
+            ]
+            ref[z.lines + y : z.lines + y + 1, :] = k_ref[at : at + 1, :]
+        ref[z.lines + z.ny :, :] = jnp.zeros((z.edge_rows - z.lines - z.ny, z.nx), F32)
     for ref, y in zip(y_refs, y_picks(z)):
         for i in range(z.nz):
             ref[i * z.species : (i + 1) * z.species, :] = c_ref[
@@ -206,14 +209,17 @@
     pay_ref[me] = jnp.zeros((z.lines, z.nx), F32)
 
 
+def per_line(z, y):
+    return slice(y * z.species, (y + 1) * z.species)
+
+
 def first_kernel(
-    z, gathered, k_ref, from_below, from_above, tiles_ref, base_ref, rates_ref, left_ref, right_ref,
-    inverse_ref, *refs
+    z, k_ref, from_below, from_above, tiles_ref, base_ref, rates_ref, left_ref, right_ref, inverse_ref,
+    *refs
 ):
     halos = 1 if z.gy == 2 else 2
     y_received = refs[:halos]
-    pay_ref, f_ref, v_ref, u_ref, ends_ref, faces, resistance = refs[halos:]
-    me = lax.axis_index("gz")
+    pay_ref, f_ref, faces = refs[halos:]
     k = k_ref[...]
     low, high = y_received[0], y_received[-1]
     low_mask, high_mask = inner("gy", z.gy)
@@ -223,96 +229,194 @@
     faces[0] = 0.5 * (k + below)
     faces[1] = 0.5 * (k + above)
 
+    z_low, z_high = inner("gz", z.devices)
     rows = lax.broadcasted_iota(jnp.int32, (z.nz, z.nx), 0)
+    pay_ref[z.faces_at + z.tiles :, :] = jnp.zeros((z.block_rows - z.faces_at - z.tiles, z.nx), F32)
     for y in range(z.ny):
-        base = y * z.nz
-
-        def invert(j):
-            here = gathered[j, base : base + z.nz, :]
-            before = gathered[jnp.maximum(j - 1, 0), base + z.nz - 1 : base + z.nz, :]
-            before = jnp.broadcast_to(jnp.where(j > 0, before, 0.0), here.shape)
-            total = here + jnp.where(rows == 0, before, pltpu.roll(here, 1, 0))
-            resistance[y, pl.ds(pl.multiple_of(j * z.nz, z.nz), z.nz), :] = 1.0 / total
-
-        z.per_device(invert)
-        last = gathered[z.devices - 1, base + z.nz - 1 : base + z.nz, :]
-        resistance[y, z.devices * z.nz :, :] = jnp.broadcast_to(1.0 / last, (z.nz, z.nx))
-
-    per_species = rates_ref[3]
-
-    def ohm(y, row):
-        return per_species * spread(resistance.at[y], row, z)
-
-    def advance(state, row):
-        out = []
-        for y in range(z.ny):
-            v, w = state[2 * y : 2 * y + 2]
-            v = v + w * ohm(y, row)
-            out += [v, w + v]
-        return tuple(out)
-
-    def forward(j, state):
-        for i in range(z.nz):
-            state = advance(state, j * z.nz + i)
-        return state
-
-    def backward(j, state):
-        for i in range(z.nz):
-            state = advance(state, (z.devices - j) * z.nz - i)
-        return state
-
-    start = (jnp.zeros(z.tile, F32), jnp.ones(z.tile, F32)) * z.ny
-    first = me * z.nz
-    state = lax.fori_loop(0, me, forward, start)
-    rising = []
-    for y in range(z.ny):
-        ends_ref[y] = state[2 * y]
-    for i in range(z.nz + 1):
-        state = advance(state, first + i)
-        rising.append(state)
-    for y in range(z.ny):
-        ends_ref[z.ny + y] = state[2 * y]
-        for i in range(z.nz):
-            v_ref[y * z.nz + i] = rising[i][2 * y]
-            row = first + i
-            faces[2, y * z.nz + i : y * z.nz + i + 1, :] = 0.5 / resistance[y, pl.ds(row, 1), :]
-            faces[3, y * z.nz + i : y * z.nz + i + 1, :] = 0.5 / resistance[y, pl.ds(row + 1, 1), :]
-    state = lax.fori_loop(0, z.devices - 1 - me, backward, start)
-    for y in range(z.ny):
-        ends_ref[3 * z.ny + y] = state[2 * y]
-    for i in reversed(range(z.nz)):
-        state = advance(state, first + i + 1)
-        for y in range(z.ny):
-            u_ref[y * z.nz + i] = state[2 * y]
-            if i == 0:
-                u, wu = state[2 * y : 2 * y + 2]
-                v, wv = rising[0][2 * y : 2 * y + 2]
-                ends_ref[4 * z.ny + y] = 1.0 / (wv * u + v * (wu - u))
-    state = advance(state, first)
-    for y in range(z.ny):
-        ends_ref[2 * z.ny + y] = state[2 * y]
-
-    z_low, z_high = inner("gz", z.devices)
+        own = slice(y * z.nz, (y + 1) * z.nz)
+        here = k[own]
+        row = z.lines + y
+        before = jnp.broadcast_to(from_below[row : row + 1, :] * z_low, here.shape)
+        after = jnp.broadcast_to(from_above[row : row + 1, :] * z_high, here.shape)
+        before = here + jnp.where(rows == 0, before, pltpu.roll(here, 1, 0))
+        after = here + jnp.where(rows == z.nz - 1, after, pltpu.roll(here, z.nz - 1, 0))
+        faces[2, own, :] = 0.5 * before
+        faces[3, own, :] = 0.5 * after
+        pay_ref[z.faces_at + y * z.nz : z.faces_at + (y + 1) * z.nz, :] = 1.0 / before
+        top = z.faces_at + z.tiles + y
+        pay_ref[top : top + 1, :] = 1.0 / after[z.nz - 1 :, :]
 
     def z_halo(side, y):
-        lines = slice(y * z.species, (y + 1) * z.species)
+        lines = per_line(z, y)
         return from_above[lines, :] * z_high if side else from_below[lines, :] * z_low
 
     def y_halo(side, row):
-        lines = slice(row * z.species, (row + 1) * z.species)
+        lines = per_line(z, row)
         return high[lines, :] * high_mask if side else low[lines, :] * low_mask
 
     right_sides(
         z, tiles_ref, base_ref, z_halo, y_halo, rates_ref, faces, left_ref, right_ref, inverse_ref, f_ref
     )
-    send_sums(z, f_ref, v_ref, u_ref, pay_ref)
-
-
-def solve_lines(z, received, f_ref, v_ref, u_ref, ends_ref, store):
+    ohms = rates_ref[3]
+    zero, one = jnp.zeros(z.tile, F32), jnp.ones(z.tile, F32)
+    for y in range(z.ny):
+        p, q, first, second = (one, zero), (zero, one), zero, zero
+        for i in range(z.nz):
+            ohm = ohms * spread(pay_ref, z.faces_at + y * z.nz + i, z)
+            p, q = advance(p, ohm), advance(q, ohm)
+            f = f_ref[y * z.nz + i]
+            first = first + p[0] * f
+            second = second + q[0] * f
+        pay_ref[per_line(z, y), :] = first
+        pay_ref[per_line(z, z.ny + y), :] = second
+
+
+def advance(state, ohm):
+    v, w = state
+    v = v + w * ohm
+    return v, w + v
+
+
+def merge_kernel(z, rates_ref, pay_ref, *refs):
+    *received, group_ref, order = refs
+    me = lax.axis_index("gz") % z.members
+    order[me] = pay_ref[...]
+    for i, ref in enumerate(received):
+        order[me ^ (i + 1)] = ref[...]
+    ohms = rates_ref[3]
+    zero, one = jnp.zeros(z.tile, F32), jnp.ones(z.tile, F32)
+    for y in range(z.ny):
+        p, q, first, second = (one, zero), (zero, one), zero, zero
+        for j in range(z.members):
+            s1, s2 = order[j, per_line(z, y), :], order[j, per_line(z, z.ny + y), :]
+            first = first + (p[0] * s1 + p[1] * s2)
+            second = second + (q[0] * s1 + q[1] * s2)
+            if j < z.members - 1:
+                for i in range(z.nz):
+                    ohm = ohms * spread(order.at[j], z.faces_at + y * z.nz + i, z)
+                    p, q = advance(p, ohm), advance(q, ohm)
+        group_ref[per_line(z, y), :] = first
+        group_ref[per_line(z, z.ny + y), :] = second
+    for j in range(z.members):
+        start = z.faces_at + j * z.tiles
+        group_ref[start : start + z.tiles, :] = order[j, z.faces_at : z.faces_at + z.tiles, :]
+    group_ref[z.group_top :, :] = order[z.members - 1, z.faces_at + z.tiles :, :]
+
+
+def both_ways(z, rates_ref, order, groups, v_ref, u_ref, ends_ref):
     me = lax.axis_index("gz")
-    halos = []
+    group, member = me // z.members, me % z.members
+    ohms = rates_ref[3]
+    zero, one = jnp.zeros(z.tile, F32), jnp.ones(z.tile, F32)
+    ys = range(z.ny)
+
+    def ohm(ref, row):
+        return ohms * spread(ref, row, z)
+
+    def totals(ref, y):
+        return ref[per_line(z, y), :], ref[per_line(z, z.ny + y), :]
+
+    def up_rows(ref, start, state):
+        state = list(state)
+        for i in range(z.nz):
+            for y in ys:
+                state[3 * y : 3 * y + 2] = advance(
+                    state[3 * y : 3 * y + 2], ohm(ref, start + y * z.nz + i)
+                )
+        return tuple(state)
+
+    def up_add(ref, state):
+        state = list(state)
+        for y in ys:
+            s1, s2 = totals(ref, y)
+            state[3 * y + 2] = state[3 * y + 2] + (state[3 * y] * s1 + state[3 * y + 1] * s2)
+        return tuple(state)
+
+    def up_group(g, state):
+        ref = groups.at[g]
+        return lax.fori_loop(
+            0,
+            z.members,
+            lambda j, s: up_rows(ref, z.faces_at + j * z.tiles, s),
+            up_add(ref, state),
+        )
+
+    def up_block(j, state):
+        ref = order.at[j]
+        return up_rows(ref, z.faces_at, up_add(ref, state))
+
+    state = (zero, one, zero) * z.ny
+    state = lax.fori_loop(0, group, up_group, state)
+    state = lax.fori_loop(0, member, up_block, state)
+    below, rising = [], []
+    mine = order.at[member]
+    for y in ys:
+        pair = state[3 * y : 3 * y + 2]
+        below.append(state[3 * y + 2])
+        ends_ref[y] = pair[0]
+        for i in range(z.nz):
+            pair = advance(pair, ohm(mine, z.faces_at + y * z.nz + i))
+            v_ref[y * z.nz + i] = pair[0]
+            if i == 0:
+                rising.append(pair)
+        ends_ref[z.ny + y] = pair[0] + pair[1] * ohm(mine, z.faces_at + z.tiles + y)
+
+    def down_rows(ref, start, state):
+        state = list(state)
+        for i in reversed(range(z.nz)):
+            for y in ys:
+                _, u, w, total = state[4 * y : 4 * y + 4]
+                w = w + u
+                state[4 * y : 4 * y + 4] = [u, u + w * ohm(ref, start + y * z.nz + i), w, total]
+        return tuple(state)
+
+    def down_add(ref, state):
+        state = list(state)
+        for y in ys:
+            s1, s2 = totals(ref, y)
+            state[4 * y + 3] = state[4 * y + 3] + (state[4 * y + 1] * s1 - state[4 * y + 2] * s2)
+        return tuple(state)
+
+    def down_group(i, state):
+        ref = groups.at[z.groups_z - 1 - i]
+        state = lax.fori_loop(
+            0,
+            z.members,
+            lambda j, s: down_rows(ref, z.faces_at + (z.members - 1 - j) * z.tiles, s),
+            state,
+        )
+        return down_add(ref, state)
+
+    def down_block(i, state):
+        ref = order.at[z.members - 1 - i]
+        return down_add(ref, down_rows(ref, z.faces_at, state))
+
+    state = ()
+    for y in ys:
+        state += (zero, ohm(groups.at[z.groups_z - 1], z.group_top + y), one, zero)
+    state = lax.fori_loop(0, z.groups_z - 1 - group, down_group, state)
+    state = lax.fori_loop(0, z.members - 1 - member, down_block, state)
+    above = []
+    for y in ys:
+        last, u, w, total = state[4 * y : 4 * y + 4]
+        above.append(total)
+        ends_ref[3 * z.ny + y] = last
+        for i in reversed(range(z.nz)):
+            u_ref[y * z.nz + i] = u
+            if i == 0:
+                v, wv = rising[y]
+                ends_ref[4 * z.ny + y] = 1.0 / (wv * u + v * w)
+            w = w + u
+            u = u + w * ohm(mine, z.faces_at + y * z.nz + i)
+        ends_ref[2 * z.ny + y] = u
+    return below, above
+
+
+def gathered_sums(z, received):
+    me = lax.axis_index("gz")
+    below, above = [], []
     for y in range(z.ny):
-        lines = slice(y * z.species, (y + 1) * z.species)
+        lines = per_line(z, y)
         zero = jnp.zeros(z.tile, F32)
         sums = [zero, zero]
 
@@ -326,7 +430,14 @@
                 sums = add(j, sums)
         else:
             sums = lax.fori_loop(0, z.devices, add, sums)
-        below, above = sums
+        below.append(sums[0])
+        above.append(sums[1])
+    return below, above
+
+
+def solve_lines(z, sums, f_ref, v_ref, u_ref, ends_ref, store):
+    halos = []
+    for y, (below, above) in enumerate(zip(*sums)):
         scale = ends_ref[4 * z.ny + y]
         tiles = range(y * z.nz, (y + 1) * z.nz)
         after = {}
@@ -344,16 +455,42 @@
     return halos
 
 
-def middle_kernel(z, received, f_ref, v_ref, u_ref, ends_ref, tiles_ref, halo_ref, *y_refs):
-    def store(t, value):
-        tiles_ref[t] = value
-
-    for y, (low, high) in enumerate(solve_lines(z, received, f_ref, v_ref, u_ref, ends_ref, store)):
+def hand_on(z, halos, tiles_ref, halo_ref, y_refs):
+    for y, (low, high) in enumerate(halos):
         halo_ref[y] = low
         halo_ref[z.ny + y] = high
     for ref, y in zip(y_refs, y_picks(z)):
         for i in range(z.nz):
             ref[i * z.species : (i + 1) * z.species, :] = tiles_ref[y * z.nz + i]
+
+
+def meet_kernel(z, rates_ref, f_ref, pay_ref, own_group, *refs):
+    inside, across = refs[: z.members - 1], refs[z.members - 1 : z.members + z.groups_z - 2]
+    refs = refs[z.members + z.groups_z - 2 :]
+    tiles_ref, halo_ref, v_ref, u_ref, ends_ref, *y_refs, order, groups = refs
+    me = lax.axis_index("gz")
+    group, member = me // z.members, me % z.members
+    order[member] = pay_ref[...]
+    for i, ref in enumerate(inside):
+        order[member ^ (i + 1)] = ref[...]
+    groups[group] = own_group[...]
+    for i, ref in enumerate(across):
+        groups[group ^ (i + 1)] = ref[...]
+    sums = both_ways(z, rates_ref, order, groups, v_ref, u_ref, ends_ref)
+
+    def store(t, value):
+        tiles_ref[t] = value
+
+    halos = solve_lines(z, sums, f_ref, v_ref, u_ref, ends_ref, store)
+    hand_on(z, halos, tiles_ref, halo_ref, y_refs)
+
+
+def middle_kernel(z, received, f_ref, v_ref, u_ref, ends_ref, tiles_ref, halo_ref, *y_refs):
+    def store(t, value):
+        tiles_ref[t] = value
+
+    halos = solve_lines(z, gathered_sums(z, received), f_ref, v_ref, u_ref, ends_ref, store)
+    hand_on(z, halos, tiles_ref, halo_ref, y_refs)
 
 
 def second_kernel(
@@ -380,7 +517,7 @@
     def store(t, value):
         out_ref[pl.ds(t, z.species, stride=z.tiles), :] = value
 
-    solve_lines(z, received, f_ref, v_ref, u_ref, ends_ref, store)
+    solve_lines(z, gathered_sums(z, received), f_ref, v_ref, u_ref, ends_ref, store)
 
 
 def per_device(z, c, k, warm, sigma, frequency, barrier, proportions):
@@ -418,13 +555,18 @@
     warm = warm.reshape(z.tiles, z.nx)
     halos = 1 if z.gy == 2 else 2
     block = shaped(z.tiles, *z.tile)
-    per_line = shaped(z.devices, z.lines, z.nx)
-
-    pay = call(spread_kernel, shaped(z.devices, z.tiles, z.nx), in_vmem(k))
-    gathered = lax.all_to_all(pay, "gz", 0, 0, tiled=True)
+    per_peer = shaped(z.devices, z.lines, z.nx)
+    ends_shape = shaped(5 * z.ny, *z.tile)
+    current = [block, shaped(2 * z.ny, *z.tile)]
+    y_edges = [shaped(z.nz * z.species, z.nx)] * halos
+
+    def exchange(value, count, unit):
+        pairs = [[(i, i ^ (k * unit)) for i in range(z.devices)] for k in range(1, count)]
+        return [lax.ppermute(value, "gz", p) for p in pairs]
+
     up, down, *sends = call(
         edges_kernel,
-        [shaped(z.lines, z.nx)] * 2 + [shaped(z.nz * (z.species + 1), z.nx)] * halos,
+        [shaped(z.edge_rows, z.nx)] * 2 + [shaped(z.nz * (z.species + 1), z.nx)] * halos,
         in_vmem(c, k),
     )
     from_below, from_above = shift(up, "gz", 1), shift(down, "gz", -1)
@@ -446,24 +588,39 @@
         + in_vmem(proportions),
         [pltpu.VMEM((z.tiles, z.nx), F32)],
     )
-    pay, f, v, u, ends, faces = call(
+    pay, f, faces = call(
         first_kernel,
-        [per_line, block, block, block, shaped(5 * z.ny, *z.tile), shaped(4, z.tiles, z.nx)],
-        in_vmem(gathered, k, from_below, from_above, tiles, base, rates, left, right, inverse, *received),
-        [pltpu.VMEM((z.ny, z.devices * z.nz + z.nz, z.nx), F32)],
-    )
-    for _ in range(STEPS - 1):
-        sums = lax.all_to_all(pay, "gz", 0, 0, tiled=True)
-        tiles, halo, *sends = call(
-            middle_kernel,
-            [block, shaped(2 * z.ny, *z.tile)] + [shaped(z.nz * z.species, z.nx)] * halos,
-            in_vmem(sums, f, v, u, ends),
-        )
+        [shaped(z.block_rows, z.nx), block, shaped(4, z.tiles, z.nx)],
+        in_vmem(k, from_below, from_above, tiles, base, rates, left, right, inverse, *received),
+    )
+    inside = exchange(pay, z.members, 1)
+    group = call(
+        merge_kernel,
+        shaped(z.group_rows, z.nx),
+        in_vmem(rates, pay, *inside),
+        [pltpu.VMEM((z.members, z.block_rows, z.nx), F32)],
+    )
+    across = exchange(group, z.groups_z, z.members)
+    tiles, halo, v, u, ends, *sends = call(
+        meet_kernel,
+        [*current, block, block, ends_shape, *y_edges],
+        in_vmem(rates, f, pay, group, *inside, *across),
+        [
+            pltpu.VMEM((z.members, z.block_rows, z.nx), F32),
+            pltpu.VMEM((z.groups_z, z.group_rows, z.nx), F32),
+        ],
+    )
+    for step in range(1, STEPS):
+        if step > 1:
+            sums = lax.all_to_all(pay, "gz", 0, 0, tiled=True)
+            tiles, halo, *sends = call(
+                middle_kernel, [*current, *y_edges], in_vmem(sums, f, v, u, ends)
+            )
         received = swap(sends)
         base = call(base_kernel, block, in_vmem(tiles, rates, x_faces, arrhenius, proportions))
         pay, f = call(
             second_kernel,
-            [per_line, block],
+            [per_peer, block],
             in_vmem(tiles, base, halo, rates, faces, left, right, inverse, v, u, *received),
         )
     sums = lax.all_to_all(pay, "gz", 0, 0, tiled=True)

time: 51.6 us -> 45.5 us (0.88)
  blocking collectives: 28.7 us -> 14.9 us
  waiting for transfers between devices: 1.61 us -> 8.01 us
  starting transfers between devices: 14.3 us -> 15.5 us
  local copies, waits for them, and re-layouts: 0.73 us -> 1.62 us
  Pallas kernels: 5.82 us -> 5.2 us
    all_to_all x2 -> x1, blocking collectives: 28.7 us -> 14.9 us  [per_device(): sums = lax.all_to_all(pay, 'gz', 0, 0, tiled=True)]
    all_to_all x1 -> x0, starting transfers between devices: 8.44 us -> none  [per_device(): gathered = lax.all_to_all(pay, 'gz', 0, 0, tiled=True)]
    ppermute x0 -> x6, starting transfers between devices: none -> 8.26 us  [exchange(): return [lax.ppermute(value, 'gz', p) for p in pairs]]
    ppermute x0 -> x6, waiting for transfers between devices: none -> 7.05 us  [exchange(): return [lax.ppermute(value, 'gz', p) for p in pairs]]
    ppermute x4, starting transfers between devices: 5.83 us -> 7.23 us  [shift(): lax.ppermute(value, axis, [(i, (i + by) % count) for i in range(count)])]
    unnamed x16 -> x14, local copies, waits for them, and re-layouts: 0.73 us -> 1.62 us
    ppermute x4, waiting for transfers between devices: 1.61 us -> 0.96 us  [shift(): lax.ppermute(value, axis, [(i, (i + by) % count) for i in range(count)])]
    pallas_call x8, Pallas kernels: 5.82 us -> 5.2 us  [call(): pl.pallas_call(functools.partial(kernel, z), out_shape=outs, in_specs=spe...]
  transfers between devices with their start and end apart: 5 -> 10, of which waited for: 2 -> 5; matrix products, arithmetic and copies ran while one was open for 0% -> 0% of each run, Pallas kernels for 4% -> 5%
where the time goes in v3:
time: 45.5 us; the launch traced here: 45.3 us
  starting transfers between devices  15.5 us (34%)
  blocking collectives  14.9 us (33%)
  waiting for transfers between devices  8.01 us (18%)
  Pallas kernels  5.2 us (11%)
  local copies, waits for them, and re-layouts  1.62 us (4%)
    all_to_all x1, blocking collectives, per_device(): sums = lax.all_to_all(pay, 'gz', 0, 0, tiled=True)  14.9 us
    ppermute x6, starting transfers between devices, exchange(): return [lax.ppermute(value, 'gz', p) for p in pairs]  8.26 us
    ppermute x4, starting transfers between devices, shift(): lax.ppermute(value, axis, [(i, (i + by) % count) for i in range(count)])  7.23 us
    ppermute x6, waiting for transfers between devices, exchange(): return [lax.ppermute(value, 'gz', p) for p in pairs]  7.05 us
    pallas_call x8, Pallas kernels, call(): pl.pallas_call(functools.partial(kernel, z), out_shape=outs, in_specs=spe...  5.2 us
    unnamed x14, local copies, waits for them, and re-layouts  1.62 us
    ppermute x4, waiting for transfers between devices, shift(): lax.ppermute(value, axis, [(i, (i + by) % count) for i in range(count)])  0.96 us
  transfers between devices with their start and end apart: 10, of which 5 were waited for; matrix products, arithmetic and copies ran while one was open for 0% of the time, Pallas kernels for 5%

profile of v3, /device:TPU:0, one launch (start us, length us, event | category | flops | bytes accessed | tf_op | source)
XLA Modules:
  0.0 45.3 jit_solution(15713474996589832918)
XLA Ops:
  0.0 0.0 copy-start
  0.0 0.9 %copy-done = f32[16,2,8,128]{3,2,1,0:T(8,128)S(1)} copy-done((f32[16,2,8,128]{3,2,1,0:T(8,128)S(1)}, f32[16,2,8,128]{3,2,1,0:T(8,128)}, u32[]{:S(2)}) %copy-start) | copy-done | bytes 131096
  0.9 0.0 copy-start.1
  0.9 0.7 %copy-done.1 = f32[2,8,128]{2,1,0:T(8,128)S(1)} copy-done((f32[2,8,128]{2,1,0:T(8,128)S(1)}, f32[2,8,128]{2,1,0:T(8,128)}, u32[]{:S(2)}) %copy-start.1) | copy-done | bytes 8216
  1.6 0.0 copy-start.2
  1.6 0.0 copy-start.3
  1.6 0.5 %collective-permute-start.2 = (f32[136,128]{1,0:T(8,128)S(1)}, f32[136,128]{1,0:T(8,128)S(1)}, u32[]{:S(2)}, u32[]{:S(2)}) collective-permute-start(f32[136,128]{1,0:T(8,128)S(1)} %get-tuple-element.35), channel_id=1, source_target_pairs={{0,1},{1,0},{2,3},{3,2},{4,5},{5,4},{6,7},{7,6},{8,9},{9,8},{10,11... | collective-permute-start | bytes 208904 | tf_op jit(solution)/shard_map/ppermute | solution.py:545
  2.2 2.6 %collective-permute-start = (f32[40,128]{1,0:T(8,128)S(1)}, f32[40,128]{1,0:T(8,128)S(1)}, u32[]{:S(2)}, u32[]{:S(2)}) collective-permute-start(f32[40,128]{1,0:T(8,128)S(1)} %get-tuple-element.28), channel_id=1, source_target_pairs={{0,2},{2,4},{4,6},{6,8},{8,10},{10,12},{12,14},{14,16},{16,18},{18... | collective-permute-start | bytes 61448 | tf_op jit(solution)/shard_map/ppermute | solution.py:545
  4.7 0.0 copy-start.4
  4.7 0.0 copy-start.5
  4.7 0.0 copy-start.6
  4.7 4.1 %collective-permute-start.1 = (f32[40,128]{1,0:T(8,128)S(1)}, f32[40,128]{1,0:T(8,128)S(1)}, u32[]{:S(2)}, u32[]{:S(2)}) collective-permute-start(f32[40,128]{1,0:T(8,128)S(1)} %get-tuple-element.29), channel_id=1, source_target_pairs={{0,30},{2,0},{4,2},{6,4},{8,6},{10,8},{12,10},{14,12},{16,14},{18,... | collective-permute-start | bytes 61448 | tf_op jit(solution)/shard_map/ppermute | solution.py:545
  8.8 0.0 copy-done.2
  8.8 0.0 copy-done.3
  8.8 0.0 copy-done.4
  8.8 0.0 copy-done.5
  8.8 0.0 copy-done.6
  8.8 2.0 %shard_map.73 = (f32[16,16,128]{2,1,0:T(8,128)S(1)}, f32[4,16,128]{2,1,0:T(8,128)S(1)}, f32[2,16,128]{2,1,0:T(8,128)S(1)}, f32[16,16,128]{2,1,0:T(8,128)S(1)}, f...) custom-call(f32[256,128]{1,0:T(8,128)S(1)} %bitcast.5, ...), custom_call_target="tpu_custom_call" | custom-call | flops 1000000 | bytes 1000000 | tf_op jit(solution)/shard_map/pallas_call | solution.py:533
  10.8 0.0 collective-permute-done.from_below
  10.8 0.0 collective-permute-done.1.from_above
  10.8 0.0 collective-permute-done.2.refs_0_
  10.8 0.7 %shard_map.75 = (f32[88,128]{1,0:T(8,128)S(1)}, f32[16,16,128]{2,1,0:T(8,128)S(1)}, f32[4,16,128]{2,1,0:T(8,128)S(1)}) custom-call(f32[16,128]{1,0:T(8,128)S(1)} %bitcast.8, f32[40,128]{1,0:T(8,128)S(1)} %collective-permute-done.from_below, f32[40,128]{1,0:T(8,128)S(1)} %collective-permute-done.1.from_above, f32[16,16,128]{2,1,0:T(8,128)S(1)} %get-tuple-element.30.tiles_ref, ...), custom_call_target="tpu_custom_call" | custom-call | flops 1000000 | bytes 1000000 | tf_op jit(solution)/shard_map/pallas_call | solution.py:533
  11.5 2.0 %collective-permute-start.5 = (f32[88,128]{1,0:T(8,128)S(1)}, f32[88,128]{1,0:T(8,128)S(1)}, u32[]{:S(2)}, u32[]{:S(2)}) collective-permute-start(f32[88,128]{1,0:T(8,128)S(1)} %get-tuple-element.37.pay_ref), channel_id=1, source_target_pairs={{0,6},{2,4},{4,2},{6,0},{8,14},{10,12},{12,10},{14,8},{16,22},{18,... | collective-permute-start | bytes 135176 | tf_op jit(solution)/shard_map/ppermute | solution.py:565
  13.5 0.0 collective-permute-start.4
  13.5 1.6 %collective-permute-start.3 = (f32[88,128]{1,0:T(8,128)S(1)}, f32[88,128]{1,0:T(8,128)S(1)}, u32[]{:S(2)}, u32[]{:S(2)}) collective-permute-start(f32[88,128]{1,0:T(8,128)S(1)} %get-tuple-element.37.pay_ref), channel_id=1, source_target_pairs={{0,2},{2,0},{4,6},{6,4},{8,10},{10,8},{12,14},{14,12},{16,18},{18,... | collective-permute-start | bytes 135176 | tf_op jit(solution)/shard_map/ppermute | solution.py:565
  15.1 1.9 %collective-permute-done.5.refs_2_ = f32[88,128]{1,0:T(8,128)S(1)} collective-permute-done((f32[88,128]{1,0:T(8,128)S(1)}, f32[88,128]{1,0:T(8,128)S(1)}, u32[]{:S(2)}, u32[]{:S(2)}) %collective-permute-start.5) | collective-permute-done | bytes 45088 | tf_op jit(solution)/shard_map/ppermute | solution.py:565
  17.0 0.6 %collective-permute-done.4.refs_1_ = f32[88,128]{1,0:T(8,128)S(1)} collective-permute-done((f32[88,128]{1,0:T(8,128)S(1)}, f32[88,128]{1,0:T(8,128)S(1)}, u32[]{:S(2)}, u32[]{:S(2)}) %collective-permute-start.4) | collective-permute-done | bytes 45088 | tf_op jit(solution)/shard_map/ppermute | solution.py:565
  17.5 0.0 collective-permute-done.3.refs_0_
  17.6 0.1 shard_map.76.own_group
  17.7 4.1 %collective-permute-start.8 = (f32[136,128]{1,0:T(8,128)S(1)}, f32[136,128]{1,0:T(8,128)S(1)}, u32[]{:S(2)}, u32[]{:S(2)}) collective-permute-start(f32[136,128]{1,0:T(8,128)S(1)} %shard_map.76.own_group), channel_id=1, source_target_pairs={{0,24},{2,26},{4,28},{6,30},{8,16},{10,18},{12,20},{14,22},{16,8},... | collective-permute-start | bytes 208904 | tf_op jit(solution)/shard_map/ppermute | solution.py:565
  21.8 0.0 collective-permute-start.7
  21.8 0.6 %collective-permute-start.6 = (f32[136,128]{1,0:T(8,128)S(1)}, f32[136,128]{1,0:T(8,128)S(1)}, u32[]{:S(2)}, u32[]{:S(2)}) collective-permute-start(f32[136,128]{1,0:T(8,128)S(1)} %shard_map.76.own_group), channel_id=1, source_target_pairs={{0,8},{2,10},{4,12},{6,14},{8,0},{10,2},{12,4},{14,6},{16,24},{18,... | collective-permute-start | bytes 208904 | tf_op jit(solution)/shard_map/ppermute | solution.py:565
  22.4 1.7 %collective-permute-done.8.refs_5_ = f32[136,128]{1,0:T(8,128)S(1)} collective-permute-done((f32[136,128]{1,0:T(8,128)S(1)}, f32[136,128]{1,0:T(8,128)S(1)}, u32[]{:S(2)}, u32[]{:S(2)}) %collective-permute-start.8) | collective-permute-done | bytes 69664 | tf_op jit(solution)/shard_map/ppermute | solution.py:565
  24.2 2.8 %collective-permute-done.7.refs_4_ = f32[136,128]{1,0:T(8,128)S(1)} collective-permute-done((f32[136,128]{1,0:T(8,128)S(1)}, f32[136,128]{1,0:T(8,128)S(1)}, u32[]{:S(2)}, u32[]{:S(2)}) %collective-permute-start.7) | collective-permute-done | bytes 69664 | tf_op jit(solution)/shard_map/ppermute | solution.py:565
  27.0 0.0 collective-permute-done.6.refs_3_
  27.0 0.6 %shard_map.77 = (f32[16,16,128]{2,1,0:T(8,128)S(1)}, f32[4,16,128]{2,1,0:T(8,128)S(1)}, f32[16,16,128]{2,1,0:T(8,128)S(1)}, f32[16,16,128]{2,1,0:T(8,128)S(1)}, ...) custom-call(f32[4,16,128]{2,1,0:T(8,128)S(1)} %get-tuple-element.27.rates_ref.refs_1_, ...), custom_call_target="tpu_custom_call" | custom-call | flops 1000000 | bytes 1000000 | tf_op jit(solution)/shard_map/pallas_call | solution.py:533
  27.6 0.1 collective-permute-start.9
  27.7 0.3 shard_map.78.base_ref
  27.9 0.9 %collective-permute-done.9.refs_0_ = f32[128,128]{1,0:T(8,128)S(1)} collective-permute-done((f32[128,128]{1,0:T(8,128)S(1)}, f32[128,128]{1,0:T(8,128)S(1)}, u32[]{:S(2)}, u32[]{:S(2)}) %collective-permute-start.9) | collective-permute-done | bytes 65568 | tf_op jit(solution)/shard_map/ppermute | solution.py:545
  28.9 0.8 %shard_map.79 = (f32[16,32,128]{2,1,0:T(8,128)S(1)}, f32[16,16,128]{2,1,0:T(8,128)S(1)}) custom-call(f32[16,16,128]{2,1,0:T(8,128)S(1)} %get-tuple-element.38.refs_0_.tiles_ref, f32[16,16,128]{2,1,0:T(8,128)S(1)} %shard_map.78.base_ref, f32[4,16,128]{2,1,0:T(8,128)S(1)} %get-tuple-element.41.halo_ref, f32[4,16,128]{2,1,0:T(8,128)S(1)} %get-tuple-element.27.rates_ref.refs_1_, ...), custom_call_target="tpu_custom_call" | custom-call | flops 1000000 | bytes 1000000 | tf_op jit(solution)/shard_map/pallas_call | solution.py:533
  29.7 14.9 %all_to_all.5.received = f32[16,32,128]{2,1,0:T(8,128)S(1)} all-to-all(f32[16,32,128]{2,1,0:T(8,128)S(1)} %get-tuple-element.46), channel_id=1, replica_groups=mesh['gz'=16,'gy'=2] {'gz'}, dimensions={0} | all-to-all | bytes 524288 | tf_op jit(solution)/shard_map/all_to_all | solution.py:626
  44.5 0.7 %shard_map.80 = f32[256,128]{1,0:T(8,128)} custom-call(f32[16,32,128]{2,1,0:T(8,128)S(1)} %all_to_all.5.received, f32[16,16,128]{2,1,0:T(8,128)S(1)} %get-tuple-element.47.f_ref, f32[16,16,128]{2,1,0:T(8,128)S(1)} %get-tuple-element.43.v_ref, f32[16,16,128]{2,1,0:T(8,128)S(1)} %get-tuple-element.44.u_ref, f32[10,16,128]{2,1,0:T(8,128)S(1)} %get-tuple-element.48.ends_ref), custom_call_target="tpu_custom_call" | custom-call | flops 1000000 | bytes 1000000 | tf_op jit(solution)/shard_map/pallas_call | solution.py:533
  (1 shorter events, 0.0 us)
Async XLA Ops:
  0.0 0.9 %copy-start = (f32[16,2,8,128]{3,2,1,0:T(8,128)S(1)}, f32[16,2,8,128]{3,2,1,0:T(8,128)}, u32[]{:S(2)}) copy-start(f32[16,2,8,128]{3,2,1,0:T(8,128)} %param.7) | copy-start | bytes 393220
  0.9 0.7 %copy-start.1 = (f32[2,8,128]{2,1,0:T(8,128)S(1)}, f32[2,8,128]{2,1,0:T(8,128)}, u32[]{:S(2)}) copy-start(f32[2,8,128]{2,1,0:T(8,128)} %param.8) | copy-start | bytes 24580
  1.6 7.2 %copy-start.2 = (f32[16,16]{1,0:T(8,128)S(1)}, f32[16,16]{1,0:T(8,128)}, u32[]{:S(2)}) copy-start(f32[16,16]{1,0:T(8,128)} %refs_4_.1) | copy-start | bytes 3076
  1.6 7.2 %copy-start.3 = (f32[2,8,128]{2,1,0:T(8,128)S(1)}, f32[2,8,128]{2,1,0:T(8,128)}, u32[]{:S(2)}) copy-start(f32[2,8,128]{2,1,0:T(8,128)} %param.9) | copy-start | bytes 24580
  1.6 9.2 %collective-permute-start.2 = (f32[136,128]{1,0:T(8,128)S(1)}, f32[136,128]{1,0:T(8,128)S(1)}, u32[]{:S(2)}, u32[]{:S(2)}) collective-permute-start(f32[136,128]{1,0:T(8,128)S(1)} %get-tuple-element.35), channel_id=1, source_target_pairs={{0,1},{1,0},{2,3},{3,2},{4,5},{5,4},{6,7},{7,6},{8,9},{9,8},{10,11... | collective-permute-start | bytes 208904 | tf_op jit(solution)/shard_map/ppermute | solution.py:545
  2.2 8.6 %collective-permute-start = (f32[40,128]{1,0:T(8,128)S(1)}, f32[40,128]{1,0:T(8,128)S(1)}, u32[]{:S(2)}, u32[]{:S(2)}) collective-permute-start(f32[40,128]{1,0:T(8,128)S(1)} %get-tuple-element.28), channel_id=1, source_target_pairs={{0,2},{2,4},{4,6},{6,8},{8,10},{10,12},{12,14},{14,16},{16,18},{18... | collective-permute-start | bytes 61448 | tf_op jit(solution)/shard_map/ppermute | solution.py:545
  4.7 4.1 %copy-start.4 = (f32[16]{0:T(128)S(1)}, f32[16]{0:T(128)}, u32[]{:S(2)}) copy-start(f32[16]{0:T(128)} %sigma_ref.1) | copy-start | bytes 196
  4.7 4.1 %copy-start.5 = (f32[16]{0:T(128)S(1)}, f32[16]{0:T(128)}, u32[]{:S(2)}) copy-start(f32[16]{0:T(128)} %frequency_ref.1) | copy-start | bytes 196
  4.7 4.1 %copy-start.6 = (f32[16]{0:T(128)S(1)}, f32[16]{0:T(128)}, u32[]{:S(2)}) copy-start(f32[16]{0:T(128)} %barrier_ref.1) | copy-start | bytes 196
  4.7 6.1 %collective-permute-start.1 = (f32[40,128]{1,0:T(8,128)S(1)}, f32[40,128]{1,0:T(8,128)S(1)}, u32[]{:S(2)}, u32[]{:S(2)}) collective-permute-start(f32[40,128]{1,0:T(8,128)S(1)} %get-tuple-element.29), channel_id=1, source_target_pairs={{0,30},{2,0},{4,2},{6,4},{8,6},{10,8},{12,10},{14,12},{16,14},{18,... | collective-permute-start | bytes 61448 | tf_op jit(solution)/shard_map/ppermute | solution.py:545
  11.5 5.5 %collective-permute-start.5 = (f32[88,128]{1,0:T(8,128)S(1)}, f32[88,128]{1,0:T(8,128)S(1)}, u32[]{:S(2)}, u32[]{:S(2)}) collective-permute-start(f32[88,128]{1,0:T(8,128)S(1)} %get-tuple-element.37.pay_ref), channel_id=1, source_target_pairs={{0,6},{2,4},{4,2},{6,0},{8,14},{10,12},{12,10},{14,8},{16,22},{18,... | collective-permute-start | bytes 135176 | tf_op jit(solution)/shard_map/ppermute | solution.py:565
  13.5 4.0 %collective-permute-start.4 = (f32[88,128]{1,0:T(8,128)S(1)}, f32[88,128]{1,0:T(8,128)S(1)}, u32[]{:S(2)}, u32[]{:S(2)}) collective-permute-start(f32[88,128]{1,0:T(8,128)S(1)} %get-tuple-element.37.pay_ref), channel_id=1, source_target_pairs={{0,4},{2,6},{4,0},{6,2},{8,12},{10,14},{12,8},{14,10},{16,20},{18,... | collective-permute-start | bytes 135176 | tf_op jit(solution)/shard_map/ppermute | solution.py:565
  13.5 4.0 %collective-permute-start.3 = (f32[88,128]{1,0:T(8,128)S(1)}, f32[88,128]{1,0:T(8,128)S(1)}, u32[]{:S(2)}, u32[]{:S(2)}) collective-permute-start(f32[88,128]{1,0:T(8,128)S(1)} %get-tuple-element.37.pay_ref), channel_id=1, source_target_pairs={{0,2},{2,0},{4,6},{6,4},{8,10},{10,8},{12,14},{14,12},{16,18},{18,... | collective-permute-start | bytes 135176 | tf_op jit(solution)/shard_map/ppermute | solution.py:565
  17.7 6.5 %collective-permute-start.8 = (f32[136,128]{1,0:T(8,128)S(1)}, f32[136,128]{1,0:T(8,128)S(1)}, u32[]{:S(2)}, u32[]{:S(2)}) collective-permute-start(f32[136,128]{1,0:T(8,128)S(1)} %shard_map.76.own_group), channel_id=1, source_target_pairs={{0,24},{2,26},{4,28},{6,30},{8,16},{10,18},{12,20},{14,22},{16,8},... | collective-permute-start | bytes 208904 | tf_op jit(solution)/shard_map/ppermute | solution.py:565
  21.8 5.2 %collective-permute-start.7 = (f32[136,128]{1,0:T(8,128)S(1)}, f32[136,128]{1,0:T(8,128)S(1)}, u32[]{:S(2)}, u32[]{:S(2)}) collective-permute-start(f32[136,128]{1,0:T(8,128)S(1)} %shard_map.76.own_group), channel_id=1, source_target_pairs={{0,16},{2,18},{4,20},{6,22},{8,24},{10,26},{12,28},{14,30},{16,0},... | collective-permute-start | bytes 208904 | tf_op jit(solution)/shard_map/ppermute | solution.py:565
  21.8 5.2 %collective-permute-start.6 = (f32[136,128]{1,0:T(8,128)S(1)}, f32[136,128]{1,0:T(8,128)S(1)}, u32[]{:S(2)}, u32[]{:S(2)}) collective-permute-start(f32[136,128]{1,0:T(8,128)S(1)} %shard_map.76.own_group), channel_id=1, source_target_pairs={{0,8},{2,10},{4,12},{6,14},{8,0},{10,2},{12,4},{14,6},{16,24},{18,... | collective-permute-start | bytes 208904 | tf_op jit(solution)/shard_map/ppermute | solution.py:565
  27.6 1.3 %collective-permute-start.9 = (f32[128,128]{1,0:T(8,128)S(1)}, f32[128,128]{1,0:T(8,128)S(1)}, u32[]{:S(2)}, u32[]{:S(2)}) collective-permute-start(f32[128,128]{1,0:T(8,128)S(1)} %get-tuple-element.45), channel_id=1, source_target_pairs={{0,1},{1,0},{2,3},{3,2},{4,5},{5,4},{6,7},{7,6},{8,9},{9,8},{10,11... | collective-permute-start | bytes 196616 | tf_op jit(solution)/shard_map/ppermute | solution.py:545

commit v4 on v3

--- a/solution.py
+++ b/solution.py
@@ -7,7 +7,6 @@
 from jax.experimental.pallas import tpu as pltpu
 from jax.sharding import PartitionSpec as P
 
-STEPS = 2
 F32 = jnp.float32
 
 
@@ -29,18 +28,6 @@
         self.group_top = self.faces_at + self.members * self.tiles
         self.group_rows = self.group_top + padded
 
-    def per_device(self, body):
-        if self.devices <= 16:
-            for j in range(self.devices):
-                body(j)
-        else:
-
-            def step(j, carry):
-                body(j)
-                return carry
-
-            lax.fori_loop(0, self.devices, step, 0)
-
     def groups(self, size):
         for base in range(0, self.tiles, size):
             yield range(base, min(base + size, self.tiles))
@@ -58,6 +45,10 @@
     return jnp.broadcast_to(ref[pl.ds(row, 1), :], z.tile)
 
 
+def per_line(z, y):
+    return slice(y * z.species, (y + 1) * z.species)
+
+
 def along_x(v, by, nx):
     return pltpu.roll(v, by % nx, v.ndim - 1)
 
@@ -71,14 +62,22 @@
     return flag(me > 0), flag(me < count - 1)
 
 
-def edges_kernel(z, c_ref, k_ref, up_ref, down_ref, *y_refs):
-    for ref, row in ((down_ref, 0), (up_ref, z.nz - 1)):
+def edges_kernel(z, c_hbm, k_hbm, c_ref, k_ref, near_ref, far_ref, *refs):
+    *y_refs, sems = refs
+    loads = [
+        pltpu.make_async_copy(k_hbm, k_ref, sems.at[0]),
+        pltpu.make_async_copy(c_hbm, c_ref, sems.at[1]),
+    ]
+    for load in loads:
+        load.start()
+    for load in loads:
+        load.wait()
+    odd = lax.axis_index("gz") % 2
+    for ref, row in ((near_ref, (1 - odd) * (z.nz - 1)), (far_ref, odd * (z.nz - 1))):
         for y in range(z.ny):
             at = y * z.nz + row
-            ref[y * z.species : (y + 1) * z.species, :] = c_ref[
-                pl.ds(at, z.species, stride=z.tiles), :
-            ]
-            ref[z.lines + y : z.lines + y + 1, :] = k_ref[at : at + 1, :]
+            ref[per_line(z, y), :] = c_ref[pl.ds(at, z.species, stride=z.tiles), :]
+            ref[z.lines + y : z.lines + y + 1, :] = k_ref[pl.ds(at, 1), :]
         ref[z.lines + z.ny :, :] = jnp.zeros((z.edge_rows - z.lines - z.ny, z.nx), F32)
     for ref, y in zip(y_refs, y_picks(z)):
         for i in range(z.nz):
@@ -195,31 +194,40 @@
 
 
 def send_sums(z, f_ref, v_ref, u_ref, pay_ref):
-    me = lax.axis_index("gz")
     for y in range(z.ny):
         tiles = range(y * z.nz, (y + 1) * z.nz)
-        up = functools.reduce(jnp.add, [v_ref[t] * f_ref[t] for t in tiles])
-        down = functools.reduce(jnp.add, [u_ref[t] * f_ref[t] for t in tiles])
-        lines = slice(y * z.species, (y + 1) * z.species)
-
-        def fill(dest):
-            pay_ref[dest, lines, :] = jnp.where(dest > me, up, down)
-
-        z.per_device(fill)
-    pay_ref[me] = jnp.zeros((z.lines, z.nx), F32)
-
-
-def per_line(z, y):
-    return slice(y * z.species, (y + 1) * z.species)
+        pay_ref[0, per_line(z, y), :] = functools.reduce(jnp.add, [v_ref[t] * f_ref[t] for t in tiles])
+        pay_ref[1, per_line(z, y), :] = functools.reduce(jnp.add, [u_ref[t] * f_ref[t] for t in tiles])
+
+
+def total_kernel(z, pay_ref, *refs):
+    inside = refs[: z.members - 1]
+    within_ref, *out_refs = refs[z.members - 1 :]
+    me = lax.axis_index("gz")
+    group, member = me // z.members, me % z.members
+    below = above = jnp.zeros((z.lines, z.nx), F32)
+    rising, falling = pay_ref[0], pay_ref[1]
+    for i, ref in enumerate(inside):
+        lower = (member ^ (i + 1)) < member
+        up, down = ref[0], ref[1]
+        rising, falling = rising + up, falling + down
+        below = below + jnp.where(lower, up, 0.0)
+        above = above + jnp.where(lower, 0.0, down)
+    within_ref[0] = below
+    within_ref[1] = above
+    for i, ref in enumerate(out_refs):
+        ref[...] = jnp.where((group ^ (i + 1)) > group, rising, falling)
 
 
 def first_kernel(
-    z, k_ref, from_below, from_above, tiles_ref, base_ref, rates_ref, left_ref, right_ref, inverse_ref,
-    *refs
+    z, k_ref, near_ref, far_ref, tiles_ref, base_ref, rates_ref, left_ref, right_ref, inverse_ref, *refs
 ):
     halos = 1 if z.gy == 2 else 2
     y_received = refs[:halos]
-    pay_ref, f_ref, faces = refs[halos:]
+    pay_ref, f_ref, faces, from_below, from_above = refs[halos:]
+    odd = lax.axis_index("gz") % 2 == 1
+    from_below[...] = jnp.where(odd, near_ref[...], far_ref[...])
+    from_above[...] = jnp.where(odd, far_ref[...], near_ref[...])
     k = k_ref[...]
     low, high = y_received[0], y_received[-1]
     low_mask, high_mask = inner("gy", z.gy)
@@ -412,29 +420,6 @@
     return below, above
 
 
-def gathered_sums(z, received):
-    me = lax.axis_index("gz")
-    below, above = [], []
-    for y in range(z.ny):
-        lines = per_line(z, y)
-        zero = jnp.zeros(z.tile, F32)
-        sums = [zero, zero]
-
-        def add(j, pair):
-            value = received[j, lines, :]
-            lower = j < me
-            return [pair[0] + jnp.where(lower, value, 0.0), pair[1] + jnp.where(lower, 0.0, value)]
-
-        if z.devices <= 16:
-            for j in range(z.devices):
-                sums = add(j, sums)
-        else:
-            sums = lax.fori_loop(0, z.devices, add, sums)
-        below.append(sums[0])
-        above.append(sums[1])
-    return below, above
-
-
 def solve_lines(z, sums, f_ref, v_ref, u_ref, ends_ref, store):
     halos = []
     for y, (below, above) in enumerate(zip(*sums)):
@@ -485,14 +470,6 @@
     hand_on(z, halos, tiles_ref, halo_ref, y_refs)
 
 
-def middle_kernel(z, received, f_ref, v_ref, u_ref, ends_ref, tiles_ref, halo_ref, *y_refs):
-    def store(t, value):
-        tiles_ref[t] = value
-
-    halos = solve_lines(z, gathered_sums(z, received), f_ref, v_ref, u_ref, ends_ref, store)
-    hand_on(z, halos, tiles_ref, halo_ref, y_refs)
-
-
 def second_kernel(
     z, tiles_ref, base_ref, halo_ref, rates_ref, faces, left_ref, right_ref, inverse_ref, v_ref, u_ref,
     *refs
@@ -513,11 +490,21 @@
     send_sums(z, f_ref, v_ref, u_ref, pay_ref)
 
 
-def last_kernel(z, received, f_ref, v_ref, u_ref, ends_ref, out_ref):
+def last_kernel(z, within_ref, f_ref, v_ref, u_ref, ends_ref, *refs):
+    *across, out_ref = refs
+    group = lax.axis_index("gz") // z.members
+    below, above = within_ref[0], within_ref[1]
+    for i, ref in enumerate(across):
+        lower = (group ^ (i + 1)) < group
+        value = ref[...]
+        below = below + jnp.where(lower, value, 0.0)
+        above = above + jnp.where(lower, 0.0, value)
+    sums = [[v[per_line(z, y)] for y in range(z.ny)] for v in (below, above)]
+
     def store(t, value):
         out_ref[pl.ds(t, z.species, stride=z.tiles), :] = value
 
-    solve_lines(z, gathered_sums(z, received), f_ref, v_ref, u_ref, ends_ref, store)
+    solve_lines(z, sums, f_ref, v_ref, u_ref, ends_ref, store)
 
 
 def per_device(z, c, k, warm, sigma, frequency, barrier, proportions):
@@ -555,22 +542,34 @@
     warm = warm.reshape(z.tiles, z.nx)
     halos = 1 if z.gy == 2 else 2
     block = shaped(z.tiles, *z.tile)
-    per_peer = shaped(z.devices, z.lines, z.nx)
     ends_shape = shaped(5 * z.ny, *z.tile)
-    current = [block, shaped(2 * z.ny, *z.tile)]
-    y_edges = [shaped(z.nz * z.species, z.nx)] * halos
 
     def exchange(value, count, unit):
+        values = value if isinstance(value, list) else [value] * (count - 1)
         pairs = [[(i, i ^ (k * unit)) for i in range(z.devices)] for k in range(1, count)]
-        return [lax.ppermute(value, "gz", p) for p in pairs]
-
-    up, down, *sends = call(
-        edges_kernel,
-        [shaped(z.edge_rows, z.nx)] * 2 + [shaped(z.nz * (z.species + 1), z.nx)] * halos,
-        in_vmem(c, k),
-    )
-    from_below, from_above = shift(up, "gz", 1), shift(down, "gz", -1)
+        return [lax.ppermute(v, "gz", p) for v, p in zip(values, pairs)]
+
+    def neighbours(near, far):
+        last = z.devices - 1
+        links = [(i, i + 1) for i in range(1, last, 2)]
+        links = [pair for i, j in links for pair in ((i, j), (j, i))]
+        ends = [(i, i) for i in (0, last)]
+        far_pairs = [(i * z.gy + n, j * z.gy + n) for i, j in links for n in range(z.gy)]
+        far_pairs += [(i * z.gy + n, j * z.gy + (n ^ 1)) for i, j in ends for n in range(z.gy)]
+        return exchange(near, 2, 1)[0], lax.ppermute(far, ("gz", "gy"), far_pairs)
+
+    c, k, near, far, *sends = pl.pallas_call(
+        functools.partial(edges_kernel, z),
+        out_shape=[shaped(z.species * z.tiles, z.nx), shaped(z.tiles, z.nx)]
+        + [shaped(z.edge_rows, z.nx)] * 2
+        + [shaped(z.nz * (z.species + 1), z.nx)] * halos,
+        in_specs=[pl.BlockSpec(memory_space=pl.ANY)] * 2,
+        out_specs=[vmem] * (4 + halos),
+        scratch_shapes=[pltpu.SemaphoreType.DMA((2,))],
+        compiler_params=params,
+    )(c, k)
     received = swap(sends)
+    near, far = neighbours(near, far)
     tiles, rates, x_faces, arrhenius, left, right, inverse, base = call(
         setup_kernel,
         [
@@ -591,7 +590,8 @@
     pay, f, faces = call(
         first_kernel,
         [shaped(z.block_rows, z.nx), block, shaped(4, z.tiles, z.nx)],
-        in_vmem(k, from_below, from_above, tiles, base, rates, left, right, inverse, *received),
+        in_vmem(k, near, far, tiles, base, rates, left, right, inverse, *received),
+        [pltpu.VMEM((z.edge_rows, z.nx), F32)] * 2,
     )
     inside = exchange(pay, z.members, 1)
     group = call(
@@ -603,28 +603,34 @@
     across = exchange(group, z.groups_z, z.members)
     tiles, halo, v, u, ends, *sends = call(
         meet_kernel,
-        [*current, block, block, ends_shape, *y_edges],
+        [block, shaped(2 * z.ny, *z.tile), block, block, ends_shape]
+        + [shaped(z.nz * z.species, z.nx)] * halos,
         in_vmem(rates, f, pay, group, *inside, *across),
         [
             pltpu.VMEM((z.members, z.block_rows, z.nx), F32),
             pltpu.VMEM((z.groups_z, z.group_rows, z.nx), F32),
         ],
     )
-    for step in range(1, STEPS):
-        if step > 1:
-            sums = lax.all_to_all(pay, "gz", 0, 0, tiled=True)
-            tiles, halo, *sends = call(
-                middle_kernel, [*current, *y_edges], in_vmem(sums, f, v, u, ends)
-            )
-        received = swap(sends)
-        base = call(base_kernel, block, in_vmem(tiles, rates, x_faces, arrhenius, proportions))
-        pay, f = call(
-            second_kernel,
-            [per_peer, block],
-            in_vmem(tiles, base, halo, rates, faces, left, right, inverse, v, u, *received),
-        )
-    sums = lax.all_to_all(pay, "gz", 0, 0, tiled=True)
-    out = call(last_kernel, shaped(z.species * z.tiles, z.nx), in_vmem(sums, f, v, u, ends))
+
+    received = swap(sends)
+    base = call(base_kernel, block, in_vmem(tiles, rates, x_faces, arrhenius, proportions))
+    pay, f = call(
+        second_kernel,
+        [shaped(2, z.lines, z.nx), block],
+        in_vmem(tiles, base, halo, rates, faces, left, right, inverse, v, u, *received),
+    )
+    inside = exchange(pay, z.members, 1)
+    within, *totals = call(
+        total_kernel,
+        [shaped(2, z.lines, z.nx)] + [shaped(z.lines, z.nx)] * (z.groups_z - 1),
+        in_vmem(pay, *inside),
+    )
+    across = exchange(totals, z.groups_z, z.members)
+    out = call(
+        last_kernel,
+        shaped(z.species * z.tiles, z.nx),
+        in_vmem(within, f, v, u, ends, *across),
+    )
     return out.reshape(z.species, z.ny, z.nz, z.nx)
 
 

time: 45.5 us -> 44.7 us (0.982)
  blocking collectives: 14.9 us -> 0 us
  waiting for transfers between devices: 8.01 us -> 16 us
  starting transfers between devices: 15.5 us -> 20.7 us
  local copies, waits for them, and re-layouts: 1.62 us -> 2.28 us
    all_to_all x1 -> x0, blocking collectives: 14.9 us -> none  [per_device(): sums = lax.all_to_all(pay, 'gz', 0, 0, tiled=True)]
    ppermute x6 -> x14, starting transfers between devices: 8.26 us -> 20.1 us  [the longest x13 20 us: exchange(): return [lax.ppermute(v, 'gz', p) for v, p in zip(values, pairs)]]
    ppermute x6 -> x14, waiting for transfers between devices: 7.05 us -> 15.1 us  [the longest x13 15.1 us: exchange(): return [lax.ppermute(v, 'gz', p) for v, p in zip(values, pairs)]]
    ppermute x4 -> x2, starting transfers between devices: 7.23 us -> 0.59 us  [shift(): lax.ppermute(value, axis, [(i, (i + by) % count) for i in range(count)])]
    unnamed x14, local copies, waits for them, and re-layouts: 1.62 us -> 2.28 us
    ppermute x4 -> x2, waiting for transfers between devices: 0.96 us -> 0.96 us  [shift(): lax.ppermute(value, axis, [(i, (i + by) % count) for i in range(count)])]
  transfers between devices with their start and end apart: 10 -> 16, of which waited for: 5 -> 10; matrix products, arithmetic and copies ran while one was open for 0% -> 0% of each run, Pallas kernels for 5% -> 5%
where the time goes in v4:
time: 44.7 us; the launch traced here: 44.5 us
  starting transfers between devices  20.7 us (46%)
  waiting for transfers between devices  16 us (36%)
  Pallas kernels  5.33 us (12%)
  local copies, waits for them, and re-layouts  2.28 us (5%)
    ppermute x13, starting transfers between devices, exchange(): return [lax.ppermute(v, 'gz', p) for v, p in zip(values, pairs)]  20 us
    ppermute x13, waiting for transfers between devices, exchange(): return [lax.ppermute(v, 'gz', p) for v, p in zip(values, pairs)]  15.1 us
    pallas_call x8, Pallas kernels, call(): pl.pallas_call(functools.partial(kernel, z), out_shape=outs, in_specs=spe...  5.11 us
    unnamed x14, local copies, waits for them, and re-layouts  2.28 us
    ppermute x2, waiting for transfers between devices, shift(): lax.ppermute(value, axis, [(i, (i + by) % count) for i in range(count)])  0.96 us
  transfers between devices with their start and end apart: 16, of which 10 were waited for; matrix products, arithmetic and copies ran while one was open for 0% of the time, Pallas kernels for 5%

profile of v4, /device:TPU:0, one launch (start us, length us, event | category | flops | bytes accessed | tf_op | source)
XLA Modules:
  0.0 44.5 jit_solution(18132774212951328145)
XLA Ops:
  0.0 0.9 %copy-done = f32[16,2,8,128]{3,2,1,0:T(8,128)S(1)} copy-done((f32[16,2,8,128]{3,2,1,0:T(8,128)S(1)}, f32[16,2,8,128]{3,2,1,0:T(8,128)}, u32[]{:S(2)}) %copy-start) | copy-done | bytes 131096
  0.9 0.7 %copy-done.2 = f32[2,8,128]{2,1,0:T(8,128)S(1)} copy-done((f32[2,8,128]{2,1,0:T(8,128)S(1)}, f32[2,8,128]{2,1,0:T(8,128)}, u32[]{:S(2)}) %copy-start.2) | copy-done | bytes 8216
  1.6 0.2 shard_map.73
  1.8 0.0 copy-start.1
  1.8 0.5 %collective-permute-start.2 = (f32[136,128]{1,0:T(8,128)S(1)}, f32[136,128]{1,0:T(8,128)S(1)}, u32[]{:S(2)}, u32[]{:S(2)}) collective-permute-start(f32[136,128]{1,0:T(8,128)S(1)} %get-tuple-element.43), channel_id=1, source_target_pairs={{0,1},{1,0},{2,3},{3,2},{4,5},{5,4},{6,7},{7,6},{8,9},{9,8},{10,11... | collective-permute-start | bytes 208904 | tf_op jit(solution)/shard_map/ppermute | solution.py:532
  2.4 2.6 %collective-permute-start = (f32[40,128]{1,0:T(8,128)S(1)}, f32[40,128]{1,0:T(8,128)S(1)}, u32[]{:S(2)}, u32[]{:S(2)}) collective-permute-start(f32[40,128]{1,0:T(8,128)S(1)} %get-tuple-element.36), channel_id=1, source_target_pairs={{0,2},{2,0},{4,6},{6,4},{8,10},{10,8},{12,14},{14,12},{16,18},{18,... | collective-permute-start | bytes 61448 | tf_op jit(solution)/shard_map/ppermute | solution.py:550
  4.9 0.2 collective-permute-start.1
  5.1 0.0 copy-done.3
  5.1 0.0 copy-done.1
  5.1 0.6 %copy-done.4 = f32[16]{0:T(128)S(1)} copy-done((f32[16]{0:T(128)S(1)}, f32[16]{0:T(128)}, u32[]{:S(2)}) %copy-start.4) | copy-done | bytes 88
  5.8 0.0 copy-done.5
  5.8 0.0 copy-done.6
  5.8 1.9 %shard_map.74 = (f32[16,16,128]{2,1,0:T(8,128)S(1)}, f32[4,16,128]{2,1,0:T(8,128)S(1)}, f32[2,16,128]{2,1,0:T(8,128)S(1)}, f32[16,16,128]{2,1,0:T(8,128)S(1)}, f...) custom-call(f32[256,128]{1,0:T(8,128)S(1)} %get-tuple-element.33.c_r, ...), custom_call_target="tpu_custom_call" | custom-call | flops 1000000 | bytes 1000000 | tf_op jit(solution)/shard_map/pallas_call | solution.py:520
  7.7 0.0 collective-permute-done.near_ref
  7.7 0.0 collective-permute-done.1.far_ref
  7.8 0.0 collective-permute-done.2.refs_0_
  7.8 0.7 %shard_map.75 = (f32[88,128]{1,0:T(8,128)S(1)}, f32[16,16,128]{2,1,0:T(8,128)S(1)}, f32[4,16,128]{2,1,0:T(8,128)S(1)}) custom-call(f32[16,128]{1,0:T(8,128)S(1)} %get-tuple-element.34.k_ref, f32[40,128]{1,0:T(8,128)S(1)} %collective-permute-done.near_ref, f32[40,128]{1,0:T(8,128)S(1)} %collective-permute-done.1.far_ref, ...), custom_call_target="tpu_custom_call" | custom-call | flops 1000000 | bytes 1000000 | tf_op jit(solution)/shard_map/pallas_call | solution.py:520
  8.4 4.3 %collective-permute-start.5 = (f32[88,128]{1,0:T(8,128)S(1)}, f32[88,128]{1,0:T(8,128)S(1)}, u32[]{:S(2)}, u32[]{:S(2)}) collective-permute-start(f32[88,128]{1,0:T(8,128)S(1)} %get-tuple-element.45.pay_ref), channel_id=1, source_target_pairs={{0,6},{2,4},{4,2},{6,0},{8,14},{10,12},{12,10},{14,8},{16,22},{18,... | collective-permute-start | bytes 135176 | tf_op jit(solution)/shard_map/ppermute | solution.py:550
  12.7 0.0 collective-permute-start.4
  12.8 0.6 %collective-permute-start.3 = (f32[88,128]{1,0:T(8,128)S(1)}, f32[88,128]{1,0:T(8,128)S(1)}, u32[]{:S(2)}, u32[]{:S(2)}) collective-permute-start(f32[88,128]{1,0:T(8,128)S(1)} %get-tuple-element.45.pay_ref), channel_id=1, source_target_pairs={{0,2},{2,0},{4,6},{6,4},{8,10},{10,8},{12,14},{14,12},{16,18},{18,... | collective-permute-start | bytes 135176 | tf_op jit(solution)/shard_map/ppermute | solution.py:550
  13.4 1.4 %collective-permute-done.5.refs_2_ = f32[88,128]{1,0:T(8,128)S(1)} collective-permute-done((f32[88,128]{1,0:T(8,128)S(1)}, f32[88,128]{1,0:T(8,128)S(1)}, u32[]{:S(2)}, u32[]{:S(2)}) %collective-permute-start.5) | collective-permute-done | bytes 45088 | tf_op jit(solution)/shard_map/ppermute | solution.py:550
  14.8 2.0 %collective-permute-done.4.refs_1_ = f32[88,128]{1,0:T(8,128)S(1)} collective-permute-done((f32[88,128]{1,0:T(8,128)S(1)}, f32[88,128]{1,0:T(8,128)S(1)}, u32[]{:S(2)}, u32[]{:S(2)}) %collective-permute-start.4) | collective-permute-done | bytes 45088 | tf_op jit(solution)/shard_map/ppermute | solution.py:550
  16.8 0.0 collective-permute-done.3.refs_0_
  16.8 0.1 shard_map.76.own_group
  17.0 3.7 %collective-permute-start.8 = (f32[136,128]{1,0:T(8,128)S(1)}, f32[136,128]{1,0:T(8,128)S(1)}, u32[]{:S(2)}, u32[]{:S(2)}) collective-permute-start(f32[136,128]{1,0:T(8,128)S(1)} %shard_map.76.own_group), channel_id=1, source_target_pairs={{0,24},{2,26},{4,28},{6,30},{8,16},{10,18},{12,20},{14,22},{16,8},... | collective-permute-start | bytes 208904 | tf_op jit(solution)/shard_map/ppermute | solution.py:550
  20.6 0.0 collective-permute-start.7
  20.6 0.8 %collective-permute-start.6 = (f32[136,128]{1,0:T(8,128)S(1)}, f32[136,128]{1,0:T(8,128)S(1)}, u32[]{:S(2)}, u32[]{:S(2)}) collective-permute-start(f32[136,128]{1,0:T(8,128)S(1)} %shard_map.76.own_group), channel_id=1, source_target_pairs={{0,8},{2,10},{4,12},{6,14},{8,0},{10,2},{12,4},{14,6},{16,24},{18,... | collective-permute-start | bytes 208904 | tf_op jit(solution)/shard_map/ppermute | solution.py:550
  21.4 1.7 %collective-permute-done.8.refs_5_ = f32[136,128]{1,0:T(8,128)S(1)} collective-permute-done((f32[136,128]{1,0:T(8,128)S(1)}, f32[136,128]{1,0:T(8,128)S(1)}, u32[]{:S(2)}, u32[]{:S(2)}) %collective-permute-start.8) | collective-permute-done | bytes 69664 | tf_op jit(solution)/shard_map/ppermute | solution.py:550
  23.2 2.8 %collective-permute-done.7.refs_4_ = f32[136,128]{1,0:T(8,128)S(1)} collective-permute-done((f32[136,128]{1,0:T(8,128)S(1)}, f32[136,128]{1,0:T(8,128)S(1)}, u32[]{:S(2)}, u32[]{:S(2)}) %collective-permute-start.7) | collective-permute-done | bytes 69664 | tf_op jit(solution)/shard_map/ppermute | solution.py:550
  25.9 0.0 collective-permute-done.6.refs_3_
  25.9 0.6 %shard_map.77 = (f32[16,16,128]{2,1,0:T(8,128)S(1)}, f32[4,16,128]{2,1,0:T(8,128)S(1)}, f32[16,16,128]{2,1,0:T(8,128)S(1)}, f32[16,16,128]{2,1,0:T(8,128)S(1)}, ...) custom-call(f32[4,16,128]{2,1,0:T(8,128)S(1)} %get-tuple-element.35.rates_ref.refs_1_, ...), custom_call_target="tpu_custom_call" | custom-call | flops 1000000 | bytes 1000000 | tf_op jit(solution)/shard_map/pallas_call | solution.py:520
  26.5 0.1 collective-permute-start.9
  26.6 0.3 shard_map.78.base_ref
  26.9 1.0 %collective-permute-done.9.refs_0_ = f32[128,128]{1,0:T(8,128)S(1)} collective-permute-done((f32[128,128]{1,0:T(8,128)S(1)}, f32[128,128]{1,0:T(8,128)S(1)}, u32[]{:S(2)}, u32[]{:S(2)}) %collective-permute-start.9) | collective-permute-done | bytes 65568 | tf_op jit(solution)/shard_map/ppermute | solution.py:532
  27.9 0.7 %shard_map.79 = (f32[2,32,128]{2,1,0:T(8,128)S(1)}, f32[16,16,128]{2,1,0:T(8,128)S(1)}) custom-call(f32[16,16,128]{2,1,0:T(8,128)S(1)} %get-tuple-element.46.refs_0_.tiles_ref, f32[16,16,128]{2,1,0:T(8,128)S(1)} %shard_map.78.base_ref, f32[4,16,128]{2,1,0:T(8,128)S(1)} %get-tuple-element.49.halo_ref, f32[4,16,128]{2,1,0:T(8,128)S(1)} %get-tuple-element.35.rates_ref.refs_1_, ...), custom_call_target="tpu_custom_call" | custom-call | flops 1000000 | bytes 1000000 | tf_op jit(solution)/shard_map/pallas_call | solution.py:520
  28.6 2.0 %collective-permute-start.12 = (f32[2,32,128]{2,1,0:T(8,128)S(1)}, f32[2,32,128]{2,1,0:T(8,128)S(1)}, u32[]{:S(2)}, u32[]{:S(2)}) collective-permute-start(f32[2,32,128]{2,1,0:T(8,128)S(1)} %get-tuple-element.54.pay_ref), channel_id=1, source_target_pairs={{0,6},{2,4},{4,2},{6,0},{8,14},{10,12},{12,10},{14,8},{16,22},{18,... | collective-permute-start | bytes 98312 | tf_op jit(solution)/shard_map/ppermute | solution.py:550
  30.6 1.4 %collective-permute-start.11 = (f32[2,32,128]{2,1,0:T(8,128)S(1)}, f32[2,32,128]{2,1,0:T(8,128)S(1)}, u32[]{:S(2)}, u32[]{:S(2)}) collective-permute-start(f32[2,32,128]{2,1,0:T(8,128)S(1)} %get-tuple-element.54.pay_ref), channel_id=1, source_target_pairs={{0,4},{2,6},{4,0},{6,2},{8,12},{10,14},{12,8},{14,10},{16,20},{18,... | collective-permute-start | bytes 98312 | tf_op jit(solution)/shard_map/ppermute | solution.py:550
  32.0 0.2 collective-permute-start.10
  32.1 1.4 %collective-permute-done.12.refs_2_ = f32[2,32,128]{2,1,0:T(8,128)S(1)} collective-permute-done((f32[2,32,128]{2,1,0:T(8,128)S(1)}, f32[2,32,128]{2,1,0:T(8,128)S(1)}, u32[]{:S(2)}, u32[]{:S(2)}) %collective-permute-start.12) | collective-permute-done | bytes 32800 | tf_op jit(solution)/shard_map/ppermute | solution.py:550
  33.6 0.9 %collective-permute-done.11.refs_1_ = f32[2,32,128]{2,1,0:T(8,128)S(1)} collective-permute-done((f32[2,32,128]{2,1,0:T(8,128)S(1)}, f32[2,32,128]{2,1,0:T(8,128)S(1)}, u32[]{:S(2)}, u32[]{:S(2)}) %collective-permute-start.11) | collective-permute-done | bytes 32800 | tf_op jit(solution)/shard_map/ppermute | solution.py:550
  34.5 1.4 %collective-permute-done.10.refs_0_ = f32[2,32,128]{2,1,0:T(8,128)S(1)} collective-permute-done((f32[2,32,128]{2,1,0:T(8,128)S(1)}, f32[2,32,128]{2,1,0:T(8,128)S(1)}, u32[]{:S(2)}, u32[]{:S(2)}) %collective-permute-start.10) | collective-permute-done | bytes 32800 | tf_op jit(solution)/shard_map/ppermute | solution.py:550
  35.9 0.7 %collective-permute-start.13 = (f32[32,128]{1,0:T(8,128)S(1)}, f32[32,128]{1,0:T(8,128)S(1)}, u32[]{:S(2)}, u32[]{:S(2)}) collective-permute-start(f32[32,128]{1,0:T(8,128)S(1)} %get-tuple-element.58), channel_id=1, source_target_pairs={{0,8},{2,10},{4,12},{6,14},{8,0},{10,2},{12,4},{14,6},{16,24},{18,... | collective-permute-start | bytes 49160 | tf_op jit(solution)/shard_map/ppermute | solution.py:550
  36.6 1.6 %collective-permute-start.14 = (f32[32,128]{1,0:T(8,128)S(1)}, f32[32,128]{1,0:T(8,128)S(1)}, u32[]{:S(2)}, u32[]{:S(2)}) collective-permute-start(f32[32,128]{1,0:T(8,128)S(1)} %get-tuple-element.59), channel_id=1, source_target_pairs={{0,16},{2,18},{4,20},{6,22},{8,24},{10,26},{12,28},{14,30},{16,0},... | collective-permute-start | bytes 49160 | tf_op jit(solution)/shard_map/ppermute | solution.py:550
  38.2 2.2 %collective-permute-start.15 = (f32[32,128]{1,0:T(8,128)S(1)}, f32[32,128]{1,0:T(8,128)S(1)}, u32[]{:S(2)}, u32[]{:S(2)}) collective-permute-start(f32[32,128]{1,0:T(8,128)S(1)} %get-tuple-element.60), channel_id=1, source_target_pairs={{0,24},{2,26},{4,28},{6,30},{8,16},{10,18},{12,20},{14,22},{16,8},... | collective-permute-start | bytes 49160 | tf_op jit(solution)/shard_map/ppermute | solution.py:550
  40.4 0.0 collective-permute-done.13.refs_0_
  40.4 0.9 %collective-permute-done.14.refs_1_ = f32[32,128]{1,0:T(8,128)S(1)} collective-permute-done((f32[32,128]{1,0:T(8,128)S(1)}, f32[32,128]{1,0:T(8,128)S(1)}, u32[]{:S(2)}, u32[]{:S(2)}) %collective-permute-start.14) | collective-permute-done | bytes 16416 | tf_op jit(solution)/shard_map/ppermute | solution.py:550
  41.3 2.4 %collective-permute-done.15.refs_2_ = f32[32,128]{1,0:T(8,128)S(1)} collective-permute-done((f32[32,128]{1,0:T(8,128)S(1)}, f32[32,128]{1,0:T(8,128)S(1)}, u32[]{:S(2)}, u32[]{:S(2)}) %collective-permute-start.15) | collective-permute-done | bytes 16416 | tf_op jit(solution)/shard_map/ppermute | solution.py:550
  43.7 0.7 %shard_map.81 = f32[256,128]{1,0:T(8,128)} custom-call(f32[2,32,128]{2,1,0:T(8,128)S(1)} %get-tuple-element.55.within_ref, f32[16,16,128]{2,1,0:T(8,128)S(1)} %get-tuple-element.56.f_ref, f32[16,16,128]{2,1,0:T(8,128)S(1)} %get-tuple-element.51.v_ref, f32[16,16,128]{2,1,0:T(8,128)S(1)} %get-tuple-element.52.u_ref, ...), custom_call_target="tpu_custom_call" | custom-call | flops 1000000 | bytes 1000000 | tf_op jit(solution)/shard_map/pallas_call | solution.py:520
  (7 shorter events, 0.0 us)
Async XLA Ops:
  0.0 0.9 %copy-start = (f32[16,2,8,128]{3,2,1,0:T(8,128)S(1)}, f32[16,2,8,128]{3,2,1,0:T(8,128)}, u32[]{:S(2)}) copy-start(f32[16,2,8,128]{3,2,1,0:T(8,128)} %param.7) | copy-start | bytes 393220
  0.9 0.7 %copy-start.2 = (f32[2,8,128]{2,1,0:T(8,128)S(1)}, f32[2,8,128]{2,1,0:T(8,128)}, u32[]{:S(2)}) copy-start(f32[2,8,128]{2,1,0:T(8,128)} %param.8) | copy-start | bytes 24580
  1.6 3.5 %copy-start.3 = (f32[2,8,128]{2,1,0:T(8,128)S(1)}, f32[2,8,128]{2,1,0:T(8,128)}, u32[]{:S(2)}) copy-start(f32[2,8,128]{2,1,0:T(8,128)} %param.9) | copy-start | bytes 24580
  1.8 3.3 %copy-start.1 = (f32[16,16]{1,0:T(8,128)S(1)}, f32[16,16]{1,0:T(8,128)}, u32[]{:S(2)}) copy-start(f32[16,16]{1,0:T(8,128)} %refs_4_.1) | copy-start | bytes 3076
  1.8 5.9 %collective-permute-start.2 = (f32[136,128]{1,0:T(8,128)S(1)}, f32[136,128]{1,0:T(8,128)S(1)}, u32[]{:S(2)}, u32[]{:S(2)}) collective-permute-start(f32[136,128]{1,0:T(8,128)S(1)} %get-tuple-element.43), channel_id=1, source_target_pairs={{0,1},{1,0},{2,3},{3,2},{4,5},{5,4},{6,7},{7,6},{8,9},{9,8},{10,11... | collective-permute-start | bytes 208904 | tf_op jit(solution)/shard_map/ppermute | solution.py:532
  2.4 5.4 %collective-permute-start = (f32[40,128]{1,0:T(8,128)S(1)}, f32[40,128]{1,0:T(8,128)S(1)}, u32[]{:S(2)}, u32[]{:S(2)}) collective-permute-start(f32[40,128]{1,0:T(8,128)S(1)} %get-tuple-element.36), channel_id=1, source_target_pairs={{0,2},{2,0},{4,6},{6,4},{8,10},{10,8},{12,14},{14,12},{16,18},{18,... | collective-permute-start | bytes 61448 | tf_op jit(solution)/shard_map/ppermute | solution.py:550
  4.9 2.8 %collective-permute-start.1 = (f32[40,128]{1,0:T(8,128)S(1)}, f32[40,128]{1,0:T(8,128)S(1)}, u32[]{:S(2)}, u32[]{:S(2)}) collective-permute-start(f32[40,128]{1,0:T(8,128)S(1)} %get-tuple-element.37), channel_id=1, source_target_pairs={{2,4},{3,5},{4,2},{5,3},{6,8},{7,9},{8,6},{9,7},{10,12},{11,13},{1... | collective-permute-start | bytes 61448 | tf_op jit(solution)/shard_map/ppermute | solution.py:559
  5.1 0.7 %copy-start.4 = (f32[16]{0:T(128)S(1)}, f32[16]{0:T(128)}, u32[]{:S(2)}) copy-start(f32[16]{0:T(128)} %sigma_ref.1) | copy-start | bytes 196
  5.1 0.7 %copy-start.5 = (f32[16]{0:T(128)S(1)}, f32[16]{0:T(128)}, u32[]{:S(2)}) copy-start(f32[16]{0:T(128)} %frequency_ref.1) | copy-start | bytes 196
  5.1 0.7 %copy-start.6 = (f32[16]{0:T(128)S(1)}, f32[16]{0:T(128)}, u32[]{:S(2)}) copy-start(f32[16]{0:T(128)} %barrier_ref.1) | copy-start | bytes 196
  8.4 6.4 %collective-permute-start.5 = (f32[88,128]{1,0:T(8,128)S(1)}, f32[88,128]{1,0:T(8,128)S(1)}, u32[]{:S(2)}, u32[]{:S(2)}) collective-permute-start(f32[88,128]{1,0:T(8,128)S(1)} %get-tuple-element.45.pay_ref), channel_id=1, source_target_pairs={{0,6},{2,4},{4,2},{6,0},{8,14},{10,12},{12,10},{14,8},{16,22},{18,... | collective-permute-start | bytes 135176 | tf_op jit(solution)/shard_map/ppermute | solution.py:550
  12.7 4.0 %collective-permute-start.4 = (f32[88,128]{1,0:T(8,128)S(1)}, f32[88,128]{1,0:T(8,128)S(1)}, u32[]{:S(2)}, u32[]{:S(2)}) collective-permute-start(f32[88,128]{1,0:T(8,128)S(1)} %get-tuple-element.45.pay_ref), channel_id=1, source_target_pairs={{0,4},{2,6},{4,0},{6,2},{8,12},{10,14},{12,8},{14,10},{16,20},{18,... | collective-permute-start | bytes 135176 | tf_op jit(solution)/shard_map/ppermute | solution.py:550
  12.8 4.0 %collective-permute-start.3 = (f32[88,128]{1,0:T(8,128)S(1)}, f32[88,128]{1,0:T(8,128)S(1)}, u32[]{:S(2)}, u32[]{:S(2)}) collective-permute-start(f32[88,128]{1,0:T(8,128)S(1)} %get-tuple-element.45.pay_ref), channel_id=1, source_target_pairs={{0,2},{2,0},{4,6},{6,4},{8,10},{10,8},{12,14},{14,12},{16,18},{18,... | collective-permute-start | bytes 135176 | tf_op jit(solution)/shard_map/ppermute | solution.py:550
  17.0 6.2 %collective-permute-start.8 = (f32[136,128]{1,0:T(8,128)S(1)}, f32[136,128]{1,0:T(8,128)S(1)}, u32[]{:S(2)}, u32[]{:S(2)}) collective-permute-start(f32[136,128]{1,0:T(8,128)S(1)} %shard_map.76.own_group), channel_id=1, source_target_pairs={{0,24},{2,26},{4,28},{6,30},{8,16},{10,18},{12,20},{14,22},{16,8},... | collective-permute-start | bytes 208904 | tf_op jit(solution)/shard_map/ppermute | solution.py:550
  20.6 5.3 %collective-permute-start.7 = (f32[136,128]{1,0:T(8,128)S(1)}, f32[136,128]{1,0:T(8,128)S(1)}, u32[]{:S(2)}, u32[]{:S(2)}) collective-permute-start(f32[136,128]{1,0:T(8,128)S(1)} %shard_map.76.own_group), channel_id=1, source_target_pairs={{0,16},{2,18},{4,20},{6,22},{8,24},{10,26},{12,28},{14,30},{16,0},... | collective-permute-start | bytes 208904 | tf_op jit(solution)/shard_map/ppermute | solution.py:550
  20.6 5.3 %collective-permute-start.6 = (f32[136,128]{1,0:T(8,128)S(1)}, f32[136,128]{1,0:T(8,128)S(1)}, u32[]{:S(2)}, u32[]{:S(2)}) collective-permute-start(f32[136,128]{1,0:T(8,128)S(1)} %shard_map.76.own_group), channel_id=1, source_target_pairs={{0,8},{2,10},{4,12},{6,14},{8,0},{10,2},{12,4},{14,6},{16,24},{18,... | collective-permute-start | bytes 208904 | tf_op jit(solution)/shard_map/ppermute | solution.py:550
  26.5 1.3 %collective-permute-start.9 = (f32[128,128]{1,0:T(8,128)S(1)}, f32[128,128]{1,0:T(8,128)S(1)}, u32[]{:S(2)}, u32[]{:S(2)}) collective-permute-start(f32[128,128]{1,0:T(8,128)S(1)} %get-tuple-element.53), channel_id=1, source_target_pairs={{0,1},{1,0},{2,3},{3,2},{4,5},{5,4},{6,7},{7,6},{8,9},{9,8},{10,11... | collective-permute-start | bytes 196616 | tf_op jit(solution)/shard_map/ppermute | solution.py:532
  28.6 5.0 %collective-permute-start.12 = (f32[2,32,128]{2,1,0:T(8,128)S(1)}, f32[2,32,128]{2,1,0:T(8,128)S(1)}, u32[]{:S(2)}, u32[]{:S(2)}) collective-permute-start(f32[2,32,128]{2,1,0:T(8,128)S(1)} %get-tuple-element.54.pay_ref), channel_id=1, source_target_pairs={{0,6},{2,4},{4,2},{6,0},{8,14},{10,12},{12,10},{14,8},{16,22},{18,... | collective-permute-start | bytes 98312 | tf_op jit(solution)/shard_map/ppermute | solution.py:550
  30.6 3.9 %collective-permute-start.11 = (f32[2,32,128]{2,1,0:T(8,128)S(1)}, f32[2,32,128]{2,1,0:T(8,128)S(1)}, u32[]{:S(2)}, u32[]{:S(2)}) collective-permute-start(f32[2,32,128]{2,1,0:T(8,128)S(1)} %get-tuple-element.54.pay_ref), channel_id=1, source_target_pairs={{0,4},{2,6},{4,0},{6,2},{8,12},{10,14},{12,8},{14,10},{16,20},{18,... | collective-permute-start | bytes 98312 | tf_op jit(solution)/shard_map/ppermute | solution.py:550
  32.0 3.9 %collective-permute-start.10 = (f32[2,32,128]{2,1,0:T(8,128)S(1)}, f32[2,32,128]{2,1,0:T(8,128)S(1)}, u32[]{:S(2)}, u32[]{:S(2)}) collective-permute-start(f32[2,32,128]{2,1,0:T(8,128)S(1)} %get-tuple-element.54.pay_ref), channel_id=1, source_target_pairs={{0,2},{2,0},{4,6},{6,4},{8,10},{10,8},{12,14},{14,12},{16,18},{18,... | collective-permute-start | bytes 98312 | tf_op jit(solution)/shard_map/ppermute | solution.py:550
  35.9 4.5 %collective-permute-start.13 = (f32[32,128]{1,0:T(8,128)S(1)}, f32[32,128]{1,0:T(8,128)S(1)}, u32[]{:S(2)}, u32[]{:S(2)}) collective-permute-start(f32[32,128]{1,0:T(8,128)S(1)} %get-tuple-element.58), channel_id=1, source_target_pairs={{0,8},{2,10},{4,12},{6,14},{8,0},{10,2},{12,4},{14,6},{16,24},{18,... | collective-permute-start | bytes 49160 | tf_op jit(solution)/shard_map/ppermute | solution.py:550
  36.6 4.7 %collective-permute-start.14 = (f32[32,128]{1,0:T(8,128)S(1)}, f32[32,128]{1,0:T(8,128)S(1)}, u32[]{:S(2)}, u32[]{:S(2)}) collective-permute-start(f32[32,128]{1,0:T(8,128)S(1)} %get-tuple-element.59), channel_id=1, source_target_pairs={{0,16},{2,18},{4,20},{6,22},{8,24},{10,26},{12,28},{14,30},{16,0},... | collective-permute-start | bytes 49160 | tf_op jit(solution)/shard_map/ppermute | solution.py:550
  38.2 5.5 %collective-permute-start.15 = (f32[32,128]{1,0:T(8,128)S(1)}, f32[32,128]{1,0:T(8,128)S(1)}, u32[]{:S(2)}, u32[]{:S(2)}) collective-permute-start(f32[32,128]{1,0:T(8,128)S(1)} %get-tuple-element.60), channel_id=1, source_target_pairs={{0,24},{2,26},{4,28},{6,30},{8,16},{10,18},{12,20},{14,22},{16,8},... | collective-permute-start | bytes 49160 | tf_op jit(solution)/shard_map/ppermute | solution.py:550

commit v5 on v4

--- a/solution.py
+++ b/solution.py
@@ -28,17 +28,24 @@
         self.group_top = self.faces_at + self.members * self.tiles
         self.group_rows = self.group_top + padded
 
+    def conductance(self, arguments):
+        start = self.species * self.tiles
+        return arguments.at[start : start + self.tiles]
+
+    def warmth(self, arguments):
+        start = (self.species + 1) * self.tiles
+        return arguments.at[start : start + self.tiles]
+
     def groups(self, size):
         for base in range(0, self.tiles, size):
             yield range(base, min(base + size, self.tiles))
 
 
 def column(ref, z):
-    rows = lax.broadcasted_iota(jnp.int32, z.tile, 0)
-    value = jnp.zeros(z.tile, F32)
-    for s in range(z.species):
-        value = jnp.where(rows == s, ref[s], value)
-    return value
+    square = (z.species, z.species)
+    mine = lax.broadcasted_iota(jnp.int32, square, 0) == lax.broadcasted_iota(jnp.int32, square, 1)
+    values = jnp.where(mine, jnp.broadcast_to(ref[...], square), 0.0)
+    return jnp.broadcast_to(jnp.sum(values, axis=1, keepdims=True), z.tile)
 
 
 def spread(ref, row, z):
@@ -62,16 +69,8 @@
     return flag(me > 0), flag(me < count - 1)
 
 
-def edges_kernel(z, c_hbm, k_hbm, c_ref, k_ref, near_ref, far_ref, *refs):
-    *y_refs, sems = refs
-    loads = [
-        pltpu.make_async_copy(k_hbm, k_ref, sems.at[0]),
-        pltpu.make_async_copy(c_hbm, c_ref, sems.at[1]),
-    ]
-    for load in loads:
-        load.start()
-    for load in loads:
-        load.wait()
+def edges_kernel(z, c_ref, far_ref, near_ref, *y_refs):
+    k_ref = z.conductance(c_ref)
     odd = lax.axis_index("gz") % 2
     for ref, row in ((near_ref, (1 - odd) * (z.nz - 1)), (far_ref, odd * (z.nz - 1))):
         for y in range(z.ny):
@@ -94,49 +93,54 @@
     return [z.ny - 1, 0]
 
 
-def setup_kernel(
-    z, c_ref, k_ref, warm_ref, sigma_ref, frequency_ref, barrier_ref, proportions_ref,
-    tiles_ref, rates_ref, faces, arrhenius_ref, left_ref, right_ref, inverse_ref, base_ref, heat_ref,
-):
+def coefficients_kernel(z, arguments, sigma_ref, rates_ref, faces, left_ref, right_ref, inverse_ref):
     sigma = column(sigma_ref, z)
-    frequency = column(frequency_ref, z)
-    barrier = column(barrier_ref, z)
-    rates_ref[0] = 4.0 * sigma
+    rho = 4.0 * sigma
+    rates_ref[0] = rho
     rates_ref[1] = 0.015 * sigma
     rates_ref[2] = 4096.0 * sigma
     rates_ref[3] = 1.0 / (1024.0 * sigma)
-    heat_ref[...] = 1.0 - 1.0 / warm_ref[...]
-    k = k_ref[...]
+    k = z.conductance(arguments)[...]
     lanes = lax.broadcasted_iota(jnp.int32, k.shape, 1)
     faces[0] = 0.5 * (k + jnp.where(lanes == 0, 0.0, along_x(k, 1, z.nx)))
     faces[1] = 0.5 * (k + jnp.where(lanes == z.nx - 1, 0.0, along_x(k, -1, z.nx)))
+    lanes = lax.broadcasted_iota(jnp.int32, z.tile, 1)
+    tiles = range(z.tiles)
+    e, d = [], []
+    for t in tiles:
+        before = rho * spread(faces.at[0], t, z)
+        after = rho * spread(faces.at[1], t, z)
+        d.append(1.0 + (before + after))
+        e.append(jnp.where(lanes == 0, 0.0, before))
+    for level in range(z.levels):
+        stride = 1 << level
+        half = 2 * stride == z.nx
+        for t in tiles:
+            r = 1.0 / d[t]
+            above = along_x(e[t], -stride, z.nx)
+            r_before = along_x(r, stride, z.nx)
+            left = e[t] * r_before
+            right = above * (r_before if half else along_x(r, -stride, z.nx))
+            left_ref[level, t] = left + right if half else left
+            if not half:
+                right_ref[level, t] = right
+            d[t] = d[t] - e[t] * left - above * right
+            if not half:
+                e[t] = left * along_x(e[t], stride, z.nx)
+    for t in tiles:
+        inverse_ref[t] = 1.0 / d[t]
+
+
+def source_kernel(
+    z, c_ref, frequency_ref, barrier_ref, proportions_ref, rates_ref, faces,
+    tiles_ref, arrhenius_ref, base_ref, heat_ref,
+):
+    frequency, barrier = column(frequency_ref, z), column(barrier_ref, z)
+    heat_ref[...] = 1.0 - 1.0 / z.warmth(c_ref)[...]
     for t in range(z.tiles):
         tiles_ref[t] = c_ref[pl.ds(t, z.species, stride=z.tiles), :]
         arrhenius_ref[t] = frequency * jnp.exp(barrier * spread(heat_ref, t, z))
     base_sides(z, tiles_ref, rates_ref, faces, arrhenius_ref, proportions_ref, base_ref)
-
-    lanes = lax.broadcasted_iota(jnp.int32, z.tile, 1)
-    rho = rates_ref[0]
-    for tiles in z.groups(8):
-        e, d = [], []
-        for t in tiles:
-            before = rho * spread(faces.at[0], t, z)
-            after = rho * spread(faces.at[1], t, z)
-            d.append(1.0 + (before + after))
-            e.append(jnp.where(lanes == 0, 0.0, before))
-        for level in range(z.levels):
-            stride = 1 << level
-            for i, t in enumerate(tiles):
-                r = 1.0 / d[i]
-                above = along_x(e[i], -stride, z.nx)
-                left = e[i] * along_x(r, stride, z.nx)
-                right = above * along_x(r, -stride, z.nx)
-                left_ref[level, t] = left
-                right_ref[level, t] = right
-                d[i] = d[i] - e[i] * left - above * right
-                e[i] = left * along_x(e[i], stride, z.nx)
-        for i, t in enumerate(tiles):
-            inverse_ref[t] = 1.0 / d[i]
 
 
 def base_sides(z, tiles_ref, rates_ref, faces, arrhenius_ref, proportions_ref, base_ref):
@@ -161,36 +165,50 @@
         base_ref[t] = v + lap + source[:, t * z.nx : (t + 1) * z.nx]
 
 
-def base_kernel(z, *refs):
-    base_sides(z, *refs)
-
-
-def right_sides(z, tiles_ref, base_ref, z_halo, y_halo, rates_ref, faces, left, right, inverse, f_ref):
+def right_sides(z, places, tiles_ref, base_ref, z_halo, y_halo, rates_ref, y_faces, z_faces, left, right, inverse, f_ref):
     rate_y, rate_z = rates_ref[1], rates_ref[2]
-    for tiles in z.groups(8):
-        section, lap = [], []
-        for t in tiles:
-            y, row = divmod(t, z.nz)
-            v = tiles_ref[t]
-            z_before = tiles_ref[t - 1] if row else z_halo(0, y)
-            z_after = tiles_ref[t + 1] if row < z.nz - 1 else z_halo(1, y)
+    section, lap = [], []
+    for y, row in places:
+        t = y * z.nz + row
+        v = tiles_ref[t]
+        z_before = tiles_ref[t - 1] if row else z_halo(0, y)
+        z_after = tiles_ref[t + 1] if row < z.nz - 1 else z_halo(1, y)
+        if isinstance(y, int):
             y_before = tiles_ref[t - z.nz] if y else y_halo(0, row)
             y_after = tiles_ref[t + z.nz] if y < z.ny - 1 else y_halo(1, row)
-            flux = [spread(faces.at[n], t, z) for n in range(4)]
-            lap_y = rate_y * (flux[1] * (y_after - v) - flux[0] * (v - y_before))
-            lap_z = rate_z * (flux[3] * (z_after - v) - flux[2] * (v - z_before))
-            lap.append(lap_z)
-            section.append(base_ref[t] + lap_y + lap_z)
-        for level in range(z.levels):
-            stride = 1 << level
-            for i, t in enumerate(tiles):
-                section[i] = (
-                    section[i]
-                    + left[level, t] * along_x(section[i], stride, z.nx)
-                    + right[level, t] * along_x(section[i], -stride, z.nx)
-                )
-        for i, t in enumerate(tiles):
-            f_ref[t] = section[i] * inverse[t] - 0.5 * lap[i]
+        else:
+            y_before = jnp.where(y > 0, tiles_ref[jnp.maximum(y - 1, 0) * z.nz + row], y_halo(0, row))
+            y_after = jnp.where(
+                y < z.ny - 1, tiles_ref[jnp.minimum(y + 1, z.ny - 1) * z.nz + row], y_halo(1, row)
+            )
+        flux = [spread(faces.at[n], t, z) for faces in (y_faces, z_faces) for n in range(2)]
+        lap_y = rate_y * (flux[1] * (y_after - v) - flux[0] * (v - y_before))
+        lap_z = rate_z * (flux[3] * (z_after - v) - flux[2] * (v - z_before))
+        lap.append(lap_z)
+        section.append(base_ref[t] + lap_y + lap_z)
+    for level in range(z.levels):
+        stride = 1 << level
+        for i, (y, row) in enumerate(places):
+            t = y * z.nz + row
+            before = along_x(section[i], stride, z.nx)
+            more = left[level, t] * before
+            if 2 * stride < z.nx:
+                more = more + right[level, t] * along_x(section[i], -stride, z.nx)
+            section[i] = section[i] + more
+    for i, (y, row) in enumerate(places):
+        t = y * z.nz + row
+        f_ref[t] = section[i] * inverse[t] - 0.5 * lap[i]
+
+
+def y_halos(z, received):
+    low, high = received[0], received[-1]
+    low_mask, high_mask = inner("gy", z.gy)
+
+    def halo(side, row):
+        lines = per_line(z, row)
+        return high[lines, :] * high_mask if side else low[lines, :] * low_mask
+
+    return halo
 
 
 def send_sums(z, f_ref, v_ref, u_ref, pay_ref):
@@ -215,41 +233,70 @@
         above = above + jnp.where(lower, 0.0, down)
     within_ref[0] = below
     within_ref[1] = above
-    for i, ref in enumerate(out_refs):
+    for i, ref in enumerate(reversed(out_refs)):
         ref[...] = jnp.where((group ^ (i + 1)) > group, rising, falling)
 
 
-def first_kernel(
-    z, k_ref, near_ref, far_ref, tiles_ref, base_ref, rates_ref, left_ref, right_ref, inverse_ref, *refs
-):
+def z_face_pair(z, k_ref, low, high):
+    rows = lax.broadcasted_iota(jnp.int32, (z.nz, z.nx), 0)
+    for y in range(z.ny):
+        here = k_ref[y * z.nz : (y + 1) * z.nz, :]
+        before, after = (jnp.broadcast_to(row, here.shape) for row in (low(y), high(y)))
+        yield (
+            here + jnp.where(rows == 0, before, pltpu.roll(here, 1, 0)),
+            here + jnp.where(rows == z.nz - 1, after, pltpu.roll(here, z.nz - 1, 0)),
+        )
+
+
+def early_kernel(z, arguments, tiles_ref, base_ref, rates_ref, left_ref, right_ref, inverse_ref, *refs):
     halos = 1 if z.gy == 2 else 2
-    y_received = refs[:halos]
-    pay_ref, f_ref, faces, from_below, from_above = refs[halos:]
-    odd = lax.axis_index("gz") % 2 == 1
-    from_below[...] = jnp.where(odd, near_ref[...], far_ref[...])
-    from_above[...] = jnp.where(odd, far_ref[...], near_ref[...])
+    received = refs[:halos]
+    f_ref, y_faces, z_faces = refs[halos:]
+    k_ref = z.conductance(arguments)
     k = k_ref[...]
-    low, high = y_received[0], y_received[-1]
+    low, high = received[0], received[-1]
     low_mask, high_mask = inner("gy", z.gy)
     k_base = z.nz * z.species
     below = jnp.concatenate([low[k_base:, :] * low_mask, k[: z.tiles - z.nz]], axis=0)
     above = jnp.concatenate([k[z.nz :], high[k_base:, :] * high_mask], axis=0)
-    faces[0] = 0.5 * (k + below)
-    faces[1] = 0.5 * (k + above)
-
+    y_faces[0] = 0.5 * (k + below)
+    y_faces[1] = 0.5 * (k + above)
+    nothing = jnp.zeros((1, z.nx), F32)
+    for y, (before, after) in enumerate(z_face_pair(z, k_ref, lambda y: nothing, lambda y: nothing)):
+        own = slice(y * z.nz, (y + 1) * z.nz)
+        z_faces[0, own, :] = 0.5 * before
+        z_faces[1, own, :] = 0.5 * after
+    places = [(y, row) for y in range(z.ny) for row in range(1, z.nz - 1)]
+    right_sides(
+        z, places, tiles_ref, base_ref, None, y_halos(z, received), rates_ref, y_faces, z_faces,
+        left_ref, right_ref, inverse_ref, f_ref,
+    )
+
+
+def first_kernel(
+    z, arguments, far_ref, near_ref, tiles_ref, base_ref, rates_ref, left_ref, right_ref, inverse_ref,
+    early_ref, y_faces, *refs
+):
+    halos = 1 if z.gy == 2 else 2
+    received = refs[:halos]
+    pay_ref, f_ref, z_faces, from_below, from_above = refs[halos:]
+    k_ref = z.conductance(arguments)
+    odd = lax.axis_index("gz") % 2 == 1
+    from_below[...] = jnp.where(odd, near_ref[...], far_ref[...])
+    from_above[...] = jnp.where(odd, far_ref[...], near_ref[...])
     z_low, z_high = inner("gz", z.devices)
-    rows = lax.broadcasted_iota(jnp.int32, (z.nz, z.nx), 0)
     pay_ref[z.faces_at + z.tiles :, :] = jnp.zeros((z.block_rows - z.faces_at - z.tiles, z.nx), F32)
-    for y in range(z.ny):
+
+    def k_low(y):
+        return from_below[z.lines + y : z.lines + y + 1, :] * z_low
+
+    def k_high(y):
+        return from_above[z.lines + y : z.lines + y + 1, :] * z_high
+
+    for y, (before, after) in enumerate(z_face_pair(z, k_ref, k_low, k_high)):
         own = slice(y * z.nz, (y + 1) * z.nz)
-        here = k[own]
-        row = z.lines + y
-        before = jnp.broadcast_to(from_below[row : row + 1, :] * z_low, here.shape)
-        after = jnp.broadcast_to(from_above[row : row + 1, :] * z_high, here.shape)
-        before = here + jnp.where(rows == 0, before, pltpu.roll(here, 1, 0))
-        after = here + jnp.where(rows == z.nz - 1, after, pltpu.roll(here, z.nz - 1, 0))
-        faces[2, own, :] = 0.5 * before
-        faces[3, own, :] = 0.5 * after
+        z_faces[0, own, :] = 0.5 * before
+        z_faces[1, own, :] = 0.5 * after
         pay_ref[z.faces_at + y * z.nz : z.faces_at + (y + 1) * z.nz, :] = 1.0 / before
         top = z.faces_at + z.tiles + y
         pay_ref[top : top + 1, :] = 1.0 / after[z.nz - 1 :, :]
@@ -258,12 +305,13 @@
         lines = per_line(z, y)
         return from_above[lines, :] * z_high if side else from_below[lines, :] * z_low
 
-    def y_halo(side, row):
-        lines = per_line(z, row)
-        return high[lines, :] * high_mask if side else low[lines, :] * low_mask
-
+    for y in range(z.ny):
+        for row in range(1, z.nz - 1):
+            f_ref[y * z.nz + row] = early_ref[y * z.nz + row]
+    places = [(y, row) for y in range(z.ny) for row in sorted({0, z.nz - 1})]
     right_sides(
-        z, tiles_ref, base_ref, z_halo, y_halo, rates_ref, faces, left_ref, right_ref, inverse_ref, f_ref
+        z, places, tiles_ref, base_ref, z_halo, y_halos(z, received), rates_ref, y_faces, z_faces,
+        left_ref, right_ref, inverse_ref, f_ref,
     )
     ohms = rates_ref[3]
     zero, one = jnp.zeros(z.tile, F32), jnp.ones(z.tile, F32)
@@ -420,7 +468,7 @@
     return below, above
 
 
-def solve_lines(z, sums, f_ref, v_ref, u_ref, ends_ref, store):
+def solve_lines(z, sums, f_ref, v_ref, u_ref, ends_ref, store, finish=None):
     halos = []
     for y, (below, above) in enumerate(zip(*sums)):
         scale = ends_ref[4 * z.ny + y]
@@ -435,6 +483,8 @@
         for t in tiles:
             total = total + v_ref[t] * f_ref[t]
             store(t, scale * (u_ref[t] * total + v_ref[t] * after[t]))
+        if finish:
+            finish(y)
         high = scale * (ends_ref[3 * z.ny + y] * total + ends_ref[z.ny + y] * above)
         halos.append((low, high))
     return halos
@@ -470,31 +520,53 @@
     hand_on(z, halos, tiles_ref, halo_ref, y_refs)
 
 
+def halo_rows(z):
+    if z.gy == 2:
+        core = lax.axis_index("gy")
+        return y_picks(z), [core + j for j in range(z.ny - 1)]
+    return list(range(z.ny)), []
+
+
+def places_of(z, ys):
+    return [(y, row) for y in ys for row in range(z.nz)]
+
+
+def inner_kernel(
+    z, tiles_ref, halo_ref, rates_ref, x_faces, arrhenius_ref, proportions_ref, y_faces, z_faces,
+    left_ref, right_ref, inverse_ref, base_ref, f_ref
+):
+    base_sides(z, tiles_ref, rates_ref, x_faces, arrhenius_ref, proportions_ref, base_ref)
+    _, ys = halo_rows(z)
+    zero = jnp.zeros(z.tile, F32)
+    if ys:
+        right_sides(
+            z, places_of(z, ys), tiles_ref, base_ref, lambda side, y: halo_ref[side * z.ny + y],
+            lambda side, row: zero, rates_ref, y_faces, z_faces, left_ref, right_ref, inverse_ref, f_ref,
+        )
+
+
 def second_kernel(
-    z, tiles_ref, base_ref, halo_ref, rates_ref, faces, left_ref, right_ref, inverse_ref, v_ref, u_ref,
-    *refs
+    z, tiles_ref, halo_ref, rates_ref, y_faces, z_faces, left_ref, right_ref, inverse_ref, base_ref,
+    inner_ref, v_ref, u_ref, *refs
 ):
     halos = 1 if z.gy == 2 else 2
-    low, high = refs[0], refs[halos - 1]
+    received = refs[:halos]
     pay_ref, f_ref = refs[halos:]
-    low_mask, high_mask = inner("gy", z.gy)
-
-    def y_halo(side, row):
-        lines = slice(row * z.species, (row + 1) * z.species)
-        return high[lines, :] * high_mask if side else low[lines, :] * low_mask
-
+    ys, done = halo_rows(z)
+    for y, row in places_of(z, done):
+        f_ref[y * z.nz + row] = inner_ref[y * z.nz + row]
     right_sides(
-        z, tiles_ref, base_ref, lambda side, y: halo_ref[side * z.ny + y], y_halo, rates_ref, faces,
-        left_ref, right_ref, inverse_ref, f_ref,
+        z, places_of(z, ys), tiles_ref, base_ref, lambda side, y: halo_ref[side * z.ny + y],
+        y_halos(z, received), rates_ref, y_faces, z_faces, left_ref, right_ref, inverse_ref, f_ref,
     )
     send_sums(z, f_ref, v_ref, u_ref, pay_ref)
 
 
 def last_kernel(z, within_ref, f_ref, v_ref, u_ref, ends_ref, *refs):
-    *across, out_ref = refs
+    *across, out_hbm, rows_ref, sems = refs
     group = lax.axis_index("gz") // z.members
     below, above = within_ref[0], within_ref[1]
-    for i, ref in enumerate(across):
+    for i, ref in enumerate(reversed(across)):
         lower = (group ^ (i + 1)) < group
         value = ref[...]
         below = below + jnp.where(lower, value, 0.0)
@@ -502,30 +574,39 @@
     sums = [[v[per_line(z, y)] for y in range(z.ny)] for v in (below, above)]
 
     def store(t, value):
-        out_ref[pl.ds(t, z.species, stride=z.tiles), :] = value
-
-    solve_lines(z, sums, f_ref, v_ref, u_ref, ends_ref, store)
+        rows_ref[pl.ds(t, z.species, stride=z.tiles), :] = value
+
+    blocks = rows_ref.reshape(z.species, z.ny, z.nz, z.nx)
+    copies = []
+
+    def send(y):
+        copies.append(pltpu.make_async_copy(blocks.at[:, y], out_hbm.at[:, y], sems.at[y]))
+        copies[-1].start()
+
+    solve_lines(z, sums, f_ref, v_ref, u_ref, ends_ref, store, send)
+    for copy in copies:
+        copy.wait()
 
 
 def per_device(z, c, k, warm, sigma, frequency, barrier, proportions):
-    vmem = pl.BlockSpec(memory_space=pltpu.VMEM)
-    smem = pl.BlockSpec(memory_space=pltpu.SMEM)
-    params = pltpu.CompilerParams(vmem_limit_bytes=48 * 2**20)
+    in_vmem = pl.BlockSpec(memory_space=pltpu.VMEM)
+    hbm = pl.BlockSpec(memory_space=pltpu.HBM)
 
     def shaped(*shape):
         return jax.ShapeDtypeStruct(shape, F32)
 
-    def call(kernel, outs, ins, scratch=(), flops=1000000):
-        specs = [spec for spec, _ in ins]
+    def call(kernel, outs, ins, scratch=(), spec=in_vmem, out_spec=in_vmem, us=0.5):
         return pl.pallas_call(
             functools.partial(kernel, z),
             out_shape=outs,
-            in_specs=specs,
-            out_specs=jax.tree.map(lambda _: vmem, outs),
+            in_specs=[spec] * len(ins),
+            out_specs=jax.tree.map(lambda _: out_spec, outs),
             scratch_shapes=list(scratch),
-            compiler_params=params,
-            cost_estimate=pl.CostEstimate(flops=flops, bytes_accessed=1000000, transcendentals=0),
-        )(*[value for _, value in ins])
+            compiler_params=pltpu.CompilerParams(vmem_limit_bytes=48 * 2**20),
+            cost_estimate=pl.CostEstimate(
+                flops=0, bytes_accessed=int(us * 3.69e6), transcendentals=0
+            ),
+        )(*ins)
 
     def shift(value, axis, by):
         count = lax.axis_size(axis)
@@ -534,12 +615,7 @@
     def swap(sends):
         return [shift(value, "gy", by) for value, by in zip(sends, (1, -1))]
 
-    def in_vmem(*values):
-        return [(vmem, value) for value in values]
-
-    c = c.reshape(z.species * z.tiles, z.nx)
-    k = k.reshape(z.tiles, z.nx)
-    warm = warm.reshape(z.tiles, z.nx)
+    arguments = jnp.concatenate([v.reshape(-1, z.nx) for v in (c, k, warm)])
     halos = 1 if z.gy == 2 else 2
     block = shaped(z.tiles, *z.tile)
     ends_shape = shaped(5 * z.ny, *z.tile)
@@ -547,6 +623,8 @@
     def exchange(value, count, unit):
         values = value if isinstance(value, list) else [value] * (count - 1)
         pairs = [[(i, i ^ (k * unit)) for i in range(z.devices)] for k in range(1, count)]
+        if isinstance(value, list):
+            return [lax.ppermute(v, "gz", p) for v, p in zip(values[::-1], pairs[::-1])][::-1]
         return [lax.ppermute(v, "gz", p) for v, p in zip(values, pairs)]
 
     def neighbours(near, far):
@@ -556,48 +634,48 @@
         ends = [(i, i) for i in (0, last)]
         far_pairs = [(i * z.gy + n, j * z.gy + n) for i, j in links for n in range(z.gy)]
         far_pairs += [(i * z.gy + n, j * z.gy + (n ^ 1)) for i, j in ends for n in range(z.gy)]
-        return exchange(near, 2, 1)[0], lax.ppermute(far, ("gz", "gy"), far_pairs)
-
-    c, k, near, far, *sends = pl.pallas_call(
-        functools.partial(edges_kernel, z),
-        out_shape=[shaped(z.species * z.tiles, z.nx), shaped(z.tiles, z.nx)]
-        + [shaped(z.edge_rows, z.nx)] * 2
-        + [shaped(z.nz * (z.species + 1), z.nx)] * halos,
-        in_specs=[pl.BlockSpec(memory_space=pl.ANY)] * 2,
-        out_specs=[vmem] * (4 + halos),
-        scratch_shapes=[pltpu.SemaphoreType.DMA((2,))],
-        compiler_params=params,
-    )(c, k)
+        far = lax.ppermute(far, ("gz", "gy"), far_pairs)
+        return exchange(near, 2, 1)[0], far
+
+    far, near, *sends = call(
+        edges_kernel,
+        [shaped(z.edge_rows, z.nx)] * 2 + [shaped(z.nz * (z.species + 1), z.nx)] * halos,
+        [arguments],
+    )
+    near, far = neighbours(near, far)
     received = swap(sends)
-    near, far = neighbours(near, far)
-    tiles, rates, x_faces, arrhenius, left, right, inverse, base = call(
-        setup_kernel,
-        [
-            block,
-            shaped(4, *z.tile),
-            shaped(2, z.tiles, z.nx),
-            block,
-            shaped(z.levels, z.tiles, *z.tile),
-            shaped(z.levels, z.tiles, *z.tile),
-            block,
-            block,
-        ],
-        in_vmem(c, k, warm)
-        + [(smem, sigma), (smem, frequency), (smem, barrier)]
-        + in_vmem(proportions),
+    levels = shaped(z.levels, z.tiles, *z.tile)
+    faces = shaped(2, z.tiles, z.nx)
+    rates, x_faces, left, right, inverse = call(
+        coefficients_kernel,
+        [shaped(4, *z.tile), faces, levels, levels, block],
+        [arguments, sigma.reshape(1, -1)],
+        us=1.0,
+    )
+    tiles, arrhenius, base = call(
+        source_kernel,
+        [block] * 3,
+        [arguments, frequency.reshape(1, -1), barrier.reshape(1, -1), proportions, rates, x_faces],
         [pltpu.VMEM((z.tiles, z.nx), F32)],
     )
-    pay, f, faces = call(
+    x_solve = [left, right, inverse]
+    early, y_faces = call(
+        early_kernel,
+        [block, faces],
+        [arguments, tiles, base, rates, *x_solve, *received],
+        [pltpu.VMEM((2, z.tiles, z.nx), F32)],
+    )
+    pay, f, z_faces = call(
         first_kernel,
-        [shaped(z.block_rows, z.nx), block, shaped(4, z.tiles, z.nx)],
-        in_vmem(k, near, far, tiles, base, rates, left, right, inverse, *received),
+        [shaped(z.block_rows, z.nx), block, faces],
+        [arguments, far, near, tiles, base, rates, *x_solve, early, y_faces, *received],
         [pltpu.VMEM((z.edge_rows, z.nx), F32)] * 2,
     )
     inside = exchange(pay, z.members, 1)
     group = call(
         merge_kernel,
         shaped(z.group_rows, z.nx),
-        in_vmem(rates, pay, *inside),
+        [rates, pay, *inside],
         [pltpu.VMEM((z.members, z.block_rows, z.nx), F32)],
     )
     across = exchange(group, z.groups_z, z.members)
@@ -605,7 +683,7 @@
         meet_kernel,
         [block, shaped(2 * z.ny, *z.tile), block, block, ends_shape]
         + [shaped(z.nz * z.species, z.nx)] * halos,
-        in_vmem(rates, f, pay, group, *inside, *across),
+        [rates, f, pay, group, *inside, *across],
         [
             pltpu.VMEM((z.members, z.block_rows, z.nx), F32),
             pltpu.VMEM((z.groups_z, z.group_rows, z.nx), F32),
@@ -613,25 +691,30 @@
     )
 
     received = swap(sends)
-    base = call(base_kernel, block, in_vmem(tiles, rates, x_faces, arrhenius, proportions))
+    base, f = call(
+        inner_kernel,
+        [block, block],
+        [tiles, halo, rates, x_faces, arrhenius, proportions, y_faces, z_faces, *x_solve],
+    )
     pay, f = call(
         second_kernel,
         [shaped(2, z.lines, z.nx), block],
-        in_vmem(tiles, base, halo, rates, faces, left, right, inverse, v, u, *received),
+        [tiles, halo, rates, y_faces, z_faces, *x_solve, base, f, v, u, *received],
     )
     inside = exchange(pay, z.members, 1)
     within, *totals = call(
         total_kernel,
         [shaped(2, z.lines, z.nx)] + [shaped(z.lines, z.nx)] * (z.groups_z - 1),
-        in_vmem(pay, *inside),
-    )
-    across = exchange(totals, z.groups_z, z.members)
-    out = call(
+        [pay, *inside],
+    )
+    across = exchange(totals[::-1], z.groups_z, z.members)
+    return call(
         last_kernel,
-        shaped(z.species * z.tiles, z.nx),
-        in_vmem(within, f, v, u, ends, *across),
-    )
-    return out.reshape(z.species, z.ny, z.nz, z.nx)
+        shaped(z.species, z.ny, z.nz, z.nx),
+        [within, f, v, u, ends, *across[::-1]],
+        [pltpu.VMEM((z.species * z.tiles, z.nx), F32), pltpu.SemaphoreType.DMA((z.ny,))],
+        out_spec=hbm,
+    )
 
 
 def solution(mesh):

time: 44.7 us -> 41.7 us (0.933)
  waiting for transfers between devices: 16 us -> 13.5 us
  local copies, waits for them, and re-layouts: 2.28 us -> 0.66 us
  other arithmetic: 0 us -> 0.95 us
    ppermute x13 -> x10, waiting for transfers between devices: 15.1 us -> 10.6 us  [exchange(): return [lax.ppermute(v, 'gz', p) for v, p in zip(values, pairs)]]
    ppermute x1 -> x4, starting transfers between devices: 0.17 us -> 4.53 us  [the longest x3 4.45 us: exchange(): lax.ppermute(v, 'gz', p)]
    ppermute x13 -> x10, starting transfers between devices: 20 us -> 15.7 us  [exchange(): return [lax.ppermute(v, 'gz', p) for v, p in zip(values, pairs)]]
    ppermute x1 -> x4, waiting for transfers between devices: 0.01 us -> 2.45 us  [the longest x3 2.44 us: exchange(): lax.ppermute(v, 'gz', p)]
    unnamed x14 -> x8, local copies, waits for them, and re-layouts: 2.28 us -> 0.66 us
    concatenate x0 -> x1, other arithmetic: none -> 0.95 us  [per_device(): arguments = jnp.concatenate([v.reshape(-1, z.nx) for v in (c, k, warm)])]
    ppermute x2, waiting for transfers between devices: 0.96 us -> 0.42 us  [shift(): lax.ppermute(value, axis, [(i, (i + by) % count) for i in range(count)])]
    pallas_call x9 -> x11, Pallas kernels: 5.33 us -> 5.51 us  [call(): pl.pallas_call(functools.partial(kernel, z), out_shape=outs, in_specs=[sp...]
  transfers between devices with their start and end apart: 16 -> 16, of which waited for: 10 -> 11; matrix products, arithmetic and copies ran while one was open for 0% -> 0% of each run, Pallas kernels for 5% -> 7%
where the time goes in v5:
time: 41.7 us; the launch traced here: 41.5 us
  starting transfers between devices  20.8 us (50%)
  waiting for transfers between devices  13.5 us (32%)
  Pallas kernels  5.51 us (13%)
  other arithmetic  0.95 us (2%)
  local copies, waits for them, and re-layouts  0.66 us (2%)
    ppermute x10, starting transfers between devices, exchange(): return [lax.ppermute(v, 'gz', p) for v, p in zip(values, pairs)]  15.7 us
    ppermute x10, waiting for transfers between devices, exchange(): return [lax.ppermute(v, 'gz', p) for v, p in zip(values, pairs)]  10.6 us
    pallas_call x11, Pallas kernels, call(): pl.pallas_call(functools.partial(kernel, z), out_shape=outs, in_specs=[sp...  5.51 us
    ppermute x3, starting transfers between devices, exchange(): lax.ppermute(v, 'gz', p)  4.45 us
    ppermute x3, waiting for transfers between devices, exchange(): lax.ppermute(v, 'gz', p)  2.44 us
    concatenate x1, other arithmetic, per_device(): arguments = jnp.concatenate([v.reshape(-1, z.nx) for v in (c, k, warm)])  0.95 us
  transfers between devices with their start and end apart: 16, of which 11 were waited for; matrix products, arithmetic and copies ran while one was open for 0% of the time, Pallas kernels for 7%

profile of v5, /device:TPU:0, one launch (start us, length us, event | category | flops | bytes accessed | tf_op | source)
XLA Modules:
  0.0 41.5 jit_solution(4127029862903140085)
XLA Ops:
  0.0 0.9 %pad_maximum_fusion.arguments.c_ref = f32[288,128]{1,0:T(8,128)S(1)} fusion(f32[16,128]{1,0:T(8,128)} %bitcast.10, f32[16,128]{1,0:T(8,128)} %bitcast.11, f32[256,128]{1,0:T(8,128)} %bitcast.9), kind=kLoop, calls=%fused_computation | loop fusion | flops 73728 | bytes 294912 | tf_op jit(solution)/shard_map/concatenate | solution.py:618
  1.0 0.5 %collective-permute-start.2 = (f32[136,128]{1,0:T(8,128)S(1)}, f32[136,128]{1,0:T(8,128)S(1)}, u32[]{:S(2)}, u32[]{:S(2)}) collective-permute-start(f32[136,128]{1,0:T(8,128)S(1)} %get-tuple-element.44), channel_id=1, source_target_pairs={{0,1},{1,0},{2,3},{3,2},{4,5},{5,4},{6,7},{7,6},{8,9},{9,8},{10,11... | collective-permute-start | bytes 208904 | tf_op jit(solution)/shard_map/ppermute | solution.py:613
  1.5 0.1 collective-permute-start
  1.6 4.0 %collective-permute-start.1 = (f32[40,128]{1,0:T(8,128)S(1)}, f32[40,128]{1,0:T(8,128)S(1)}, u32[]{:S(2)}, u32[]{:S(2)}) collective-permute-start(f32[40,128]{1,0:T(8,128)S(1)} %get-tuple-element.37), channel_id=1, source_target_pairs={{0,2},{2,0},{4,6},{6,4},{8,10},{10,8},{12,14},{14,12},{16,18},{18,... | collective-permute-start | bytes 61448 | tf_op jit(solution)/shard_map/ppermute | solution.py:628
  5.6 0.0 copy-done.1
  5.6 1.1 %shard_map.73 = (f32[4,16,128]{2,1,0:T(8,128)S(1)}, f32[2,16,128]{2,1,0:T(8,128)S(1)}, f32[7,16,16,128]{3,2,1,0:T(8,128)S(1)}, f32[7,16,16,128]{3,2,1,0:T(8,128)S(1)}, f32[16,16,128]{2,1,0:T(8,128)S(1)}) custom-call(f32[288,128]{1,0:T(8,128)S(1)} %pad_maximum_fusion.arguments.c_ref, f32[1,16]{1,0:T(1,128)S(1)} %bitcast.6), custom_call_target="tpu_custom_call" | custom-call | bytes 3690000 | tf_op jit(solution)/shard_map/pallas_call | solution.py:599
  6.7 0.0 copy-start.2
  6.7 0.0 copy-start.3
  6.7 0.0 copy-done
  6.7 0.6 %copy-done.2 = f32[16]{0:T(128)S(1)} copy-done((f32[16]{0:T(128)S(1)}, f32[16]{0:T(128)}, u32[]{:S(2)}) %copy-start.2) | copy-done | bytes 88
  7.3 0.0 copy-done.3
  7.3 0.4 shard_map.75
  7.7 0.0 collective-permute-done.2.refs_0_
  7.7 0.6 %shard_map.76 = (f32[16,16,128]{2,1,0:T(8,128)S(1)}, f32[2,16,128]{2,1,0:T(8,128)S(1)}) custom-call(f32[288,128]{1,0:T(8,128)S(1)} %pad_maximum_fusion.arguments.c_ref, f32[16,16,128]{2,1,0:T(8,128)S(1)} %get-tuple-element.39.tiles_ref, f32[16,16,128]{2,1,0:T(8,128)S(1)} %get-tuple-element.40.base_ref, f32[4,16,128]{2,1,0:T(8,128)S(1)} %get-tuple-element.35.rates_ref, ...), custom_call_target="tpu_custom_call" | custom-call | bytes 1845000 | tf_op jit(solution)/shard_map/pallas_call | solution.py:599
  8.3 0.0 collective-permute-done.far_ref
  8.3 0.0 collective-permute-done.1.near_ref
  8.3 0.6 %shard_map.77 = (f32[88,128]{1,0:T(8,128)S(1)}, f32[16,16,128]{2,1,0:T(8,128)S(1)}, f32[2,16,128]{2,1,0:T(8,128)S(1)}) custom-call(f32[288,128]{1,0:T(8,128)S(1)} %pad_maximum_fusion.arguments.c_ref, f32[40,128]{1,0:T(8,128)S(1)} %collective-permute-done.far_ref, f32[40,128]{1,0:T(8,128)S(1)} %collective-permute-done.1.near_ref, ...), custom_call_target="tpu_custom_call" | custom-call | bytes 1845000 | tf_op jit(solution)/shard_map/pallas_call | solution.py:599
  8.9 2.4 %collective-permute-start.5 = (f32[88,128]{1,0:T(8,128)S(1)}, f32[88,128]{1,0:T(8,128)S(1)}, u32[]{:S(2)}, u32[]{:S(2)}) collective-permute-start(f32[88,128]{1,0:T(8,128)S(1)} %get-tuple-element.48.pay_ref), channel_id=1, source_target_pairs={{0,6},{2,4},{4,2},{6,0},{8,14},{10,12},{12,10},{14,8},{16,22},{18,... | collective-permute-start | bytes 135176 | tf_op jit(solution)/shard_map/ppermute | solution.py:628
  11.3 0.3 collective-permute-start.4
  11.5 0.9 %collective-permute-start.3 = (f32[88,128]{1,0:T(8,128)S(1)}, f32[88,128]{1,0:T(8,128)S(1)}, u32[]{:S(2)}, u32[]{:S(2)}) collective-permute-start(f32[88,128]{1,0:T(8,128)S(1)} %get-tuple-element.48.pay_ref), channel_id=1, source_target_pairs={{0,2},{2,0},{4,6},{6,4},{8,10},{10,8},{12,14},{14,12},{16,18},{18,... | collective-permute-start | bytes 135176 | tf_op jit(solution)/shard_map/ppermute | solution.py:628
  12.4 1.6 %collective-permute-done.5.refs_2_ = f32[88,128]{1,0:T(8,128)S(1)} collective-permute-done((f32[88,128]{1,0:T(8,128)S(1)}, f32[88,128]{1,0:T(8,128)S(1)}, u32[]{:S(2)}, u32[]{:S(2)}) %collective-permute-start.5) | collective-permute-done | bytes 45088 | tf_op jit(solution)/shard_map/ppermute | solution.py:628
  14.0 1.3 %collective-permute-done.4.refs_1_ = f32[88,128]{1,0:T(8,128)S(1)} collective-permute-done((f32[88,128]{1,0:T(8,128)S(1)}, f32[88,128]{1,0:T(8,128)S(1)}, u32[]{:S(2)}, u32[]{:S(2)}) %collective-permute-start.4) | collective-permute-done | bytes 45088 | tf_op jit(solution)/shard_map/ppermute | solution.py:628
  15.3 0.3 collective-permute-done.3.refs_0_
  15.6 0.1 shard_map.78.own_group
  15.7 3.9 %collective-permute-start.8 = (f32[136,128]{1,0:T(8,128)S(1)}, f32[136,128]{1,0:T(8,128)S(1)}, u32[]{:S(2)}, u32[]{:S(2)}) collective-permute-start(f32[136,128]{1,0:T(8,128)S(1)} %shard_map.78.own_group), channel_id=1, source_target_pairs={{0,24},{2,26},{4,28},{6,30},{8,16},{10,18},{12,20},{14,22},{16,8},... | collective-permute-start | bytes 208904 | tf_op jit(solution)/shard_map/ppermute | solution.py:628
  19.7 0.0 collective-permute-start.7
  19.7 0.6 %collective-permute-start.6 = (f32[136,128]{1,0:T(8,128)S(1)}, f32[136,128]{1,0:T(8,128)S(1)}, u32[]{:S(2)}, u32[]{:S(2)}) collective-permute-start(f32[136,128]{1,0:T(8,128)S(1)} %shard_map.78.own_group), channel_id=1, source_target_pairs={{0,8},{2,10},{4,12},{6,14},{8,0},{10,2},{12,4},{14,6},{16,24},{18,... | collective-permute-start | bytes 208904 | tf_op jit(solution)/shard_map/ppermute | solution.py:628
  20.3 1.9 %collective-permute-done.8.refs_5_ = f32[136,128]{1,0:T(8,128)S(1)} collective-permute-done((f32[136,128]{1,0:T(8,128)S(1)}, f32[136,128]{1,0:T(8,128)S(1)}, u32[]{:S(2)}, u32[]{:S(2)}) %collective-permute-start.8) | collective-permute-done | bytes 69664 | tf_op jit(solution)/shard_map/ppermute | solution.py:628
  22.2 2.9 %collective-permute-done.7.refs_4_ = f32[136,128]{1,0:T(8,128)S(1)} collective-permute-done((f32[136,128]{1,0:T(8,128)S(1)}, f32[136,128]{1,0:T(8,128)S(1)}, u32[]{:S(2)}, u32[]{:S(2)}) %collective-permute-start.7) | collective-permute-done | bytes 69664 | tf_op jit(solution)/shard_map/ppermute | solution.py:628
  25.0 0.0 collective-permute-done.6.refs_3_
  25.0 0.6 %shard_map.79 = (f32[16,16,128]{2,1,0:T(8,128)S(1)}, f32[4,16,128]{2,1,0:T(8,128)S(1)}, f32[16,16,128]{2,1,0:T(8,128)S(1)}, f32[16,16,128]{2,1,0:T(8,128)S(1)}, ...) custom-call(f32[4,16,128]{2,1,0:T(8,128)S(1)} %get-tuple-element.35.rates_ref, ...), custom_call_target="tpu_custom_call" | custom-call | bytes 1845000 | tf_op jit(solution)/shard_map/pallas_call | solution.py:599
  25.7 0.1 collective-permute-start.9
  25.7 0.8 %shard_map.80 = (f32[16,16,128]{2,1,0:T(8,128)S(1)}, f32[16,16,128]{2,1,0:T(8,128)S(1)}) custom-call(f32[16,16,128]{2,1,0:T(8,128)S(1)} %get-tuple-element.49.tiles_ref, f32[4,16,128]{2,1,0:T(8,128)S(1)} %get-tuple-element.50.halo_ref, f32[4,16,128]{2,1,0:T(8,128)S(1)} %get-tuple-element.35.rates_ref, f32[2,16,128]{2,1,0:T(8,128)S(1)} %get-tuple-element.38.faces.x_faces, ...), custom_call_target="tpu_custom_call" | custom-call | bytes 1845000 | tf_op jit(solution)/shard_map/pallas_call | solution.py:599
  26.5 0.4 %collective-permute-done.9.refs_0_ = f32[128,128]{1,0:T(8,128)S(1)} collective-permute-done((f32[128,128]{1,0:T(8,128)S(1)}, f32[128,128]{1,0:T(8,128)S(1)}, u32[]{:S(2)}, u32[]{:S(2)}) %collective-permute-start.9) | collective-permute-done | bytes 65568 | tf_op jit(solution)/shard_map/ppermute | solution.py:613
  27.0 0.6 %shard_map.81 = (f32[2,32,128]{2,1,0:T(8,128)S(1)}, f32[16,16,128]{2,1,0:T(8,128)S(1)}) custom-call(f32[16,16,128]{2,1,0:T(8,128)S(1)} %get-tuple-element.49.tiles_ref, f32[4,16,128]{2,1,0:T(8,128)S(1)} %get-tuple-element.50.halo_ref, f32[4,16,128]{2,1,0:T(8,128)S(1)} %get-tuple-element.35.rates_ref, f32[2,16,128]{2,1,0:T(8,128)S(1)} %get-tuple-element.46.y_faces, ...), custom_call_target="tpu_custom_call" | custom-call | bytes 1845000 | tf_op jit(solution)/shard_map/pallas_call | solution.py:599
  27.5 1.4 %collective-permute-start.12 = (f32[2,32,128]{2,1,0:T(8,128)S(1)}, f32[2,32,128]{2,1,0:T(8,128)S(1)}, u32[]{:S(2)}, u32[]{:S(2)}) collective-permute-start(f32[2,32,128]{2,1,0:T(8,128)S(1)} %get-tuple-element.58.pay_ref), channel_id=1, source_target_pairs={{0,6},{2,4},{4,2},{6,0},{8,14},{10,12},{12,10},{14,8},{16,22},{18,... | collective-permute-start | bytes 98312 | tf_op jit(solution)/shard_map/ppermute | solution.py:628
  29.0 1.0 %collective-permute-start.11 = (f32[2,32,128]{2,1,0:T(8,128)S(1)}, f32[2,32,128]{2,1,0:T(8,128)S(1)}, u32[]{:S(2)}, u32[]{:S(2)}) collective-permute-start(f32[2,32,128]{2,1,0:T(8,128)S(1)} %get-tuple-element.58.pay_ref), channel_id=1, source_target_pairs={{0,4},{2,6},{4,0},{6,2},{8,12},{10,14},{12,8},{14,10},{16,20},{18,... | collective-permute-start | bytes 98312 | tf_op jit(solution)/shard_map/ppermute | solution.py:628
  29.9 1.2 %collective-permute-start.10 = (f32[2,32,128]{2,1,0:T(8,128)S(1)}, f32[2,32,128]{2,1,0:T(8,128)S(1)}, u32[]{:S(2)}, u32[]{:S(2)}) collective-permute-start(f32[2,32,128]{2,1,0:T(8,128)S(1)} %get-tuple-element.58.pay_ref), channel_id=1, source_target_pairs={{0,2},{2,0},{4,6},{6,4},{8,10},{10,8},{12,14},{14,12},{16,18},{18,... | collective-permute-start | bytes 98312 | tf_op jit(solution)/shard_map/ppermute | solution.py:628
  31.1 1.3 %collective-permute-done.12.refs_2_ = f32[2,32,128]{2,1,0:T(8,128)S(1)} collective-permute-done((f32[2,32,128]{2,1,0:T(8,128)S(1)}, f32[2,32,128]{2,1,0:T(8,128)S(1)}, u32[]{:S(2)}, u32[]{:S(2)}) %collective-permute-start.12) | collective-permute-done | bytes 32800 | tf_op jit(solution)/shard_map/ppermute | solution.py:628
  32.4 0.5 %collective-permute-done.11.refs_1_ = f32[2,32,128]{2,1,0:T(8,128)S(1)} collective-permute-done((f32[2,32,128]{2,1,0:T(8,128)S(1)}, f32[2,32,128]{2,1,0:T(8,128)S(1)}, u32[]{:S(2)}, u32[]{:S(2)}) %collective-permute-start.11) | collective-permute-done | bytes 32800 | tf_op jit(solution)/shard_map/ppermute | solution.py:628
  32.9 1.0 %collective-permute-done.10.refs_0_ = f32[2,32,128]{2,1,0:T(8,128)S(1)} collective-permute-done((f32[2,32,128]{2,1,0:T(8,128)S(1)}, f32[2,32,128]{2,1,0:T(8,128)S(1)}, u32[]{:S(2)}, u32[]{:S(2)}) %collective-permute-start.10) | collective-permute-done | bytes 32800 | tf_op jit(solution)/shard_map/ppermute | solution.py:628
  33.9 2.1 %collective-permute-start.13 = (f32[32,128]{1,0:T(8,128)S(1)}, f32[32,128]{1,0:T(8,128)S(1)}, u32[]{:S(2)}, u32[]{:S(2)}) collective-permute-start(f32[32,128]{1,0:T(8,128)S(1)} %get-tuple-element.62), channel_id=1, source_target_pairs={{0,24},{2,26},{4,28},{6,30},{8,16},{10,18},{12,20},{14,22},{16,8},... | collective-permute-start | bytes 49160 | tf_op jit(solution)/shard_map/ppermute | solution.py:627
  36.0 0.1 collective-permute-start.14
  36.0 2.3 %collective-permute-start.15 = (f32[32,128]{1,0:T(8,128)S(1)}, f32[32,128]{1,0:T(8,128)S(1)}, u32[]{:S(2)}, u32[]{:S(2)}) collective-permute-start(f32[32,128]{1,0:T(8,128)S(1)} %get-tuple-element.64), channel_id=1, source_target_pairs={{0,8},{2,10},{4,12},{6,14},{8,0},{10,2},{12,4},{14,6},{16,24},{18,... | collective-permute-start | bytes 49160 | tf_op jit(solution)/shard_map/ppermute | solution.py:627
  38.3 1.1 %collective-permute-done.13.refs_0_ = f32[32,128]{1,0:T(8,128)S(1)} collective-permute-done((f32[32,128]{1,0:T(8,128)S(1)}, f32[32,128]{1,0:T(8,128)S(1)}, u32[]{:S(2)}, u32[]{:S(2)}) %collective-permute-start.13) | collective-permute-done | bytes 16416 | tf_op jit(solution)/shard_map/ppermute | solution.py:627
  39.5 1.3 %collective-permute-done.14.refs_1_ = f32[32,128]{1,0:T(8,128)S(1)} collective-permute-done((f32[32,128]{1,0:T(8,128)S(1)}, f32[32,128]{1,0:T(8,128)S(1)}, u32[]{:S(2)}, u32[]{:S(2)}) %collective-permute-start.14) | collective-permute-done | bytes 16416 | tf_op jit(solution)/shard_map/ppermute | solution.py:627
  40.8 0.0 collective-permute-done.15.refs_2_
  40.8 0.7 %shard_map.83 = f32[16,2,8,128]{3,2,1,0:T(8,128)} custom-call(f32[2,32,128]{2,1,0:T(8,128)S(1)} %get-tuple-element.59.within_ref, f32[16,16,128]{2,1,0:T(8,128)S(1)} %get-tuple-element.60.f_ref, f32[16,16,128]{2,1,0:T(8,128)S(1)} %get-tuple-element.55.v_ref, f32[16,16,128]{2,1,0:T(8,128)S(1)} %get-tuple-element.56.u_ref, ...), custom_call_target="tpu_custom_call" | custom-call | bytes 1845000 | tf_op jit(solution)/shard_map/pallas_call | solution.py:599
  (4 shorter events, 0.1 us)
Async XLA Ops:
  1.0 6.7 %collective-permute-start.2 = (f32[136,128]{1,0:T(8,128)S(1)}, f32[136,128]{1,0:T(8,128)S(1)}, u32[]{:S(2)}, u32[]{:S(2)}) collective-permute-start(f32[136,128]{1,0:T(8,128)S(1)} %get-tuple-element.44), channel_id=1, source_target_pairs={{0,1},{1,0},{2,3},{3,2},{4,5},{5,4},{6,7},{7,6},{8,9},{9,8},{10,11... | collective-permute-start | bytes 208904 | tf_op jit(solution)/shard_map/ppermute | solution.py:613
  1.5 6.8 %collective-permute-start = (f32[40,128]{1,0:T(8,128)S(1)}, f32[40,128]{1,0:T(8,128)S(1)}, u32[]{:S(2)}, u32[]{:S(2)}) collective-permute-start(f32[40,128]{1,0:T(8,128)S(1)} %get-tuple-element.36), channel_id=1, source_target_pairs={{2,4},{3,5},{4,2},{5,3},{6,8},{7,9},{8,6},{9,7},{10,12},{11,13},{1... | collective-permute-start | bytes 61448 | tf_op jit(solution)/shard_map/ppermute | solution.py:637
  1.6 4.0 %copy-start.1 = (f32[16]{0:T(128)S(1)}, f32[16]{0:T(128)}, u32[]{:S(2)}) copy-start(f32[16]{0:T(128)} %param.10) | copy-start | bytes 196
  1.6 6.7 %collective-permute-start.1 = (f32[40,128]{1,0:T(8,128)S(1)}, f32[40,128]{1,0:T(8,128)S(1)}, u32[]{:S(2)}, u32[]{:S(2)}) collective-permute-start(f32[40,128]{1,0:T(8,128)S(1)} %get-tuple-element.37), channel_id=1, source_target_pairs={{0,2},{2,0},{4,6},{6,4},{8,10},{10,8},{12,14},{14,12},{16,18},{18,... | collective-permute-start | bytes 61448 | tf_op jit(solution)/shard_map/ppermute | solution.py:628
  5.6 1.1 %copy-start = (f32[16,16]{1,0:T(8,128)S(1)}, f32[16,16]{1,0:T(8,128)}, u32[]{:S(2)}) copy-start(f32[16,16]{1,0:T(8,128)} %proportions_ref.3) | copy-start | bytes 3076
  6.7 0.7 %copy-start.2 = (f32[16]{0:T(128)S(1)}, f32[16]{0:T(128)}, u32[]{:S(2)}) copy-start(f32[16]{0:T(128)} %param.11) | copy-start | bytes 196
  6.7 0.7 %copy-start.3 = (f32[16]{0:T(128)S(1)}, f32[16]{0:T(128)}, u32[]{:S(2)}) copy-start(f32[16]{0:T(128)} %param.12) | copy-start | bytes 196
  8.9 5.1 %collective-permute-start.5 = (f32[88,128]{1,0:T(8,128)S(1)}, f32[88,128]{1,0:T(8,128)S(1)}, u32[]{:S(2)}, u32[]{:S(2)}) collective-permute-start(f32[88,128]{1,0:T(8,128)S(1)} %get-tuple-element.48.pay_ref), channel_id=1, source_target_pairs={{0,6},{2,4},{4,2},{6,0},{8,14},{10,12},{12,10},{14,8},{16,22},{18,... | collective-permute-start | bytes 135176 | tf_op jit(solution)/shard_map/ppermute | solution.py:628
  11.3 4.0 %collective-permute-start.4 = (f32[88,128]{1,0:T(8,128)S(1)}, f32[88,128]{1,0:T(8,128)S(1)}, u32[]{:S(2)}, u32[]{:S(2)}) collective-permute-start(f32[88,128]{1,0:T(8,128)S(1)} %get-tuple-element.48.pay_ref), channel_id=1, source_target_pairs={{0,4},{2,6},{4,0},{6,2},{8,12},{10,14},{12,8},{14,10},{16,20},{18,... | collective-permute-start | bytes 135176 | tf_op jit(solution)/shard_map/ppermute | solution.py:628
  11.5 4.0 %collective-permute-start.3 = (f32[88,128]{1,0:T(8,128)S(1)}, f32[88,128]{1,0:T(8,128)S(1)}, u32[]{:S(2)}, u32[]{:S(2)}) collective-permute-start(f32[88,128]{1,0:T(8,128)S(1)} %get-tuple-element.48.pay_ref), channel_id=1, source_target_pairs={{0,2},{2,0},{4,6},{6,4},{8,10},{10,8},{12,14},{14,12},{16,18},{18,... | collective-permute-start | bytes 135176 | tf_op jit(solution)/shard_map/ppermute | solution.py:628
  15.7 6.5 %collective-permute-start.8 = (f32[136,128]{1,0:T(8,128)S(1)}, f32[136,128]{1,0:T(8,128)S(1)}, u32[]{:S(2)}, u32[]{:S(2)}) collective-permute-start(f32[136,128]{1,0:T(8,128)S(1)} %shard_map.78.own_group), channel_id=1, source_target_pairs={{0,24},{2,26},{4,28},{6,30},{8,16},{10,18},{12,20},{14,22},{16,8},... | collective-permute-start | bytes 208904 | tf_op jit(solution)/shard_map/ppermute | solution.py:628
  19.7 5.4 %collective-permute-start.7 = (f32[136,128]{1,0:T(8,128)S(1)}, f32[136,128]{1,0:T(8,128)S(1)}, u32[]{:S(2)}, u32[]{:S(2)}) collective-permute-start(f32[136,128]{1,0:T(8,128)S(1)} %shard_map.78.own_group), channel_id=1, source_target_pairs={{0,16},{2,18},{4,20},{6,22},{8,24},{10,26},{12,28},{14,30},{16,0},... | collective-permute-start | bytes 208904 | tf_op jit(solution)/shard_map/ppermute | solution.py:628
  19.7 5.4 %collective-permute-start.6 = (f32[136,128]{1,0:T(8,128)S(1)}, f32[136,128]{1,0:T(8,128)S(1)}, u32[]{:S(2)}, u32[]{:S(2)}) collective-permute-start(f32[136,128]{1,0:T(8,128)S(1)} %shard_map.78.own_group), channel_id=1, source_target_pairs={{0,8},{2,10},{4,12},{6,14},{8,0},{10,2},{12,4},{14,6},{16,24},{18,... | collective-permute-start | bytes 208904 | tf_op jit(solution)/shard_map/ppermute | solution.py:628
  25.7 1.3 %collective-permute-start.9 = (f32[128,128]{1,0:T(8,128)S(1)}, f32[128,128]{1,0:T(8,128)S(1)}, u32[]{:S(2)}, u32[]{:S(2)}) collective-permute-start(f32[128,128]{1,0:T(8,128)S(1)} %get-tuple-element.57), channel_id=1, source_target_pairs={{0,1},{1,0},{2,3},{3,2},{4,5},{5,4},{6,7},{7,6},{8,9},{9,8},{10,11... | collective-permute-start | bytes 196616 | tf_op jit(solution)/shard_map/ppermute | solution.py:613
  27.5 4.9 %collective-permute-start.12 = (f32[2,32,128]{2,1,0:T(8,128)S(1)}, f32[2,32,128]{2,1,0:T(8,128)S(1)}, u32[]{:S(2)}, u32[]{:S(2)}) collective-permute-start(f32[2,32,128]{2,1,0:T(8,128)S(1)} %get-tuple-element.58.pay_ref), channel_id=1, source_target_pairs={{0,6},{2,4},{4,2},{6,0},{8,14},{10,12},{12,10},{14,8},{16,22},{18,... | collective-permute-start | bytes 98312 | tf_op jit(solution)/shard_map/ppermute | solution.py:628
  29.0 3.9 %collective-permute-start.11 = (f32[2,32,128]{2,1,0:T(8,128)S(1)}, f32[2,32,128]{2,1,0:T(8,128)S(1)}, u32[]{:S(2)}, u32[]{:S(2)}) collective-permute-start(f32[2,32,128]{2,1,0:T(8,128)S(1)} %get-tuple-element.58.pay_ref), channel_id=1, source_target_pairs={{0,4},{2,6},{4,0},{6,2},{8,12},{10,14},{12,8},{14,10},{16,20},{18,... | collective-permute-start | bytes 98312 | tf_op jit(solution)/shard_map/ppermute | solution.py:628
  29.9 3.9 %collective-permute-start.10 = (f32[2,32,128]{2,1,0:T(8,128)S(1)}, f32[2,32,128]{2,1,0:T(8,128)S(1)}, u32[]{:S(2)}, u32[]{:S(2)}) collective-permute-start(f32[2,32,128]{2,1,0:T(8,128)S(1)} %get-tuple-element.58.pay_ref), channel_id=1, source_target_pairs={{0,2},{2,0},{4,6},{6,4},{8,10},{10,8},{12,14},{14,12},{16,18},{18,... | collective-permute-start | bytes 98312 | tf_op jit(solution)/shard_map/ppermute | solution.py:628
  33.9 5.6 %collective-permute-start.13 = (f32[32,128]{1,0:T(8,128)S(1)}, f32[32,128]{1,0:T(8,128)S(1)}, u32[]{:S(2)}, u32[]{:S(2)}) collective-permute-start(f32[32,128]{1,0:T(8,128)S(1)} %get-tuple-element.62), channel_id=1, source_target_pairs={{0,24},{2,26},{4,28},{6,30},{8,16},{10,18},{12,20},{14,22},{16,8},... | collective-permute-start | bytes 49160 | tf_op jit(solution)/shard_map/ppermute | solution.py:627
  36.0 4.8 %collective-permute-start.14 = (f32[32,128]{1,0:T(8,128)S(1)}, f32[32,128]{1,0:T(8,128)S(1)}, u32[]{:S(2)}, u32[]{:S(2)}) collective-permute-start(f32[32,128]{1,0:T(8,128)S(1)} %get-tuple-element.63), channel_id=1, source_target_pairs={{0,16},{2,18},{4,20},{6,22},{8,24},{10,26},{12,28},{14,30},{16,0},... | collective-permute-start | bytes 49160 | tf_op jit(solution)/shard_map/ppermute | solution.py:627
  36.0 4.7 %collective-permute-start.15 = (f32[32,128]{1,0:T(8,128)S(1)}, f32[32,128]{1,0:T(8,128)S(1)}, u32[]{:S(2)}, u32[]{:S(2)}) collective-permute-start(f32[32,128]{1,0:T(8,128)S(1)} %get-tuple-element.64), channel_id=1, source_target_pairs={{0,8},{2,10},{4,12},{6,14},{8,0},{10,2},{12,4},{14,6},{16,24},{18,... | collective-permute-start | bytes 49160 | tf_op jit(solution)/shard_map/ppermute | solution.py:627

commit v6 on v5

--- a/solution.py
+++ b/solution.py
@@ -359,7 +359,43 @@
     group_ref[z.group_top :, :] = order[z.members - 1, z.faces_at + z.tiles :, :]
 
 
-def both_ways(z, rates_ref, order, groups, v_ref, u_ref, ends_ref):
+def transfers(z, rates_ref, refs, blocks):
+    ohms = rates_ref[3]
+    zero, one = jnp.zeros(z.tile, F32), jnp.ones(z.tile, F32)
+
+    def block(j, state):
+        state = list(state)
+        start = z.faces_at + j * z.tiles
+        for i in range(z.nz):
+            for n, ref in enumerate(refs):
+                for y in range(z.ny):
+                    ohm = ohms * spread(ref, start + y * z.nz + i, z)
+                    at = 4 * (n * z.ny + y)
+                    state[at : at + 2] = advance(state[at : at + 2], ohm)
+                    state[at + 2 : at + 4] = advance(state[at + 2 : at + 4], ohm)
+        return tuple(state)
+
+    state = (one, zero, zero, one) * (z.ny * len(refs))
+    state = lax.fori_loop(0, blocks, block, state) if blocks > 1 else block(0, state)
+    return [state[4 * z.ny * n : 4 * z.ny * (n + 1)] for n in range(len(refs))]
+
+
+def inside_kernel(z, rates_ref, *refs):
+    *blocks, sums_ref, transfers_ref = refs
+    me = lax.axis_index("gz") % z.members
+    for i, matrix in enumerate(transfers(z, rates_ref, blocks, 1)):
+        sums_ref[me ^ i] = blocks[i][: 2 * z.lines, :]
+        for n, value in enumerate(matrix):
+            transfers_ref[me ^ i, n] = value
+
+
+def far_kernel(z, rates_ref, group_ref, out_ref):
+    (matrix,) = transfers(z, rates_ref, [group_ref], z.members)
+    for n, value in enumerate(matrix):
+        out_ref[n] = value
+
+
+def both_ways(z, rates_ref, own_ref, blocks, groups, top_ref, v_ref, u_ref, ends_ref, sums_ref):
     me = lax.axis_index("gz")
     group, member = me // z.members, me % z.members
     ohms = rates_ref[3]
@@ -369,155 +405,120 @@
     def ohm(ref, row):
         return ohms * spread(ref, row, z)
 
-    def totals(ref, y):
-        return ref[per_line(z, y), :], ref[per_line(z, z.ny + y), :]
-
-    def up_rows(ref, start, state):
-        state = list(state)
-        for i in range(z.nz):
-            for y in ys:
-                state[3 * y : 3 * y + 2] = advance(
-                    state[3 * y : 3 * y + 2], ohm(ref, start + y * z.nz + i)
-                )
-        return tuple(state)
-
-    def up_add(ref, state):
-        state = list(state)
+    def totals(sums, j, y):
+        return sums[j, per_line(z, y), :], sums[j, per_line(z, z.ny + y), :]
+
+    def up(refs, j, state):
+        sums, matrices = refs
+        out = []
         for y in ys:
-            s1, s2 = totals(ref, y)
-            state[3 * y + 2] = state[3 * y + 2] + (state[3 * y] * s1 + state[3 * y + 1] * s2)
-        return tuple(state)
-
-    def up_group(g, state):
-        ref = groups.at[g]
-        return lax.fori_loop(
-            0,
-            z.members,
-            lambda j, s: up_rows(ref, z.faces_at + j * z.tiles, s),
-            up_add(ref, state),
-        )
-
-    def up_block(j, state):
-        ref = order.at[j]
-        return up_rows(ref, z.faces_at, up_add(ref, state))
+            v, w, total = state[3 * y : 3 * y + 3]
+            s1, s2 = totals(sums, j, y)
+            pv, pw, qv, qw = (matrices[j, 4 * y + n] for n in range(4))
+            out += [pv * v + qv * w, pw * v + qw * w, total + (v * s1 + w * s2)]
+        return tuple(out)
+
+    def down(refs, j, state):
+        sums, matrices = refs
+        out = []
+        for y in ys:
+            u, w, total = state[3 * y : 3 * y + 3]
+            s1, s2 = totals(sums, j, y)
+            pv, pw, qv, qw = (matrices[j, 4 * y + n] for n in range(4))
+            u, w = qw * u + qv * w, pw * u + pv * w
+            out += [u, w, total + (u * s1 - w * s2)]
+        return tuple(out)
 
     state = (zero, one, zero) * z.ny
-    state = lax.fori_loop(0, group, up_group, state)
-    state = lax.fori_loop(0, member, up_block, state)
-    below, rising = [], []
-    mine = order.at[member]
+    state = lax.fori_loop(0, group, lambda j, s: up(groups, j, s), state)
+    state = lax.fori_loop(0, member, lambda j, s: up(blocks, j, s), state)
+    rising = []
     for y in ys:
         pair = state[3 * y : 3 * y + 2]
-        below.append(state[3 * y + 2])
+        sums_ref[y] = state[3 * y + 2]
         ends_ref[y] = pair[0]
         for i in range(z.nz):
-            pair = advance(pair, ohm(mine, z.faces_at + y * z.nz + i))
+            pair = advance(pair, ohm(own_ref, z.faces_at + y * z.nz + i))
             v_ref[y * z.nz + i] = pair[0]
             if i == 0:
                 rising.append(pair)
-        ends_ref[z.ny + y] = pair[0] + pair[1] * ohm(mine, z.faces_at + z.tiles + y)
-
-    def down_rows(ref, start, state):
-        state = list(state)
-        for i in reversed(range(z.nz)):
-            for y in ys:
-                _, u, w, total = state[4 * y : 4 * y + 4]
-                w = w + u
-                state[4 * y : 4 * y + 4] = [u, u + w * ohm(ref, start + y * z.nz + i), w, total]
-        return tuple(state)
-
-    def down_add(ref, state):
-        state = list(state)
-        for y in ys:
-            s1, s2 = totals(ref, y)
-            state[4 * y + 3] = state[4 * y + 3] + (state[4 * y + 1] * s1 - state[4 * y + 2] * s2)
-        return tuple(state)
-
-    def down_group(i, state):
-        ref = groups.at[z.groups_z - 1 - i]
-        state = lax.fori_loop(
-            0,
-            z.members,
-            lambda j, s: down_rows(ref, z.faces_at + (z.members - 1 - j) * z.tiles, s),
-            state,
-        )
-        return down_add(ref, state)
-
-    def down_block(i, state):
-        ref = order.at[z.members - 1 - i]
-        return down_add(ref, down_rows(ref, z.faces_at, state))
+        ends_ref[z.ny + y] = pair[0] + pair[1] * ohm(own_ref, z.faces_at + z.tiles + y)
 
     state = ()
     for y in ys:
-        state += (zero, ohm(groups.at[z.groups_z - 1], z.group_top + y), one, zero)
-    state = lax.fori_loop(0, z.groups_z - 1 - group, down_group, state)
-    state = lax.fori_loop(0, z.members - 1 - member, down_block, state)
-    above = []
+        state += (ohm(top_ref, y), one, zero)
+    last = z.groups_z - 1
+    state = lax.fori_loop(0, last - group, lambda i, s: down(groups, last - i, s), state)
+    last = z.members - 1
+    state = lax.fori_loop(0, last - member, lambda i, s: down(blocks, last - i, s), state)
     for y in ys:
-        last, u, w, total = state[4 * y : 4 * y + 4]
-        above.append(total)
-        ends_ref[3 * z.ny + y] = last
+        u, w, total = state[3 * y : 3 * y + 3]
+        sums_ref[z.ny + y] = total
+        ends_ref[3 * z.ny + y] = u - w * ohm(own_ref, z.faces_at + z.tiles + y)
         for i in reversed(range(z.nz)):
             u_ref[y * z.nz + i] = u
             if i == 0:
                 v, wv = rising[y]
                 ends_ref[4 * z.ny + y] = 1.0 / (wv * u + v * w)
             w = w + u
-            u = u + w * ohm(mine, z.faces_at + y * z.nz + i)
+            u = u + w * ohm(own_ref, z.faces_at + y * z.nz + i)
         ends_ref[2 * z.ny + y] = u
-    return below, above
-
-
-def solve_lines(z, sums, f_ref, v_ref, u_ref, ends_ref, store, finish=None):
-    halos = []
-    for y, (below, above) in enumerate(zip(*sums)):
-        scale = ends_ref[4 * z.ny + y]
-        tiles = range(y * z.nz, (y + 1) * z.nz)
-        after = {}
-        total = above
-        for t in reversed(tiles):
-            after[t] = total
-            total = total + u_ref[t] * f_ref[t]
-        low = scale * (ends_ref[2 * z.ny + y] * below + ends_ref[y] * total)
-        total = below
-        for t in tiles:
-            total = total + v_ref[t] * f_ref[t]
-            store(t, scale * (u_ref[t] * total + v_ref[t] * after[t]))
-        if finish:
-            finish(y)
-        high = scale * (ends_ref[3 * z.ny + y] * total + ends_ref[z.ny + y] * above)
-        halos.append((low, high))
-    return halos
-
-
-def hand_on(z, halos, tiles_ref, halo_ref, y_refs):
-    for y, (low, high) in enumerate(halos):
+
+
+def solve_row(z, y, sums, f_ref, v_ref, u_ref, ends_ref, store):
+    below, above = sums
+    scale = ends_ref[4 * z.ny + y]
+    after = [None] * z.nz
+    total = above
+    for i in reversed(range(z.nz)):
+        t = y * z.nz + i
+        after[i] = total
+        total = total + u_ref[t] * f_ref[t]
+    low = scale * (ends_ref[2 * z.ny + y] * below + ends_ref[y] * total)
+    total = below
+    for i in range(z.nz):
+        t = y * z.nz + i
+        total = total + v_ref[t] * f_ref[t]
+        store(i, scale * (u_ref[t] * total + v_ref[t] * after[i]))
+    high = scale * (ends_ref[3 * z.ny + y] * total + ends_ref[z.ny + y] * above)
+    return low, high
+
+
+def meet_kernel(z, rates_ref, f_ref, pay_ref, own_group, block_sums, block_transfers, far_transfer, *refs):
+    across, refs = refs[: z.groups_z - 1], refs[z.groups_z - 1 :]
+    v_ref, u_ref, ends_ref, sums_ref, *y_refs, group_sums, group_transfers, tops = refs
+    group = lax.axis_index("gz") // z.members
+    near = transfers(z, rates_ref, across[:-1], z.members)
+    for i, ref in enumerate((own_group, *across)):
+        group_sums[group ^ i] = ref[: 2 * z.lines, :]
+        tops[group ^ i] = ref[z.group_top :, :]
+    for i, matrix in enumerate(near):
+        for n, value in enumerate(matrix):
+            group_transfers[group ^ (i + 1), n] = value
+    group_transfers[group ^ len(across)] = far_transfer[...]
+    both_ways(
+        z, rates_ref, pay_ref, (block_sums, block_transfers), (group_sums, group_transfers),
+        tops.at[z.groups_z - 1], v_ref, u_ref, ends_ref, sums_ref,
+    )
+    for ref, y in zip(y_refs, y_picks(z)):
+
+        def store(i, value):
+            ref[i * z.species : (i + 1) * z.species, :] = value
+
+        solve_row(z, y, (sums_ref[y], sums_ref[z.ny + y]), f_ref, v_ref, u_ref, ends_ref, store)
+
+
+def rows_kernel(z, f_ref, v_ref, u_ref, ends_ref, sums_ref, tiles_ref, halo_ref):
+    for y in range(z.ny):
+
+        def store(i, value):
+            tiles_ref[y * z.nz + i] = value
+
+        low, high = solve_row(
+            z, y, (sums_ref[y], sums_ref[z.ny + y]), f_ref, v_ref, u_ref, ends_ref, store
+        )
         halo_ref[y] = low
         halo_ref[z.ny + y] = high
-    for ref, y in zip(y_refs, y_picks(z)):
-        for i in range(z.nz):
-            ref[i * z.species : (i + 1) * z.species, :] = tiles_ref[y * z.nz + i]
-
-
-def meet_kernel(z, rates_ref, f_ref, pay_ref, own_group, *refs):
-    inside, across = refs[: z.members - 1], refs[z.members - 1 : z.members + z.groups_z - 2]
-    refs = refs[z.members + z.groups_z - 2 :]
-    tiles_ref, halo_ref, v_ref, u_ref, ends_ref, *y_refs, order, groups = refs
-    me = lax.axis_index("gz")
-    group, member = me // z.members, me % z.members
-    order[member] = pay_ref[...]
-    for i, ref in enumerate(inside):
-        order[member ^ (i + 1)] = ref[...]
-    groups[group] = own_group[...]
-    for i, ref in enumerate(across):
-        groups[group ^ (i + 1)] = ref[...]
-    sums = both_ways(z, rates_ref, order, groups, v_ref, u_ref, ends_ref)
-
-    def store(t, value):
-        tiles_ref[t] = value
-
-    halos = solve_lines(z, sums, f_ref, v_ref, u_ref, ends_ref, store)
-    hand_on(z, halos, tiles_ref, halo_ref, y_refs)
 
 
 def halo_rows(z):
@@ -571,19 +572,17 @@
         value = ref[...]
         below = below + jnp.where(lower, value, 0.0)
         above = above + jnp.where(lower, 0.0, value)
-    sums = [[v[per_line(z, y)] for y in range(z.ny)] for v in (below, above)]
-
-    def store(t, value):
-        rows_ref[pl.ds(t, z.species, stride=z.tiles), :] = value
-
     blocks = rows_ref.reshape(z.species, z.ny, z.nz, z.nx)
     copies = []
-
-    def send(y):
+    for y in range(z.ny):
+
+        def store(i, value):
+            rows_ref[pl.ds(y * z.nz + i, z.species, stride=z.tiles), :] = value
+
+        sums = below[per_line(z, y)], above[per_line(z, y)]
+        solve_row(z, y, sums, f_ref, v_ref, u_ref, ends_ref, store)
         copies.append(pltpu.make_async_copy(blocks.at[:, y], out_hbm.at[:, y], sems.at[y]))
         copies[-1].start()
-
-    solve_lines(z, sums, f_ref, v_ref, u_ref, ends_ref, store, send)
     for copy in copies:
         copy.wait()
 
@@ -679,18 +678,27 @@
         [pltpu.VMEM((z.members, z.block_rows, z.nx), F32)],
     )
     across = exchange(group, z.groups_z, z.members)
-    tiles, halo, v, u, ends, *sends = call(
+    matrices = shaped(4 * z.ny, *z.tile)
+    block_sums, block_transfers = call(
+        inside_kernel,
+        [shaped(z.members, 2 * z.lines, z.nx), shaped(z.members, *matrices.shape)],
+        [rates, pay, *inside],
+    )
+    far_transfer = call(far_kernel, matrices, [rates, across[-1]])
+    v, u, ends, sums, *sends = call(
         meet_kernel,
-        [block, shaped(2 * z.ny, *z.tile), block, block, ends_shape]
+        [block, block, ends_shape, shaped(2 * z.ny, *z.tile)]
         + [shaped(z.nz * z.species, z.nx)] * halos,
-        [rates, f, pay, group, *inside, *across],
+        [rates, f, pay, group, block_sums, block_transfers, far_transfer, *across],
         [
-            pltpu.VMEM((z.members, z.block_rows, z.nx), F32),
-            pltpu.VMEM((z.groups_z, z.group_rows, z.nx), F32),
+            pltpu.VMEM((z.groups_z, 2 * z.lines, z.nx), F32),
+            pltpu.VMEM((z.groups_z, *matrices.shape), F32),
+            pltpu.VMEM((z.groups_z, z.group_rows - z.group_top, z.nx), F32),
         ],
     )
 
     received = swap(sends)
+    tiles, halo = call(rows_kernel, [block, shaped(2 * z.ny, *z.tile)], [f, v, u, ends, sums])
     base, f = call(
         inner_kernel,
         [block, block],

time: 41.7 us -> 41.6 us (level)
    pallas_call x11 -> x14, Pallas kernels: 5.51 us -> 5.7 us  [call(): pl.pallas_call(functools.partial(kernel, z), out_shape=outs, in_specs=[sp...]
  transfers between devices with their start and end apart: 16 -> 16, of which waited for: 11 -> 11; matrix products, arithmetic and copies ran while one was open for 0% -> 0% of each run, Pallas kernels for 7% -> 8%
where the time goes in v6:
time: 41.6 us; the launch traced here: 41.4 us
  starting transfers between devices  20.8 us (50%)
  waiting for transfers between devices  13.2 us (32%)
  Pallas kernels  5.7 us (14%)
  other arithmetic  0.95 us (2%)
  local copies, waits for them, and re-layouts  0.66 us (2%)
    ppermute x10, starting transfers between devices, exchange(): return [lax.ppermute(v, 'gz', p) for v, p in zip(values, pairs)]  15.7 us
    ppermute x10, waiting for transfers between devices, exchange(): return [lax.ppermute(v, 'gz', p) for v, p in zip(values, pairs)]  10.4 us
    pallas_call x14, Pallas kernels, call(): pl.pallas_call(functools.partial(kernel, z), out_shape=outs, in_specs=[sp...  5.7 us
    ppermute x3, starting transfers between devices, exchange(): lax.ppermute(v, 'gz', p)  4.45 us
    ppermute x3, waiting for transfers between devices, exchange(): lax.ppermute(v, 'gz', p)  2.44 us
    concatenate x1, other arithmetic, per_device(): arguments = jnp.concatenate([v.reshape(-1, z.nx) for v in (c, k, warm)])  0.95 us
  transfers between devices with their start and end apart: 16, of which 11 were waited for; matrix products, arithmetic and copies ran while one was open for 0% of the time, Pallas kernels for 8%

profile of v6, /device:TPU:0, one launch (start us, length us, event | category | flops | bytes accessed | tf_op | source)
XLA Modules:
  0.0 41.4 jit_solution(3411171235127441784)
XLA Ops:
  0.0 0.9 %pad_maximum_fusion.c_ref.arguments = f32[288,128]{1,0:T(8,128)S(1)} fusion(f32[16,128]{1,0:T(8,128)} %bitcast.10, f32[16,128]{1,0:T(8,128)} %bitcast.11, f32[256,128]{1,0:T(8,128)} %bitcast.9), kind=kLoop, calls=%fused_computation | loop fusion | flops 73728 | bytes 294912 | tf_op jit(solution)/shard_map/concatenate | solution.py:617
  1.0 0.5 %collective-permute-start.2 = (f32[136,128]{1,0:T(8,128)S(1)}, f32[136,128]{1,0:T(8,128)S(1)}, u32[]{:S(2)}, u32[]{:S(2)}) collective-permute-start(f32[136,128]{1,0:T(8,128)S(1)} %get-tuple-element.47), channel_id=1, source_target_pairs={{0,1},{1,0},{2,3},{3,2},{4,5},{5,4},{6,7},{7,6},{8,9},{9,8},{10,11... | collective-permute-start | bytes 208904 | tf_op jit(solution)/shard_map/ppermute | solution.py:612
  1.5 0.1 collective-permute-start
  1.6 4.0 %collective-permute-start.1 = (f32[40,128]{1,0:T(8,128)S(1)}, f32[40,128]{1,0:T(8,128)S(1)}, u32[]{:S(2)}, u32[]{:S(2)}) collective-permute-start(f32[40,128]{1,0:T(8,128)S(1)} %get-tuple-element.39), channel_id=1, source_target_pairs={{0,2},{2,0},{4,6},{6,4},{8,10},{10,8},{12,14},{14,12},{16,18},{18,... | collective-permute-start | bytes 61448 | tf_op jit(solution)/shard_map/ppermute | solution.py:627
  5.6 1.1 %shard_map.74 = (f32[4,16,128]{2,1,0:T(8,128)S(1)}, f32[2,16,128]{2,1,0:T(8,128)S(1)}, f32[7,16,16,128]{3,2,1,0:T(8,128)S(1)}, f32[7,16,16,128]{3,2,1,0:T(8,128)S(1)}, f32[16,16,128]{2,1,0:T(8,128)S(1)}) custom-call(f32[288,128]{1,0:T(8,128)S(1)} %pad_maximum_fusion.c_ref.arguments, f32[1,16]{1,0:T(1,128)S(1)} %bitcast.6), custom_call_target="tpu_custom_call" | custom-call | bytes 3690000 | tf_op jit(solution)/shard_map/pallas_call | solution.py:598
  6.7 0.0 copy-start.2
  6.7 0.0 copy-start.3
  6.7 0.6 %copy-done.2 = f32[16]{0:T(128)S(1)} copy-done((f32[16]{0:T(128)S(1)}, f32[16]{0:T(128)}, u32[]{:S(2)}) %copy-start.2) | copy-done | bytes 88
  7.3 0.0 copy-done.3
  7.3 0.4 shard_map.75
  7.7 0.6 %shard_map.76 = (f32[16,16,128]{2,1,0:T(8,128)S(1)}, f32[2,16,128]{2,1,0:T(8,128)S(1)}) custom-call(f32[288,128]{1,0:T(8,128)S(1)} %pad_maximum_fusion.c_ref.arguments, f32[16,16,128]{2,1,0:T(8,128)S(1)} %get-tuple-element.42.tiles_ref, f32[16,16,128]{2,1,0:T(8,128)S(1)} %get-tuple-element.43.base_ref, f32[4,16,128]{2,1,0:T(8,128)S(1)} %get-tuple-element.40.rates_ref, ...), custom_call_target="tpu_custom_call" | custom-call | bytes 1845000 | tf_op jit(solution)/shard_map/pallas_call | solution.py:598
  8.3 0.0 collective-permute-done.far_ref
  8.3 0.0 collective-permute-done.1.near_ref
  8.3 0.6 %shard_map.77 = (f32[88,128]{1,0:T(8,128)S(1)}, f32[16,16,128]{2,1,0:T(8,128)S(1)}, f32[2,16,128]{2,1,0:T(8,128)S(1)}) custom-call(f32[288,128]{1,0:T(8,128)S(1)} %pad_maximum_fusion.c_ref.arguments, f32[40,128]{1,0:T(8,128)S(1)} %collective-permute-done.far_ref, f32[40,128]{1,0:T(8,128)S(1)} %collective-permute-done.1.near_ref, ...), custom_call_target="tpu_custom_call" | custom-call | bytes 1845000 | tf_op jit(solution)/shard_map/pallas_call | solution.py:598
  8.9 2.4 %collective-permute-start.5 = (f32[88,128]{1,0:T(8,128)S(1)}, f32[88,128]{1,0:T(8,128)S(1)}, u32[]{:S(2)}, u32[]{:S(2)}) collective-permute-start(f32[88,128]{1,0:T(8,128)S(1)} %get-tuple-element.51.pay_ref.refs_0_), channel_id=1, source_target_pairs={{0,6},{2,4},{4,2},{6,0},{8,14},{10,12},{12,10},{14,8},{16,22},{18,... | collective-permute-start | bytes 135176 | tf_op jit(solution)/shard_map/ppermute | solution.py:627
  11.3 0.3 collective-permute-start.4
  11.5 0.9 %collective-permute-start.3 = (f32[88,128]{1,0:T(8,128)S(1)}, f32[88,128]{1,0:T(8,128)S(1)}, u32[]{:S(2)}, u32[]{:S(2)}) collective-permute-start(f32[88,128]{1,0:T(8,128)S(1)} %get-tuple-element.51.pay_ref.refs_0_), channel_id=1, source_target_pairs={{0,2},{2,0},{4,6},{6,4},{8,10},{10,8},{12,14},{14,12},{16,18},{18,... | collective-permute-start | bytes 135176 | tf_op jit(solution)/shard_map/ppermute | solution.py:627
  12.4 1.6 %collective-permute-done.5.refs_2_.refs_3_ = f32[88,128]{1,0:T(8,128)S(1)} collective-permute-done((f32[88,128]{1,0:T(8,128)S(1)}, f32[88,128]{1,0:T(8,128)S(1)}, u32[]{:S(2)}, u32[]{:S(2)}) %collective-permute-start.5) | collective-permute-done | bytes 45088 | tf_op jit(solution)/shard_map/ppermute | solution.py:627
  14.0 1.3 %collective-permute-done.4.refs_1_.refs_2_ = f32[88,128]{1,0:T(8,128)S(1)} collective-permute-done((f32[88,128]{1,0:T(8,128)S(1)}, f32[88,128]{1,0:T(8,128)S(1)}, u32[]{:S(2)}, u32[]{:S(2)}) %collective-permute-start.4) | collective-permute-done | bytes 45088 | tf_op jit(solution)/shard_map/ppermute | solution.py:627
  15.3 0.3 collective-permute-done.3.refs_0_.refs_1_
  15.6 0.1 shard_map.78.own_group
  15.7 3.9 %collective-permute-start.6 = (f32[136,128]{1,0:T(8,128)S(1)}, f32[136,128]{1,0:T(8,128)S(1)}, u32[]{:S(2)}, u32[]{:S(2)}) collective-permute-start(f32[136,128]{1,0:T(8,128)S(1)} %shard_map.78.own_group), channel_id=1, source_target_pairs={{0,24},{2,26},{4,28},{6,30},{8,16},{10,18},{12,20},{14,22},{16,8},... | collective-permute-start | bytes 208904 | tf_op jit(solution)/shard_map/ppermute | solution.py:627
  19.7 0.0 collective-permute-start.8
  19.7 0.6 %collective-permute-start.7 = (f32[136,128]{1,0:T(8,128)S(1)}, f32[136,128]{1,0:T(8,128)S(1)}, u32[]{:S(2)}, u32[]{:S(2)}) collective-permute-start(f32[136,128]{1,0:T(8,128)S(1)} %shard_map.78.own_group), channel_id=1, source_target_pairs={{0,8},{2,10},{4,12},{6,14},{8,0},{10,2},{12,4},{14,6},{16,24},{18,... | collective-permute-start | bytes 208904 | tf_op jit(solution)/shard_map/ppermute | solution.py:627
  20.3 0.1 shard_map.79
  20.4 1.7 %collective-permute-done.6.group_ref.refs_2_ = f32[136,128]{1,0:T(8,128)S(1)} collective-permute-done((f32[136,128]{1,0:T(8,128)S(1)}, f32[136,128]{1,0:T(8,128)S(1)}, u32[]{:S(2)}, u32[]{:S(2)}) %collective-permute-start.6) | collective-permute-done | bytes 69664 | tf_op jit(solution)/shard_map/ppermute | solution.py:627
  22.2 0.1 shard_map.80.far_transfer
  22.3 2.7 %collective-permute-done.8.refs_1_ = f32[136,128]{1,0:T(8,128)S(1)} collective-permute-done((f32[136,128]{1,0:T(8,128)S(1)}, f32[136,128]{1,0:T(8,128)S(1)}, u32[]{:S(2)}, u32[]{:S(2)}) %collective-permute-start.8) | collective-permute-done | bytes 69664 | tf_op jit(solution)/shard_map/ppermute | solution.py:627
  25.0 0.0 collective-permute-done.7.refs_0_
  25.0 0.5 %shard_map.81 = (f32[16,16,128]{2,1,0:T(8,128)S(1)}, f32[16,16,128]{2,1,0:T(8,128)S(1)}, f32[10,16,128]{2,1,0:T(8,128)S(1)}, f32[4,16,128]{2,1,0:T(8,128)S(1)}, f32[128,128]{1,0:T(8,128)S(1)}) custom-call(f32[4,16,128]{2,1,0:T(8,128)S(1)} %get-tuple-element.40.rates_ref, f32[16,16,128]{2,1,0:T(8,128)S(1)} %get-tuple-element.50.f_ref, ...), custom_call_target="tpu_custom_call" | custom-call | bytes 1845000 | tf_op jit(solution)/shard_map/pallas_call | solution.py:598
  25.5 0.1 collective-permute-start.9
  25.6 0.1 shard_map.82
  25.7 0.8 %shard_map.83 = (f32[16,16,128]{2,1,0:T(8,128)S(1)}, f32[16,16,128]{2,1,0:T(8,128)S(1)}) custom-call(f32[16,16,128]{2,1,0:T(8,128)S(1)} %get-tuple-element.58.tiles_ref, f32[4,16,128]{2,1,0:T(8,128)S(1)} %get-tuple-element.59.halo_ref, f32[4,16,128]{2,1,0:T(8,128)S(1)} %get-tuple-element.40.rates_ref, f32[2,16,128]{2,1,0:T(8,128)S(1)} %get-tuple-element.41.faces.x_faces, ...), custom_call_target="tpu_custom_call" | custom-call | bytes 1845000 | tf_op jit(solution)/shard_map/pallas_call | solution.py:598
  26.5 0.4 collective-permute-done.9.refs_0_
  26.8 0.6 %shard_map.84 = (f32[2,32,128]{2,1,0:T(8,128)S(1)}, f32[16,16,128]{2,1,0:T(8,128)S(1)}) custom-call(f32[16,16,128]{2,1,0:T(8,128)S(1)} %get-tuple-element.58.tiles_ref, f32[4,16,128]{2,1,0:T(8,128)S(1)} %get-tuple-element.59.halo_ref, f32[4,16,128]{2,1,0:T(8,128)S(1)} %get-tuple-element.40.rates_ref, f32[2,16,128]{2,1,0:T(8,128)S(1)} %get-tuple-element.49.y_faces, ...), custom_call_target="tpu_custom_call" | custom-call | bytes 1845000 | tf_op jit(solution)/shard_map/pallas_call | solution.py:598
  27.4 1.4 %collective-permute-start.12 = (f32[2,32,128]{2,1,0:T(8,128)S(1)}, f32[2,32,128]{2,1,0:T(8,128)S(1)}, u32[]{:S(2)}, u32[]{:S(2)}) collective-permute-start(f32[2,32,128]{2,1,0:T(8,128)S(1)} %get-tuple-element.65.pay_ref), channel_id=1, source_target_pairs={{0,6},{2,4},{4,2},{6,0},{8,14},{10,12},{12,10},{14,8},{16,22},{18,... | collective-permute-start | bytes 98312 | tf_op jit(solution)/shard_map/ppermute | solution.py:627
  28.8 1.0 %collective-permute-start.11 = (f32[2,32,128]{2,1,0:T(8,128)S(1)}, f32[2,32,128]{2,1,0:T(8,128)S(1)}, u32[]{:S(2)}, u32[]{:S(2)}) collective-permute-start(f32[2,32,128]{2,1,0:T(8,128)S(1)} %get-tuple-element.65.pay_ref), channel_id=1, source_target_pairs={{0,4},{2,6},{4,0},{6,2},{8,12},{10,14},{12,8},{14,10},{16,20},{18,... | collective-permute-start | bytes 98312 | tf_op jit(solution)/shard_map/ppermute | solution.py:627
  29.8 1.2 %collective-permute-start.10 = (f32[2,32,128]{2,1,0:T(8,128)S(1)}, f32[2,32,128]{2,1,0:T(8,128)S(1)}, u32[]{:S(2)}, u32[]{:S(2)}) collective-permute-start(f32[2,32,128]{2,1,0:T(8,128)S(1)} %get-tuple-element.65.pay_ref), channel_id=1, source_target_pairs={{0,2},{2,0},{4,6},{6,4},{8,10},{10,8},{12,14},{14,12},{16,18},{18,... | collective-permute-start | bytes 98312 | tf_op jit(solution)/shard_map/ppermute | solution.py:627
  31.0 1.3 %collective-permute-done.12.refs_2_ = f32[2,32,128]{2,1,0:T(8,128)S(1)} collective-permute-done((f32[2,32,128]{2,1,0:T(8,128)S(1)}, f32[2,32,128]{2,1,0:T(8,128)S(1)}, u32[]{:S(2)}, u32[]{:S(2)}) %collective-permute-start.12) | collective-permute-done | bytes 32800 | tf_op jit(solution)/shard_map/ppermute | solution.py:627
  32.3 0.5 %collective-permute-done.11.refs_1_ = f32[2,32,128]{2,1,0:T(8,128)S(1)} collective-permute-done((f32[2,32,128]{2,1,0:T(8,128)S(1)}, f32[2,32,128]{2,1,0:T(8,128)S(1)}, u32[]{:S(2)}, u32[]{:S(2)}) %collective-permute-start.11) | collective-permute-done | bytes 32800 | tf_op jit(solution)/shard_map/ppermute | solution.py:627
  32.8 1.0 %collective-permute-done.10.refs_0_ = f32[2,32,128]{2,1,0:T(8,128)S(1)} collective-permute-done((f32[2,32,128]{2,1,0:T(8,128)S(1)}, f32[2,32,128]{2,1,0:T(8,128)S(1)}, u32[]{:S(2)}, u32[]{:S(2)}) %collective-permute-start.10) | collective-permute-done | bytes 32800 | tf_op jit(solution)/shard_map/ppermute | solution.py:627
  33.8 2.1 %collective-permute-start.13 = (f32[32,128]{1,0:T(8,128)S(1)}, f32[32,128]{1,0:T(8,128)S(1)}, u32[]{:S(2)}, u32[]{:S(2)}) collective-permute-start(f32[32,128]{1,0:T(8,128)S(1)} %get-tuple-element.68), channel_id=1, source_target_pairs={{0,24},{2,26},{4,28},{6,30},{8,16},{10,18},{12,20},{14,22},{16,8},... | collective-permute-start | bytes 49160 | tf_op jit(solution)/shard_map/ppermute | solution.py:626
  35.8 0.1 collective-permute-start.14
  35.9 2.3 %collective-permute-start.15 = (f32[32,128]{1,0:T(8,128)S(1)}, f32[32,128]{1,0:T(8,128)S(1)}, u32[]{:S(2)}, u32[]{:S(2)}) collective-permute-start(f32[32,128]{1,0:T(8,128)S(1)} %get-tuple-element.70), channel_id=1, source_target_pairs={{0,8},{2,10},{4,12},{6,14},{8,0},{10,2},{12,4},{14,6},{16,24},{18,... | collective-permute-start | bytes 49160 | tf_op jit(solution)/shard_map/ppermute | solution.py:626
  38.2 1.1 %collective-permute-done.13.refs_0_ = f32[32,128]{1,0:T(8,128)S(1)} collective-permute-done((f32[32,128]{1,0:T(8,128)S(1)}, f32[32,128]{1,0:T(8,128)S(1)}, u32[]{:S(2)}, u32[]{:S(2)}) %collective-permute-start.13) | collective-permute-done | bytes 16416 | tf_op jit(solution)/shard_map/ppermute | solution.py:626
  39.4 1.3 %collective-permute-done.14.refs_1_ = f32[32,128]{1,0:T(8,128)S(1)} collective-permute-done((f32[32,128]{1,0:T(8,128)S(1)}, f32[32,128]{1,0:T(8,128)S(1)}, u32[]{:S(2)}, u32[]{:S(2)}) %collective-permute-start.14) | collective-permute-done | bytes 16416 | tf_op jit(solution)/shard_map/ppermute | solution.py:626
  40.6 0.0 collective-permute-done.15.refs_2_
  40.6 0.7 %shard_map.86 = f32[16,2,8,128]{3,2,1,0:T(8,128)} custom-call(f32[2,32,128]{2,1,0:T(8,128)S(1)} %get-tuple-element.66.within_ref, f32[16,16,128]{2,1,0:T(8,128)S(1)} %get-tuple-element.67.f_ref, f32[16,16,128]{2,1,0:T(8,128)S(1)} %get-tuple-element.54.v_ref, f32[16,16,128]{2,1,0:T(8,128)S(1)} %get-tuple-element.55.u_ref, ...), custom_call_target="tpu_custom_call" | custom-call | bytes 1845000 | tf_op jit(solution)/shard_map/pallas_call | solution.py:598
  (7 shorter events, 0.1 us)
Async XLA Ops:
  1.0 6.7 %collective-permute-start.2 = (f32[136,128]{1,0:T(8,128)S(1)}, f32[136,128]{1,0:T(8,128)S(1)}, u32[]{:S(2)}, u32[]{:S(2)}) collective-permute-start(f32[136,128]{1,0:T(8,128)S(1)} %get-tuple-element.47), channel_id=1, source_target_pairs={{0,1},{1,0},{2,3},{3,2},{4,5},{5,4},{6,7},{7,6},{8,9},{9,8},{10,11... | collective-permute-start | bytes 208904 | tf_op jit(solution)/shard_map/ppermute | solution.py:612
  1.5 6.8 %collective-permute-start = (f32[40,128]{1,0:T(8,128)S(1)}, f32[40,128]{1,0:T(8,128)S(1)}, u32[]{:S(2)}, u32[]{:S(2)}) collective-permute-start(f32[40,128]{1,0:T(8,128)S(1)} %get-tuple-element.38), channel_id=1, source_target_pairs={{2,4},{3,5},{4,2},{5,3},{6,8},{7,9},{8,6},{9,7},{10,12},{11,13},{1... | collective-permute-start | bytes 61448 | tf_op jit(solution)/shard_map/ppermute | solution.py:636
  1.6 4.0 %copy-start.1 = (f32[16]{0:T(128)S(1)}, f32[16]{0:T(128)}, u32[]{:S(2)}) copy-start(f32[16]{0:T(128)} %param.10) | copy-start | bytes 196
  1.6 6.7 %collective-permute-start.1 = (f32[40,128]{1,0:T(8,128)S(1)}, f32[40,128]{1,0:T(8,128)S(1)}, u32[]{:S(2)}, u32[]{:S(2)}) collective-permute-start(f32[40,128]{1,0:T(8,128)S(1)} %get-tuple-element.39), channel_id=1, source_target_pairs={{0,2},{2,0},{4,6},{6,4},{8,10},{10,8},{12,14},{14,12},{16,18},{18,... | collective-permute-start | bytes 61448 | tf_op jit(solution)/shard_map/ppermute | solution.py:627
  5.6 1.1 %copy-start = (f32[16,16]{1,0:T(8,128)S(1)}, f32[16,16]{1,0:T(8,128)}, u32[]{:S(2)}) copy-start(f32[16,16]{1,0:T(8,128)} %proportions_ref.3) | copy-start | bytes 3076
  6.7 0.7 %copy-start.2 = (f32[16]{0:T(128)S(1)}, f32[16]{0:T(128)}, u32[]{:S(2)}) copy-start(f32[16]{0:T(128)} %param.11) | copy-start | bytes 196
  6.7 0.7 %copy-start.3 = (f32[16]{0:T(128)S(1)}, f32[16]{0:T(128)}, u32[]{:S(2)}) copy-start(f32[16]{0:T(128)} %param.12) | copy-start | bytes 196
  8.9 5.1 %collective-permute-start.5 = (f32[88,128]{1,0:T(8,128)S(1)}, f32[88,128]{1,0:T(8,128)S(1)}, u32[]{:S(2)}, u32[]{:S(2)}) collective-permute-start(f32[88,128]{1,0:T(8,128)S(1)} %get-tuple-element.51.pay_ref.refs_0_), channel_id=1, source_target_pairs={{0,6},{2,4},{4,2},{6,0},{8,14},{10,12},{12,10},{14,8},{16,22},{18,... | collective-permute-start | bytes 135176 | tf_op jit(solution)/shard_map/ppermute | solution.py:627
  11.3 4.0 %collective-permute-start.4 = (f32[88,128]{1,0:T(8,128)S(1)}, f32[88,128]{1,0:T(8,128)S(1)}, u32[]{:S(2)}, u32[]{:S(2)}) collective-permute-start(f32[88,128]{1,0:T(8,128)S(1)} %get-tuple-element.51.pay_ref.refs_0_), channel_id=1, source_target_pairs={{0,4},{2,6},{4,0},{6,2},{8,12},{10,14},{12,8},{14,10},{16,20},{18,... | collective-permute-start | bytes 135176 | tf_op jit(solution)/shard_map/ppermute | solution.py:627
  11.5 4.0 %collective-permute-start.3 = (f32[88,128]{1,0:T(8,128)S(1)}, f32[88,128]{1,0:T(8,128)S(1)}, u32[]{:S(2)}, u32[]{:S(2)}) collective-permute-start(f32[88,128]{1,0:T(8,128)S(1)} %get-tuple-element.51.pay_ref.refs_0_), channel_id=1, source_target_pairs={{0,2},{2,0},{4,6},{6,4},{8,10},{10,8},{12,14},{14,12},{16,18},{18,... | collective-permute-start | bytes 135176 | tf_op jit(solution)/shard_map/ppermute | solution.py:627
  15.7 6.4 %collective-permute-start.6 = (f32[136,128]{1,0:T(8,128)S(1)}, f32[136,128]{1,0:T(8,128)S(1)}, u32[]{:S(2)}, u32[]{:S(2)}) collective-permute-start(f32[136,128]{1,0:T(8,128)S(1)} %shard_map.78.own_group), channel_id=1, source_target_pairs={{0,24},{2,26},{4,28},{6,30},{8,16},{10,18},{12,20},{14,22},{16,8},... | collective-permute-start | bytes 208904 | tf_op jit(solution)/shard_map/ppermute | solution.py:627
  19.7 5.4 %collective-permute-start.8 = (f32[136,128]{1,0:T(8,128)S(1)}, f32[136,128]{1,0:T(8,128)S(1)}, u32[]{:S(2)}, u32[]{:S(2)}) collective-permute-start(f32[136,128]{1,0:T(8,128)S(1)} %shard_map.78.own_group), channel_id=1, source_target_pairs={{0,16},{2,18},{4,20},{6,22},{8,24},{10,26},{12,28},{14,30},{16,0},... | collective-permute-start | bytes 208904 | tf_op jit(solution)/shard_map/ppermute | solution.py:627
  19.7 5.4 %collective-permute-start.7 = (f32[136,128]{1,0:T(8,128)S(1)}, f32[136,128]{1,0:T(8,128)S(1)}, u32[]{:S(2)}, u32[]{:S(2)}) collective-permute-start(f32[136,128]{1,0:T(8,128)S(1)} %shard_map.78.own_group), channel_id=1, source_target_pairs={{0,8},{2,10},{4,12},{6,14},{8,0},{10,2},{12,4},{14,6},{16,24},{18,... | collective-permute-start | bytes 208904 | tf_op jit(solution)/shard_map/ppermute | solution.py:627
  25.5 1.3 %collective-permute-start.9 = (f32[128,128]{1,0:T(8,128)S(1)}, f32[128,128]{1,0:T(8,128)S(1)}, u32[]{:S(2)}, u32[]{:S(2)}) collective-permute-start(f32[128,128]{1,0:T(8,128)S(1)} %get-tuple-element.64), channel_id=1, source_target_pairs={{0,1},{1,0},{2,3},{3,2},{4,5},{5,4},{6,7},{7,6},{8,9},{9,8},{10,11... | collective-permute-start | bytes 196616 | tf_op jit(solution)/shard_map/ppermute | solution.py:612
  27.4 4.9 %collective-permute-start.12 = (f32[2,32,128]{2,1,0:T(8,128)S(1)}, f32[2,32,128]{2,1,0:T(8,128)S(1)}, u32[]{:S(2)}, u32[]{:S(2)}) collective-permute-start(f32[2,32,128]{2,1,0:T(8,128)S(1)} %get-tuple-element.65.pay_ref), channel_id=1, source_target_pairs={{0,6},{2,4},{4,2},{6,0},{8,14},{10,12},{12,10},{14,8},{16,22},{18,... | collective-permute-start | bytes 98312 | tf_op jit(solution)/shard_map/ppermute | solution.py:627
  28.8 3.9 %collective-permute-start.11 = (f32[2,32,128]{2,1,0:T(8,128)S(1)}, f32[2,32,128]{2,1,0:T(8,128)S(1)}, u32[]{:S(2)}, u32[]{:S(2)}) collective-permute-start(f32[2,32,128]{2,1,0:T(8,128)S(1)} %get-tuple-element.65.pay_ref), channel_id=1, source_target_pairs={{0,4},{2,6},{4,0},{6,2},{8,12},{10,14},{12,8},{14,10},{16,20},{18,... | collective-permute-start | bytes 98312 | tf_op jit(solution)/shard_map/ppermute | solution.py:627
  29.8 3.9 %collective-permute-start.10 = (f32[2,32,128]{2,1,0:T(8,128)S(1)}, f32[2,32,128]{2,1,0:T(8,128)S(1)}, u32[]{:S(2)}, u32[]{:S(2)}) collective-permute-start(f32[2,32,128]{2,1,0:T(8,128)S(1)} %get-tuple-element.65.pay_ref), channel_id=1, source_target_pairs={{0,2},{2,0},{4,6},{6,4},{8,10},{10,8},{12,14},{14,12},{16,18},{18,... | collective-permute-start | bytes 98312 | tf_op jit(solution)/shard_map/ppermute | solution.py:627
  33.8 5.6 %collective-permute-start.13 = (f32[32,128]{1,0:T(8,128)S(1)}, f32[32,128]{1,0:T(8,128)S(1)}, u32[]{:S(2)}, u32[]{:S(2)}) collective-permute-start(f32[32,128]{1,0:T(8,128)S(1)} %get-tuple-element.68), channel_id=1, source_target_pairs={{0,24},{2,26},{4,28},{6,30},{8,16},{10,18},{12,20},{14,22},{16,8},... | collective-permute-start | bytes 49160 | tf_op jit(solution)/shard_map/ppermute | solution.py:626
  35.8 4.8 %collective-permute-start.14 = (f32[32,128]{1,0:T(8,128)S(1)}, f32[32,128]{1,0:T(8,128)S(1)}, u32[]{:S(2)}, u32[]{:S(2)}) collective-permute-start(f32[32,128]{1,0:T(8,128)S(1)} %get-tuple-element.69), channel_id=1, source_target_pairs={{0,16},{2,18},{4,20},{6,22},{8,24},{10,26},{12,28},{14,30},{16,0},... | collective-permute-start | bytes 49160 | tf_op jit(solution)/shard_map/ppermute | solution.py:626
  35.9 4.7 %collective-permute-start.15 = (f32[32,128]{1,0:T(8,128)S(1)}, f32[32,128]{1,0:T(8,128)S(1)}, u32[]{:S(2)}, u32[]{:S(2)}) collective-permute-start(f32[32,128]{1,0:T(8,128)S(1)} %get-tuple-element.70), channel_id=1, source_target_pairs={{0,8},{2,10},{4,12},{6,14},{8,0},{10,2},{12,4},{14,6},{16,24},{18,... | collective-permute-start | bytes 49160 | tf_op jit(solution)/shard_map/ppermute | solution.py:626

commit v7 on v6

--- a/solution.py
+++ b/solution.py
@@ -651,10 +651,11 @@
         [arguments, sigma.reshape(1, -1)],
         us=1.0,
     )
+    vectors = [shift(v, "gy", 1).reshape(1, -1) for v in (frequency, barrier)]
     tiles, arrhenius, base = call(
         source_kernel,
         [block] * 3,
-        [arguments, frequency.reshape(1, -1), barrier.reshape(1, -1), proportions, rates, x_faces],
+        [arguments, *vectors, proportions, rates, x_faces],
         [pltpu.VMEM((z.tiles, z.nx), F32)],
     )
     x_solve = [left, right, inverse]

time: 41.6 us -> 41.2 us (level)
  local copies, waits for them, and re-layouts: 0.66 us -> 0.01 us
    unnamed x8, local copies, waits for them, and re-layouts: 0.66 us -> 0.01 us
    ppermute x2 -> x4, starting transfers between devices: 0.59 us -> 1.1 us  [shift(): lax.ppermute(value, axis, [(i, (i + by) % count) for i in range(count)])]
  transfers between devices with their start and end apart: 16 -> 18, of which waited for: 11 -> 11; matrix products, arithmetic and copies ran while one was open for 0% -> 0% of each run, Pallas kernels for 8% -> 8%
where the time goes in v7:
time: 41.2 us; the launch traced here: 41 us
  starting transfers between devices  21.2 us (51%)
  waiting for transfers between devices  13 us (32%)
  Pallas kernels  5.7 us (14%)
  other arithmetic  0.95 us (2%)
    ppermute x10, starting transfers between devices, exchange(): return [lax.ppermute(v, 'gz', p) for v, p in zip(values, pairs)]  15.6 us
    ppermute x10, waiting for transfers between devices, exchange(): return [lax.ppermute(v, 'gz', p) for v, p in zip(values, pairs)]  10.6 us
    pallas_call x14, Pallas kernels, call(): pl.pallas_call(functools.partial(kernel, z), out_shape=outs, in_specs=[sp...  5.7 us
    ppermute x3, starting transfers between devices, exchange(): lax.ppermute(v, 'gz', p)  4.45 us
    ppermute x3, waiting for transfers between devices, exchange(): lax.ppermute(v, 'gz', p)  2.04 us
    ppermute x4, starting transfers between devices, shift(): lax.ppermute(value, axis, [(i, (i + by) % count) for i in range(count)])  1.1 us
    concatenate x1, other arithmetic, per_device(): arguments = jnp.concatenate([v.reshape(-1, z.nx) for v in (c, k, warm)])  0.95 us
  transfers between devices with their start and end apart: 18, of which 11 were waited for; matrix products, arithmetic and copies ran while one was open for 0% of the time, Pallas kernels for 8%

profile of v7, /device:TPU:0, one launch (start us, length us, event | category | flops | bytes accessed | tf_op | source)
XLA Modules:
  0.0 41.0 jit_solution(9077404278298524858)
XLA Ops:
  0.0 0.9 %pad_maximum_fusion.c_ref.arguments = f32[288,128]{1,0:T(8,128)S(1)} fusion(f32[16,128]{1,0:T(8,128)} %bitcast.10, f32[16,128]{1,0:T(8,128)} %bitcast.11, f32[256,128]{1,0:T(8,128)} %bitcast.9), kind=kLoop, calls=%fused_computation | loop fusion | flops 73728 | bytes 294912 | tf_op jit(solution)/shard_map/concatenate | solution.py:617
  1.0 0.5 %collective-permute-start.4 = (f32[136,128]{1,0:T(8,128)S(1)}, f32[136,128]{1,0:T(8,128)S(1)}, u32[]{:S(2)}, u32[]{:S(2)}) collective-permute-start(f32[136,128]{1,0:T(8,128)S(1)} %get-tuple-element.47), channel_id=1, source_target_pairs={{0,1},{1,0},{2,3},{3,2},{4,5},{5,4},{6,7},{7,6},{8,9},{9,8},{10,11... | collective-permute-start | bytes 208904 | tf_op jit(solution)/shard_map/ppermute | solution.py:612
  1.5 0.1 collective-permute-start
  1.6 4.0 %collective-permute-start.1 = (f32[40,128]{1,0:T(8,128)S(1)}, f32[40,128]{1,0:T(8,128)S(1)}, u32[]{:S(2)}, u32[]{:S(2)}) collective-permute-start(f32[40,128]{1,0:T(8,128)S(1)} %get-tuple-element.39), channel_id=1, source_target_pairs={{0,2},{2,0},{4,6},{6,4},{8,10},{10,8},{12,14},{14,12},{16,18},{18,... | collective-permute-start | bytes 61448 | tf_op jit(solution)/shard_map/ppermute | solution.py:627
  5.6 0.0 collective-permute-start.2
  5.6 0.5 %collective-permute-start.3 = (f32[16]{0:T(128)S(1)}, f32[16]{0:T(128)S(1)}, u32[]{:S(2)}, u32[]{:S(2)}) collective-permute-start(f32[16]{0:T(128)S(1)} %copy-done.3), channel_id=1, source_target_pairs={{0,1},{1,0},{2,3},{3,2},{4,5},{5,4},{6,7},{7,6},{8,9},{9,8},{10,11... | collective-permute-start | bytes 200 | tf_op jit(solution)/shard_map/ppermute | solution.py:612
  6.1 1.1 %shard_map.74 = (f32[4,16,128]{2,1,0:T(8,128)S(1)}, f32[2,16,128]{2,1,0:T(8,128)S(1)}, f32[7,16,16,128]{3,2,1,0:T(8,128)S(1)}, f32[7,16,16,128]{3,2,1,0:T(8,128)S(1)}, f32[16,16,128]{2,1,0:T(8,128)S(1)}) custom-call(f32[288,128]{1,0:T(8,128)S(1)} %pad_maximum_fusion.c_ref.arguments, f32[1,16]{1,0:T(1,128)S(1)} %bitcast.6), custom_call_target="tpu_custom_call" | custom-call | bytes 3690000 | tf_op jit(solution)/shard_map/pallas_call | solution.py:598
  7.2 0.0 collective-permute-done.2
  7.2 0.0 collective-permute-done.3
  7.2 0.4 shard_map.75
  7.6 0.0 collective-permute-done.4.refs_0_
  7.6 0.6 %shard_map.76 = (f32[16,16,128]{2,1,0:T(8,128)S(1)}, f32[2,16,128]{2,1,0:T(8,128)S(1)}) custom-call(f32[288,128]{1,0:T(8,128)S(1)} %pad_maximum_fusion.c_ref.arguments, f32[16,16,128]{2,1,0:T(8,128)S(1)} %get-tuple-element.42.tiles_ref, f32[16,16,128]{2,1,0:T(8,128)S(1)} %get-tuple-element.43.base_ref, f32[4,16,128]{2,1,0:T(8,128)S(1)} %get-tuple-element.40.rates_ref, ...), custom_call_target="tpu_custom_call" | custom-call | bytes 1845000 | tf_op jit(solution)/shard_map/pallas_call | solution.py:598
  8.2 0.0 collective-permute-done.far_ref
  8.2 0.0 collective-permute-done.1.near_ref
  8.2 0.6 %shard_map.77 = (f32[88,128]{1,0:T(8,128)S(1)}, f32[16,16,128]{2,1,0:T(8,128)S(1)}, f32[2,16,128]{2,1,0:T(8,128)S(1)}) custom-call(f32[288,128]{1,0:T(8,128)S(1)} %pad_maximum_fusion.c_ref.arguments, f32[40,128]{1,0:T(8,128)S(1)} %collective-permute-done.far_ref, f32[40,128]{1,0:T(8,128)S(1)} %collective-permute-done.1.near_ref, ...), custom_call_target="tpu_custom_call" | custom-call | bytes 1845000 | tf_op jit(solution)/shard_map/pallas_call | solution.py:598
  8.8 2.5 %collective-permute-start.7 = (f32[88,128]{1,0:T(8,128)S(1)}, f32[88,128]{1,0:T(8,128)S(1)}, u32[]{:S(2)}, u32[]{:S(2)}) collective-permute-start(f32[88,128]{1,0:T(8,128)S(1)} %get-tuple-element.51.pay_ref.refs_0_), channel_id=1, source_target_pairs={{0,6},{2,4},{4,2},{6,0},{8,14},{10,12},{12,10},{14,8},{16,22},{18,... | collective-permute-start | bytes 135176 | tf_op jit(solution)/shard_map/ppermute | solution.py:627
  11.3 0.2 collective-permute-start.6
  11.5 0.8 %collective-permute-start.5 = (f32[88,128]{1,0:T(8,128)S(1)}, f32[88,128]{1,0:T(8,128)S(1)}, u32[]{:S(2)}, u32[]{:S(2)}) collective-permute-start(f32[88,128]{1,0:T(8,128)S(1)} %get-tuple-element.51.pay_ref.refs_0_), channel_id=1, source_target_pairs={{0,2},{2,0},{4,6},{6,4},{8,10},{10,8},{12,14},{14,12},{16,18},{18,... | collective-permute-start | bytes 135176 | tf_op jit(solution)/shard_map/ppermute | solution.py:627
  12.3 1.5 %collective-permute-done.7.refs_2_.refs_3_ = f32[88,128]{1,0:T(8,128)S(1)} collective-permute-done((f32[88,128]{1,0:T(8,128)S(1)}, f32[88,128]{1,0:T(8,128)S(1)}, u32[]{:S(2)}, u32[]{:S(2)}) %collective-permute-start.7) | collective-permute-done | bytes 45088 | tf_op jit(solution)/shard_map/ppermute | solution.py:627
  13.8 1.5 %collective-permute-done.6.refs_1_.refs_2_ = f32[88,128]{1,0:T(8,128)S(1)} collective-permute-done((f32[88,128]{1,0:T(8,128)S(1)}, f32[88,128]{1,0:T(8,128)S(1)}, u32[]{:S(2)}, u32[]{:S(2)}) %collective-permute-start.6) | collective-permute-done | bytes 45088 | tf_op jit(solution)/shard_map/ppermute | solution.py:627
  15.3 0.2 collective-permute-done.5.refs_0_.refs_1_
  15.6 0.1 shard_map.78.own_group
  15.7 3.8 %collective-permute-start.8 = (f32[136,128]{1,0:T(8,128)S(1)}, f32[136,128]{1,0:T(8,128)S(1)}, u32[]{:S(2)}, u32[]{:S(2)}) collective-permute-start(f32[136,128]{1,0:T(8,128)S(1)} %shard_map.78.own_group), channel_id=1, source_target_pairs={{0,24},{2,26},{4,28},{6,30},{8,16},{10,18},{12,20},{14,22},{16,8},... | collective-permute-start | bytes 208904 | tf_op jit(solution)/shard_map/ppermute | solution.py:627
  19.6 0.0 collective-permute-start.10
  19.6 0.6 %collective-permute-start.9 = (f32[136,128]{1,0:T(8,128)S(1)}, f32[136,128]{1,0:T(8,128)S(1)}, u32[]{:S(2)}, u32[]{:S(2)}) collective-permute-start(f32[136,128]{1,0:T(8,128)S(1)} %shard_map.78.own_group), channel_id=1, source_target_pairs={{0,8},{2,10},{4,12},{6,14},{8,0},{10,2},{12,4},{14,6},{16,24},{18,... | collective-permute-start | bytes 208904 | tf_op jit(solution)/shard_map/ppermute | solution.py:627
  20.2 0.1 shard_map.79
  20.3 1.7 %collective-permute-done.8.group_ref.refs_2_ = f32[136,128]{1,0:T(8,128)S(1)} collective-permute-done((f32[136,128]{1,0:T(8,128)S(1)}, f32[136,128]{1,0:T(8,128)S(1)}, u32[]{:S(2)}, u32[]{:S(2)}) %collective-permute-start.8) | collective-permute-done | bytes 69664 | tf_op jit(solution)/shard_map/ppermute | solution.py:627
  22.1 0.1 shard_map.80.far_transfer
  22.2 2.7 %collective-permute-done.10.refs_1_ = f32[136,128]{1,0:T(8,128)S(1)} collective-permute-done((f32[136,128]{1,0:T(8,128)S(1)}, f32[136,128]{1,0:T(8,128)S(1)}, u32[]{:S(2)}, u32[]{:S(2)}) %collective-permute-start.10) | collective-permute-done | bytes 69664 | tf_op jit(solution)/shard_map/ppermute | solution.py:627
  24.9 0.5 %shard_map.81 = (f32[16,16,128]{2,1,0:T(8,128)S(1)}, f32[16,16,128]{2,1,0:T(8,128)S(1)}, f32[10,16,128]{2,1,0:T(8,128)S(1)}, f32[4,16,128]{2,1,0:T(8,128)S(1)}, f32[128,128]{1,0:T(8,128)S(1)}) custom-call(f32[4,16,128]{2,1,0:T(8,128)S(1)} %get-tuple-element.40.rates_ref, f32[16,16,128]{2,1,0:T(8,128)S(1)} %get-tuple-element.50.f_ref, ...), custom_call_target="tpu_custom_call" | custom-call | bytes 1845000 | tf_op jit(solution)/shard_map/pallas_call | solution.py:598
  25.4 0.1 collective-permute-start.11
  25.5 0.1 shard_map.82
  25.6 0.8 %shard_map.83 = (f32[16,16,128]{2,1,0:T(8,128)S(1)}, f32[16,16,128]{2,1,0:T(8,128)S(1)}) custom-call(f32[16,16,128]{2,1,0:T(8,128)S(1)} %get-tuple-element.58.tiles_ref, f32[4,16,128]{2,1,0:T(8,128)S(1)} %get-tuple-element.59.halo_ref, f32[4,16,128]{2,1,0:T(8,128)S(1)} %get-tuple-element.40.rates_ref, f32[2,16,128]{2,1,0:T(8,128)S(1)} %get-tuple-element.41.faces.x_faces, ...), custom_call_target="tpu_custom_call" | custom-call | bytes 1845000 | tf_op jit(solution)/shard_map/pallas_call | solution.py:598
  26.4 0.4 collective-permute-done.11.refs_0_
  26.7 0.6 %shard_map.84 = (f32[2,32,128]{2,1,0:T(8,128)S(1)}, f32[16,16,128]{2,1,0:T(8,128)S(1)}) custom-call(f32[16,16,128]{2,1,0:T(8,128)S(1)} %get-tuple-element.58.tiles_ref, f32[4,16,128]{2,1,0:T(8,128)S(1)} %get-tuple-element.59.halo_ref, f32[4,16,128]{2,1,0:T(8,128)S(1)} %get-tuple-element.40.rates_ref, f32[2,16,128]{2,1,0:T(8,128)S(1)} %get-tuple-element.49.y_faces, ...), custom_call_target="tpu_custom_call" | custom-call | bytes 1845000 | tf_op jit(solution)/shard_map/pallas_call | solution.py:598
  27.3 1.6 %collective-permute-start.14 = (f32[2,32,128]{2,1,0:T(8,128)S(1)}, f32[2,32,128]{2,1,0:T(8,128)S(1)}, u32[]{:S(2)}, u32[]{:S(2)}) collective-permute-start(f32[2,32,128]{2,1,0:T(8,128)S(1)} %get-tuple-element.65.pay_ref), channel_id=1, source_target_pairs={{0,6},{2,4},{4,2},{6,0},{8,14},{10,12},{12,10},{14,8},{16,22},{18,... | collective-permute-start | bytes 98312 | tf_op jit(solution)/shard_map/ppermute | solution.py:627
  28.9 0.9 %collective-permute-start.13 = (f32[2,32,128]{2,1,0:T(8,128)S(1)}, f32[2,32,128]{2,1,0:T(8,128)S(1)}, u32[]{:S(2)}, u32[]{:S(2)}) collective-permute-start(f32[2,32,128]{2,1,0:T(8,128)S(1)} %get-tuple-element.65.pay_ref), channel_id=1, source_target_pairs={{0,4},{2,6},{4,0},{6,2},{8,12},{10,14},{12,8},{14,10},{16,20},{18,... | collective-permute-start | bytes 98312 | tf_op jit(solution)/shard_map/ppermute | solution.py:627
  29.8 1.0 %collective-permute-start.12 = (f32[2,32,128]{2,1,0:T(8,128)S(1)}, f32[2,32,128]{2,1,0:T(8,128)S(1)}, u32[]{:S(2)}, u32[]{:S(2)}) collective-permute-start(f32[2,32,128]{2,1,0:T(8,128)S(1)} %get-tuple-element.65.pay_ref), channel_id=1, source_target_pairs={{0,2},{2,0},{4,6},{6,4},{8,10},{10,8},{12,14},{14,12},{16,18},{18,... | collective-permute-start | bytes 98312 | tf_op jit(solution)/shard_map/ppermute | solution.py:627
  30.9 1.3 %collective-permute-done.14.refs_2_ = f32[2,32,128]{2,1,0:T(8,128)S(1)} collective-permute-done((f32[2,32,128]{2,1,0:T(8,128)S(1)}, f32[2,32,128]{2,1,0:T(8,128)S(1)}, u32[]{:S(2)}, u32[]{:S(2)}) %collective-permute-start.14) | collective-permute-done | bytes 32800 | tf_op jit(solution)/shard_map/ppermute | solution.py:627
  32.2 0.6 %collective-permute-done.13.refs_1_ = f32[2,32,128]{2,1,0:T(8,128)S(1)} collective-permute-done((f32[2,32,128]{2,1,0:T(8,128)S(1)}, f32[2,32,128]{2,1,0:T(8,128)S(1)}, u32[]{:S(2)}, u32[]{:S(2)}) %collective-permute-start.13) | collective-permute-done | bytes 32800 | tf_op jit(solution)/shard_map/ppermute | solution.py:627
  32.8 0.9 %collective-permute-done.12.refs_0_ = f32[2,32,128]{2,1,0:T(8,128)S(1)} collective-permute-done((f32[2,32,128]{2,1,0:T(8,128)S(1)}, f32[2,32,128]{2,1,0:T(8,128)S(1)}, u32[]{:S(2)}, u32[]{:S(2)}) %collective-permute-start.12) | collective-permute-done | bytes 32800 | tf_op jit(solution)/shard_map/ppermute | solution.py:627
  33.8 1.9 %collective-permute-start.15 = (f32[32,128]{1,0:T(8,128)S(1)}, f32[32,128]{1,0:T(8,128)S(1)}, u32[]{:S(2)}, u32[]{:S(2)}) collective-permute-start(f32[32,128]{1,0:T(8,128)S(1)} %get-tuple-element.68), channel_id=1, source_target_pairs={{0,24},{2,26},{4,28},{6,30},{8,16},{10,18},{12,20},{14,22},{16,8},... | collective-permute-start | bytes 49160 | tf_op jit(solution)/shard_map/ppermute | solution.py:626
  35.6 0.3 collective-permute-start.16
  35.9 2.3 %collective-permute-start.17 = (f32[32,128]{1,0:T(8,128)S(1)}, f32[32,128]{1,0:T(8,128)S(1)}, u32[]{:S(2)}, u32[]{:S(2)}) collective-permute-start(f32[32,128]{1,0:T(8,128)S(1)} %get-tuple-element.70), channel_id=1, source_target_pairs={{0,8},{2,10},{4,12},{6,14},{8,0},{10,2},{12,4},{14,6},{16,24},{18,... | collective-permute-start | bytes 49160 | tf_op jit(solution)/shard_map/ppermute | solution.py:626
  38.2 1.1 %collective-permute-done.15.refs_0_ = f32[32,128]{1,0:T(8,128)S(1)} collective-permute-done((f32[32,128]{1,0:T(8,128)S(1)}, f32[32,128]{1,0:T(8,128)S(1)}, u32[]{:S(2)}, u32[]{:S(2)}) %collective-permute-start.15) | collective-permute-done | bytes 16416 | tf_op jit(solution)/shard_map/ppermute | solution.py:626
  39.4 0.9 %collective-permute-done.16.refs_1_ = f32[32,128]{1,0:T(8,128)S(1)} collective-permute-done((f32[32,128]{1,0:T(8,128)S(1)}, f32[32,128]{1,0:T(8,128)S(1)}, u32[]{:S(2)}, u32[]{:S(2)}) %collective-permute-start.16) | collective-permute-done | bytes 16416 | tf_op jit(solution)/shard_map/ppermute | solution.py:626
  40.3 0.0 collective-permute-done.17.refs_2_
  40.3 0.7 %shard_map.86 = f32[16,2,8,128]{3,2,1,0:T(8,128)} custom-call(f32[2,32,128]{2,1,0:T(8,128)S(1)} %get-tuple-element.66.within_ref, f32[16,16,128]{2,1,0:T(8,128)S(1)} %get-tuple-element.67.f_ref, f32[16,16,128]{2,1,0:T(8,128)S(1)} %get-tuple-element.54.v_ref, f32[16,16,128]{2,1,0:T(8,128)S(1)} %get-tuple-element.55.u_ref, ...), custom_call_target="tpu_custom_call" | custom-call | bytes 1845000 | tf_op jit(solution)/shard_map/pallas_call | solution.py:598
  (11 shorter events, 0.1 us)
Async XLA Ops:
  1.0 6.6 %collective-permute-start.4 = (f32[136,128]{1,0:T(8,128)S(1)}, f32[136,128]{1,0:T(8,128)S(1)}, u32[]{:S(2)}, u32[]{:S(2)}) collective-permute-start(f32[136,128]{1,0:T(8,128)S(1)} %get-tuple-element.47), channel_id=1, source_target_pairs={{0,1},{1,0},{2,3},{3,2},{4,5},{5,4},{6,7},{7,6},{8,9},{9,8},{10,11... | collective-permute-start | bytes 208904 | tf_op jit(solution)/shard_map/ppermute | solution.py:612
  1.5 4.1 %copy-start.2 = (f32[16]{0:T(128)S(1)}, f32[16]{0:T(128)}, u32[]{:S(2)}) copy-start(f32[16]{0:T(128)} %param.11) | copy-start | bytes 196
  1.5 4.1 %copy-start.3 = (f32[16]{0:T(128)S(1)}, f32[16]{0:T(128)}, u32[]{:S(2)}) copy-start(f32[16]{0:T(128)} %param.12) | copy-start | bytes 196
  1.5 6.7 %collective-permute-start = (f32[40,128]{1,0:T(8,128)S(1)}, f32[40,128]{1,0:T(8,128)S(1)}, u32[]{:S(2)}, u32[]{:S(2)}) collective-permute-start(f32[40,128]{1,0:T(8,128)S(1)} %get-tuple-element.38), channel_id=1, source_target_pairs={{2,4},{3,5},{4,2},{5,3},{6,8},{7,9},{8,6},{9,7},{10,12},{11,13},{1... | collective-permute-start | bytes 61448 | tf_op jit(solution)/shard_map/ppermute | solution.py:636
  1.6 4.5 %copy-start.1 = (f32[16]{0:T(128)S(1)}, f32[16]{0:T(128)}, u32[]{:S(2)}) copy-start(f32[16]{0:T(128)} %param.10) | copy-start | bytes 196
  1.6 6.6 %collective-permute-start.1 = (f32[40,128]{1,0:T(8,128)S(1)}, f32[40,128]{1,0:T(8,128)S(1)}, u32[]{:S(2)}, u32[]{:S(2)}) collective-permute-start(f32[40,128]{1,0:T(8,128)S(1)} %get-tuple-element.39), channel_id=1, source_target_pairs={{0,2},{2,0},{4,6},{6,4},{8,10},{10,8},{12,14},{14,12},{16,18},{18,... | collective-permute-start | bytes 61448 | tf_op jit(solution)/shard_map/ppermute | solution.py:627
  5.6 1.6 %collective-permute-start.2 = (f32[16]{0:T(128)S(1)}, f32[16]{0:T(128)S(1)}, u32[]{:S(2)}, u32[]{:S(2)}) collective-permute-start(f32[16]{0:T(128)S(1)} %copy-done.2), channel_id=1, source_target_pairs={{0,1},{1,0},{2,3},{3,2},{4,5},{5,4},{6,7},{7,6},{8,9},{9,8},{10,11... | collective-permute-start | bytes 200 | tf_op jit(solution)/shard_map/ppermute | solution.py:612
  5.6 1.6 %collective-permute-start.3 = (f32[16]{0:T(128)S(1)}, f32[16]{0:T(128)S(1)}, u32[]{:S(2)}, u32[]{:S(2)}) collective-permute-start(f32[16]{0:T(128)S(1)} %copy-done.3), channel_id=1, source_target_pairs={{0,1},{1,0},{2,3},{3,2},{4,5},{5,4},{6,7},{7,6},{8,9},{9,8},{10,11... | collective-permute-start | bytes 200 | tf_op jit(solution)/shard_map/ppermute | solution.py:612
  6.1 1.1 %copy-start = (f32[16,16]{1,0:T(8,128)S(1)}, f32[16,16]{1,0:T(8,128)}, u32[]{:S(2)}) copy-start(f32[16,16]{1,0:T(8,128)} %proportions_ref.3) | copy-start | bytes 3076
  8.8 5.1 %collective-permute-start.7 = (f32[88,128]{1,0:T(8,128)S(1)}, f32[88,128]{1,0:T(8,128)S(1)}, u32[]{:S(2)}, u32[]{:S(2)}) collective-permute-start(f32[88,128]{1,0:T(8,128)S(1)} %get-tuple-element.51.pay_ref.refs_0_), channel_id=1, source_target_pairs={{0,6},{2,4},{4,2},{6,0},{8,14},{10,12},{12,10},{14,8},{16,22},{18,... | collective-permute-start | bytes 135176 | tf_op jit(solution)/shard_map/ppermute | solution.py:627
  11.3 4.0 %collective-permute-start.6 = (f32[88,128]{1,0:T(8,128)S(1)}, f32[88,128]{1,0:T(8,128)S(1)}, u32[]{:S(2)}, u32[]{:S(2)}) collective-permute-start(f32[88,128]{1,0:T(8,128)S(1)} %get-tuple-element.51.pay_ref.refs_0_), channel_id=1, source_target_pairs={{0,4},{2,6},{4,0},{6,2},{8,12},{10,14},{12,8},{14,10},{16,20},{18,... | collective-permute-start | bytes 135176 | tf_op jit(solution)/shard_map/ppermute | solution.py:627
  11.5 4.0 %collective-permute-start.5 = (f32[88,128]{1,0:T(8,128)S(1)}, f32[88,128]{1,0:T(8,128)S(1)}, u32[]{:S(2)}, u32[]{:S(2)}) collective-permute-start(f32[88,128]{1,0:T(8,128)S(1)} %get-tuple-element.51.pay_ref.refs_0_), channel_id=1, source_target_pairs={{0,2},{2,0},{4,6},{6,4},{8,10},{10,8},{12,14},{14,12},{16,18},{18,... | collective-permute-start | bytes 135176 | tf_op jit(solution)/shard_map/ppermute | solution.py:627
  15.7 6.3 %collective-permute-start.8 = (f32[136,128]{1,0:T(8,128)S(1)}, f32[136,128]{1,0:T(8,128)S(1)}, u32[]{:S(2)}, u32[]{:S(2)}) collective-permute-start(f32[136,128]{1,0:T(8,128)S(1)} %shard_map.78.own_group), channel_id=1, source_target_pairs={{0,24},{2,26},{4,28},{6,30},{8,16},{10,18},{12,20},{14,22},{16,8},... | collective-permute-start | bytes 208904 | tf_op jit(solution)/shard_map/ppermute | solution.py:627
  19.6 5.4 %collective-permute-start.10 = (f32[136,128]{1,0:T(8,128)S(1)}, f32[136,128]{1,0:T(8,128)S(1)}, u32[]{:S(2)}, u32[]{:S(2)}) collective-permute-start(f32[136,128]{1,0:T(8,128)S(1)} %shard_map.78.own_group), channel_id=1, source_target_pairs={{0,16},{2,18},{4,20},{6,22},{8,24},{10,26},{12,28},{14,30},{16,0},... | collective-permute-start | bytes 208904 | tf_op jit(solution)/shard_map/ppermute | solution.py:627
  19.6 5.4 %collective-permute-start.9 = (f32[136,128]{1,0:T(8,128)S(1)}, f32[136,128]{1,0:T(8,128)S(1)}, u32[]{:S(2)}, u32[]{:S(2)}) collective-permute-start(f32[136,128]{1,0:T(8,128)S(1)} %shard_map.78.own_group), channel_id=1, source_target_pairs={{0,8},{2,10},{4,12},{6,14},{8,0},{10,2},{12,4},{14,6},{16,24},{18,... | collective-permute-start | bytes 208904 | tf_op jit(solution)/shard_map/ppermute | solution.py:627
  25.4 1.3 %collective-permute-start.11 = (f32[128,128]{1,0:T(8,128)S(1)}, f32[128,128]{1,0:T(8,128)S(1)}, u32[]{:S(2)}, u32[]{:S(2)}) collective-permute-start(f32[128,128]{1,0:T(8,128)S(1)} %get-tuple-element.64), channel_id=1, source_target_pairs={{0,1},{1,0},{2,3},{3,2},{4,5},{5,4},{6,7},{7,6},{8,9},{9,8},{10,11... | collective-permute-start | bytes 196616 | tf_op jit(solution)/shard_map/ppermute | solution.py:612
  27.3 4.9 %collective-permute-start.14 = (f32[2,32,128]{2,1,0:T(8,128)S(1)}, f32[2,32,128]{2,1,0:T(8,128)S(1)}, u32[]{:S(2)}, u32[]{:S(2)}) collective-permute-start(f32[2,32,128]{2,1,0:T(8,128)S(1)} %get-tuple-element.65.pay_ref), channel_id=1, source_target_pairs={{0,6},{2,4},{4,2},{6,0},{8,14},{10,12},{12,10},{14,8},{16,22},{18,... | collective-permute-start | bytes 98312 | tf_op jit(solution)/shard_map/ppermute | solution.py:627
  28.9 3.9 %collective-permute-start.13 = (f32[2,32,128]{2,1,0:T(8,128)S(1)}, f32[2,32,128]{2,1,0:T(8,128)S(1)}, u32[]{:S(2)}, u32[]{:S(2)}) collective-permute-start(f32[2,32,128]{2,1,0:T(8,128)S(1)} %get-tuple-element.65.pay_ref), channel_id=1, source_target_pairs={{0,4},{2,6},{4,0},{6,2},{8,12},{10,14},{12,8},{14,10},{16,20},{18,... | collective-permute-start | bytes 98312 | tf_op jit(solution)/shard_map/ppermute | solution.py:627
  29.8 3.9 %collective-permute-start.12 = (f32[2,32,128]{2,1,0:T(8,128)S(1)}, f32[2,32,128]{2,1,0:T(8,128)S(1)}, u32[]{:S(2)}, u32[]{:S(2)}) collective-permute-start(f32[2,32,128]{2,1,0:T(8,128)S(1)} %get-tuple-element.65.pay_ref), channel_id=1, source_target_pairs={{0,2},{2,0},{4,6},{6,4},{8,10},{10,8},{12,14},{14,12},{16,18},{18,... | collective-permute-start | bytes 98312 | tf_op jit(solution)/shard_map/ppermute | solution.py:627
  33.8 5.6 %collective-permute-start.15 = (f32[32,128]{1,0:T(8,128)S(1)}, f32[32,128]{1,0:T(8,128)S(1)}, u32[]{:S(2)}, u32[]{:S(2)}) collective-permute-start(f32[32,128]{1,0:T(8,128)S(1)} %get-tuple-element.68), channel_id=1, source_target_pairs={{0,24},{2,26},{4,28},{6,30},{8,16},{10,18},{12,20},{14,22},{16,8},... | collective-permute-start | bytes 49160 | tf_op jit(solution)/shard_map/ppermute | solution.py:626
  35.6 4.6 %collective-permute-start.16 = (f32[32,128]{1,0:T(8,128)S(1)}, f32[32,128]{1,0:T(8,128)S(1)}, u32[]{:S(2)}, u32[]{:S(2)}) collective-permute-start(f32[32,128]{1,0:T(8,128)S(1)} %get-tuple-element.69), channel_id=1, source_target_pairs={{0,16},{2,18},{4,20},{6,22},{8,24},{10,26},{12,28},{14,30},{16,0},... | collective-permute-start | bytes 49160 | tf_op jit(solution)/shard_map/ppermute | solution.py:626
  35.9 4.3 %collective-permute-start.17 = (f32[32,128]{1,0:T(8,128)S(1)}, f32[32,128]{1,0:T(8,128)S(1)}, u32[]{:S(2)}, u32[]{:S(2)}) collective-permute-start(f32[32,128]{1,0:T(8,128)S(1)} %get-tuple-element.70), channel_id=1, source_target_pairs={{0,8},{2,10},{4,12},{6,14},{8,0},{10,2},{12,4},{14,6},{16,24},{18,... | collective-permute-start | bytes 49160 | tf_op jit(solution)/shard_map/ppermute | solution.py:626

commit v8 on v7

--- a/solution.py
+++ b/solution.py
@@ -18,6 +18,7 @@
         self.devices = mesh.shape["gz"]
         self.gy = mesh.shape["gy"]
         self.levels = (self.nx - 1).bit_length()
+        self.pairs = (self.levels - 1) // 2
         self.tile = (self.species, self.nx)
         padded = -(-self.ny // 8) * 8
         self.edge_rows = self.lines + padded
@@ -165,7 +166,28 @@
         base_ref[t] = v + lap + source[:, t * z.nx : (t + 1) * z.nx]
 
 
-def right_sides(z, places, tiles_ref, base_ref, z_halo, y_halo, rates_ref, y_faces, z_faces, left, right, inverse, f_ref):
+def edge_places(z):
+    return [(y, row) for y in range(z.ny) for row in sorted({0, z.nz - 1})]
+
+
+def join_levels(z, t, left, right, joined, at):
+    for pair in range(z.pairs):
+        stride = 4**pair
+        l1, r1, l2, r2 = (ref[2 * pair + n, t] for n in range(2) for ref in (left, right))
+        factors = (
+            l1 + l2 * along_x(r1, 2 * stride, z.nx),
+            r1 + r2 * along_x(l1, -2 * stride, z.nx),
+            l2 * along_x(l1, 2 * stride, z.nx),
+            r2 * along_x(r1, -2 * stride, z.nx),
+        )
+        for n, factor in enumerate(factors):
+            joined[4 * pair + n, at] = factor
+
+
+def right_sides(
+    z, places, tiles_ref, base_ref, z_halo, y_halo, rates_ref, y_faces, z_faces, left, right, inverse, f_ref,
+    joined=None,
+):
     rate_y, rate_z = rates_ref[1], rates_ref[2]
     section, lap = [], []
     for y, row in places:
@@ -186,7 +208,18 @@
         lap_z = rate_z * (flux[3] * (z_after - v) - flux[2] * (v - z_before))
         lap.append(lap_z)
         section.append(base_ref[t] + lap_y + lap_z)
-    for level in range(z.levels):
+    pairs = z.pairs if joined else 0
+    for pair in range(pairs):
+        stride = 4**pair
+        for i, (y, row) in enumerate(places):
+            t = y * z.nz + row
+            factors = [joined(4 * pair + n, i) for n in range(4)]
+            factors[2:2] = left[2 * pair + 1, t], right[2 * pair + 1, t]
+            terms = []
+            for factor, by in zip(factors, (1, -1, 2, -2, 3, -3)):
+                terms.append(factor * along_x(section[i], by * stride, z.nx))
+            section[i] = section[i] + ((terms[0] + terms[1]) + (terms[2] + terms[3])) + (terms[4] + terms[5])
+    for level in range(2 * pairs, z.levels):
         stride = 1 << level
         for i, (y, row) in enumerate(places):
             t = y * z.nz + row
@@ -251,7 +284,9 @@
 def early_kernel(z, arguments, tiles_ref, base_ref, rates_ref, left_ref, right_ref, inverse_ref, *refs):
     halos = 1 if z.gy == 2 else 2
     received = refs[:halos]
-    f_ref, y_faces, z_faces = refs[halos:]
+    f_ref, y_faces, joined_ref, z_faces = refs[halos:]
+    for i, (y, row) in enumerate(edge_places(z)):
+        join_levels(z, y * z.nz + row, left_ref, right_ref, joined_ref, i)
     k_ref = z.conductance(arguments)
     k = k_ref[...]
     low, high = received[0], received[-1]
@@ -275,7 +310,7 @@
 
 def first_kernel(
     z, arguments, far_ref, near_ref, tiles_ref, base_ref, rates_ref, left_ref, right_ref, inverse_ref,
-    early_ref, y_faces, *refs
+    early_ref, y_faces, joined_ref, *refs
 ):
     halos = 1 if z.gy == 2 else 2
     received = refs[:halos]
@@ -308,10 +343,9 @@
     for y in range(z.ny):
         for row in range(1, z.nz - 1):
             f_ref[y * z.nz + row] = early_ref[y * z.nz + row]
-    places = [(y, row) for y in range(z.ny) for row in sorted({0, z.nz - 1})]
     right_sides(
-        z, places, tiles_ref, base_ref, z_halo, y_halos(z, received), rates_ref, y_faces, z_faces,
-        left_ref, right_ref, inverse_ref, f_ref,
+        z, edge_places(z), tiles_ref, base_ref, z_halo, y_halos(z, received), rates_ref, y_faces, z_faces,
+        left_ref, right_ref, inverse_ref, f_ref, lambda n, i: joined_ref[n, i],
     )
     ohms = rates_ref[3]
     zero, one = jnp.zeros(z.tile, F32), jnp.ones(z.tile, F32)
@@ -534,8 +568,11 @@
 
 def inner_kernel(
     z, tiles_ref, halo_ref, rates_ref, x_faces, arrhenius_ref, proportions_ref, y_faces, z_faces,
-    left_ref, right_ref, inverse_ref, base_ref, f_ref
+    left_ref, right_ref, inverse_ref, base_ref, f_ref, joined_ref
 ):
+    ys, _ = halo_rows(z)
+    for i, (y, row) in enumerate(places_of(z, ys)):
+        join_levels(z, y * z.nz + row, left_ref, right_ref, joined_ref, i)
     base_sides(z, tiles_ref, rates_ref, x_faces, arrhenius_ref, proportions_ref, base_ref)
     _, ys = halo_rows(z)
     zero = jnp.zeros(z.tile, F32)
@@ -548,7 +585,7 @@
 
 def second_kernel(
     z, tiles_ref, halo_ref, rates_ref, y_faces, z_faces, left_ref, right_ref, inverse_ref, base_ref,
-    inner_ref, v_ref, u_ref, *refs
+    inner_ref, joined_ref, v_ref, u_ref, *refs
 ):
     halos = 1 if z.gy == 2 else 2
     received = refs[:halos]
@@ -559,6 +596,7 @@
     right_sides(
         z, places_of(z, ys), tiles_ref, base_ref, lambda side, y: halo_ref[side * z.ny + y],
         y_halos(z, received), rates_ref, y_faces, z_faces, left_ref, right_ref, inverse_ref, f_ref,
+        lambda n, i: joined_ref[n, i],
     )
     send_sums(z, f_ref, v_ref, u_ref, pay_ref)
 
@@ -659,16 +697,16 @@
         [pltpu.VMEM((z.tiles, z.nx), F32)],
     )
     x_solve = [left, right, inverse]
-    early, y_faces = call(
+    early, y_faces, edge_joined = call(
         early_kernel,
-        [block, faces],
+        [block, faces, shaped(4 * z.pairs, len(edge_places(z)), *z.tile)],
         [arguments, tiles, base, rates, *x_solve, *received],
         [pltpu.VMEM((2, z.tiles, z.nx), F32)],
     )
     pay, f, z_faces = call(
         first_kernel,
         [shaped(z.block_rows, z.nx), block, faces],
-        [arguments, far, near, tiles, base, rates, *x_solve, early, y_faces, *received],
+        [arguments, far, near, tiles, base, rates, *x_solve, early, y_faces, edge_joined, *received],
         [pltpu.VMEM((z.edge_rows, z.nx), F32)] * 2,
     )
     inside = exchange(pay, z.members, 1)
@@ -700,15 +738,16 @@
 
     received = swap(sends)
     tiles, halo = call(rows_kernel, [block, shaped(2 * z.ny, *z.tile)], [f, v, u, ends, sums])
-    base, f = call(
+    rows_with_halo = 1 if z.gy == 2 else z.ny
+    base, f, joined = call(
         inner_kernel,
-        [block, block],
+        [block, block, shaped(4 * z.pairs, rows_with_halo * z.nz, *z.tile)],
         [tiles, halo, rates, x_faces, arrhenius, proportions, y_faces, z_faces, *x_solve],
     )
     pay, f = call(
         second_kernel,
         [shaped(2, z.lines, z.nx), block],
-        [tiles, halo, rates, y_faces, z_faces, *x_solve, base, f, v, u, *received],
+        [tiles, halo, rates, y_faces, z_faces, *x_solve, base, f, joined, v, u, *received],
     )
     inside = exchange(pay, z.members, 1)
     within, *totals = call(

time: 41.2 us -> 41 us (level)
  no operation moved by 1% of the time
where the time goes in v8:
time: 41 us; the launch traced here: 40.8 us
  starting transfers between devices  21.3 us (52%)
  waiting for transfers between devices  12.8 us (31%)
  Pallas kernels  5.61 us (14%)
  other arithmetic  0.95 us (2%)
    ppermute x10, starting transfers between devices, exchange(): return [lax.ppermute(v, 'gz', p) for v, p in zip(values, pairs)]  15.6 us
    ppermute x10, waiting for transfers between devices, exchange(): return [lax.ppermute(v, 'gz', p) for v, p in zip(values, pairs)]  10.4 us
    pallas_call x14, Pallas kernels, call(): pl.pallas_call(functools.partial(kernel, z), out_shape=outs, in_specs=[sp...  5.61 us
    ppermute x3, starting transfers between devices, exchange(): lax.ppermute(v, 'gz', p)  4.45 us
    ppermute x3, waiting for transfers between devices, exchange(): lax.ppermute(v, 'gz', p)  2.14 us
    ppermute x4, starting transfers between devices, shift(): lax.ppermute(value, axis, [(i, (i + by) % count) for i in range(count)])  1.1 us
    concatenate x1, other arithmetic, per_device(): arguments = jnp.concatenate([v.reshape(-1, z.nx) for v in (c, k, warm)])  0.95 us
  transfers between devices with their start and end apart: 18, of which 11 were waited for; matrix products, arithmetic and copies ran while one was open for 0% of the time, Pallas kernels for 8%

profile of v8, /device:TPU:0, one launch (start us, length us, event | category | flops | bytes accessed | tf_op | source)
XLA Modules:
  0.0 40.8 jit_solution(11106267474953086336)
XLA Ops:
  0.0 0.9 %pad_maximum_fusion.c_ref.arguments = f32[288,128]{1,0:T(8,128)S(1)} fusion(f32[16,128]{1,0:T(8,128)} %bitcast.10, f32[16,128]{1,0:T(8,128)} %bitcast.11, f32[256,128]{1,0:T(8,128)} %bitcast.9), kind=kLoop, calls=%fused_computation | loop fusion | flops 73728 | bytes 294912 | tf_op jit(solution)/shard_map/concatenate | solution.py:655
  1.0 0.5 %collective-permute-start.4 = (f32[136,128]{1,0:T(8,128)S(1)}, f32[136,128]{1,0:T(8,128)S(1)}, u32[]{:S(2)}, u32[]{:S(2)}) collective-permute-start(f32[136,128]{1,0:T(8,128)S(1)} %get-tuple-element.49), channel_id=1, source_target_pairs={{0,1},{1,0},{2,3},{3,2},{4,5},{5,4},{6,7},{7,6},{8,9},{9,8},{10,11... | collective-permute-start | bytes 208904 | tf_op jit(solution)/shard_map/ppermute | solution.py:650
  1.5 0.1 collective-permute-start
  1.6 4.0 %collective-permute-start.1 = (f32[40,128]{1,0:T(8,128)S(1)}, f32[40,128]{1,0:T(8,128)S(1)}, u32[]{:S(2)}, u32[]{:S(2)}) collective-permute-start(f32[40,128]{1,0:T(8,128)S(1)} %get-tuple-element.41), channel_id=1, source_target_pairs={{0,2},{2,0},{4,6},{6,4},{8,10},{10,8},{12,14},{14,12},{16,18},{18,... | collective-permute-start | bytes 61448 | tf_op jit(solution)/shard_map/ppermute | solution.py:665
  5.6 0.0 collective-permute-start.2
  5.6 0.5 %collective-permute-start.3 = (f32[16]{0:T(128)S(1)}, f32[16]{0:T(128)S(1)}, u32[]{:S(2)}, u32[]{:S(2)}) collective-permute-start(f32[16]{0:T(128)S(1)} %copy-done.3), channel_id=1, source_target_pairs={{0,1},{1,0},{2,3},{3,2},{4,5},{5,4},{6,7},{7,6},{8,9},{9,8},{10,11... | collective-permute-start | bytes 200 | tf_op jit(solution)/shard_map/ppermute | solution.py:650
  6.1 1.1 %shard_map.74 = (f32[4,16,128]{2,1,0:T(8,128)S(1)}, f32[2,16,128]{2,1,0:T(8,128)S(1)}, f32[7,16,16,128]{3,2,1,0:T(8,128)S(1)}, f32[7,16,16,128]{3,2,1,0:T(8,128)S(1)}, f32[16,16,128]{2,1,0:T(8,128)S(1)}) custom-call(f32[288,128]{1,0:T(8,128)S(1)} %pad_maximum_fusion.c_ref.arguments, f32[1,16]{1,0:T(1,128)S(1)} %bitcast.6), custom_call_target="tpu_custom_call" | custom-call | bytes 3690000 | tf_op jit(solution)/shard_map/pallas_call | solution.py:636
  7.2 0.0 collective-permute-done.2
  7.2 0.0 collective-permute-done.3
  7.2 0.4 shard_map.75
  7.6 0.0 collective-permute-done.4.refs_0_
  7.6 0.7 %shard_map.76 = (f32[16,16,128]{2,1,0:T(8,128)S(1)}, f32[2,16,128]{2,1,0:T(8,128)S(1)}, f32[12,4,16,128]{3,2,1,0:T(8,128)S(1)}) custom-call(f32[288,128]{1,0:T(8,128)S(1)} %pad_maximum_fusion.c_ref.arguments, f32[16,16,128]{2,1,0:T(8,128)S(1)} %get-tuple-element.44.tiles_ref, f32[16,16,128]{2,1,0:T(8,128)S(1)} %get-tuple-element.45.base_ref, ...), custom_call_target="tpu_custom_call" | custom-call | bytes 1845000 | tf_op jit(solution)/shard_map/pallas_call | solution.py:636
  8.3 0.0 collective-permute-done.far_ref
  8.3 0.0 collective-permute-done.1.near_ref
  8.3 0.4 %shard_map.77 = (f32[88,128]{1,0:T(8,128)S(1)}, f32[16,16,128]{2,1,0:T(8,128)S(1)}, f32[2,16,128]{2,1,0:T(8,128)S(1)}) custom-call(f32[288,128]{1,0:T(8,128)S(1)} %pad_maximum_fusion.c_ref.arguments, f32[40,128]{1,0:T(8,128)S(1)} %collective-permute-done.far_ref, f32[40,128]{1,0:T(8,128)S(1)} %collective-permute-done.1.near_ref, ...), custom_call_target="tpu_custom_call" | custom-call | bytes 1845000 | tf_op jit(solution)/shard_map/pallas_call | solution.py:636
  8.7 2.4 %collective-permute-start.7 = (f32[88,128]{1,0:T(8,128)S(1)}, f32[88,128]{1,0:T(8,128)S(1)}, u32[]{:S(2)}, u32[]{:S(2)}) collective-permute-start(f32[88,128]{1,0:T(8,128)S(1)} %get-tuple-element.54.pay_ref.refs_0_), channel_id=1, source_target_pairs={{0,6},{2,4},{4,2},{6,0},{8,14},{10,12},{12,10},{14,8},{16,22},{18,... | collective-permute-start | bytes 135176 | tf_op jit(solution)/shard_map/ppermute | solution.py:665
  11.1 0.2 collective-permute-start.6
  11.4 0.9 %collective-permute-start.5 = (f32[88,128]{1,0:T(8,128)S(1)}, f32[88,128]{1,0:T(8,128)S(1)}, u32[]{:S(2)}, u32[]{:S(2)}) collective-permute-start(f32[88,128]{1,0:T(8,128)S(1)} %get-tuple-element.54.pay_ref.refs_0_), channel_id=1, source_target_pairs={{0,2},{2,0},{4,6},{6,4},{8,10},{10,8},{12,14},{14,12},{16,18},{18,... | collective-permute-start | bytes 135176 | tf_op jit(solution)/shard_map/ppermute | solution.py:665
  12.3 1.5 %collective-permute-done.7.refs_2_.refs_3_ = f32[88,128]{1,0:T(8,128)S(1)} collective-permute-done((f32[88,128]{1,0:T(8,128)S(1)}, f32[88,128]{1,0:T(8,128)S(1)}, u32[]{:S(2)}, u32[]{:S(2)}) %collective-permute-start.7) | collective-permute-done | bytes 45088 | tf_op jit(solution)/shard_map/ppermute | solution.py:665
  13.8 1.4 %collective-permute-done.6.refs_1_.refs_2_ = f32[88,128]{1,0:T(8,128)S(1)} collective-permute-done((f32[88,128]{1,0:T(8,128)S(1)}, f32[88,128]{1,0:T(8,128)S(1)}, u32[]{:S(2)}, u32[]{:S(2)}) %collective-permute-start.6) | collective-permute-done | bytes 45088 | tf_op jit(solution)/shard_map/ppermute | solution.py:665
  15.2 0.2 collective-permute-done.5.refs_0_.refs_1_
  15.4 0.1 shard_map.78.own_group
  15.6 3.9 %collective-permute-start.8 = (f32[136,128]{1,0:T(8,128)S(1)}, f32[136,128]{1,0:T(8,128)S(1)}, u32[]{:S(2)}, u32[]{:S(2)}) collective-permute-start(f32[136,128]{1,0:T(8,128)S(1)} %shard_map.78.own_group), channel_id=1, source_target_pairs={{0,24},{2,26},{4,28},{6,30},{8,16},{10,18},{12,20},{14,22},{16,8},... | collective-permute-start | bytes 208904 | tf_op jit(solution)/shard_map/ppermute | solution.py:665
  19.5 0.0 collective-permute-start.10
  19.5 0.6 %collective-permute-start.9 = (f32[136,128]{1,0:T(8,128)S(1)}, f32[136,128]{1,0:T(8,128)S(1)}, u32[]{:S(2)}, u32[]{:S(2)}) collective-permute-start(f32[136,128]{1,0:T(8,128)S(1)} %shard_map.78.own_group), channel_id=1, source_target_pairs={{0,8},{2,10},{4,12},{6,14},{8,0},{10,2},{12,4},{14,6},{16,24},{18,... | collective-permute-start | bytes 208904 | tf_op jit(solution)/shard_map/ppermute | solution.py:665
  20.1 0.1 shard_map.79
  20.2 1.7 %collective-permute-done.8.group_ref.refs_2_ = f32[136,128]{1,0:T(8,128)S(1)} collective-permute-done((f32[136,128]{1,0:T(8,128)S(1)}, f32[136,128]{1,0:T(8,128)S(1)}, u32[]{:S(2)}, u32[]{:S(2)}) %collective-permute-start.8) | collective-permute-done | bytes 69664 | tf_op jit(solution)/shard_map/ppermute | solution.py:665
  22.0 0.1 shard_map.80.far_transfer
  22.1 2.7 %collective-permute-done.10.refs_1_ = f32[136,128]{1,0:T(8,128)S(1)} collective-permute-done((f32[136,128]{1,0:T(8,128)S(1)}, f32[136,128]{1,0:T(8,128)S(1)}, u32[]{:S(2)}, u32[]{:S(2)}) %collective-permute-start.10) | collective-permute-done | bytes 69664 | tf_op jit(solution)/shard_map/ppermute | solution.py:665
  24.9 0.5 %shard_map.81 = (f32[16,16,128]{2,1,0:T(8,128)S(1)}, f32[16,16,128]{2,1,0:T(8,128)S(1)}, f32[10,16,128]{2,1,0:T(8,128)S(1)}, f32[4,16,128]{2,1,0:T(8,128)S(1)}, f32[128,128]{1,0:T(8,128)S(1)}) custom-call(f32[4,16,128]{2,1,0:T(8,128)S(1)} %get-tuple-element.42.rates_ref, f32[16,16,128]{2,1,0:T(8,128)S(1)} %get-tuple-element.53.f_ref, ...), custom_call_target="tpu_custom_call" | custom-call | bytes 1845000 | tf_op jit(solution)/shard_map/pallas_call | solution.py:636
  25.4 0.1 collective-permute-start.11
  25.4 0.1 shard_map.82
  25.5 0.9 %shard_map.83 = (f32[16,16,128]{2,1,0:T(8,128)S(1)}, f32[16,16,128]{2,1,0:T(8,128)S(1)}, f32[12,8,16,128]{3,2,1,0:T(8,128)S(1)}) custom-call(f32[16,16,128]{2,1,0:T(8,128)S(1)} %get-tuple-element.61.tiles_ref, f32[4,16,128]{2,1,0:T(8,128)S(1)} %get-tuple-element.62.halo_ref, f32[4,16,128]{2,1,0:T(8,128)S(1)} %get-tuple-element.42.rates_ref, ...), custom_call_target="tpu_custom_call" | custom-call | bytes 1845000 | tf_op jit(solution)/shard_map/pallas_call | solution.py:636
  26.4 0.3 collective-permute-done.11.refs_0_
  26.7 0.5 %shard_map.84 = (f32[2,32,128]{2,1,0:T(8,128)S(1)}, f32[16,16,128]{2,1,0:T(8,128)S(1)}) custom-call(f32[16,16,128]{2,1,0:T(8,128)S(1)} %get-tuple-element.61.tiles_ref, f32[4,16,128]{2,1,0:T(8,128)S(1)} %get-tuple-element.62.halo_ref, f32[4,16,128]{2,1,0:T(8,128)S(1)} %get-tuple-element.42.rates_ref, f32[2,16,128]{2,1,0:T(8,128)S(1)} %get-tuple-element.51.y_faces, ...), custom_call_target="tpu_custom_call" | custom-call | bytes 1845000 | tf_op jit(solution)/shard_map/pallas_call | solution.py:636
  27.1 1.6 %collective-permute-start.14 = (f32[2,32,128]{2,1,0:T(8,128)S(1)}, f32[2,32,128]{2,1,0:T(8,128)S(1)}, u32[]{:S(2)}, u32[]{:S(2)}) collective-permute-start(f32[2,32,128]{2,1,0:T(8,128)S(1)} %get-tuple-element.69.pay_ref), channel_id=1, source_target_pairs={{0,6},{2,4},{4,2},{6,0},{8,14},{10,12},{12,10},{14,8},{16,22},{18,... | collective-permute-start | bytes 98312 | tf_op jit(solution)/shard_map/ppermute | solution.py:665
  28.8 0.8 %collective-permute-start.13 = (f32[2,32,128]{2,1,0:T(8,128)S(1)}, f32[2,32,128]{2,1,0:T(8,128)S(1)}, u32[]{:S(2)}, u32[]{:S(2)}) collective-permute-start(f32[2,32,128]{2,1,0:T(8,128)S(1)} %get-tuple-element.69.pay_ref), channel_id=1, source_target_pairs={{0,4},{2,6},{4,0},{6,2},{8,12},{10,14},{12,8},{14,10},{16,20},{18,... | collective-permute-start | bytes 98312 | tf_op jit(solution)/shard_map/ppermute | solution.py:665
  29.6 1.1 %collective-permute-start.12 = (f32[2,32,128]{2,1,0:T(8,128)S(1)}, f32[2,32,128]{2,1,0:T(8,128)S(1)}, u32[]{:S(2)}, u32[]{:S(2)}) collective-permute-start(f32[2,32,128]{2,1,0:T(8,128)S(1)} %get-tuple-element.69.pay_ref), channel_id=1, source_target_pairs={{0,2},{2,0},{4,6},{6,4},{8,10},{10,8},{12,14},{14,12},{16,18},{18,... | collective-permute-start | bytes 98312 | tf_op jit(solution)/shard_map/ppermute | solution.py:665
  30.7 1.3 %collective-permute-done.14.refs_2_ = f32[2,32,128]{2,1,0:T(8,128)S(1)} collective-permute-done((f32[2,32,128]{2,1,0:T(8,128)S(1)}, f32[2,32,128]{2,1,0:T(8,128)S(1)}, u32[]{:S(2)}, u32[]{:S(2)}) %collective-permute-start.14) | collective-permute-done | bytes 32800 | tf_op jit(solution)/shard_map/ppermute | solution.py:665
  32.0 0.6 %collective-permute-done.13.refs_1_ = f32[2,32,128]{2,1,0:T(8,128)S(1)} collective-permute-done((f32[2,32,128]{2,1,0:T(8,128)S(1)}, f32[2,32,128]{2,1,0:T(8,128)S(1)}, u32[]{:S(2)}, u32[]{:S(2)}) %collective-permute-start.13) | collective-permute-done | bytes 32800 | tf_op jit(solution)/shard_map/ppermute | solution.py:665
  32.7 0.8 %collective-permute-done.12.refs_0_ = f32[2,32,128]{2,1,0:T(8,128)S(1)} collective-permute-done((f32[2,32,128]{2,1,0:T(8,128)S(1)}, f32[2,32,128]{2,1,0:T(8,128)S(1)}, u32[]{:S(2)}, u32[]{:S(2)}) %collective-permute-start.12) | collective-permute-done | bytes 32800 | tf_op jit(solution)/shard_map/ppermute | solution.py:665
  33.5 1.9 %collective-permute-start.15 = (f32[32,128]{1,0:T(8,128)S(1)}, f32[32,128]{1,0:T(8,128)S(1)}, u32[]{:S(2)}, u32[]{:S(2)}) collective-permute-start(f32[32,128]{1,0:T(8,128)S(1)} %get-tuple-element.72), channel_id=1, source_target_pairs={{0,24},{2,26},{4,28},{6,30},{8,16},{10,18},{12,20},{14,22},{16,8},... | collective-permute-start | bytes 49160 | tf_op jit(solution)/shard_map/ppermute | solution.py:664
  35.5 0.2 collective-permute-start.16
  35.7 2.3 %collective-permute-start.17 = (f32[32,128]{1,0:T(8,128)S(1)}, f32[32,128]{1,0:T(8,128)S(1)}, u32[]{:S(2)}, u32[]{:S(2)}) collective-permute-start(f32[32,128]{1,0:T(8,128)S(1)} %get-tuple-element.74), channel_id=1, source_target_pairs={{0,8},{2,10},{4,12},{6,14},{8,0},{10,2},{12,4},{14,6},{16,24},{18,... | collective-permute-start | bytes 49160 | tf_op jit(solution)/shard_map/ppermute | solution.py:664
  38.0 1.1 %collective-permute-done.15.refs_0_ = f32[32,128]{1,0:T(8,128)S(1)} collective-permute-done((f32[32,128]{1,0:T(8,128)S(1)}, f32[32,128]{1,0:T(8,128)S(1)}, u32[]{:S(2)}, u32[]{:S(2)}) %collective-permute-start.15) | collective-permute-done | bytes 16416 | tf_op jit(solution)/shard_map/ppermute | solution.py:664
  39.1 1.0 %collective-permute-done.16.refs_1_ = f32[32,128]{1,0:T(8,128)S(1)} collective-permute-done((f32[32,128]{1,0:T(8,128)S(1)}, f32[32,128]{1,0:T(8,128)S(1)}, u32[]{:S(2)}, u32[]{:S(2)}) %collective-permute-start.16) | collective-permute-done | bytes 16416 | tf_op jit(solution)/shard_map/ppermute | solution.py:664
  40.1 0.0 collective-permute-done.17.refs_2_
  40.1 0.7 %shard_map.86 = f32[16,2,8,128]{3,2,1,0:T(8,128)} custom-call(f32[2,32,128]{2,1,0:T(8,128)S(1)} %get-tuple-element.70.within_ref, f32[16,16,128]{2,1,0:T(8,128)S(1)} %get-tuple-element.71.f_ref, f32[16,16,128]{2,1,0:T(8,128)S(1)} %get-tuple-element.57.v_ref, f32[16,16,128]{2,1,0:T(8,128)S(1)} %get-tuple-element.58.u_ref, ...), custom_call_target="tpu_custom_call" | custom-call | bytes 1845000 | tf_op jit(solution)/shard_map/pallas_call | solution.py:636
  (11 shorter events, 0.1 us)
Async XLA Ops:
  1.0 6.6 %collective-permute-start.4 = (f32[136,128]{1,0:T(8,128)S(1)}, f32[136,128]{1,0:T(8,128)S(1)}, u32[]{:S(2)}, u32[]{:S(2)}) collective-permute-start(f32[136,128]{1,0:T(8,128)S(1)} %get-tuple-element.49), channel_id=1, source_target_pairs={{0,1},{1,0},{2,3},{3,2},{4,5},{5,4},{6,7},{7,6},{8,9},{9,8},{10,11... | collective-permute-start | bytes 208904 | tf_op jit(solution)/shard_map/ppermute | solution.py:650
  1.5 4.1 %copy-start.2 = (f32[16]{0:T(128)S(1)}, f32[16]{0:T(128)}, u32[]{:S(2)}) copy-start(f32[16]{0:T(128)} %param.11) | copy-start | bytes 196
  1.5 4.1 %copy-start.3 = (f32[16]{0:T(128)S(1)}, f32[16]{0:T(128)}, u32[]{:S(2)}) copy-start(f32[16]{0:T(128)} %param.12) | copy-start | bytes 196
  1.5 6.8 %collective-permute-start = (f32[40,128]{1,0:T(8,128)S(1)}, f32[40,128]{1,0:T(8,128)S(1)}, u32[]{:S(2)}, u32[]{:S(2)}) collective-permute-start(f32[40,128]{1,0:T(8,128)S(1)} %get-tuple-element.40), channel_id=1, source_target_pairs={{2,4},{3,5},{4,2},{5,3},{6,8},{7,9},{8,6},{9,7},{10,12},{11,13},{1... | collective-permute-start | bytes 61448 | tf_op jit(solution)/shard_map/ppermute | solution.py:674
  1.6 4.5 %copy-start.1 = (f32[16]{0:T(128)S(1)}, f32[16]{0:T(128)}, u32[]{:S(2)}) copy-start(f32[16]{0:T(128)} %param.10) | copy-start | bytes 196
  1.6 6.7 %collective-permute-start.1 = (f32[40,128]{1,0:T(8,128)S(1)}, f32[40,128]{1,0:T(8,128)S(1)}, u32[]{:S(2)}, u32[]{:S(2)}) collective-permute-start(f32[40,128]{1,0:T(8,128)S(1)} %get-tuple-element.41), channel_id=1, source_target_pairs={{0,2},{2,0},{4,6},{6,4},{8,10},{10,8},{12,14},{14,12},{16,18},{18,... | collective-permute-start | bytes 61448 | tf_op jit(solution)/shard_map/ppermute | solution.py:665
  5.6 1.6 %collective-permute-start.2 = (f32[16]{0:T(128)S(1)}, f32[16]{0:T(128)S(1)}, u32[]{:S(2)}, u32[]{:S(2)}) collective-permute-start(f32[16]{0:T(128)S(1)} %copy-done.2), channel_id=1, source_target_pairs={{0,1},{1,0},{2,3},{3,2},{4,5},{5,4},{6,7},{7,6},{8,9},{9,8},{10,11... | collective-permute-start | bytes 200 | tf_op jit(solution)/shard_map/ppermute | solution.py:650
  5.6 1.6 %collective-permute-start.3 = (f32[16]{0:T(128)S(1)}, f32[16]{0:T(128)S(1)}, u32[]{:S(2)}, u32[]{:S(2)}) collective-permute-start(f32[16]{0:T(128)S(1)} %copy-done.3), channel_id=1, source_target_pairs={{0,1},{1,0},{2,3},{3,2},{4,5},{5,4},{6,7},{7,6},{8,9},{9,8},{10,11... | collective-permute-start | bytes 200 | tf_op jit(solution)/shard_map/ppermute | solution.py:650
  6.1 1.1 %copy-start = (f32[16,16]{1,0:T(8,128)S(1)}, f32[16,16]{1,0:T(8,128)}, u32[]{:S(2)}) copy-start(f32[16,16]{1,0:T(8,128)} %proportions_ref.3) | copy-start | bytes 3076
  8.7 5.1 %collective-permute-start.7 = (f32[88,128]{1,0:T(8,128)S(1)}, f32[88,128]{1,0:T(8,128)S(1)}, u32[]{:S(2)}, u32[]{:S(2)}) collective-permute-start(f32[88,128]{1,0:T(8,128)S(1)} %get-tuple-element.54.pay_ref.refs_0_), channel_id=1, source_target_pairs={{0,6},{2,4},{4,2},{6,0},{8,14},{10,12},{12,10},{14,8},{16,22},{18,... | collective-permute-start | bytes 135176 | tf_op jit(solution)/shard_map/ppermute | solution.py:665
  11.1 4.0 %collective-permute-start.6 = (f32[88,128]{1,0:T(8,128)S(1)}, f32[88,128]{1,0:T(8,128)S(1)}, u32[]{:S(2)}, u32[]{:S(2)}) collective-permute-start(f32[88,128]{1,0:T(8,128)S(1)} %get-tuple-element.54.pay_ref.refs_0_), channel_id=1, source_target_pairs={{0,4},{2,6},{4,0},{6,2},{8,12},{10,14},{12,8},{14,10},{16,20},{18,... | collective-permute-start | bytes 135176 | tf_op jit(solution)/shard_map/ppermute | solution.py:665
  11.4 4.0 %collective-permute-start.5 = (f32[88,128]{1,0:T(8,128)S(1)}, f32[88,128]{1,0:T(8,128)S(1)}, u32[]{:S(2)}, u32[]{:S(2)}) collective-permute-start(f32[88,128]{1,0:T(8,128)S(1)} %get-tuple-element.54.pay_ref.refs_0_), channel_id=1, source_target_pairs={{0,2},{2,0},{4,6},{6,4},{8,10},{10,8},{12,14},{14,12},{16,18},{18,... | collective-permute-start | bytes 135176 | tf_op jit(solution)/shard_map/ppermute | solution.py:665
  15.6 6.4 %collective-permute-start.8 = (f32[136,128]{1,0:T(8,128)S(1)}, f32[136,128]{1,0:T(8,128)S(1)}, u32[]{:S(2)}, u32[]{:S(2)}) collective-permute-start(f32[136,128]{1,0:T(8,128)S(1)} %shard_map.78.own_group), channel_id=1, source_target_pairs={{0,24},{2,26},{4,28},{6,30},{8,16},{10,18},{12,20},{14,22},{16,8},... | collective-permute-start | bytes 208904 | tf_op jit(solution)/shard_map/ppermute | solution.py:665
  19.5 5.4 %collective-permute-start.10 = (f32[136,128]{1,0:T(8,128)S(1)}, f32[136,128]{1,0:T(8,128)S(1)}, u32[]{:S(2)}, u32[]{:S(2)}) collective-permute-start(f32[136,128]{1,0:T(8,128)S(1)} %shard_map.78.own_group), channel_id=1, source_target_pairs={{0,16},{2,18},{4,20},{6,22},{8,24},{10,26},{12,28},{14,30},{16,0},... | collective-permute-start | bytes 208904 | tf_op jit(solution)/shard_map/ppermute | solution.py:665
  19.5 5.4 %collective-permute-start.9 = (f32[136,128]{1,0:T(8,128)S(1)}, f32[136,128]{1,0:T(8,128)S(1)}, u32[]{:S(2)}, u32[]{:S(2)}) collective-permute-start(f32[136,128]{1,0:T(8,128)S(1)} %shard_map.78.own_group), channel_id=1, source_target_pairs={{0,8},{2,10},{4,12},{6,14},{8,0},{10,2},{12,4},{14,6},{16,24},{18,... | collective-permute-start | bytes 208904 | tf_op jit(solution)/shard_map/ppermute | solution.py:665
  25.4 1.3 %collective-permute-start.11 = (f32[128,128]{1,0:T(8,128)S(1)}, f32[128,128]{1,0:T(8,128)S(1)}, u32[]{:S(2)}, u32[]{:S(2)}) collective-permute-start(f32[128,128]{1,0:T(8,128)S(1)} %get-tuple-element.68), channel_id=1, source_target_pairs={{0,1},{1,0},{2,3},{3,2},{4,5},{5,4},{6,7},{7,6},{8,9},{9,8},{10,11... | collective-permute-start | bytes 196616 | tf_op jit(solution)/shard_map/ppermute | solution.py:650
  27.1 4.9 %collective-permute-start.14 = (f32[2,32,128]{2,1,0:T(8,128)S(1)}, f32[2,32,128]{2,1,0:T(8,128)S(1)}, u32[]{:S(2)}, u32[]{:S(2)}) collective-permute-start(f32[2,32,128]{2,1,0:T(8,128)S(1)} %get-tuple-element.69.pay_ref), channel_id=1, source_target_pairs={{0,6},{2,4},{4,2},{6,0},{8,14},{10,12},{12,10},{14,8},{16,22},{18,... | collective-permute-start | bytes 98312 | tf_op jit(solution)/shard_map/ppermute | solution.py:665
  28.8 3.9 %collective-permute-start.13 = (f32[2,32,128]{2,1,0:T(8,128)S(1)}, f32[2,32,128]{2,1,0:T(8,128)S(1)}, u32[]{:S(2)}, u32[]{:S(2)}) collective-permute-start(f32[2,32,128]{2,1,0:T(8,128)S(1)} %get-tuple-element.69.pay_ref), channel_id=1, source_target_pairs={{0,4},{2,6},{4,0},{6,2},{8,12},{10,14},{12,8},{14,10},{16,20},{18,... | collective-permute-start | bytes 98312 | tf_op jit(solution)/shard_map/ppermute | solution.py:665
  29.6 3.9 %collective-permute-start.12 = (f32[2,32,128]{2,1,0:T(8,128)S(1)}, f32[2,32,128]{2,1,0:T(8,128)S(1)}, u32[]{:S(2)}, u32[]{:S(2)}) collective-permute-start(f32[2,32,128]{2,1,0:T(8,128)S(1)} %get-tuple-element.69.pay_ref), channel_id=1, source_target_pairs={{0,2},{2,0},{4,6},{6,4},{8,10},{10,8},{12,14},{14,12},{16,18},{18,... | collective-permute-start | bytes 98312 | tf_op jit(solution)/shard_map/ppermute | solution.py:665
  33.5 5.6 %collective-permute-start.15 = (f32[32,128]{1,0:T(8,128)S(1)}, f32[32,128]{1,0:T(8,128)S(1)}, u32[]{:S(2)}, u32[]{:S(2)}) collective-permute-start(f32[32,128]{1,0:T(8,128)S(1)} %get-tuple-element.72), channel_id=1, source_target_pairs={{0,24},{2,26},{4,28},{6,30},{8,16},{10,18},{12,20},{14,22},{16,8},... | collective-permute-start | bytes 49160 | tf_op jit(solution)/shard_map/ppermute | solution.py:664
  35.5 4.6 %collective-permute-start.16 = (f32[32,128]{1,0:T(8,128)S(1)}, f32[32,128]{1,0:T(8,128)S(1)}, u32[]{:S(2)}, u32[]{:S(2)}) collective-permute-start(f32[32,128]{1,0:T(8,128)S(1)} %get-tuple-element.73), channel_id=1, source_target_pairs={{0,16},{2,18},{4,20},{6,22},{8,24},{10,26},{12,28},{14,30},{16,0},... | collective-permute-start | bytes 49160 | tf_op jit(solution)/shard_map/ppermute | solution.py:664
  35.7 4.4 %collective-permute-start.17 = (f32[32,128]{1,0:T(8,128)S(1)}, f32[32,128]{1,0:T(8,128)S(1)}, u32[]{:S(2)}, u32[]{:S(2)}) collective-permute-start(f32[32,128]{1,0:T(8,128)S(1)} %get-tuple-element.74), channel_id=1, source_target_pairs={{0,8},{2,10},{4,12},{6,14},{8,0},{10,2},{12,4},{14,6},{16,24},{18,... | collective-permute-start | bytes 49160 | tf_op jit(solution)/shard_map/ppermute | solution.py:664

commit v9 on v8

--- a/solution.py
+++ b/solution.py
@@ -24,6 +24,7 @@
         self.edge_rows = self.lines + padded
         self.members = 1 << (self.devices.bit_length() // 2)
         self.groups_z = self.devices // self.members
+        self.partners = (1, 3, 2) if self.members == 4 else tuple(range(1, self.members))
         self.faces_at = 2 * self.lines
         self.block_rows = self.faces_at + self.tiles + padded
         self.group_top = self.faces_at + self.members * self.tiles
@@ -258,8 +259,8 @@
     group, member = me // z.members, me % z.members
     below = above = jnp.zeros((z.lines, z.nx), F32)
     rising, falling = pay_ref[0], pay_ref[1]
-    for i, ref in enumerate(inside):
-        lower = (member ^ (i + 1)) < member
+    for k, ref in zip(z.partners, inside):
+        lower = (member ^ k) < member
         up, down = ref[0], ref[1]
         rising, falling = rising + up, falling + down
         below = below + jnp.where(lower, up, 0.0)
@@ -371,8 +372,8 @@
     *received, group_ref, order = refs
     me = lax.axis_index("gz") % z.members
     order[me] = pay_ref[...]
-    for i, ref in enumerate(received):
-        order[me ^ (i + 1)] = ref[...]
+    for k, ref in zip(z.partners, received):
+        order[me ^ k] = ref[...]
     ohms = rates_ref[3]
     zero, one = jnp.zeros(z.tile, F32), jnp.ones(z.tile, F32)
     for y in range(z.ny):
@@ -417,10 +418,10 @@
 def inside_kernel(z, rates_ref, *refs):
     *blocks, sums_ref, transfers_ref = refs
     me = lax.axis_index("gz") % z.members
-    for i, matrix in enumerate(transfers(z, rates_ref, blocks, 1)):
-        sums_ref[me ^ i] = blocks[i][: 2 * z.lines, :]
+    for k, ref, matrix in zip((0, *z.partners), blocks, transfers(z, rates_ref, blocks, 1)):
+        sums_ref[me ^ k] = ref[: 2 * z.lines, :]
         for n, value in enumerate(matrix):
-            transfers_ref[me ^ i, n] = value
+            transfers_ref[me ^ k, n] = value
 
 
 def far_kernel(z, rates_ref, group_ref, out_ref):
@@ -664,6 +665,10 @@
             return [lax.ppermute(v, "gz", p) for v, p in zip(values[::-1], pairs[::-1])][::-1]
         return [lax.ppermute(v, "gz", p) for v, p in zip(values, pairs)]
 
+    def exchange_inside(value):
+        received = exchange(value, z.members, 1)
+        return [received[k - 1] for k in z.partners]
+
     def neighbours(near, far):
         last = z.devices - 1
         links = [(i, i + 1) for i in range(1, last, 2)]
@@ -709,7 +714,7 @@
         [arguments, far, near, tiles, base, rates, *x_solve, early, y_faces, edge_joined, *received],
         [pltpu.VMEM((z.edge_rows, z.nx), F32)] * 2,
     )
-    inside = exchange(pay, z.members, 1)
+    inside = exchange_inside(pay)
     group = call(
         merge_kernel,
         shaped(z.group_rows, z.nx),
@@ -749,7 +754,7 @@
         [shaped(2, z.lines, z.nx), block],
         [tiles, halo, rates, y_faces, z_faces, *x_solve, base, f, joined, v, u, *received],
     )
-    inside = exchange(pay, z.members, 1)
+    inside = exchange_inside(pay)
     within, *totals = call(
         total_kernel,
         [shaped(2, z.lines, z.nx)] + [shaped(z.lines, z.nx)] * (z.groups_z - 1),

time: 41 us -> 40.8 us (level)
  no operation moved by 1% of the time
where the time goes in v9:
time: 40.8 us; the launch traced here: 40.6 us
  starting transfers between devices  21.3 us (52%)
  waiting for transfers between devices  12.6 us (31%)
  Pallas kernels  5.61 us (14%)
  other arithmetic  0.95 us (2%)
    ppermute x10, starting transfers between devices, exchange(): return [lax.ppermute(v, 'gz', p) for v, p in zip(values, pairs)]  15.6 us
    ppermute x10, waiting for transfers between devices, exchange(): return [lax.ppermute(v, 'gz', p) for v, p in zip(values, pairs)]  10.4 us
    pallas_call x14, Pallas kernels, call(): pl.pallas_call(functools.partial(kernel, z), out_shape=outs, in_specs=[sp...  5.61 us
    ppermute x3, starting transfers between devices, exchange(): lax.ppermute(v, 'gz', p)  4.45 us
    ppermute x3, waiting for transfers between devices, exchange(): lax.ppermute(v, 'gz', p)  1.95 us
    ppermute x4, starting transfers between devices, shift(): lax.ppermute(value, axis, [(i, (i + by) % count) for i in range(count)])  1.1 us
    concatenate x1, other arithmetic, per_device(): arguments = jnp.concatenate([v.reshape(-1, z.nx) for v in (c, k, warm)])  0.95 us
  transfers between devices with their start and end apart: 18, of which 11 were waited for; matrix products, arithmetic and copies ran while one was open for 0% of the time, Pallas kernels for 8%

profile of v9, /device:TPU:0, one launch (start us, length us, event | category | flops | bytes accessed | tf_op | source)
XLA Modules:
  0.0 40.6 jit_solution(9511383155950127016)
XLA Ops:
  0.0 0.9 %pad_maximum_fusion.c_ref.arguments = f32[288,128]{1,0:T(8,128)S(1)} fusion(f32[16,128]{1,0:T(8,128)} %bitcast.10, f32[16,128]{1,0:T(8,128)} %bitcast.11, f32[256,128]{1,0:T(8,128)} %bitcast.9), kind=kLoop, calls=%fused_computation | loop fusion | flops 73728 | bytes 294912 | tf_op jit(solution)/shard_map/concatenate | solution.py:656
  1.0 0.5 %collective-permute-start.4 = (f32[136,128]{1,0:T(8,128)S(1)}, f32[136,128]{1,0:T(8,128)S(1)}, u32[]{:S(2)}, u32[]{:S(2)}) collective-permute-start(f32[136,128]{1,0:T(8,128)S(1)} %get-tuple-element.49), channel_id=1, source_target_pairs={{0,1},{1,0},{2,3},{3,2},{4,5},{5,4},{6,7},{7,6},{8,9},{9,8},{10,11... | collective-permute-start | bytes 208904 | tf_op jit(solution)/shard_map/ppermute | solution.py:651
  1.5 0.1 collective-permute-start
  1.6 4.0 %collective-permute-start.1 = (f32[40,128]{1,0:T(8,128)S(1)}, f32[40,128]{1,0:T(8,128)S(1)}, u32[]{:S(2)}, u32[]{:S(2)}) collective-permute-start(f32[40,128]{1,0:T(8,128)S(1)} %get-tuple-element.41), channel_id=1, source_target_pairs={{0,2},{2,0},{4,6},{6,4},{8,10},{10,8},{12,14},{14,12},{16,18},{18,... | collective-permute-start | bytes 61448 | tf_op jit(solution)/shard_map/ppermute | solution.py:666
  5.6 0.0 collective-permute-start.2
  5.6 0.5 %collective-permute-start.3 = (f32[16]{0:T(128)S(1)}, f32[16]{0:T(128)S(1)}, u32[]{:S(2)}, u32[]{:S(2)}) collective-permute-start(f32[16]{0:T(128)S(1)} %copy-done.3), channel_id=1, source_target_pairs={{0,1},{1,0},{2,3},{3,2},{4,5},{5,4},{6,7},{7,6},{8,9},{9,8},{10,11... | collective-permute-start | bytes 200 | tf_op jit(solution)/shard_map/ppermute | solution.py:651
  6.1 1.1 %shard_map.74 = (f32[4,16,128]{2,1,0:T(8,128)S(1)}, f32[2,16,128]{2,1,0:T(8,128)S(1)}, f32[7,16,16,128]{3,2,1,0:T(8,128)S(1)}, f32[7,16,16,128]{3,2,1,0:T(8,128)S(1)}, f32[16,16,128]{2,1,0:T(8,128)S(1)}) custom-call(f32[288,128]{1,0:T(8,128)S(1)} %pad_maximum_fusion.c_ref.arguments, f32[1,16]{1,0:T(1,128)S(1)} %bitcast.6), custom_call_target="tpu_custom_call" | custom-call | bytes 3690000 | tf_op jit(solution)/shard_map/pallas_call | solution.py:637
  7.2 0.0 collective-permute-done.2
  7.2 0.0 collective-permute-done.3
  7.2 0.4 shard_map.75
  7.6 0.0 collective-permute-done.4.refs_0_
  7.6 0.7 %shard_map.76 = (f32[16,16,128]{2,1,0:T(8,128)S(1)}, f32[2,16,128]{2,1,0:T(8,128)S(1)}, f32[12,4,16,128]{3,2,1,0:T(8,128)S(1)}) custom-call(f32[288,128]{1,0:T(8,128)S(1)} %pad_maximum_fusion.c_ref.arguments, f32[16,16,128]{2,1,0:T(8,128)S(1)} %get-tuple-element.44.tiles_ref, f32[16,16,128]{2,1,0:T(8,128)S(1)} %get-tuple-element.45.base_ref, ...), custom_call_target="tpu_custom_call" | custom-call | bytes 1845000 | tf_op jit(solution)/shard_map/pallas_call | solution.py:637
  8.3 0.0 collective-permute-done.far_ref
  8.3 0.0 collective-permute-done.1.near_ref
  8.3 0.4 %shard_map.77 = (f32[88,128]{1,0:T(8,128)S(1)}, f32[16,16,128]{2,1,0:T(8,128)S(1)}, f32[2,16,128]{2,1,0:T(8,128)S(1)}) custom-call(f32[288,128]{1,0:T(8,128)S(1)} %pad_maximum_fusion.c_ref.arguments, f32[40,128]{1,0:T(8,128)S(1)} %collective-permute-done.far_ref, f32[40,128]{1,0:T(8,128)S(1)} %collective-permute-done.1.near_ref, ...), custom_call_target="tpu_custom_call" | custom-call | bytes 1845000 | tf_op jit(solution)/shard_map/pallas_call | solution.py:637
  8.7 1.6 %collective-permute-start.7 = (f32[88,128]{1,0:T(8,128)S(1)}, f32[88,128]{1,0:T(8,128)S(1)}, u32[]{:S(2)}, u32[]{:S(2)}) collective-permute-start(f32[88,128]{1,0:T(8,128)S(1)} %get-tuple-element.54.pay_ref.refs_0_), channel_id=1, source_target_pairs={{0,4},{2,6},{4,0},{6,2},{8,12},{10,14},{12,8},{14,10},{16,20},{18,... | collective-permute-start | bytes 135176 | tf_op jit(solution)/shard_map/ppermute | solution.py:666
  10.3 1.1 %collective-permute-start.6 = (f32[88,128]{1,0:T(8,128)S(1)}, f32[88,128]{1,0:T(8,128)S(1)}, u32[]{:S(2)}, u32[]{:S(2)}) collective-permute-start(f32[88,128]{1,0:T(8,128)S(1)} %get-tuple-element.54.pay_ref.refs_0_), channel_id=1, source_target_pairs={{0,6},{2,4},{4,2},{6,0},{8,14},{10,12},{12,10},{14,8},{16,22},{18,... | collective-permute-start | bytes 135176 | tf_op jit(solution)/shard_map/ppermute | solution.py:666
  11.4 0.9 %collective-permute-start.5 = (f32[88,128]{1,0:T(8,128)S(1)}, f32[88,128]{1,0:T(8,128)S(1)}, u32[]{:S(2)}, u32[]{:S(2)}) collective-permute-start(f32[88,128]{1,0:T(8,128)S(1)} %get-tuple-element.54.pay_ref.refs_0_), channel_id=1, source_target_pairs={{0,2},{2,0},{4,6},{6,4},{8,10},{10,8},{12,14},{14,12},{16,18},{18,... | collective-permute-start | bytes 135176 | tf_op jit(solution)/shard_map/ppermute | solution.py:666
  12.3 0.6 %collective-permute-done.7.refs_2_.refs_3_ = f32[88,128]{1,0:T(8,128)S(1)} collective-permute-done((f32[88,128]{1,0:T(8,128)S(1)}, f32[88,128]{1,0:T(8,128)S(1)}, u32[]{:S(2)}, u32[]{:S(2)}) %collective-permute-start.7) | collective-permute-done | bytes 45088 | tf_op jit(solution)/shard_map/ppermute | solution.py:666
  12.8 2.4 %collective-permute-done.6.refs_1_.refs_2_ = f32[88,128]{1,0:T(8,128)S(1)} collective-permute-done((f32[88,128]{1,0:T(8,128)S(1)}, f32[88,128]{1,0:T(8,128)S(1)}, u32[]{:S(2)}, u32[]{:S(2)}) %collective-permute-start.6) | collective-permute-done | bytes 45088 | tf_op jit(solution)/shard_map/ppermute | solution.py:666
  15.2 0.2 collective-permute-done.5.refs_0_.refs_1_
  15.4 0.1 shard_map.78.own_group
  15.6 3.9 %collective-permute-start.8 = (f32[136,128]{1,0:T(8,128)S(1)}, f32[136,128]{1,0:T(8,128)S(1)}, u32[]{:S(2)}, u32[]{:S(2)}) collective-permute-start(f32[136,128]{1,0:T(8,128)S(1)} %shard_map.78.own_group), channel_id=1, source_target_pairs={{0,24},{2,26},{4,28},{6,30},{8,16},{10,18},{12,20},{14,22},{16,8},... | collective-permute-start | bytes 208904 | tf_op jit(solution)/shard_map/ppermute | solution.py:666
  19.5 0.0 collective-permute-start.10
  19.5 0.6 %collective-permute-start.9 = (f32[136,128]{1,0:T(8,128)S(1)}, f32[136,128]{1,0:T(8,128)S(1)}, u32[]{:S(2)}, u32[]{:S(2)}) collective-permute-start(f32[136,128]{1,0:T(8,128)S(1)} %shard_map.78.own_group), channel_id=1, source_target_pairs={{0,8},{2,10},{4,12},{6,14},{8,0},{10,2},{12,4},{14,6},{16,24},{18,... | collective-permute-start | bytes 208904 | tf_op jit(solution)/shard_map/ppermute | solution.py:666
  20.1 0.1 shard_map.79
  20.2 1.5 %collective-permute-done.8.group_ref.refs_2_ = f32[136,128]{1,0:T(8,128)S(1)} collective-permute-done((f32[136,128]{1,0:T(8,128)S(1)}, f32[136,128]{1,0:T(8,128)S(1)}, u32[]{:S(2)}, u32[]{:S(2)}) %collective-permute-start.8) | collective-permute-done | bytes 69664 | tf_op jit(solution)/shard_map/ppermute | solution.py:666
  21.8 0.1 shard_map.80.far_transfer
  21.9 2.8 %collective-permute-done.10.refs_1_ = f32[136,128]{1,0:T(8,128)S(1)} collective-permute-done((f32[136,128]{1,0:T(8,128)S(1)}, f32[136,128]{1,0:T(8,128)S(1)}, u32[]{:S(2)}, u32[]{:S(2)}) %collective-permute-start.10) | collective-permute-done | bytes 69664 | tf_op jit(solution)/shard_map/ppermute | solution.py:666
  24.7 0.0 collective-permute-done.9.refs_0_
  24.7 0.5 %shard_map.81 = (f32[16,16,128]{2,1,0:T(8,128)S(1)}, f32[16,16,128]{2,1,0:T(8,128)S(1)}, f32[10,16,128]{2,1,0:T(8,128)S(1)}, f32[4,16,128]{2,1,0:T(8,128)S(1)}, f32[128,128]{1,0:T(8,128)S(1)}) custom-call(f32[4,16,128]{2,1,0:T(8,128)S(1)} %get-tuple-element.42.rates_ref, f32[16,16,128]{2,1,0:T(8,128)S(1)} %get-tuple-element.53.f_ref, ...), custom_call_target="tpu_custom_call" | custom-call | bytes 1845000 | tf_op jit(solution)/shard_map/pallas_call | solution.py:637
  25.2 0.1 collective-permute-start.11
  25.2 0.1 shard_map.82
  25.3 0.9 %shard_map.83 = (f32[16,16,128]{2,1,0:T(8,128)S(1)}, f32[16,16,128]{2,1,0:T(8,128)S(1)}, f32[12,8,16,128]{3,2,1,0:T(8,128)S(1)}) custom-call(f32[16,16,128]{2,1,0:T(8,128)S(1)} %get-tuple-element.61.tiles_ref, f32[4,16,128]{2,1,0:T(8,128)S(1)} %get-tuple-element.62.halo_ref, f32[4,16,128]{2,1,0:T(8,128)S(1)} %get-tuple-element.42.rates_ref, ...), custom_call_target="tpu_custom_call" | custom-call | bytes 1845000 | tf_op jit(solution)/shard_map/pallas_call | solution.py:637
  26.2 0.3 collective-permute-done.11.refs_0_
  26.5 0.5 %shard_map.84 = (f32[2,32,128]{2,1,0:T(8,128)S(1)}, f32[16,16,128]{2,1,0:T(8,128)S(1)}) custom-call(f32[16,16,128]{2,1,0:T(8,128)S(1)} %get-tuple-element.61.tiles_ref, f32[4,16,128]{2,1,0:T(8,128)S(1)} %get-tuple-element.62.halo_ref, f32[4,16,128]{2,1,0:T(8,128)S(1)} %get-tuple-element.42.rates_ref, f32[2,16,128]{2,1,0:T(8,128)S(1)} %get-tuple-element.51.y_faces, ...), custom_call_target="tpu_custom_call" | custom-call | bytes 1845000 | tf_op jit(solution)/shard_map/pallas_call | solution.py:637
  27.0 1.3 %collective-permute-start.14 = (f32[2,32,128]{2,1,0:T(8,128)S(1)}, f32[2,32,128]{2,1,0:T(8,128)S(1)}, u32[]{:S(2)}, u32[]{:S(2)}) collective-permute-start(f32[2,32,128]{2,1,0:T(8,128)S(1)} %get-tuple-element.69.pay_ref), channel_id=1, source_target_pairs={{0,4},{2,6},{4,0},{6,2},{8,12},{10,14},{12,8},{14,10},{16,20},{18,... | collective-permute-start | bytes 98312 | tf_op jit(solution)/shard_map/ppermute | solution.py:666
  28.3 1.3 %collective-permute-start.13 = (f32[2,32,128]{2,1,0:T(8,128)S(1)}, f32[2,32,128]{2,1,0:T(8,128)S(1)}, u32[]{:S(2)}, u32[]{:S(2)}) collective-permute-start(f32[2,32,128]{2,1,0:T(8,128)S(1)} %get-tuple-element.69.pay_ref), channel_id=1, source_target_pairs={{0,6},{2,4},{4,2},{6,0},{8,14},{10,12},{12,10},{14,8},{16,22},{18,... | collective-permute-start | bytes 98312 | tf_op jit(solution)/shard_map/ppermute | solution.py:666
  29.6 0.9 %collective-permute-start.12 = (f32[2,32,128]{2,1,0:T(8,128)S(1)}, f32[2,32,128]{2,1,0:T(8,128)S(1)}, u32[]{:S(2)}, u32[]{:S(2)}) collective-permute-start(f32[2,32,128]{2,1,0:T(8,128)S(1)} %get-tuple-element.69.pay_ref), channel_id=1, source_target_pairs={{0,2},{2,0},{4,6},{6,4},{8,10},{10,8},{12,14},{14,12},{16,18},{18,... | collective-permute-start | bytes 98312 | tf_op jit(solution)/shard_map/ppermute | solution.py:666
  30.5 0.4 %collective-permute-done.14.refs_2_ = f32[2,32,128]{2,1,0:T(8,128)S(1)} collective-permute-done((f32[2,32,128]{2,1,0:T(8,128)S(1)}, f32[2,32,128]{2,1,0:T(8,128)S(1)}, u32[]{:S(2)}, u32[]{:S(2)}) %collective-permute-start.14) | collective-permute-done | bytes 32800 | tf_op jit(solution)/shard_map/ppermute | solution.py:666
  30.9 2.2 %collective-permute-done.13.refs_1_ = f32[2,32,128]{2,1,0:T(8,128)S(1)} collective-permute-done((f32[2,32,128]{2,1,0:T(8,128)S(1)}, f32[2,32,128]{2,1,0:T(8,128)S(1)}, u32[]{:S(2)}, u32[]{:S(2)}) %collective-permute-start.13) | collective-permute-done | bytes 32800 | tf_op jit(solution)/shard_map/ppermute | solution.py:666
  33.1 0.4 collective-permute-done.12.refs_0_
  33.5 1.8 %collective-permute-start.15 = (f32[32,128]{1,0:T(8,128)S(1)}, f32[32,128]{1,0:T(8,128)S(1)}, u32[]{:S(2)}, u32[]{:S(2)}) collective-permute-start(f32[32,128]{1,0:T(8,128)S(1)} %get-tuple-element.72), channel_id=1, source_target_pairs={{0,24},{2,26},{4,28},{6,30},{8,16},{10,18},{12,20},{14,22},{16,8},... | collective-permute-start | bytes 49160 | tf_op jit(solution)/shard_map/ppermute | solution.py:665
  35.3 0.4 collective-permute-start.16
  35.7 2.3 %collective-permute-start.17 = (f32[32,128]{1,0:T(8,128)S(1)}, f32[32,128]{1,0:T(8,128)S(1)}, u32[]{:S(2)}, u32[]{:S(2)}) collective-permute-start(f32[32,128]{1,0:T(8,128)S(1)} %get-tuple-element.74), channel_id=1, source_target_pairs={{0,8},{2,10},{4,12},{6,14},{8,0},{10,2},{12,4},{14,6},{16,24},{18,... | collective-permute-start | bytes 49160 | tf_op jit(solution)/shard_map/ppermute | solution.py:665
  38.0 1.1 %collective-permute-done.15.refs_0_ = f32[32,128]{1,0:T(8,128)S(1)} collective-permute-done((f32[32,128]{1,0:T(8,128)S(1)}, f32[32,128]{1,0:T(8,128)S(1)}, u32[]{:S(2)}, u32[]{:S(2)}) %collective-permute-start.15) | collective-permute-done | bytes 16416 | tf_op jit(solution)/shard_map/ppermute | solution.py:665
  39.1 0.8 %collective-permute-done.16.refs_1_ = f32[32,128]{1,0:T(8,128)S(1)} collective-permute-done((f32[32,128]{1,0:T(8,128)S(1)}, f32[32,128]{1,0:T(8,128)S(1)}, u32[]{:S(2)}, u32[]{:S(2)}) %collective-permute-start.16) | collective-permute-done | bytes 16416 | tf_op jit(solution)/shard_map/ppermute | solution.py:665
  39.9 0.7 %shard_map.86 = f32[16,2,8,128]{3,2,1,0:T(8,128)} custom-call(f32[2,32,128]{2,1,0:T(8,128)S(1)} %get-tuple-element.70.within_ref, f32[16,16,128]{2,1,0:T(8,128)S(1)} %get-tuple-element.71.f_ref, f32[16,16,128]{2,1,0:T(8,128)S(1)} %get-tuple-element.57.v_ref, f32[16,16,128]{2,1,0:T(8,128)S(1)} %get-tuple-element.58.u_ref, ...), custom_call_target="tpu_custom_call" | custom-call | bytes 1845000 | tf_op jit(solution)/shard_map/pallas_call | solution.py:637
  (11 shorter events, 0.1 us)
Async XLA Ops:
  1.0 6.6 %collective-permute-start.4 = (f32[136,128]{1,0:T(8,128)S(1)}, f32[136,128]{1,0:T(8,128)S(1)}, u32[]{:S(2)}, u32[]{:S(2)}) collective-permute-start(f32[136,128]{1,0:T(8,128)S(1)} %get-tuple-element.49), channel_id=1, source_target_pairs={{0,1},{1,0},{2,3},{3,2},{4,5},{5,4},{6,7},{7,6},{8,9},{9,8},{10,11... | collective-permute-start | bytes 208904 | tf_op jit(solution)/shard_map/ppermute | solution.py:651
  1.5 4.1 %copy-start.2 = (f32[16]{0:T(128)S(1)}, f32[16]{0:T(128)}, u32[]{:S(2)}) copy-start(f32[16]{0:T(128)} %param.11) | copy-start | bytes 196
  1.5 4.1 %copy-start.3 = (f32[16]{0:T(128)S(1)}, f32[16]{0:T(128)}, u32[]{:S(2)}) copy-start(f32[16]{0:T(128)} %param.12) | copy-start | bytes 196
  1.5 6.8 %collective-permute-start = (f32[40,128]{1,0:T(8,128)S(1)}, f32[40,128]{1,0:T(8,128)S(1)}, u32[]{:S(2)}, u32[]{:S(2)}) collective-permute-start(f32[40,128]{1,0:T(8,128)S(1)} %get-tuple-element.40), channel_id=1, source_target_pairs={{2,4},{3,5},{4,2},{5,3},{6,8},{7,9},{8,6},{9,7},{10,12},{11,13},{1... | collective-permute-start | bytes 61448 | tf_op jit(solution)/shard_map/ppermute | solution.py:679
  1.6 4.5 %copy-start.1 = (f32[16]{0:T(128)S(1)}, f32[16]{0:T(128)}, u32[]{:S(2)}) copy-start(f32[16]{0:T(128)} %param.10) | copy-start | bytes 196
  1.6 6.7 %collective-permute-start.1 = (f32[40,128]{1,0:T(8,128)S(1)}, f32[40,128]{1,0:T(8,128)S(1)}, u32[]{:S(2)}, u32[]{:S(2)}) collective-permute-start(f32[40,128]{1,0:T(8,128)S(1)} %get-tuple-element.41), channel_id=1, source_target_pairs={{0,2},{2,0},{4,6},{6,4},{8,10},{10,8},{12,14},{14,12},{16,18},{18,... | collective-permute-start | bytes 61448 | tf_op jit(solution)/shard_map/ppermute | solution.py:666
  5.6 1.6 %collective-permute-start.2 = (f32[16]{0:T(128)S(1)}, f32[16]{0:T(128)S(1)}, u32[]{:S(2)}, u32[]{:S(2)}) collective-permute-start(f32[16]{0:T(128)S(1)} %copy-done.2), channel_id=1, source_target_pairs={{0,1},{1,0},{2,3},{3,2},{4,5},{5,4},{6,7},{7,6},{8,9},{9,8},{10,11... | collective-permute-start | bytes 200 | tf_op jit(solution)/shard_map/ppermute | solution.py:651
  5.6 1.6 %collective-permute-start.3 = (f32[16]{0:T(128)S(1)}, f32[16]{0:T(128)S(1)}, u32[]{:S(2)}, u32[]{:S(2)}) collective-permute-start(f32[16]{0:T(128)S(1)} %copy-done.3), channel_id=1, source_target_pairs={{0,1},{1,0},{2,3},{3,2},{4,5},{5,4},{6,7},{7,6},{8,9},{9,8},{10,11... | collective-permute-start | bytes 200 | tf_op jit(solution)/shard_map/ppermute | solution.py:651
  6.1 1.1 %copy-start = (f32[16,16]{1,0:T(8,128)S(1)}, f32[16,16]{1,0:T(8,128)}, u32[]{:S(2)}) copy-start(f32[16,16]{1,0:T(8,128)} %proportions_ref.3) | copy-start | bytes 3076
  8.7 4.1 %collective-permute-start.7 = (f32[88,128]{1,0:T(8,128)S(1)}, f32[88,128]{1,0:T(8,128)S(1)}, u32[]{:S(2)}, u32[]{:S(2)}) collective-permute-start(f32[88,128]{1,0:T(8,128)S(1)} %get-tuple-element.54.pay_ref.refs_0_), channel_id=1, source_target_pairs={{0,4},{2,6},{4,0},{6,2},{8,12},{10,14},{12,8},{14,10},{16,20},{18,... | collective-permute-start | bytes 135176 | tf_op jit(solution)/shard_map/ppermute | solution.py:666
  10.3 4.9 %collective-permute-start.6 = (f32[88,128]{1,0:T(8,128)S(1)}, f32[88,128]{1,0:T(8,128)S(1)}, u32[]{:S(2)}, u32[]{:S(2)}) collective-permute-start(f32[88,128]{1,0:T(8,128)S(1)} %get-tuple-element.54.pay_ref.refs_0_), channel_id=1, source_target_pairs={{0,6},{2,4},{4,2},{6,0},{8,14},{10,12},{12,10},{14,8},{16,22},{18,... | collective-permute-start | bytes 135176 | tf_op jit(solution)/shard_map/ppermute | solution.py:666
  11.4 4.0 %collective-permute-start.5 = (f32[88,128]{1,0:T(8,128)S(1)}, f32[88,128]{1,0:T(8,128)S(1)}, u32[]{:S(2)}, u32[]{:S(2)}) collective-permute-start(f32[88,128]{1,0:T(8,128)S(1)} %get-tuple-element.54.pay_ref.refs_0_), channel_id=1, source_target_pairs={{0,2},{2,0},{4,6},{6,4},{8,10},{10,8},{12,14},{14,12},{16,18},{18,... | collective-permute-start | bytes 135176 | tf_op jit(solution)/shard_map/ppermute | solution.py:666
  15.6 6.2 %collective-permute-start.8 = (f32[136,128]{1,0:T(8,128)S(1)}, f32[136,128]{1,0:T(8,128)S(1)}, u32[]{:S(2)}, u32[]{:S(2)}) collective-permute-start(f32[136,128]{1,0:T(8,128)S(1)} %shard_map.78.own_group), channel_id=1, source_target_pairs={{0,24},{2,26},{4,28},{6,30},{8,16},{10,18},{12,20},{14,22},{16,8},... | collective-permute-start | bytes 208904 | tf_op jit(solution)/shard_map/ppermute | solution.py:666
  19.5 5.2 %collective-permute-start.10 = (f32[136,128]{1,0:T(8,128)S(1)}, f32[136,128]{1,0:T(8,128)S(1)}, u32[]{:S(2)}, u32[]{:S(2)}) collective-permute-start(f32[136,128]{1,0:T(8,128)S(1)} %shard_map.78.own_group), channel_id=1, source_target_pairs={{0,16},{2,18},{4,20},{6,22},{8,24},{10,26},{12,28},{14,30},{16,0},... | collective-permute-start | bytes 208904 | tf_op jit(solution)/shard_map/ppermute | solution.py:666
  19.5 5.2 %collective-permute-start.9 = (f32[136,128]{1,0:T(8,128)S(1)}, f32[136,128]{1,0:T(8,128)S(1)}, u32[]{:S(2)}, u32[]{:S(2)}) collective-permute-start(f32[136,128]{1,0:T(8,128)S(1)} %shard_map.78.own_group), channel_id=1, source_target_pairs={{0,8},{2,10},{4,12},{6,14},{8,0},{10,2},{12,4},{14,6},{16,24},{18,... | collective-permute-start | bytes 208904 | tf_op jit(solution)/shard_map/ppermute | solution.py:666
  25.2 1.3 %collective-permute-start.11 = (f32[128,128]{1,0:T(8,128)S(1)}, f32[128,128]{1,0:T(8,128)S(1)}, u32[]{:S(2)}, u32[]{:S(2)}) collective-permute-start(f32[128,128]{1,0:T(8,128)S(1)} %get-tuple-element.68), channel_id=1, source_target_pairs={{0,1},{1,0},{2,3},{3,2},{4,5},{5,4},{6,7},{7,6},{8,9},{9,8},{10,11... | collective-permute-start | bytes 196616 | tf_op jit(solution)/shard_map/ppermute | solution.py:651
  27.0 4.0 %collective-permute-start.14 = (f32[2,32,128]{2,1,0:T(8,128)S(1)}, f32[2,32,128]{2,1,0:T(8,128)S(1)}, u32[]{:S(2)}, u32[]{:S(2)}) collective-permute-start(f32[2,32,128]{2,1,0:T(8,128)S(1)} %get-tuple-element.69.pay_ref), channel_id=1, source_target_pairs={{0,4},{2,6},{4,0},{6,2},{8,12},{10,14},{12,8},{14,10},{16,20},{18,... | collective-permute-start | bytes 98312 | tf_op jit(solution)/shard_map/ppermute | solution.py:666
  28.3 4.8 %collective-permute-start.13 = (f32[2,32,128]{2,1,0:T(8,128)S(1)}, f32[2,32,128]{2,1,0:T(8,128)S(1)}, u32[]{:S(2)}, u32[]{:S(2)}) collective-permute-start(f32[2,32,128]{2,1,0:T(8,128)S(1)} %get-tuple-element.69.pay_ref), channel_id=1, source_target_pairs={{0,6},{2,4},{4,2},{6,0},{8,14},{10,12},{12,10},{14,8},{16,22},{18,... | collective-permute-start | bytes 98312 | tf_op jit(solution)/shard_map/ppermute | solution.py:666
  29.6 3.9 %collective-permute-start.12 = (f32[2,32,128]{2,1,0:T(8,128)S(1)}, f32[2,32,128]{2,1,0:T(8,128)S(1)}, u32[]{:S(2)}, u32[]{:S(2)}) collective-permute-start(f32[2,32,128]{2,1,0:T(8,128)S(1)} %get-tuple-element.69.pay_ref), channel_id=1, source_target_pairs={{0,2},{2,0},{4,6},{6,4},{8,10},{10,8},{12,14},{14,12},{16,18},{18,... | collective-permute-start | bytes 98312 | tf_op jit(solution)/shard_map/ppermute | solution.py:666
  33.5 5.6 %collective-permute-start.15 = (f32[32,128]{1,0:T(8,128)S(1)}, f32[32,128]{1,0:T(8,128)S(1)}, u32[]{:S(2)}, u32[]{:S(2)}) collective-permute-start(f32[32,128]{1,0:T(8,128)S(1)} %get-tuple-element.72), channel_id=1, source_target_pairs={{0,24},{2,26},{4,28},{6,30},{8,16},{10,18},{12,20},{14,22},{16,8},... | collective-permute-start | bytes 49160 | tf_op jit(solution)/shard_map/ppermute | solution.py:665
  35.3 4.6 %collective-permute-start.16 = (f32[32,128]{1,0:T(8,128)S(1)}, f32[32,128]{1,0:T(8,128)S(1)}, u32[]{:S(2)}, u32[]{:S(2)}) collective-permute-start(f32[32,128]{1,0:T(8,128)S(1)} %get-tuple-element.73), channel_id=1, source_target_pairs={{0,16},{2,18},{4,20},{6,22},{8,24},{10,26},{12,28},{14,30},{16,0},... | collective-permute-start | bytes 49160 | tf_op jit(solution)/shard_map/ppermute | solution.py:665
  35.7 4.2 %collective-permute-start.17 = (f32[32,128]{1,0:T(8,128)S(1)}, f32[32,128]{1,0:T(8,128)S(1)}, u32[]{:S(2)}, u32[]{:S(2)}) collective-permute-start(f32[32,128]{1,0:T(8,128)S(1)} %get-tuple-element.74), channel_id=1, source_target_pairs={{0,8},{2,10},{4,12},{6,14},{8,0},{10,2},{12,4},{14,6},{16,24},{18,... | collective-permute-start | bytes 49160 | tf_op jit(solution)/shard_map/ppermute | solution.py:665

commit v10 on v9

--- a/solution.py
+++ b/solution.py
@@ -411,7 +411,11 @@
         return tuple(state)
 
     state = (one, zero, zero, one) * (z.ny * len(refs))
-    state = lax.fori_loop(0, blocks, block, state) if blocks > 1 else block(0, state)
+    if blocks <= 4:
+        for j in range(blocks):
+            state = block(j, state)
+    else:
+        state = lax.fori_loop(0, blocks, block, state)
     return [state[4 * z.ny * n : 4 * z.ny * (n + 1)] for n in range(len(refs))]
 
 

time: 40.8 us -> 40.8 us (level)
  no operation moved by 1% of the time
where the time goes in v10:
time: 40.8 us; the launch traced here: 40.6 us
  starting transfers between devices  21.3 us (52%)
  waiting for transfers between devices  12.6 us (31%)
  Pallas kernels  5.6 us (14%)
  other arithmetic  0.95 us (2%)
    ppermute x10, starting transfers between devices, exchange(): return [lax.ppermute(v, 'gz', p) for v, p in zip(values, pairs)]  15.6 us
    ppermute x10, waiting for transfers between devices, exchange(): return [lax.ppermute(v, 'gz', p) for v, p in zip(values, pairs)]  10.4 us
    pallas_call x14, Pallas kernels, call(): pl.pallas_call(functools.partial(kernel, z), out_shape=outs, in_specs=[sp...  5.6 us
    ppermute x3, starting transfers between devices, exchange(): lax.ppermute(v, 'gz', p)  4.45 us
    ppermute x3, waiting for transfers between devices, exchange(): lax.ppermute(v, 'gz', p)  1.95 us
    ppermute x4, starting transfers between devices, shift(): lax.ppermute(value, axis, [(i, (i + by) % count) for i in range(count)])  1.1 us
    concatenate x1, other arithmetic, per_device(): arguments = jnp.concatenate([v.reshape(-1, z.nx) for v in (c, k, warm)])  0.95 us
  transfers between devices with their start and end apart: 18, of which 11 were waited for; matrix products, arithmetic and copies ran while one was open for 0% of the time, Pallas kernels for 8%

profile of v10, /device:TPU:0, one launch (start us, length us, event | category | flops | bytes accessed | tf_op | source)
XLA Modules:
  0.0 40.6 jit_solution(16304934236454342565)
XLA Ops:
  0.0 0.9 %pad_maximum_fusion.c_ref.arguments = f32[288,128]{1,0:T(8,128)S(1)} fusion(f32[16,128]{1,0:T(8,128)} %bitcast.10, f32[16,128]{1,0:T(8,128)} %bitcast.11, f32[256,128]{1,0:T(8,128)} %bitcast.9), kind=kLoop, calls=%fused_computation | loop fusion | flops 73728 | bytes 294912 | tf_op jit(solution)/shard_map/concatenate | solution.py:660
  1.0 0.5 %collective-permute-start.4 = (f32[136,128]{1,0:T(8,128)S(1)}, f32[136,128]{1,0:T(8,128)S(1)}, u32[]{:S(2)}, u32[]{:S(2)}) collective-permute-start(f32[136,128]{1,0:T(8,128)S(1)} %get-tuple-element.49), channel_id=1, source_target_pairs={{0,1},{1,0},{2,3},{3,2},{4,5},{5,4},{6,7},{7,6},{8,9},{9,8},{10,11... | collective-permute-start | bytes 208904 | tf_op jit(solution)/shard_map/ppermute | solution.py:655
  1.5 0.1 collective-permute-start
  1.6 4.0 %collective-permute-start.1 = (f32[40,128]{1,0:T(8,128)S(1)}, f32[40,128]{1,0:T(8,128)S(1)}, u32[]{:S(2)}, u32[]{:S(2)}) collective-permute-start(f32[40,128]{1,0:T(8,128)S(1)} %get-tuple-element.41), channel_id=1, source_target_pairs={{0,2},{2,0},{4,6},{6,4},{8,10},{10,8},{12,14},{14,12},{16,18},{18,... | collective-permute-start | bytes 61448 | tf_op jit(solution)/shard_map/ppermute | solution.py:670
  5.6 0.0 collective-permute-start.2
  5.6 0.5 %collective-permute-start.3 = (f32[16]{0:T(128)S(1)}, f32[16]{0:T(128)S(1)}, u32[]{:S(2)}, u32[]{:S(2)}) collective-permute-start(f32[16]{0:T(128)S(1)} %copy-done.3), channel_id=1, source_target_pairs={{0,1},{1,0},{2,3},{3,2},{4,5},{5,4},{6,7},{7,6},{8,9},{9,8},{10,11... | collective-permute-start | bytes 200 | tf_op jit(solution)/shard_map/ppermute | solution.py:655
  6.1 1.1 %shard_map.74 = (f32[4,16,128]{2,1,0:T(8,128)S(1)}, f32[2,16,128]{2,1,0:T(8,128)S(1)}, f32[7,16,16,128]{3,2,1,0:T(8,128)S(1)}, f32[7,16,16,128]{3,2,1,0:T(8,128)S(1)}, f32[16,16,128]{2,1,0:T(8,128)S(1)}) custom-call(f32[288,128]{1,0:T(8,128)S(1)} %pad_maximum_fusion.c_ref.arguments, f32[1,16]{1,0:T(1,128)S(1)} %bitcast.6), custom_call_target="tpu_custom_call" | custom-call | bytes 3690000 | tf_op jit(solution)/shard_map/pallas_call | solution.py:641
  7.2 0.0 collective-permute-done.2
  7.2 0.0 collective-permute-done.3
  7.2 0.4 shard_map.75
  7.6 0.0 collective-permute-done.4.refs_0_
  7.6 0.7 %shard_map.76 = (f32[16,16,128]{2,1,0:T(8,128)S(1)}, f32[2,16,128]{2,1,0:T(8,128)S(1)}, f32[12,4,16,128]{3,2,1,0:T(8,128)S(1)}) custom-call(f32[288,128]{1,0:T(8,128)S(1)} %pad_maximum_fusion.c_ref.arguments, f32[16,16,128]{2,1,0:T(8,128)S(1)} %get-tuple-element.44.tiles_ref, f32[16,16,128]{2,1,0:T(8,128)S(1)} %get-tuple-element.45.base_ref, ...), custom_call_target="tpu_custom_call" | custom-call | bytes 1845000 | tf_op jit(solution)/shard_map/pallas_call | solution.py:641
  8.3 0.0 collective-permute-done.far_ref
  8.3 0.0 collective-permute-done.1.near_ref
  8.3 0.4 %shard_map.77 = (f32[88,128]{1,0:T(8,128)S(1)}, f32[16,16,128]{2,1,0:T(8,128)S(1)}, f32[2,16,128]{2,1,0:T(8,128)S(1)}) custom-call(f32[288,128]{1,0:T(8,128)S(1)} %pad_maximum_fusion.c_ref.arguments, f32[40,128]{1,0:T(8,128)S(1)} %collective-permute-done.far_ref, f32[40,128]{1,0:T(8,128)S(1)} %collective-permute-done.1.near_ref, ...), custom_call_target="tpu_custom_call" | custom-call | bytes 1845000 | tf_op jit(solution)/shard_map/pallas_call | solution.py:641
  8.7 1.6 %collective-permute-start.7 = (f32[88,128]{1,0:T(8,128)S(1)}, f32[88,128]{1,0:T(8,128)S(1)}, u32[]{:S(2)}, u32[]{:S(2)}) collective-permute-start(f32[88,128]{1,0:T(8,128)S(1)} %get-tuple-element.54.pay_ref.refs_0_), channel_id=1, source_target_pairs={{0,4},{2,6},{4,0},{6,2},{8,12},{10,14},{12,8},{14,10},{16,20},{18,... | collective-permute-start | bytes 135176 | tf_op jit(solution)/shard_map/ppermute | solution.py:670
  10.3 1.1 %collective-permute-start.6 = (f32[88,128]{1,0:T(8,128)S(1)}, f32[88,128]{1,0:T(8,128)S(1)}, u32[]{:S(2)}, u32[]{:S(2)}) collective-permute-start(f32[88,128]{1,0:T(8,128)S(1)} %get-tuple-element.54.pay_ref.refs_0_), channel_id=1, source_target_pairs={{0,6},{2,4},{4,2},{6,0},{8,14},{10,12},{12,10},{14,8},{16,22},{18,... | collective-permute-start | bytes 135176 | tf_op jit(solution)/shard_map/ppermute | solution.py:670
  11.4 0.9 %collective-permute-start.5 = (f32[88,128]{1,0:T(8,128)S(1)}, f32[88,128]{1,0:T(8,128)S(1)}, u32[]{:S(2)}, u32[]{:S(2)}) collective-permute-start(f32[88,128]{1,0:T(8,128)S(1)} %get-tuple-element.54.pay_ref.refs_0_), channel_id=1, source_target_pairs={{0,2},{2,0},{4,6},{6,4},{8,10},{10,8},{12,14},{14,12},{16,18},{18,... | collective-permute-start | bytes 135176 | tf_op jit(solution)/shard_map/ppermute | solution.py:670
  12.3 0.6 %collective-permute-done.7.refs_2_.refs_3_ = f32[88,128]{1,0:T(8,128)S(1)} collective-permute-done((f32[88,128]{1,0:T(8,128)S(1)}, f32[88,128]{1,0:T(8,128)S(1)}, u32[]{:S(2)}, u32[]{:S(2)}) %collective-permute-start.7) | collective-permute-done | bytes 45088 | tf_op jit(solution)/shard_map/ppermute | solution.py:670
  12.8 2.4 %collective-permute-done.6.refs_1_.refs_2_ = f32[88,128]{1,0:T(8,128)S(1)} collective-permute-done((f32[88,128]{1,0:T(8,128)S(1)}, f32[88,128]{1,0:T(8,128)S(1)}, u32[]{:S(2)}, u32[]{:S(2)}) %collective-permute-start.6) | collective-permute-done | bytes 45088 | tf_op jit(solution)/shard_map/ppermute | solution.py:670
  15.2 0.2 collective-permute-done.5.refs_0_.refs_1_
  15.4 0.1 shard_map.78.own_group
  15.6 3.9 %collective-permute-start.8 = (f32[136,128]{1,0:T(8,128)S(1)}, f32[136,128]{1,0:T(8,128)S(1)}, u32[]{:S(2)}, u32[]{:S(2)}) collective-permute-start(f32[136,128]{1,0:T(8,128)S(1)} %shard_map.78.own_group), channel_id=1, source_target_pairs={{0,24},{2,26},{4,28},{6,30},{8,16},{10,18},{12,20},{14,22},{16,8},... | collective-permute-start | bytes 208904 | tf_op jit(solution)/shard_map/ppermute | solution.py:670
  19.5 0.0 collective-permute-start.10
  19.5 0.6 %collective-permute-start.9 = (f32[136,128]{1,0:T(8,128)S(1)}, f32[136,128]{1,0:T(8,128)S(1)}, u32[]{:S(2)}, u32[]{:S(2)}) collective-permute-start(f32[136,128]{1,0:T(8,128)S(1)} %shard_map.78.own_group), channel_id=1, source_target_pairs={{0,8},{2,10},{4,12},{6,14},{8,0},{10,2},{12,4},{14,6},{16,24},{18,... | collective-permute-start | bytes 208904 | tf_op jit(solution)/shard_map/ppermute | solution.py:670
  20.1 0.1 shard_map.79
  20.2 1.5 %collective-permute-done.8.group_ref.refs_2_ = f32[136,128]{1,0:T(8,128)S(1)} collective-permute-done((f32[136,128]{1,0:T(8,128)S(1)}, f32[136,128]{1,0:T(8,128)S(1)}, u32[]{:S(2)}, u32[]{:S(2)}) %collective-permute-start.8) | collective-permute-done | bytes 69664 | tf_op jit(solution)/shard_map/ppermute | solution.py:670
  21.8 0.1 shard_map.80.far_transfer
  21.9 2.8 %collective-permute-done.10.refs_1_ = f32[136,128]{1,0:T(8,128)S(1)} collective-permute-done((f32[136,128]{1,0:T(8,128)S(1)}, f32[136,128]{1,0:T(8,128)S(1)}, u32[]{:S(2)}, u32[]{:S(2)}) %collective-permute-start.10) | collective-permute-done | bytes 69664 | tf_op jit(solution)/shard_map/ppermute | solution.py:670
  24.7 0.4 %shard_map.81 = (f32[16,16,128]{2,1,0:T(8,128)S(1)}, f32[16,16,128]{2,1,0:T(8,128)S(1)}, f32[10,16,128]{2,1,0:T(8,128)S(1)}, f32[4,16,128]{2,1,0:T(8,128)S(1)}, f32[128,128]{1,0:T(8,128)S(1)}) custom-call(f32[4,16,128]{2,1,0:T(8,128)S(1)} %get-tuple-element.42.rates_ref, f32[16,16,128]{2,1,0:T(8,128)S(1)} %get-tuple-element.53.f_ref, ...), custom_call_target="tpu_custom_call" | custom-call | bytes 1845000 | tf_op jit(solution)/shard_map/pallas_call | solution.py:641
  25.1 0.1 collective-permute-start.11
  25.2 0.1 shard_map.82
  25.3 0.9 %shard_map.83 = (f32[16,16,128]{2,1,0:T(8,128)S(1)}, f32[16,16,128]{2,1,0:T(8,128)S(1)}, f32[12,8,16,128]{3,2,1,0:T(8,128)S(1)}) custom-call(f32[16,16,128]{2,1,0:T(8,128)S(1)} %get-tuple-element.61.tiles_ref, f32[4,16,128]{2,1,0:T(8,128)S(1)} %get-tuple-element.62.halo_ref, f32[4,16,128]{2,1,0:T(8,128)S(1)} %get-tuple-element.42.rates_ref, ...), custom_call_target="tpu_custom_call" | custom-call | bytes 1845000 | tf_op jit(solution)/shard_map/pallas_call | solution.py:641
  26.2 0.3 collective-permute-done.11.refs_0_
  26.5 0.5 %shard_map.84 = (f32[2,32,128]{2,1,0:T(8,128)S(1)}, f32[16,16,128]{2,1,0:T(8,128)S(1)}) custom-call(f32[16,16,128]{2,1,0:T(8,128)S(1)} %get-tuple-element.61.tiles_ref, f32[4,16,128]{2,1,0:T(8,128)S(1)} %get-tuple-element.62.halo_ref, f32[4,16,128]{2,1,0:T(8,128)S(1)} %get-tuple-element.42.rates_ref, f32[2,16,128]{2,1,0:T(8,128)S(1)} %get-tuple-element.51.y_faces, ...), custom_call_target="tpu_custom_call" | custom-call | bytes 1845000 | tf_op jit(solution)/shard_map/pallas_call | solution.py:641
  26.9 1.3 %collective-permute-start.14 = (f32[2,32,128]{2,1,0:T(8,128)S(1)}, f32[2,32,128]{2,1,0:T(8,128)S(1)}, u32[]{:S(2)}, u32[]{:S(2)}) collective-permute-start(f32[2,32,128]{2,1,0:T(8,128)S(1)} %get-tuple-element.69.pay_ref), channel_id=1, source_target_pairs={{0,4},{2,6},{4,0},{6,2},{8,12},{10,14},{12,8},{14,10},{16,20},{18,... | collective-permute-start | bytes 98312 | tf_op jit(solution)/shard_map/ppermute | solution.py:670
  28.3 1.3 %collective-permute-start.13 = (f32[2,32,128]{2,1,0:T(8,128)S(1)}, f32[2,32,128]{2,1,0:T(8,128)S(1)}, u32[]{:S(2)}, u32[]{:S(2)}) collective-permute-start(f32[2,32,128]{2,1,0:T(8,128)S(1)} %get-tuple-element.69.pay_ref), channel_id=1, source_target_pairs={{0,6},{2,4},{4,2},{6,0},{8,14},{10,12},{12,10},{14,8},{16,22},{18,... | collective-permute-start | bytes 98312 | tf_op jit(solution)/shard_map/ppermute | solution.py:670
  29.5 0.9 %collective-permute-start.12 = (f32[2,32,128]{2,1,0:T(8,128)S(1)}, f32[2,32,128]{2,1,0:T(8,128)S(1)}, u32[]{:S(2)}, u32[]{:S(2)}) collective-permute-start(f32[2,32,128]{2,1,0:T(8,128)S(1)} %get-tuple-element.69.pay_ref), channel_id=1, source_target_pairs={{0,2},{2,0},{4,6},{6,4},{8,10},{10,8},{12,14},{14,12},{16,18},{18,... | collective-permute-start | bytes 98312 | tf_op jit(solution)/shard_map/ppermute | solution.py:670
  30.5 0.4 %collective-permute-done.14.refs_2_ = f32[2,32,128]{2,1,0:T(8,128)S(1)} collective-permute-done((f32[2,32,128]{2,1,0:T(8,128)S(1)}, f32[2,32,128]{2,1,0:T(8,128)S(1)}, u32[]{:S(2)}, u32[]{:S(2)}) %collective-permute-start.14) | collective-permute-done | bytes 32800 | tf_op jit(solution)/shard_map/ppermute | solution.py:670
  30.9 2.2 %collective-permute-done.13.refs_1_ = f32[2,32,128]{2,1,0:T(8,128)S(1)} collective-permute-done((f32[2,32,128]{2,1,0:T(8,128)S(1)}, f32[2,32,128]{2,1,0:T(8,128)S(1)}, u32[]{:S(2)}, u32[]{:S(2)}) %collective-permute-start.13) | collective-permute-done | bytes 32800 | tf_op jit(solution)/shard_map/ppermute | solution.py:670
  33.1 0.4 collective-permute-done.12.refs_0_
  33.5 1.8 %collective-permute-start.15 = (f32[32,128]{1,0:T(8,128)S(1)}, f32[32,128]{1,0:T(8,128)S(1)}, u32[]{:S(2)}, u32[]{:S(2)}) collective-permute-start(f32[32,128]{1,0:T(8,128)S(1)} %get-tuple-element.72), channel_id=1, source_target_pairs={{0,24},{2,26},{4,28},{6,30},{8,16},{10,18},{12,20},{14,22},{16,8},... | collective-permute-start | bytes 49160 | tf_op jit(solution)/shard_map/ppermute | solution.py:669
  35.3 0.4 collective-permute-start.16
  35.6 2.3 %collective-permute-start.17 = (f32[32,128]{1,0:T(8,128)S(1)}, f32[32,128]{1,0:T(8,128)S(1)}, u32[]{:S(2)}, u32[]{:S(2)}) collective-permute-start(f32[32,128]{1,0:T(8,128)S(1)} %get-tuple-element.74), channel_id=1, source_target_pairs={{0,8},{2,10},{4,12},{6,14},{8,0},{10,2},{12,4},{14,6},{16,24},{18,... | collective-permute-start | bytes 49160 | tf_op jit(solution)/shard_map/ppermute | solution.py:669
  37.9 1.1 %collective-permute-done.15.refs_0_ = f32[32,128]{1,0:T(8,128)S(1)} collective-permute-done((f32[32,128]{1,0:T(8,128)S(1)}, f32[32,128]{1,0:T(8,128)S(1)}, u32[]{:S(2)}, u32[]{:S(2)}) %collective-permute-start.15) | collective-permute-done | bytes 16416 | tf_op jit(solution)/shard_map/ppermute | solution.py:669
  39.1 0.8 %collective-permute-done.16.refs_1_ = f32[32,128]{1,0:T(8,128)S(1)} collective-permute-done((f32[32,128]{1,0:T(8,128)S(1)}, f32[32,128]{1,0:T(8,128)S(1)}, u32[]{:S(2)}, u32[]{:S(2)}) %collective-permute-start.16) | collective-permute-done | bytes 16416 | tf_op jit(solution)/shard_map/ppermute | solution.py:669
  39.9 0.0 collective-permute-done.17.refs_2_
  39.9 0.7 %shard_map.86 = f32[16,2,8,128]{3,2,1,0:T(8,128)} custom-call(f32[2,32,128]{2,1,0:T(8,128)S(1)} %get-tuple-element.70.within_ref, f32[16,16,128]{2,1,0:T(8,128)S(1)} %get-tuple-element.71.f_ref, f32[16,16,128]{2,1,0:T(8,128)S(1)} %get-tuple-element.57.v_ref, f32[16,16,128]{2,1,0:T(8,128)S(1)} %get-tuple-element.58.u_ref, ...), custom_call_target="tpu_custom_call" | custom-call | bytes 1845000 | tf_op jit(solution)/shard_map/pallas_call | solution.py:641
  (11 shorter events, 0.1 us)
Async XLA Ops:
  1.0 6.6 %collective-permute-start.4 = (f32[136,128]{1,0:T(8,128)S(1)}, f32[136,128]{1,0:T(8,128)S(1)}, u32[]{:S(2)}, u32[]{:S(2)}) collective-permute-start(f32[136,128]{1,0:T(8,128)S(1)} %get-tuple-element.49), channel_id=1, source_target_pairs={{0,1},{1,0},{2,3},{3,2},{4,5},{5,4},{6,7},{7,6},{8,9},{9,8},{10,11... | collective-permute-start | bytes 208904 | tf_op jit(solution)/shard_map/ppermute | solution.py:655
  1.5 4.1 %copy-start.2 = (f32[16]{0:T(128)S(1)}, f32[16]{0:T(128)}, u32[]{:S(2)}) copy-start(f32[16]{0:T(128)} %param.11) | copy-start | bytes 196
  1.5 4.1 %copy-start.3 = (f32[16]{0:T(128)S(1)}, f32[16]{0:T(128)}, u32[]{:S(2)}) copy-start(f32[16]{0:T(128)} %param.12) | copy-start | bytes 196
  1.5 6.8 %collective-permute-start = (f32[40,128]{1,0:T(8,128)S(1)}, f32[40,128]{1,0:T(8,128)S(1)}, u32[]{:S(2)}, u32[]{:S(2)}) collective-permute-start(f32[40,128]{1,0:T(8,128)S(1)} %get-tuple-element.40), channel_id=1, source_target_pairs={{2,4},{3,5},{4,2},{5,3},{6,8},{7,9},{8,6},{9,7},{10,12},{11,13},{1... | collective-permute-start | bytes 61448 | tf_op jit(solution)/shard_map/ppermute | solution.py:683
  1.6 4.5 %copy-start.1 = (f32[16]{0:T(128)S(1)}, f32[16]{0:T(128)}, u32[]{:S(2)}) copy-start(f32[16]{0:T(128)} %param.10) | copy-start | bytes 196
  1.6 6.7 %collective-permute-start.1 = (f32[40,128]{1,0:T(8,128)S(1)}, f32[40,128]{1,0:T(8,128)S(1)}, u32[]{:S(2)}, u32[]{:S(2)}) collective-permute-start(f32[40,128]{1,0:T(8,128)S(1)} %get-tuple-element.41), channel_id=1, source_target_pairs={{0,2},{2,0},{4,6},{6,4},{8,10},{10,8},{12,14},{14,12},{16,18},{18,... | collective-permute-start | bytes 61448 | tf_op jit(solution)/shard_map/ppermute | solution.py:670
  5.6 1.6 %collective-permute-start.2 = (f32[16]{0:T(128)S(1)}, f32[16]{0:T(128)S(1)}, u32[]{:S(2)}, u32[]{:S(2)}) collective-permute-start(f32[16]{0:T(128)S(1)} %copy-done.2), channel_id=1, source_target_pairs={{0,1},{1,0},{2,3},{3,2},{4,5},{5,4},{6,7},{7,6},{8,9},{9,8},{10,11... | collective-permute-start | bytes 200 | tf_op jit(solution)/shard_map/ppermute | solution.py:655
  5.6 1.6 %collective-permute-start.3 = (f32[16]{0:T(128)S(1)}, f32[16]{0:T(128)S(1)}, u32[]{:S(2)}, u32[]{:S(2)}) collective-permute-start(f32[16]{0:T(128)S(1)} %copy-done.3), channel_id=1, source_target_pairs={{0,1},{1,0},{2,3},{3,2},{4,5},{5,4},{6,7},{7,6},{8,9},{9,8},{10,11... | collective-permute-start | bytes 200 | tf_op jit(solution)/shard_map/ppermute | solution.py:655
  6.1 1.1 %copy-start = (f32[16,16]{1,0:T(8,128)S(1)}, f32[16,16]{1,0:T(8,128)}, u32[]{:S(2)}) copy-start(f32[16,16]{1,0:T(8,128)} %proportions_ref.3) | copy-start | bytes 3076
  8.7 4.1 %collective-permute-start.7 = (f32[88,128]{1,0:T(8,128)S(1)}, f32[88,128]{1,0:T(8,128)S(1)}, u32[]{:S(2)}, u32[]{:S(2)}) collective-permute-start(f32[88,128]{1,0:T(8,128)S(1)} %get-tuple-element.54.pay_ref.refs_0_), channel_id=1, source_target_pairs={{0,4},{2,6},{4,0},{6,2},{8,12},{10,14},{12,8},{14,10},{16,20},{18,... | collective-permute-start | bytes 135176 | tf_op jit(solution)/shard_map/ppermute | solution.py:670
  10.3 4.9 %collective-permute-start.6 = (f32[88,128]{1,0:T(8,128)S(1)}, f32[88,128]{1,0:T(8,128)S(1)}, u32[]{:S(2)}, u32[]{:S(2)}) collective-permute-start(f32[88,128]{1,0:T(8,128)S(1)} %get-tuple-element.54.pay_ref.refs_0_), channel_id=1, source_target_pairs={{0,6},{2,4},{4,2},{6,0},{8,14},{10,12},{12,10},{14,8},{16,22},{18,... | collective-permute-start | bytes 135176 | tf_op jit(solution)/shard_map/ppermute | solution.py:670
  11.4 4.0 %collective-permute-start.5 = (f32[88,128]{1,0:T(8,128)S(1)}, f32[88,128]{1,0:T(8,128)S(1)}, u32[]{:S(2)}, u32[]{:S(2)}) collective-permute-start(f32[88,128]{1,0:T(8,128)S(1)} %get-tuple-element.54.pay_ref.refs_0_), channel_id=1, source_target_pairs={{0,2},{2,0},{4,6},{6,4},{8,10},{10,8},{12,14},{14,12},{16,18},{18,... | collective-permute-start | bytes 135176 | tf_op jit(solution)/shard_map/ppermute | solution.py:670
  15.6 6.2 %collective-permute-start.8 = (f32[136,128]{1,0:T(8,128)S(1)}, f32[136,128]{1,0:T(8,128)S(1)}, u32[]{:S(2)}, u32[]{:S(2)}) collective-permute-start(f32[136,128]{1,0:T(8,128)S(1)} %shard_map.78.own_group), channel_id=1, source_target_pairs={{0,24},{2,26},{4,28},{6,30},{8,16},{10,18},{12,20},{14,22},{16,8},... | collective-permute-start | bytes 208904 | tf_op jit(solution)/shard_map/ppermute | solution.py:670
  19.5 5.2 %collective-permute-start.10 = (f32[136,128]{1,0:T(8,128)S(1)}, f32[136,128]{1,0:T(8,128)S(1)}, u32[]{:S(2)}, u32[]{:S(2)}) collective-permute-start(f32[136,128]{1,0:T(8,128)S(1)} %shard_map.78.own_group), channel_id=1, source_target_pairs={{0,16},{2,18},{4,20},{6,22},{8,24},{10,26},{12,28},{14,30},{16,0},... | collective-permute-start | bytes 208904 | tf_op jit(solution)/shard_map/ppermute | solution.py:670
  19.5 5.2 %collective-permute-start.9 = (f32[136,128]{1,0:T(8,128)S(1)}, f32[136,128]{1,0:T(8,128)S(1)}, u32[]{:S(2)}, u32[]{:S(2)}) collective-permute-start(f32[136,128]{1,0:T(8,128)S(1)} %shard_map.78.own_group), channel_id=1, source_target_pairs={{0,8},{2,10},{4,12},{6,14},{8,0},{10,2},{12,4},{14,6},{16,24},{18,... | collective-permute-start | bytes 208904 | tf_op jit(solution)/shard_map/ppermute | solution.py:670
  25.1 1.3 %collective-permute-start.11 = (f32[128,128]{1,0:T(8,128)S(1)}, f32[128,128]{1,0:T(8,128)S(1)}, u32[]{:S(2)}, u32[]{:S(2)}) collective-permute-start(f32[128,128]{1,0:T(8,128)S(1)} %get-tuple-element.68), channel_id=1, source_target_pairs={{0,1},{1,0},{2,3},{3,2},{4,5},{5,4},{6,7},{7,6},{8,9},{9,8},{10,11... | collective-permute-start | bytes 196616 | tf_op jit(solution)/shard_map/ppermute | solution.py:655
  26.9 4.0 %collective-permute-start.14 = (f32[2,32,128]{2,1,0:T(8,128)S(1)}, f32[2,32,128]{2,1,0:T(8,128)S(1)}, u32[]{:S(2)}, u32[]{:S(2)}) collective-permute-start(f32[2,32,128]{2,1,0:T(8,128)S(1)} %get-tuple-element.69.pay_ref), channel_id=1, source_target_pairs={{0,4},{2,6},{4,0},{6,2},{8,12},{10,14},{12,8},{14,10},{16,20},{18,... | collective-permute-start | bytes 98312 | tf_op jit(solution)/shard_map/ppermute | solution.py:670
  28.3 4.8 %collective-permute-start.13 = (f32[2,32,128]{2,1,0:T(8,128)S(1)}, f32[2,32,128]{2,1,0:T(8,128)S(1)}, u32[]{:S(2)}, u32[]{:S(2)}) collective-permute-start(f32[2,32,128]{2,1,0:T(8,128)S(1)} %get-tuple-element.69.pay_ref), channel_id=1, source_target_pairs={{0,6},{2,4},{4,2},{6,0},{8,14},{10,12},{12,10},{14,8},{16,22},{18,... | collective-permute-start | bytes 98312 | tf_op jit(solution)/shard_map/ppermute | solution.py:670
  29.5 3.9 %collective-permute-start.12 = (f32[2,32,128]{2,1,0:T(8,128)S(1)}, f32[2,32,128]{2,1,0:T(8,128)S(1)}, u32[]{:S(2)}, u32[]{:S(2)}) collective-permute-start(f32[2,32,128]{2,1,0:T(8,128)S(1)} %get-tuple-element.69.pay_ref), channel_id=1, source_target_pairs={{0,2},{2,0},{4,6},{6,4},{8,10},{10,8},{12,14},{14,12},{16,18},{18,... | collective-permute-start | bytes 98312 | tf_op jit(solution)/shard_map/ppermute | solution.py:670
  33.5 5.6 %collective-permute-start.15 = (f32[32,128]{1,0:T(8,128)S(1)}, f32[32,128]{1,0:T(8,128)S(1)}, u32[]{:S(2)}, u32[]{:S(2)}) collective-permute-start(f32[32,128]{1,0:T(8,128)S(1)} %get-tuple-element.72), channel_id=1, source_target_pairs={{0,24},{2,26},{4,28},{6,30},{8,16},{10,18},{12,20},{14,22},{16,8},... | collective-permute-start | bytes 49160 | tf_op jit(solution)/shard_map/ppermute | solution.py:669
  35.3 4.6 %collective-permute-start.16 = (f32[32,128]{1,0:T(8,128)S(1)}, f32[32,128]{1,0:T(8,128)S(1)}, u32[]{:S(2)}, u32[]{:S(2)}) collective-permute-start(f32[32,128]{1,0:T(8,128)S(1)} %get-tuple-element.73), channel_id=1, source_target_pairs={{0,16},{2,18},{4,20},{6,22},{8,24},{10,26},{12,28},{14,30},{16,0},... | collective-permute-start | bytes 49160 | tf_op jit(solution)/shard_map/ppermute | solution.py:669
  35.6 4.2 %collective-permute-start.17 = (f32[32,128]{1,0:T(8,128)S(1)}, f32[32,128]{1,0:T(8,128)S(1)}, u32[]{:S(2)}, u32[]{:S(2)}) collective-permute-start(f32[32,128]{1,0:T(8,128)S(1)} %get-tuple-element.74), channel_id=1, source_target_pairs={{0,8},{2,10},{4,12},{6,14},{8,0},{10,2},{12,4},{14,6},{16,24},{18,... | collective-permute-start | bytes 49160 | tf_op jit(solution)/shard_map/ppermute | solution.py:669

commit v11 on v10

--- a/solution.py
+++ b/solution.py
@@ -469,8 +469,10 @@
         return tuple(out)
 
     state = (zero, one, zero) * z.ny
-    state = lax.fori_loop(0, group, lambda j, s: up(groups, j, s), state)
-    state = lax.fori_loop(0, member, lambda j, s: up(blocks, j, s), state)
+    for j in range(z.groups_z - 1):
+        state = tuple(jnp.where(j < group, a, b) for a, b in zip(up(groups, j, state), state))
+    for j in range(z.members - 1):
+        state = tuple(jnp.where(j < member, a, b) for a, b in zip(up(blocks, j, state), state))
     rising = []
     for y in ys:
         pair = state[3 * y : 3 * y + 2]
@@ -486,10 +488,10 @@
     state = ()
     for y in ys:
         state += (ohm(top_ref, y), one, zero)
-    last = z.groups_z - 1
-    state = lax.fori_loop(0, last - group, lambda i, s: down(groups, last - i, s), state)
-    last = z.members - 1
-    state = lax.fori_loop(0, last - member, lambda i, s: down(blocks, last - i, s), state)
+    for j in reversed(range(1, z.groups_z)):
+        state = tuple(jnp.where(j > group, a, b) for a, b in zip(down(groups, j, state), state))
+    for j in reversed(range(1, z.members)):
+        state = tuple(jnp.where(j > member, a, b) for a, b in zip(down(blocks, j, state), state))
     for y in ys:
         u, w, total = state[3 * y : 3 * y + 3]
         sums_ref[z.ny + y] = total

time: 40.8 us -> 40.8 us (level)
  no operation moved by 1% of the time
where the time goes in v11:
time: 40.8 us; the launch traced here: 40.6 us
  starting transfers between devices  21.3 us (52%)
  waiting for transfers between devices  12.6 us (31%)
  Pallas kernels  5.56 us (14%)
  other arithmetic  0.95 us (2%)
    ppermute x10, starting transfers between devices, exchange(): return [lax.ppermute(v, 'gz', p) for v, p in zip(values, pairs)]  15.6 us
    ppermute x10, waiting for transfers between devices, exchange(): return [lax.ppermute(v, 'gz', p) for v, p in zip(values, pairs)]  10.4 us
    pallas_call x14, Pallas kernels, call(): pl.pallas_call(functools.partial(kernel, z), out_shape=outs, in_specs=[sp...  5.56 us
    ppermute x3, starting transfers between devices, exchange(): lax.ppermute(v, 'gz', p)  4.45 us
    ppermute x3, waiting for transfers between devices, exchange(): lax.ppermute(v, 'gz', p)  1.96 us
    ppermute x4, starting transfers between devices, shift(): lax.ppermute(value, axis, [(i, (i + by) % count) for i in range(count)])  1.1 us
    concatenate x1, other arithmetic, per_device(): arguments = jnp.concatenate([v.reshape(-1, z.nx) for v in (c, k, warm)])  0.95 us
  transfers between devices with their start and end apart: 18, of which 11 were waited for; matrix products, arithmetic and copies ran while one was open for 0% of the time, Pallas kernels for 8%

profile of v11, /device:TPU:0, one launch (start us, length us, event | category | flops | bytes accessed | tf_op | source)
XLA Modules:
  0.0 40.6 jit_solution(10176999516114993857)
XLA Ops:
  0.0 0.9 %pad_maximum_fusion.c_ref.arguments = f32[288,128]{1,0:T(8,128)S(1)} fusion(f32[16,128]{1,0:T(8,128)} %bitcast.10, f32[16,128]{1,0:T(8,128)} %bitcast.11, f32[256,128]{1,0:T(8,128)} %bitcast.9), kind=kLoop, calls=%fused_computation | loop fusion | flops 73728 | bytes 294912 | tf_op jit(solution)/shard_map/concatenate | solution.py:662
  1.0 0.5 %collective-permute-start.4 = (f32[136,128]{1,0:T(8,128)S(1)}, f32[136,128]{1,0:T(8,128)S(1)}, u32[]{:S(2)}, u32[]{:S(2)}) collective-permute-start(f32[136,128]{1,0:T(8,128)S(1)} %get-tuple-element.49), channel_id=1, source_target_pairs={{0,1},{1,0},{2,3},{3,2},{4,5},{5,4},{6,7},{7,6},{8,9},{9,8},{10,11... | collective-permute-start | bytes 208904 | tf_op jit(solution)/shard_map/ppermute | solution.py:657
  1.5 0.1 collective-permute-start
  1.6 4.0 %collective-permute-start.1 = (f32[40,128]{1,0:T(8,128)S(1)}, f32[40,128]{1,0:T(8,128)S(1)}, u32[]{:S(2)}, u32[]{:S(2)}) collective-permute-start(f32[40,128]{1,0:T(8,128)S(1)} %get-tuple-element.41), channel_id=1, source_target_pairs={{0,2},{2,0},{4,6},{6,4},{8,10},{10,8},{12,14},{14,12},{16,18},{18,... | collective-permute-start | bytes 61448 | tf_op jit(solution)/shard_map/ppermute | solution.py:672
  5.6 0.0 collective-permute-start.2
  5.6 0.5 %collective-permute-start.3 = (f32[16]{0:T(128)S(1)}, f32[16]{0:T(128)S(1)}, u32[]{:S(2)}, u32[]{:S(2)}) collective-permute-start(f32[16]{0:T(128)S(1)} %copy-done.3), channel_id=1, source_target_pairs={{0,1},{1,0},{2,3},{3,2},{4,5},{5,4},{6,7},{7,6},{8,9},{9,8},{10,11... | collective-permute-start | bytes 200 | tf_op jit(solution)/shard_map/ppermute | solution.py:657
  6.1 1.1 %shard_map.74 = (f32[4,16,128]{2,1,0:T(8,128)S(1)}, f32[2,16,128]{2,1,0:T(8,128)S(1)}, f32[7,16,16,128]{3,2,1,0:T(8,128)S(1)}, f32[7,16,16,128]{3,2,1,0:T(8,128)S(1)}, f32[16,16,128]{2,1,0:T(8,128)S(1)}) custom-call(f32[288,128]{1,0:T(8,128)S(1)} %pad_maximum_fusion.c_ref.arguments, f32[1,16]{1,0:T(1,128)S(1)} %bitcast.6), custom_call_target="tpu_custom_call" | custom-call | bytes 3690000 | tf_op jit(solution)/shard_map/pallas_call | solution.py:643
  7.2 0.0 collective-permute-done.2
  7.2 0.0 collective-permute-done.3
  7.2 0.4 shard_map.75
  7.6 0.0 collective-permute-done.4.refs_0_
  7.6 0.7 %shard_map.76 = (f32[16,16,128]{2,1,0:T(8,128)S(1)}, f32[2,16,128]{2,1,0:T(8,128)S(1)}, f32[12,4,16,128]{3,2,1,0:T(8,128)S(1)}) custom-call(f32[288,128]{1,0:T(8,128)S(1)} %pad_maximum_fusion.c_ref.arguments, f32[16,16,128]{2,1,0:T(8,128)S(1)} %get-tuple-element.44.tiles_ref, f32[16,16,128]{2,1,0:T(8,128)S(1)} %get-tuple-element.45.base_ref, ...), custom_call_target="tpu_custom_call" | custom-call | bytes 1845000 | tf_op jit(solution)/shard_map/pallas_call | solution.py:643
  8.3 0.0 collective-permute-done.far_ref
  8.3 0.0 collective-permute-done.1.near_ref
  8.3 0.4 %shard_map.77 = (f32[88,128]{1,0:T(8,128)S(1)}, f32[16,16,128]{2,1,0:T(8,128)S(1)}, f32[2,16,128]{2,1,0:T(8,128)S(1)}) custom-call(f32[288,128]{1,0:T(8,128)S(1)} %pad_maximum_fusion.c_ref.arguments, f32[40,128]{1,0:T(8,128)S(1)} %collective-permute-done.far_ref, f32[40,128]{1,0:T(8,128)S(1)} %collective-permute-done.1.near_ref, ...), custom_call_target="tpu_custom_call" | custom-call | bytes 1845000 | tf_op jit(solution)/shard_map/pallas_call | solution.py:643
  8.7 1.6 %collective-permute-start.7 = (f32[88,128]{1,0:T(8,128)S(1)}, f32[88,128]{1,0:T(8,128)S(1)}, u32[]{:S(2)}, u32[]{:S(2)}) collective-permute-start(f32[88,128]{1,0:T(8,128)S(1)} %get-tuple-element.54.pay_ref.refs_0_), channel_id=1, source_target_pairs={{0,4},{2,6},{4,0},{6,2},{8,12},{10,14},{12,8},{14,10},{16,20},{18,... | collective-permute-start | bytes 135176 | tf_op jit(solution)/shard_map/ppermute | solution.py:672
  10.3 1.1 %collective-permute-start.6 = (f32[88,128]{1,0:T(8,128)S(1)}, f32[88,128]{1,0:T(8,128)S(1)}, u32[]{:S(2)}, u32[]{:S(2)}) collective-permute-start(f32[88,128]{1,0:T(8,128)S(1)} %get-tuple-element.54.pay_ref.refs_0_), channel_id=1, source_target_pairs={{0,6},{2,4},{4,2},{6,0},{8,14},{10,12},{12,10},{14,8},{16,22},{18,... | collective-permute-start | bytes 135176 | tf_op jit(solution)/shard_map/ppermute | solution.py:672
  11.4 0.9 %collective-permute-start.5 = (f32[88,128]{1,0:T(8,128)S(1)}, f32[88,128]{1,0:T(8,128)S(1)}, u32[]{:S(2)}, u32[]{:S(2)}) collective-permute-start(f32[88,128]{1,0:T(8,128)S(1)} %get-tuple-element.54.pay_ref.refs_0_), channel_id=1, source_target_pairs={{0,2},{2,0},{4,6},{6,4},{8,10},{10,8},{12,14},{14,12},{16,18},{18,... | collective-permute-start | bytes 135176 | tf_op jit(solution)/shard_map/ppermute | solution.py:672
  12.3 0.6 %collective-permute-done.7.refs_2_.refs_3_ = f32[88,128]{1,0:T(8,128)S(1)} collective-permute-done((f32[88,128]{1,0:T(8,128)S(1)}, f32[88,128]{1,0:T(8,128)S(1)}, u32[]{:S(2)}, u32[]{:S(2)}) %collective-permute-start.7) | collective-permute-done | bytes 45088 | tf_op jit(solution)/shard_map/ppermute | solution.py:672
  12.8 2.4 %collective-permute-done.6.refs_1_.refs_2_ = f32[88,128]{1,0:T(8,128)S(1)} collective-permute-done((f32[88,128]{1,0:T(8,128)S(1)}, f32[88,128]{1,0:T(8,128)S(1)}, u32[]{:S(2)}, u32[]{:S(2)}) %collective-permute-start.6) | collective-permute-done | bytes 45088 | tf_op jit(solution)/shard_map/ppermute | solution.py:672
  15.2 0.2 collective-permute-done.5.refs_0_.refs_1_
  15.4 0.1 shard_map.78.own_group
  15.6 3.9 %collective-permute-start.8 = (f32[136,128]{1,0:T(8,128)S(1)}, f32[136,128]{1,0:T(8,128)S(1)}, u32[]{:S(2)}, u32[]{:S(2)}) collective-permute-start(f32[136,128]{1,0:T(8,128)S(1)} %shard_map.78.own_group), channel_id=1, source_target_pairs={{0,24},{2,26},{4,28},{6,30},{8,16},{10,18},{12,20},{14,22},{16,8},... | collective-permute-start | bytes 208904 | tf_op jit(solution)/shard_map/ppermute | solution.py:672
  19.5 0.0 collective-permute-start.10
  19.5 0.6 %collective-permute-start.9 = (f32[136,128]{1,0:T(8,128)S(1)}, f32[136,128]{1,0:T(8,128)S(1)}, u32[]{:S(2)}, u32[]{:S(2)}) collective-permute-start(f32[136,128]{1,0:T(8,128)S(1)} %shard_map.78.own_group), channel_id=1, source_target_pairs={{0,8},{2,10},{4,12},{6,14},{8,0},{10,2},{12,4},{14,6},{16,24},{18,... | collective-permute-start | bytes 208904 | tf_op jit(solution)/shard_map/ppermute | solution.py:672
  20.1 0.1 shard_map.79
  20.2 1.5 %collective-permute-done.8.group_ref.refs_2_ = f32[136,128]{1,0:T(8,128)S(1)} collective-permute-done((f32[136,128]{1,0:T(8,128)S(1)}, f32[136,128]{1,0:T(8,128)S(1)}, u32[]{:S(2)}, u32[]{:S(2)}) %collective-permute-start.8) | collective-permute-done | bytes 69664 | tf_op jit(solution)/shard_map/ppermute | solution.py:672
  21.8 0.1 shard_map.80.far_transfer
  21.9 2.8 %collective-permute-done.10.refs_1_ = f32[136,128]{1,0:T(8,128)S(1)} collective-permute-done((f32[136,128]{1,0:T(8,128)S(1)}, f32[136,128]{1,0:T(8,128)S(1)}, u32[]{:S(2)}, u32[]{:S(2)}) %collective-permute-start.10) | collective-permute-done | bytes 69664 | tf_op jit(solution)/shard_map/ppermute | solution.py:672
  24.7 0.4 shard_map.81
  25.1 0.1 collective-permute-start.11
  25.2 0.1 shard_map.82
  25.2 0.9 %shard_map.83 = (f32[16,16,128]{2,1,0:T(8,128)S(1)}, f32[16,16,128]{2,1,0:T(8,128)S(1)}, f32[12,8,16,128]{3,2,1,0:T(8,128)S(1)}) custom-call(f32[16,16,128]{2,1,0:T(8,128)S(1)} %get-tuple-element.61.tiles_ref, f32[4,16,128]{2,1,0:T(8,128)S(1)} %get-tuple-element.62.halo_ref, f32[4,16,128]{2,1,0:T(8,128)S(1)} %get-tuple-element.42.rates_ref, ...), custom_call_target="tpu_custom_call" | custom-call | bytes 1845000 | tf_op jit(solution)/shard_map/pallas_call | solution.py:643
  26.1 0.3 collective-permute-done.11.refs_0_
  26.4 0.5 %shard_map.84 = (f32[2,32,128]{2,1,0:T(8,128)S(1)}, f32[16,16,128]{2,1,0:T(8,128)S(1)}) custom-call(f32[16,16,128]{2,1,0:T(8,128)S(1)} %get-tuple-element.61.tiles_ref, f32[4,16,128]{2,1,0:T(8,128)S(1)} %get-tuple-element.62.halo_ref, f32[4,16,128]{2,1,0:T(8,128)S(1)} %get-tuple-element.42.rates_ref, f32[2,16,128]{2,1,0:T(8,128)S(1)} %get-tuple-element.51.y_faces, ...), custom_call_target="tpu_custom_call" | custom-call | bytes 1845000 | tf_op jit(solution)/shard_map/pallas_call | solution.py:643
  26.9 1.3 %collective-permute-start.14 = (f32[2,32,128]{2,1,0:T(8,128)S(1)}, f32[2,32,128]{2,1,0:T(8,128)S(1)}, u32[]{:S(2)}, u32[]{:S(2)}) collective-permute-start(f32[2,32,128]{2,1,0:T(8,128)S(1)} %get-tuple-element.69.pay_ref), channel_id=1, source_target_pairs={{0,4},{2,6},{4,0},{6,2},{8,12},{10,14},{12,8},{14,10},{16,20},{18,... | collective-permute-start | bytes 98312 | tf_op jit(solution)/shard_map/ppermute | solution.py:672
  28.2 1.3 %collective-permute-start.13 = (f32[2,32,128]{2,1,0:T(8,128)S(1)}, f32[2,32,128]{2,1,0:T(8,128)S(1)}, u32[]{:S(2)}, u32[]{:S(2)}) collective-permute-start(f32[2,32,128]{2,1,0:T(8,128)S(1)} %get-tuple-element.69.pay_ref), channel_id=1, source_target_pairs={{0,6},{2,4},{4,2},{6,0},{8,14},{10,12},{12,10},{14,8},{16,22},{18,... | collective-permute-start | bytes 98312 | tf_op jit(solution)/shard_map/ppermute | solution.py:672
  29.5 0.9 %collective-permute-start.12 = (f32[2,32,128]{2,1,0:T(8,128)S(1)}, f32[2,32,128]{2,1,0:T(8,128)S(1)}, u32[]{:S(2)}, u32[]{:S(2)}) collective-permute-start(f32[2,32,128]{2,1,0:T(8,128)S(1)} %get-tuple-element.69.pay_ref), channel_id=1, source_target_pairs={{0,2},{2,0},{4,6},{6,4},{8,10},{10,8},{12,14},{14,12},{16,18},{18,... | collective-permute-start | bytes 98312 | tf_op jit(solution)/shard_map/ppermute | solution.py:672
  30.5 0.4 %collective-permute-done.14.refs_2_ = f32[2,32,128]{2,1,0:T(8,128)S(1)} collective-permute-done((f32[2,32,128]{2,1,0:T(8,128)S(1)}, f32[2,32,128]{2,1,0:T(8,128)S(1)}, u32[]{:S(2)}, u32[]{:S(2)}) %collective-permute-start.14) | collective-permute-done | bytes 32800 | tf_op jit(solution)/shard_map/ppermute | solution.py:672
  30.9 2.2 %collective-permute-done.13.refs_1_ = f32[2,32,128]{2,1,0:T(8,128)S(1)} collective-permute-done((f32[2,32,128]{2,1,0:T(8,128)S(1)}, f32[2,32,128]{2,1,0:T(8,128)S(1)}, u32[]{:S(2)}, u32[]{:S(2)}) %collective-permute-start.13) | collective-permute-done | bytes 32800 | tf_op jit(solution)/shard_map/ppermute | solution.py:672
  33.0 0.4 collective-permute-done.12.refs_0_
  33.4 1.8 %collective-permute-start.15 = (f32[32,128]{1,0:T(8,128)S(1)}, f32[32,128]{1,0:T(8,128)S(1)}, u32[]{:S(2)}, u32[]{:S(2)}) collective-permute-start(f32[32,128]{1,0:T(8,128)S(1)} %get-tuple-element.72), channel_id=1, source_target_pairs={{0,24},{2,26},{4,28},{6,30},{8,16},{10,18},{12,20},{14,22},{16,8},... | collective-permute-start | bytes 49160 | tf_op jit(solution)/shard_map/ppermute | solution.py:671
  35.2 0.4 collective-permute-start.16
  35.6 2.3 %collective-permute-start.17 = (f32[32,128]{1,0:T(8,128)S(1)}, f32[32,128]{1,0:T(8,128)S(1)}, u32[]{:S(2)}, u32[]{:S(2)}) collective-permute-start(f32[32,128]{1,0:T(8,128)S(1)} %get-tuple-element.74), channel_id=1, source_target_pairs={{0,8},{2,10},{4,12},{6,14},{8,0},{10,2},{12,4},{14,6},{16,24},{18,... | collective-permute-start | bytes 49160 | tf_op jit(solution)/shard_map/ppermute | solution.py:671
  37.9 1.1 %collective-permute-done.15.refs_0_ = f32[32,128]{1,0:T(8,128)S(1)} collective-permute-done((f32[32,128]{1,0:T(8,128)S(1)}, f32[32,128]{1,0:T(8,128)S(1)}, u32[]{:S(2)}, u32[]{:S(2)}) %collective-permute-start.15) | collective-permute-done | bytes 16416 | tf_op jit(solution)/shard_map/ppermute | solution.py:671
  39.0 0.8 %collective-permute-done.16.refs_1_ = f32[32,128]{1,0:T(8,128)S(1)} collective-permute-done((f32[32,128]{1,0:T(8,128)S(1)}, f32[32,128]{1,0:T(8,128)S(1)}, u32[]{:S(2)}, u32[]{:S(2)}) %collective-permute-start.16) | collective-permute-done | bytes 16416 | tf_op jit(solution)/shard_map/ppermute | solution.py:671
  39.9 0.0 collective-permute-done.17.refs_2_
  39.9 0.7 %shard_map.86 = f32[16,2,8,128]{3,2,1,0:T(8,128)} custom-call(f32[2,32,128]{2,1,0:T(8,128)S(1)} %get-tuple-element.70.within_ref, f32[16,16,128]{2,1,0:T(8,128)S(1)} %get-tuple-element.71.f_ref, f32[16,16,128]{2,1,0:T(8,128)S(1)} %get-tuple-element.57.v_ref, f32[16,16,128]{2,1,0:T(8,128)S(1)} %get-tuple-element.58.u_ref, ...), custom_call_target="tpu_custom_call" | custom-call | bytes 1845000 | tf_op jit(solution)/shard_map/pallas_call | solution.py:643
  (11 shorter events, 0.1 us)
Async XLA Ops:
  1.0 6.6 %collective-permute-start.4 = (f32[136,128]{1,0:T(8,128)S(1)}, f32[136,128]{1,0:T(8,128)S(1)}, u32[]{:S(2)}, u32[]{:S(2)}) collective-permute-start(f32[136,128]{1,0:T(8,128)S(1)} %get-tuple-element.49), channel_id=1, source_target_pairs={{0,1},{1,0},{2,3},{3,2},{4,5},{5,4},{6,7},{7,6},{8,9},{9,8},{10,11... | collective-permute-start | bytes 208904 | tf_op jit(solution)/shard_map/ppermute | solution.py:657
  1.5 4.1 %copy-start.2 = (f32[16]{0:T(128)S(1)}, f32[16]{0:T(128)}, u32[]{:S(2)}) copy-start(f32[16]{0:T(128)} %param.11) | copy-start | bytes 196
  1.5 4.1 %copy-start.3 = (f32[16]{0:T(128)S(1)}, f32[16]{0:T(128)}, u32[]{:S(2)}) copy-start(f32[16]{0:T(128)} %param.12) | copy-start | bytes 196
  1.5 6.8 %collective-permute-start = (f32[40,128]{1,0:T(8,128)S(1)}, f32[40,128]{1,0:T(8,128)S(1)}, u32[]{:S(2)}, u32[]{:S(2)}) collective-permute-start(f32[40,128]{1,0:T(8,128)S(1)} %get-tuple-element.40), channel_id=1, source_target_pairs={{2,4},{3,5},{4,2},{5,3},{6,8},{7,9},{8,6},{9,7},{10,12},{11,13},{1... | collective-permute-start | bytes 61448 | tf_op jit(solution)/shard_map/ppermute | solution.py:685
  1.6 4.5 %copy-start.1 = (f32[16]{0:T(128)S(1)}, f32[16]{0:T(128)}, u32[]{:S(2)}) copy-start(f32[16]{0:T(128)} %param.10) | copy-start | bytes 196
  1.6 6.7 %collective-permute-start.1 = (f32[40,128]{1,0:T(8,128)S(1)}, f32[40,128]{1,0:T(8,128)S(1)}, u32[]{:S(2)}, u32[]{:S(2)}) collective-permute-start(f32[40,128]{1,0:T(8,128)S(1)} %get-tuple-element.41), channel_id=1, source_target_pairs={{0,2},{2,0},{4,6},{6,4},{8,10},{10,8},{12,14},{14,12},{16,18},{18,... | collective-permute-start | bytes 61448 | tf_op jit(solution)/shard_map/ppermute | solution.py:672
  5.6 1.6 %collective-permute-start.2 = (f32[16]{0:T(128)S(1)}, f32[16]{0:T(128)S(1)}, u32[]{:S(2)}, u32[]{:S(2)}) collective-permute-start(f32[16]{0:T(128)S(1)} %copy-done.2), channel_id=1, source_target_pairs={{0,1},{1,0},{2,3},{3,2},{4,5},{5,4},{6,7},{7,6},{8,9},{9,8},{10,11... | collective-permute-start | bytes 200 | tf_op jit(solution)/shard_map/ppermute | solution.py:657
  5.6 1.6 %collective-permute-start.3 = (f32[16]{0:T(128)S(1)}, f32[16]{0:T(128)S(1)}, u32[]{:S(2)}, u32[]{:S(2)}) collective-permute-start(f32[16]{0:T(128)S(1)} %copy-done.3), channel_id=1, source_target_pairs={{0,1},{1,0},{2,3},{3,2},{4,5},{5,4},{6,7},{7,6},{8,9},{9,8},{10,11... | collective-permute-start | bytes 200 | tf_op jit(solution)/shard_map/ppermute | solution.py:657
  6.1 1.1 %copy-start = (f32[16,16]{1,0:T(8,128)S(1)}, f32[16,16]{1,0:T(8,128)}, u32[]{:S(2)}) copy-start(f32[16,16]{1,0:T(8,128)} %proportions_ref.3) | copy-start | bytes 3076
  8.7 4.1 %collective-permute-start.7 = (f32[88,128]{1,0:T(8,128)S(1)}, f32[88,128]{1,0:T(8,128)S(1)}, u32[]{:S(2)}, u32[]{:S(2)}) collective-permute-start(f32[88,128]{1,0:T(8,128)S(1)} %get-tuple-element.54.pay_ref.refs_0_), channel_id=1, source_target_pairs={{0,4},{2,6},{4,0},{6,2},{8,12},{10,14},{12,8},{14,10},{16,20},{18,... | collective-permute-start | bytes 135176 | tf_op jit(solution)/shard_map/ppermute | solution.py:672
  10.3 4.9 %collective-permute-start.6 = (f32[88,128]{1,0:T(8,128)S(1)}, f32[88,128]{1,0:T(8,128)S(1)}, u32[]{:S(2)}, u32[]{:S(2)}) collective-permute-start(f32[88,128]{1,0:T(8,128)S(1)} %get-tuple-element.54.pay_ref.refs_0_), channel_id=1, source_target_pairs={{0,6},{2,4},{4,2},{6,0},{8,14},{10,12},{12,10},{14,8},{16,22},{18,... | collective-permute-start | bytes 135176 | tf_op jit(solution)/shard_map/ppermute | solution.py:672
  11.4 4.0 %collective-permute-start.5 = (f32[88,128]{1,0:T(8,128)S(1)}, f32[88,128]{1,0:T(8,128)S(1)}, u32[]{:S(2)}, u32[]{:S(2)}) collective-permute-start(f32[88,128]{1,0:T(8,128)S(1)} %get-tuple-element.54.pay_ref.refs_0_), channel_id=1, source_target_pairs={{0,2},{2,0},{4,6},{6,4},{8,10},{10,8},{12,14},{14,12},{16,18},{18,... | collective-permute-start | bytes 135176 | tf_op jit(solution)/shard_map/ppermute | solution.py:672
  15.6 6.2 %collective-permute-start.8 = (f32[136,128]{1,0:T(8,128)S(1)}, f32[136,128]{1,0:T(8,128)S(1)}, u32[]{:S(2)}, u32[]{:S(2)}) collective-permute-start(f32[136,128]{1,0:T(8,128)S(1)} %shard_map.78.own_group), channel_id=1, source_target_pairs={{0,24},{2,26},{4,28},{6,30},{8,16},{10,18},{12,20},{14,22},{16,8},... | collective-permute-start | bytes 208904 | tf_op jit(solution)/shard_map/ppermute | solution.py:672
  19.5 5.2 %collective-permute-start.10 = (f32[136,128]{1,0:T(8,128)S(1)}, f32[136,128]{1,0:T(8,128)S(1)}, u32[]{:S(2)}, u32[]{:S(2)}) collective-permute-start(f32[136,128]{1,0:T(8,128)S(1)} %shard_map.78.own_group), channel_id=1, source_target_pairs={{0,16},{2,18},{4,20},{6,22},{8,24},{10,26},{12,28},{14,30},{16,0},... | collective-permute-start | bytes 208904 | tf_op jit(solution)/shard_map/ppermute | solution.py:672
  19.5 5.2 %collective-permute-start.9 = (f32[136,128]{1,0:T(8,128)S(1)}, f32[136,128]{1,0:T(8,128)S(1)}, u32[]{:S(2)}, u32[]{:S(2)}) collective-permute-start(f32[136,128]{1,0:T(8,128)S(1)} %shard_map.78.own_group), channel_id=1, source_target_pairs={{0,8},{2,10},{4,12},{6,14},{8,0},{10,2},{12,4},{14,6},{16,24},{18,... | collective-permute-start | bytes 208904 | tf_op jit(solution)/shard_map/ppermute | solution.py:672
  25.1 1.3 %collective-permute-start.11 = (f32[128,128]{1,0:T(8,128)S(1)}, f32[128,128]{1,0:T(8,128)S(1)}, u32[]{:S(2)}, u32[]{:S(2)}) collective-permute-start(f32[128,128]{1,0:T(8,128)S(1)} %get-tuple-element.68), channel_id=1, source_target_pairs={{0,1},{1,0},{2,3},{3,2},{4,5},{5,4},{6,7},{7,6},{8,9},{9,8},{10,11... | collective-permute-start | bytes 196616 | tf_op jit(solution)/shard_map/ppermute | solution.py:657
  26.9 4.0 %collective-permute-start.14 = (f32[2,32,128]{2,1,0:T(8,128)S(1)}, f32[2,32,128]{2,1,0:T(8,128)S(1)}, u32[]{:S(2)}, u32[]{:S(2)}) collective-permute-start(f32[2,32,128]{2,1,0:T(8,128)S(1)} %get-tuple-element.69.pay_ref), channel_id=1, source_target_pairs={{0,4},{2,6},{4,0},{6,2},{8,12},{10,14},{12,8},{14,10},{16,20},{18,... | collective-permute-start | bytes 98312 | tf_op jit(solution)/shard_map/ppermute | solution.py:672
  28.2 4.8 %collective-permute-start.13 = (f32[2,32,128]{2,1,0:T(8,128)S(1)}, f32[2,32,128]{2,1,0:T(8,128)S(1)}, u32[]{:S(2)}, u32[]{:S(2)}) collective-permute-start(f32[2,32,128]{2,1,0:T(8,128)S(1)} %get-tuple-element.69.pay_ref), channel_id=1, source_target_pairs={{0,6},{2,4},{4,2},{6,0},{8,14},{10,12},{12,10},{14,8},{16,22},{18,... | collective-permute-start | bytes 98312 | tf_op jit(solution)/shard_map/ppermute | solution.py:672
  29.5 3.9 %collective-permute-start.12 = (f32[2,32,128]{2,1,0:T(8,128)S(1)}, f32[2,32,128]{2,1,0:T(8,128)S(1)}, u32[]{:S(2)}, u32[]{:S(2)}) collective-permute-start(f32[2,32,128]{2,1,0:T(8,128)S(1)} %get-tuple-element.69.pay_ref), channel_id=1, source_target_pairs={{0,2},{2,0},{4,6},{6,4},{8,10},{10,8},{12,14},{14,12},{16,18},{18,... | collective-permute-start | bytes 98312 | tf_op jit(solution)/shard_map/ppermute | solution.py:672
  33.4 5.6 %collective-permute-start.15 = (f32[32,128]{1,0:T(8,128)S(1)}, f32[32,128]{1,0:T(8,128)S(1)}, u32[]{:S(2)}, u32[]{:S(2)}) collective-permute-start(f32[32,128]{1,0:T(8,128)S(1)} %get-tuple-element.72), channel_id=1, source_target_pairs={{0,24},{2,26},{4,28},{6,30},{8,16},{10,18},{12,20},{14,22},{16,8},... | collective-permute-start | bytes 49160 | tf_op jit(solution)/shard_map/ppermute | solution.py:671
  35.2 4.6 %collective-permute-start.16 = (f32[32,128]{1,0:T(8,128)S(1)}, f32[32,128]{1,0:T(8,128)S(1)}, u32[]{:S(2)}, u32[]{:S(2)}) collective-permute-start(f32[32,128]{1,0:T(8,128)S(1)} %get-tuple-element.73), channel_id=1, source_target_pairs={{0,16},{2,18},{4,20},{6,22},{8,24},{10,26},{12,28},{14,30},{16,0},... | collective-permute-start | bytes 49160 | tf_op jit(solution)/shard_map/ppermute | solution.py:671
  35.6 4.2 %collective-permute-start.17 = (f32[32,128]{1,0:T(8,128)S(1)}, f32[32,128]{1,0:T(8,128)S(1)}, u32[]{:S(2)}, u32[]{:S(2)}) collective-permute-start(f32[32,128]{1,0:T(8,128)S(1)} %get-tuple-element.74), channel_id=1, source_target_pairs={{0,8},{2,10},{4,12},{6,14},{8,0},{10,2},{12,4},{14,6},{16,24},{18,... | collective-permute-start | bytes 49160 | tf_op jit(solution)/shard_map/ppermute | solution.py:671
